TPU v7x, 256 devices: a whole 4x4x8 slice. The times are simulated.
256 devices in a mesh: rep: 16 (over y, x_hi, core), fsdp: 16 (over x_lo, z).
Axes of the slice: x: 4 (x_hi: 2, x_lo: 2; x = x_hi * 2 + x_lo), y: 4, z: 8, core: 2. Of those that a mesh axis runs over, the one named last changes fastest.
Arguments:
- activations: bfloat16 [16, 4096, 5120], P('rep', 'fsdp'), may hold values from -6 to 6
- key_weights: bfloat16 [16, 5120, 1024], P('rep', 'fsdp'), may hold values from -0.078125 to 0.078125
- key_cotangent: bfloat16 [16, 4096, 1024], P('rep', 'fsdp'), may hold values from -6 to 6
- fragment: bfloat16 [5120, 1024], P('fsdp'), may hold values from -3 to 3
- pseudo_grads: float32 [16, 5120, 1024], P('rep', 'fsdp'), may hold values from -6 to 6
- momentum: float32 [5120, 1024], P('fsdp', 'rep'), may hold values from -6 to 6
Outputs:
- key_out: bfloat16 [16, 4096, 1024], P('rep', 'fsdp')
- act_grad: bfloat16 [16, 4096, 5120], P('rep', 'fsdp')
- weight_grad: bfloat16 [16, 5120, 1024], P('rep', 'fsdp')
- new_fragment: bfloat16 [5120, 1024], P('fsdp')
- new_momentum: float32 [5120, 1024], P('fsdp', 'rep')
All inputs are finite; a program needn't handle non-finite values.
Results may differ from a plain program's by a relative error of at most 0.00125.
Values may be sent and summed in bfloat16 or wider, within the bound.
No kernel may reach another device: no remote copies, remote signals or barrier semaphores. Data moves between devices by JAX's collectives and lax.ppermute only.
A program may use at most 128 MiB of HBM per device.

v0:
```python
import jax
import jax.numpy as jnp
from jax import lax
from jax.sharding import Mesh
from jax.sharding import PartitionSpec as P

OUTER_RATE = 0.7
NESTEROV = 0.9
BF16 = jnp.bfloat16
F32 = jnp.float32
F16 = jnp.float16

SIZES = {"y": 4, "xh": 2, "c": 2, "xl": 2, "z": 8}
REP = ("y", "xh", "c")
FSDP = ("xl", "z")
N_Z = 8
EVEN = [(i, i ^ 1) for i in range(N_Z)]
ODD = [(i, (i - 1) % N_Z if i % 2 == 0 else (i + 1) % N_Z) for i in range(N_Z)]


def swap(value, axis, mask=1):
    return lax.ppermute(value, axis, [(i, i ^ mask) for i in range(SIZES[axis])])


class Sequence:
    def __init__(self):
        self.last = ()

    def step(self, *values):
        held = lax.optimization_barrier((*values, *self.last))[: len(values)]
        return held[0] if len(held) == 1 else held

    def did(self, *values):
        self.last = values


def rows_of(array, start, size):
    return lax.dynamic_slice_in_dim(array, start, size, 0)


def columns_of(array, start, size):
    return lax.dynamic_slice_in_dim(array, start, size, 1)


def in_order(here, mine, theirs, axis):
    first = here == 0
    return jnp.concatenate(
        [jnp.where(first, mine, theirs), jnp.where(first, theirs, mine)], axis=axis
    )


def encode(scaled):
    return (scaled * jnp.abs(scaled)).astype(F16)


def decode(sent):
    wide = sent.astype(F32)
    return jnp.sign(wide) * jnp.sqrt(jnp.abs(wide))


def local_peaks(tokens, cotangent):
    peak_a = jnp.max(jnp.sum(jnp.abs(tokens.astype(F32)), axis=0))
    peak_c = jnp.max(jnp.abs(cotangent)).astype(F32)
    row = lax.broadcasted_iota(jnp.int32, (8, 128), 0)
    return jnp.where(row < 4, peak_a, peak_c)


def join_peaks(peaks, other):
    row = lax.broadcasted_iota(jnp.int32, (8, 128), 0)
    return jnp.where(row < 4, peaks + other, jnp.maximum(peaks, other))


def shards(activations, key_weights, key_cotangent, fragment, pseudo_grads, momentum):
    tokens, weight, cotangent, pseudo = (
        a[0] for a in (activations, key_weights, key_cotangent, pseudo_grads)
    )
    y, xh, c, x, z = (lax.axis_index(a) for a in SIZES)
    order = Sequence()
    half = tokens.shape[1] // 2
    cut = weight.shape[1] * 3 // 4
    rows = pseudo.shape[0] // 2
    mine, theirs = c * rows, (1 - c) * rows
    width = momentum.shape[1]
    pair = 2 * width

    weight_left = lax.all_gather(weight[:, :cut], "z", axis=0, tiled=True)

    give = rows_of(pseudo, theirs, rows)
    order.did(give)
    pseudo_other = swap(give, "c")
    peaks = local_peaks(order.step(tokens), cotangent)
    order.did(peaks)
    peaks_other = swap(peaks, "xl")
    total = rows_of(pseudo, mine, rows) + order.step(pseudo_other)

    def every_other(array, first):
        parts = [columns_of(array, (2 * k + first) * pair, pair) for k in range(4)]
        return jnp.concatenate(parts, axis=1)

    give = every_other(total, 1 - xh)
    order.did(give)
    total_other = swap(give, "xh")
    sent = columns_of(order.step(tokens), (1 - x) * half, half)
    sent = jnp.concatenate([sent, cotangent], axis=1)
    order.did(sent)
    pair_other = swap(sent, "xl")
    peaks = join_peaks(peaks, order.step(peaks_other))
    order.did(peaks)
    peaks_other = swap(peaks, "z", 1)
    old_give = rows_of(order.step(momentum), theirs, rows)
    order.did(old_give)
    old_other = swap(old_give, "c")
    peaks = join_peaks(peaks, order.step(peaks_other))
    order.did(peaks)
    peaks_other = swap(peaks, "z", 2)
    total = every_other(total, xh) + order.step(total_other)
    gives = [columns_of(total, (y ^ m) * pair, pair) for m in (1, 2, 3)]
    order.did(*gives)
    others = [swap(g, "y", m) for g, m in zip(gives, (1, 2, 3))]
    peaks = join_peaks(peaks, order.step(peaks_other))
    order.did(peaks)
    peaks_other = swap(peaks, "z", 4)

    *others, old_other = order.step(*others, old_other)
    summed = columns_of(total, y * pair, pair) + others[0] + others[1] + others[2]
    average = summed / 16
    old = in_order(c, rows_of(momentum, mine, rows), old_other, 1)
    new = NESTEROV * old + average
    here = lax.dynamic_slice(fragment, (mine, (2 * y + xh) * pair), (rows, pair))
    updated = (here.astype(F32) - OUTER_RATE * (average + NESTEROV * new)).astype(BF16)
    keep = jnp.where(c == 0, new[:, :width], new[:, width:])
    give = jnp.where(c == 0, new[:, width:], new[:, :width])
    order.did(updated, keep, give)
    updates = [swap(updated, "y", m) for m in (1, 2, 3)]
    new_other = swap(give, "c")
    weight_right = lax.all_gather(order.step(weight)[:, cut:], "z", axis=0, tiled=True)
    peaks = join_peaks(peaks, order.step(peaks_other))
    bound = jnp.maximum(peaks[0, 0] * peaks[4, 0], 1e-32)
    scale, back = 240.0 / bound, bound / (64.0 * 240.0)
    tokens_mine = columns_of(tokens, x * half, half)
    order.did(scale, back, tokens_mine)
    *updates, new_other = order.step(*updates, new_other)
    new_momentum = in_order(c, keep, new_other, 0)
    wide = jnp.zeros((rows, 4 * pair), BF16)
    wide = lax.dynamic_update_slice(wide, updated, (0, y * pair))
    for got, m in zip(updates, (1, 2, 3)):
        wide = lax.dynamic_update_slice(wide, got, (0, (y ^ m) * pair))
    order.did(wide, new_momentum)
    wide_other = swap(wide, "xh")

    pair_other = order.step(pair_other)
    tokens_other, cotangent_other = pair_other[:, :half], pair_other[:, half:]
    partial = lax.dot_general(
        jnp.concatenate([tokens_mine, tokens_other], axis=0),
        jnp.concatenate([cotangent, cotangent_other], axis=0),
        (((0,), (0,)), ((), ())),
        preferred_element_type=F32,
    )
    order.did(partial)
    chunk = partial.shape[0] // N_Z
    part = chunk // 2
    sign = 1 - 2 * (z % 2)

    def own(distance, start=0, size=chunk):
        return rows_of(partial, (z + N_Z + distance) % N_Z * chunk + start, size) * scale

    def send(even, odd):
        even, odd = encode(even), encode(odd)
        order.did(even, odd)
        return lax.ppermute(even, "z", EVEN), lax.ppermute(odd, "z", ODD)

    def ring_step(distance, got):
        even_in, odd_in = order.step(*got)
        return send(own(sign * distance) + decode(odd_in), own(-sign * distance) + decode(even_in))

    def keys(left, right):
        return jnp.dot(left, right, preferred_element_type=F32)

    def grads(left, right):
        return lax.dot_general(left, right, (((1,), (1,)), ((), ())), preferred_element_type=F32)

    far = send(own(4, 0, part), own(4, part, part))

    weight_left = order.step(weight_left)
    keys_left = keys(tokens_other, weight_left)
    grads_left = grads(cotangent_other[:, :cut], weight_left)
    order.did(keys_left, grads_left)
    keys_left_back = swap(keys_left, "xl")

    even_in, odd_in = order.step(*far)
    even = jnp.concatenate([own(3 * sign, 0, part), own(3 * sign, part, part) + decode(odd_in)])
    odd = jnp.concatenate([own(-3 * sign, 0, part) + decode(even_in), own(-3 * sign, part, part)])
    ring = send(even, odd)

    wide_other = order.step(wide_other)
    first = jnp.where(xh == 0, wide, wide_other)
    second = jnp.where(xh == 0, wide_other, wide)
    block = jnp.concatenate(
        [side[:, k * pair : (k + 1) * pair] for k in range(4) for side in (first, second)], axis=1
    )
    order.did(block)
    block_other = swap(block, "c")

    weight_right = order.step(weight_right)
    keys_right = keys(tokens_other, weight_right)
    grads_other = (grads_left + grads(cotangent_other[:, cut:], weight_right)).astype(BF16)
    order.did(keys_right, grads_other)
    grads_back = swap(grads_other, "xl")
    keys_right_back = swap(keys_right, "xl")

    key_left = (keys(tokens_mine, weight_left) + order.step(keys_left_back)).astype(BF16)
    order.did(key_left)
    ring = ring_step(2, ring)
    new_fragment = in_order(c, block, order.step(block_other), 0)
    key_right = keys(tokens_mine, weight_right)
    grads_mine = grads(cotangent[:, :cut], weight_left)
    grads_mine = (grads_mine + grads(cotangent[:, cut:], weight_right)).astype(BF16)
    order.did(new_fragment, key_right, grads_mine)
    ring = ring_step(1, ring)
    even_in, odd_in = order.step(*ring)
    weight_grad = ((own(0) + decode(even_in) + decode(odd_in)) * back).astype(BF16)
    order.did(weight_grad)
    keys_right_back, grads_back = order.step(keys_right_back, grads_back)
    key_right = (key_right + keys_right_back).astype(BF16)
    return (
        jnp.concatenate([key_left, key_right], axis=1)[None],
        in_order(x, grads_mine, grads_back, 1)[None],
        weight_grad[None],
        new_fragment,
        new_momentum,
    )


def solution(mesh):
    fine = Mesh(mesh.devices.reshape(tuple(SIZES.values())), tuple(SIZES))
    return jax.shard_map(
        shards,
        mesh=fine,
        in_specs=(
            P(REP, FSDP, None),
            P(REP, FSDP, None),
            P(REP, FSDP, None),
            P(FSDP, None),
            P(REP, FSDP, None),
            P(FSDP, REP),
        ),
        out_specs=(
            P(REP, FSDP, None),
            P(REP, FSDP, None),
            P(REP, FSDP, None),
            P(FSDP, None),
            P(FSDP, REP),
        ),
        check_vma=False,
    )
```

profile of v0, /device:TPU:2, one launch (start us, length us, event | category | flops | bytes accessed | tf_op | source)
XLA Modules:
  0.0 179.8 jit_solution(5643549709694390195)
XLA Ops:
  7.2 2.0 %slice.84 = bf16[320,768]{1,0:T(8,128)(2,1)} slice(bf16[320,1024]{1,0:T(8,128)(2,1)} %bitcast.36), slice={[0:320], [0:768]} | slice | bytes 983040 | tf_op jit(solution)/shard_map/slice | solution.py:86
  9.3 2.0 %dynamic-slice_bitcast_fusion.1 = f32[160,1024]{1,0:T(8,128)} fusion(f32[1,320,1024]{2,1,0:T(8,128)} %param.10, s32[]{:T(128)S(6)} %select_n.220), kind=kLoop, calls=%fused_computation.81 | loop fusion | bytes 1310724 | tf_op jit(solution)/shard_map/dynamic_slice | solution.py:38
  15.6 2.3 %collective-permute-start.3 = (f32[8,128]{1,0:T(8,128)}, f32[8,128]{1,0:T(8,128)}, u32[]{:S(2)}, u32[]{:S(2)}) collective-permute-start(f32[8,128]{1,0:T(8,128)} %iota.31), channel_id=1, source_target_pairs={{0,8},{8,0},{1,9},{9,1},{2,10},{10,2},{3,11},{11,3},{4,12},{12,4},... | collective-permute-start | bytes 12296 | tf_op jit(solution)/shard_map/ppermute | solution.py:22
  18.2 1.2 dynamic-slice_bitcast_fusion
  20.0 1.2 bitcast_add_fusion
  22.8 1.3 pad_maximum_fusion
  25.0 1.9 %collective-permute-start.4 = (f32[8,128]{1,0:T(8,128)S(1)}, f32[8,128]{1,0:T(8,128)S(1)}, u32[]{:S(2)}, u32[]{:S(2)}) collective-permute-start(f32[8,128]{1,0:T(8,128)S(1)} %maximum_select_fusion.3), channel_id=1, source_target_pairs={{0,1},{1,0},{2,3},{3,2},{4,5},{5,4},{6,7},{7,6},{8,9},{9,8},{10,11... | collective-permute-start | bytes 12296 | tf_op jit(solution)/shard_map/ppermute | solution.py:22
  26.9 1.8 %collective-permute-start.1 = (bf16[256,3584]{1,0:T(8,128)(2,1)}, bf16[256,3584]{1,0:T(8,128)(2,1)S(1)}, u32[]{:S(2)}, u32[]{:S(2)}) collective-permute-start(bf16[256,3584]{1,0:T(8,128)(2,1)} %pad_maximum_fusion), channel_id=1, source_target_pairs={{0,8},{8,0},{1,9},{9,1},{2,10},{10,2},{3,11},{11,3},{4,12},{12,4},... | collective-permute-start | bytes 5505032 | tf_op jit(solution)/shard_map/ppermute | solution.py:22
  29.7 3.3 %collective-permute-start.9 = (f32[8,128]{1,0:T(8,128)S(1)}, f32[8,128]{1,0:T(8,128)S(1)}, u32[]{:S(2)}, u32[]{:S(2)}) collective-permute-start(f32[8,128]{1,0:T(8,128)S(1)} %maximum_select_fusion.2), channel_id=1, source_target_pairs={{0,2},{1,3},{2,0},{3,1},{4,6},{5,7},{6,4},{7,5},{8,10},{9,11},{10,... | collective-permute-start | bytes 12296 | tf_op jit(solution)/shard_map/ppermute | solution.py:22
  33.0 1.5 collective-permute-done.2
  34.4 1.0 maximum_add_fusion
  35.7 2.9 %collective-permute-start.6 = (f32[160,128]{1,0:T(8,128)S(1)}, f32[160,128]{1,0:T(8,128)S(1)}, u32[]{:S(2)}, u32[]{:S(2)}) collective-permute-start(f32[160,128]{1,0:T(8,128)S(1)} %get-tuple-element.106), channel_id=1, source_target_pairs={{0,128},{64,192},{128,0},{192,64},{1,129},{65,193},{129,1},{193,65... | collective-permute-start | bytes 245768 | tf_op jit(solution)/shard_map/ppermute | solution.py:22
  38.6 1.7 collective-permute-start.7
  40.4 5.5 %collective-permute-start.14 = (f32[8,128]{1,0:T(8,128)S(1)}, f32[8,128]{1,0:T(8,128)S(1)}, u32[]{:S(2)}, u32[]{:S(2)}) collective-permute-start(f32[8,128]{1,0:T(8,128)S(1)} %maximum_select_fusion.1), channel_id=1, source_target_pairs={{0,4},{1,5},{2,6},{3,7},{4,0},{5,1},{6,2},{7,3},{8,12},{9,13},{10,... | collective-permute-start | bytes 12296 | tf_op jit(solution)/shard_map/ppermute | solution.py:22
  47.3 4.1 %collective-permute-start.11 = (bf16[160,128]{1,0:T(8,128)(2,1)S(1)}, bf16[160,128]{1,0:T(8,128)(2,1)S(1)}, u32[]{:S(2)}, u32[]{:S(2)}) collective-permute-start(bf16[160,128]{1,0:T(8,128)(2,1)S(1)} %get-tuple-element.79), channel_id=1, source_target_pairs={{0,128},{64,192},{128,0},{192,64},{1,129},{65,193},{129,1},{193,65... | collective-permute-start | bytes 122888 | tf_op jit(solution)/shard_map/ppermute | solution.py:22
  52.4 1.6 slice.71
  55.4 1.2 collective-permute-done.12
  56.7 2.7 %collective-permute-start.16 = (bf16[160,512]{1,0:T(8,128)(2,1)S(1)}, bf16[160,512]{1,0:T(8,128)(2,1)}, u32[]{:S(2)}, u32[]{:S(2)}) collective-permute-start(bf16[160,512]{1,0:T(8,128)(2,1)S(1)} %constant_dynamic-update-slice_fusion), channel_id=1, source_target_pairs={{0,32},{32,0},{1,33},{33,1},{2,34},{34,2},{3,35},{35,3},{4,36},{36... | collective-permute-start | bytes 491528 | tf_op jit(solution)/shard_map/ppermute | solution.py:22
  60.0 12.5 %collective-permute-done.1 = bf16[256,3584]{1,0:T(8,128)(2,1)S(1)} collective-permute-done((bf16[256,3584]{1,0:T(8,128)(2,1)}, bf16[256,3584]{1,0:T(8,128)(2,1)S(1)}, u32[]{:S(2)}, u32[]{:S(2)}) %collective-permute-start.1) | collective-permute-done | bytes 1835040 | tf_op jit(solution)/shard_map/ppermute | solution.py:22
  72.7 2.9 %fusion.3 = f32[2560,1024]{1,0:T(8,128)S(1)} fusion(bf16[256,2560]{1,0:T(8,128)(2,1)S(1)} %slice.69, bf16[256,2560]{1,0:T(8,128)(2,1)S(1)} %copy-done.4, bf16[256,1024]{1,0:T(8,128)(2,1)S(1)} %slice.70, bf16[256,1024]{1,0:T(8,128)(2,1)S(1)} %bitcast.32), kind=kOutput, calls=%fused_computation.6 | convolution fusion | flops 2691694592 | bytes 14155776 | tf_op jit(solution)/shard_map/dot_general | solution.py:153
  75.7 3.9 %copy-done.2 = f32[2560,1024]{1,0:T(8,128)} copy-done((f32[2560,1024]{1,0:T(8,128)}, f32[2560,1024]{1,0:T(8,128)S(1)}, u32[]{:S(2)}) %copy-start.2) | copy-done | bytes 10485784
  79.6 1.0 fusion.43
  80.6 1.9 %collective-permute-start.17 = (f16[160,1024]{1,0:T(8,128)(2,1)}, f16[160,1024]{1,0:T(8,128)(2,1)S(1)}, u32[]{:S(2)}, u32[]{:S(2)}) collective-permute-start(f16[160,1024]{1,0:T(8,128)(2,1)} %get-tuple-element.90), channel_id=1, source_target_pairs={{0,1},{1,0},{2,3},{3,2},{4,5},{5,4},{6,7},{7,6},{8,9},{9,8},{10,11... | collective-permute-start | bytes 983048 | tf_op jit(solution)/shard_map/ppermute | solution.py:170
  82.6 4.9 %collective-permute-start.18 = (f16[160,1024]{1,0:T(8,128)(2,1)}, f16[160,1024]{1,0:T(8,128)(2,1)S(1)}, u32[]{:S(2)}, u32[]{:S(2)}) collective-permute-start(f16[160,1024]{1,0:T(8,128)(2,1)} %get-tuple-element.89), channel_id=1, source_target_pairs={{0,7},{1,2},{2,1},{3,4},{4,3},{5,6},{6,5},{7,0},{8,15},{9,10},{10,... | collective-permute-start | bytes 983048 | tf_op jit(solution)/shard_map/ppermute | solution.py:170
  87.5 4.3 %fusion.54 = f32[256,768]{1,0:T(8,128)} fusion(bf16[2560,768]{1,0:T(8,128)(2,1)} %all-gather.3.cloned.1.call-done, bf16[256,3584]{1,0:T(8,128)(2,1)S(1)} %collective-permute-done.1), kind=kOutput, calls=%fused_computation.143 | convolution fusion | flops 1006632960 | bytes 6029312 | tf_op jit(solution)/shard_map/dot_general | solution.py:177
  92.1 2.7 %fusion.46 = f32[256,2560]{1,0:T(8,128)} fusion(bf16[2560,768]{1,0:T(8,128)(2,1)S(1)} %copy-done, bf16[256,3584]{1,0:T(8,128)(2,1)S(1)} %collective-permute-done.1), kind=kOutput, calls=%fused_computation.86 | convolution fusion | flops 1006632960 | bytes 6946816 | tf_op jit(solution)/shard_map/dot_general | solution.py:180
  94.8 5.0 %collective-permute-done.18 = f16[160,1024]{1,0:T(8,128)(2,1)S(1)} collective-permute-done((f16[160,1024]{1,0:T(8,128)(2,1)}, f16[160,1024]{1,0:T(8,128)(2,1)S(1)}, u32[]{:S(2)}, u32[]{:S(2)}) %collective-permute-start.18) | collective-permute-done | bytes 327712 | tf_op jit(solution)/shard_map/ppermute | solution.py:170
  99.8 2.5 %fusion.40 = (f32[160,1024]{1,0:T(8,128)S(1)}, f32[160,1024]{1,0:T(8,128)S(1)}, f32[160,1024]{1,0:T(8,128)S(1)}, f32[160,1024]{1,0:T(8,128)S(1)}) fusion(f16[160,1024]{1,0:T(8,128)(2,1)S(1)} %collective-permute-done.17, f32[2560,1024]{1,0:T(8,128)} %copy-done.2, s32[]{:T(128)S(6)} %select_n.256, f32[]{:T(128)} %bitcast.6, s32[]{:T(128)S(6)} %select_n.257, ...), kind=kLoop, calls=%fused_computation.73 | loop fusion | flops 2293760 | bytes 5898260 | tf_op jit(solution)/shard_map/add | solution.py:192
  104.3 3.4 %collective-permute-start.22 = (f16[320,1024]{1,0:T(8,128)(2,1)}, f16[320,1024]{1,0:T(8,128)(2,1)}, u32[]{:S(2)}, u32[]{:S(2)}) collective-permute-start(f16[320,1024]{1,0:T(8,128)(2,1)} %fusion.28), channel_id=1, source_target_pairs={{0,7},{1,2},{2,1},{3,4},{4,3},{5,6},{6,5},{7,0},{8,15},{9,10},{10,... | collective-permute-start | bytes 1966088 | tf_op jit(solution)/shard_map/ppermute | solution.py:170
  109.2 1.2 fusion.44
  110.4 2.1 %fusion.58 = f32[256,768]{1,0:T(8,128)} fusion(bf16[256,2560]{1,0:T(8,128)(2,1)S(1)} %copy-done.5, bf16[2560,768]{1,0:T(8,128)(2,1)S(1)} %copy-done), kind=kOutput, calls=%fused_computation.146 | convolution fusion | flops 1006632960 | bytes 6029312 | tf_op jit(solution)/shard_map/dot_general | solution.py:177
  112.5 3.9 %fusion = bf16[256,2560]{1,0:T(8,128)(2,1)} fusion(f32[256,2560]{1,0:T(8,128)} %fusion.46, bf16[2560,256]{1,0:T(8,128)(2,1)} %all-gather.5.cloned.1.call-done, bf16[256,3584]{1,0:T(8,128)(2,1)} %copy-done.9), kind=kOutput, calls=%fused_computation.3 | convolution fusion | flops 336855040 | bytes 5373952 | tf_op jit(solution)/shard_map/dot_general | solution.py:180
  116.4 1.2 fusion.52
  117.7 1.6 fusion.2
  119.3 1.2 add_convert_fusion
  120.6 4.1 %fusion.30 = (f16[320,1024]{1,0:T(8,128)(2,1)S(1)}, f16[320,1024]{1,0:T(8,128)(2,1)S(1)}) fusion(f16[320,1024]{1,0:T(8,128)(2,1)} %collective-permute-done.21, f32[2560,1024]{1,0:T(8,128)} %copy-done.2, s32[]{:T(128)S(6)} %select_n.267, f32[]{:T(128)} %bitcast.6, f16[320,1024]{1,0:T(8,128)(2,1)} %collective-permute-done.22, s32[]{:T(128)S(6)} %select_n.265), kind=kLoop, calls=%fused_computation.53 | loop fusion | flops 5898240 | bytes 5242892 | tf_op jit(solution)/shard_map/convert_element_type | solution.py:53
  125.1 3.0 %collective-permute-start.24 = (f16[320,1024]{1,0:T(8,128)(2,1)S(1)}, f16[320,1024]{1,0:T(8,128)(2,1)S(1)}, u32[]{:S(2)}, u32[]{:S(2)}) collective-permute-start(f16[320,1024]{1,0:T(8,128)(2,1)S(1)} %get-tuple-element.83), channel_id=1, source_target_pairs={{0,7},{1,2},{2,1},{3,4},{4,3},{5,6},{6,5},{7,0},{8,15},{9,10},{10,... | collective-permute-start | bytes 1966088 | tf_op jit(solution)/shard_map/ppermute | solution.py:170
  128.7 1.0 broadcast_select_fusion.3
  130.7 11.2 %collective-permute-done.23 = f16[320,1024]{1,0:T(8,128)(2,1)S(1)} collective-permute-done((f16[320,1024]{1,0:T(8,128)(2,1)S(1)}, f16[320,1024]{1,0:T(8,128)(2,1)S(1)}, u32[]{:S(2)}, u32[]{:S(2)}) %collective-permute-start.23) | collective-permute-done | bytes 655392 | tf_op jit(solution)/shard_map/ppermute | solution.py:170
  141.9 1.3 collective-permute-done.24
  143.2 3.6 %fusion.32 = (f16[320,1024]{1,0:T(8,128)(2,1)S(1)}, f16[320,1024]{1,0:T(8,128)(2,1)S(1)}) fusion(f16[320,1024]{1,0:T(8,128)(2,1)S(1)} %collective-permute-done.23, f32[2560,1024]{1,0:T(8,128)} %copy-done.2, s32[]{:T(128)S(6)} %select_n.272, f32[]{:T(128)} %bitcast.6, f16[320,1024]{1,0:T(8,128)(2,1)S(1)} %collective-permute-done.24, s32[]{:T(128)S(6)} %select_n.263), kind=kLoop, calls=%fused_computation.55 | loop fusion | flops 5898240 | bytes 5242892 | tf_op jit(solution)/shard_map/convert_element_type | solution.py:53
  147.3 2.4 %collective-permute-start.27 = (f16[320,1024]{1,0:T(8,128)(2,1)S(1)}, f16[320,1024]{1,0:T(8,128)(2,1)S(1)}, u32[]{:S(2)}, u32[]{:S(2)}) collective-permute-start(f16[320,1024]{1,0:T(8,128)(2,1)S(1)} %get-tuple-element.81), channel_id=1, source_target_pairs={{0,7},{1,2},{2,1},{3,4},{4,3},{5,6},{6,5},{7,0},{8,15},{9,10},{10,... | collective-permute-start | bytes 1966088 | tf_op jit(solution)/shard_map/ppermute | solution.py:170
  150.6 1.4 collective-permute-start.19
  152.0 11.0 %collective-permute-done.26 = f16[320,1024]{1,0:T(8,128)(2,1)S(1)} collective-permute-done((f16[320,1024]{1,0:T(8,128)(2,1)S(1)}, f16[320,1024]{1,0:T(8,128)(2,1)S(1)}, u32[]{:S(2)}, u32[]{:S(2)}) %collective-permute-start.26) | collective-permute-done | bytes 655392 | tf_op jit(solution)/shard_map/ppermute | solution.py:170
  162.9 1.4 collective-permute-done.27
  164.4 3.8 %fusion.23 = bf16[320,1024]{1,0:T(8,128)(2,1)} fusion(f16[320,1024]{1,0:T(8,128)(2,1)S(1)} %collective-permute-done.26, f16[320,1024]{1,0:T(8,128)(2,1)S(1)} %collective-permute-done.27, f32[2560,1024]{1,0:T(8,128)} %copy-done.2, s32[]{:T(128)S(6)} %select_n.261, f32[]{:T(128)} %bitcast.7, f32[]{:T(128)} %bitcast.6), kind=kLoop, calls=%fused_computation.46 | loop fusion | flops 4259840 | bytes 3276812 | tf_op jit(solution)/shard_map/convert_element_type | solution.py:221
  169.7 1.5 broadcast_select_fusion.1
  171.2 1.8 %maximum_bitcast_fusion = bf16[1,256,5120]{2,1,0:T(8,128)(2,1)} fusion(bf16[256,2560]{1,0:T(8,128)(2,1)S(1)} %get-tuple-element.92, bf16[256,2560]{1,0:T(8,128)(2,1)S(1)} %get-tuple-element.91), kind=kLoop, calls=%fused_computation.10 | loop fusion | flops 5242880 | bytes 5242880 | tf_op jit(solution)/shard_map/broadcast_in_dim | solution.py:227
  (127 shorter events, 20.1 us)
Async XLA Ops:
  7.2 80.3 %all-gather.3.cloned.1.call-start = ((), (), s32[]{:S(2)}) async-start(), calls=%async_computation | async-start | bytes 4423680 | tf_op jit(solution)/shard_map/all_gather | solution.py:86
  7.2 4.1 %copy-start.8 = (bf16[1,256,1024]{2,1,0:T(8,128)(2,1)S(1)}, bf16[1,256,1024]{2,1,0:T(8,128)(2,1)}, u32[]{:S(2)}) copy-start(bf16[1,256,1024]{2,1,0:T(8,128)(2,1)} %param.8) | copy-start | bytes 1572868
  7.2 5.4 %copy-start.3 = (bf16[1,256,5120]{2,1,0:T(8,128)(2,1)S(1)}, bf16[1,256,5120]{2,1,0:T(8,128)(2,1)}, u32[]{:S(2)}) copy-start(bf16[1,256,5120]{2,1,0:T(8,128)(2,1)} %param.6) | copy-start | bytes 7864324
  9.2 103.2 %all-gather.5.cloned.1.call-start = ((), (), s32[]{:S(2)}) async-start(), calls=%async_computation.1 | async-start | bytes 1474560 | tf_op jit(solution)/shard_map/all_gather | solution.py:136
  11.3 8.1 %collective-permute-start = (f32[160,1024]{1,0:T(8,128)}, f32[160,1024]{1,0:T(8,128)}, u32[]{:S(2)}, u32[]{:S(2)}) collective-permute-start(f32[160,1024]{1,0:T(8,128)} %dynamic-slice_bitcast_fusion.1), channel_id=1, source_target_pairs={{0,16},{16,0},{1,17},{17,1},{2,18},{18,2},{3,19},{19,3},{4,20},{20... | collective-permute-start | bytes 1966088 | tf_op jit(solution)/shard_map/ppermute | solution.py:22
  12.6 5.3 %copy-start.14 = (f32[320,64]{0,1:T(8,128)S(1)}, f32[320,64]{0,1:T(8,128)}, u32[]{:S(2)}) copy-start(f32[320,64]{0,1:T(8,128)} %param.11) | copy-start | bytes 245764
  15.6 8.6 %collective-permute-start.3 = (f32[8,128]{1,0:T(8,128)}, f32[8,128]{1,0:T(8,128)}, u32[]{:S(2)}, u32[]{:S(2)}) collective-permute-start(f32[8,128]{1,0:T(8,128)} %iota.31), channel_id=1, source_target_pairs={{0,8},{8,0},{1,9},{9,1},{2,10},{10,2},{3,11},{11,3},{4,12},{12,4},... | collective-permute-start | bytes 12296 | tf_op jit(solution)/shard_map/ppermute | solution.py:22
  18.2 6.0 %copy-start.16 = (pred[8]{0:T(512)(128)(4,1)}, pred[8]{0:T(512)(128)(4,1)S(1)}, u32[]{:S(2)}) copy-start(pred[8]{0:T(512)(128)(4,1)S(1)} %iota_compare_fusion) | copy-start | bytes 28
  18.2 1.8 copy-start.11
  22.0 12.4 %collective-permute-start.2 = (f32[160,512]{1,0:T(8,128)}, f32[160,512]{1,0:T(8,128)}, u32[]{:S(2)}, u32[]{:S(2)}) collective-permute-start(f32[160,512]{1,0:T(8,128)} %pad_maximum_fusion.2), channel_id=1, source_target_pairs={{0,32},{32,0},{1,33},{33,1},{2,34},{34,2},{3,35},{35,3},{4,36},{36... | collective-permute-start | bytes 983048 | tf_op jit(solution)/shard_map/ppermute | solution.py:22
  22.8 5.9 %copy-start.15 = (f32[320,64]{0,1:T(8,128)S(1)}, f32[320,64]{0,1:T(8,128)}, u32[]{:S(2)}) copy-start(f32[320,64]{0,1:T(8,128)} %param.11) | copy-start | bytes 245764
  25.0 15.3 %copy-start.17 = (pred[8]{0:T(512)(128)(4,1)S(1)}, pred[8]{0:T(512)(128)(4,1)}, u32[]{:S(2)}) copy-start(pred[8]{0:T(512)(128)(4,1)} %copy-done.16) | copy-start | bytes 28
  25.0 4.0 %collective-permute-start.4 = (f32[8,128]{1,0:T(8,128)S(1)}, f32[8,128]{1,0:T(8,128)S(1)}, u32[]{:S(2)}, u32[]{:S(2)}) collective-permute-start(f32[8,128]{1,0:T(8,128)S(1)} %maximum_select_fusion.3), channel_id=1, source_target_pairs={{0,1},{1,0},{2,3},{3,2},{4,5},{5,4},{6,7},{7,6},{8,9},{9,8},{10,11... | collective-permute-start | bytes 12296 | tf_op jit(solution)/shard_map/ppermute | solution.py:22
  26.9 45.7 %collective-permute-start.1 = (bf16[256,3584]{1,0:T(8,128)(2,1)}, bf16[256,3584]{1,0:T(8,128)(2,1)S(1)}, u32[]{:S(2)}, u32[]{:S(2)}) collective-permute-start(bf16[256,3584]{1,0:T(8,128)(2,1)} %pad_maximum_fusion), channel_id=1, source_target_pairs={{0,8},{8,0},{1,9},{9,1},{2,10},{10,2},{3,11},{11,3},{4,12},{12,4},... | collective-permute-start | bytes 5505032 | tf_op jit(solution)/shard_map/ppermute | solution.py:22
  28.8 11.5 %collective-permute-start.8 = (f32[160,64]{1,0:T(8,128)S(1)}, f32[160,64]{1,0:T(8,128)S(1)}, u32[]{:S(2)}, u32[]{:S(2)}) collective-permute-start(f32[160,64]{1,0:T(8,128)S(1)} %constant_dynamic-slice_fusion.4), channel_id=1, source_target_pairs={{0,16},{16,0},{1,17},{17,1},{2,18},{18,2},{3,19},{19,3},{4,20},{20... | collective-permute-start | bytes 122888 | tf_op jit(solution)/shard_map/ppermute | solution.py:22
  29.7 8.9 %collective-permute-start.9 = (f32[8,128]{1,0:T(8,128)S(1)}, f32[8,128]{1,0:T(8,128)S(1)}, u32[]{:S(2)}, u32[]{:S(2)}) collective-permute-start(f32[8,128]{1,0:T(8,128)S(1)} %maximum_select_fusion.2), channel_id=1, source_target_pairs={{0,2},{1,3},{2,0},{3,1},{4,6},{5,7},{6,4},{7,5},{8,10},{9,11},{10,... | collective-permute-start | bytes 12296 | tf_op jit(solution)/shard_map/ppermute | solution.py:22
  34.4 17.4 %copy-start.18 = (pred[8]{0:T(512)(128)(4,1)S(1)}, pred[8]{0:T(512)(128)(4,1)}, u32[]{:S(2)}) copy-start(pred[8]{0:T(512)(128)(4,1)} %copy-done.16) | copy-start | bytes 28
  35.5 10.3 %collective-permute-start.5 = (f32[160,128]{1,0:T(8,128)S(1)}, f32[160,128]{1,0:T(8,128)S(1)}, u32[]{:S(2)}, u32[]{:S(2)}) collective-permute-start(f32[160,128]{1,0:T(8,128)S(1)} %get-tuple-element.107), channel_id=1, source_target_pairs={{0,64},{64,0},{128,192},{192,128},{1,65},{65,1},{129,193},{193,129... | collective-permute-start | bytes 245768 | tf_op jit(solution)/shard_map/ppermute | solution.py:22
  35.7 10.1 %collective-permute-start.6 = (f32[160,128]{1,0:T(8,128)S(1)}, f32[160,128]{1,0:T(8,128)S(1)}, u32[]{:S(2)}, u32[]{:S(2)}) collective-permute-start(f32[160,128]{1,0:T(8,128)S(1)} %get-tuple-element.106), channel_id=1, source_target_pairs={{0,128},{64,192},{128,0},{192,64},{1,129},{65,193},{129,1},{193,65... | collective-permute-start | bytes 245768 | tf_op jit(solution)/shard_map/ppermute | solution.py:22
  38.6 7.2 %collective-permute-start.7 = (f32[160,128]{1,0:T(8,128)S(1)}, f32[160,128]{1,0:T(8,128)S(1)}, u32[]{:S(2)}, u32[]{:S(2)}) collective-permute-start(f32[160,128]{1,0:T(8,128)S(1)} %get-tuple-element.105), channel_id=1, source_target_pairs={{0,192},{64,128},{128,64},{192,0},{1,193},{65,129},{129,65},{193,1... | collective-permute-start | bytes 245768 | tf_op jit(solution)/shard_map/ppermute | solution.py:22
  40.4 11.3 %collective-permute-start.14 = (f32[8,128]{1,0:T(8,128)S(1)}, f32[8,128]{1,0:T(8,128)S(1)}, u32[]{:S(2)}, u32[]{:S(2)}) collective-permute-start(f32[8,128]{1,0:T(8,128)S(1)} %maximum_select_fusion.1), channel_id=1, source_target_pairs={{0,4},{1,5},{2,6},{3,7},{4,0},{5,1},{6,2},{7,3},{8,12},{9,13},{10,... | collective-permute-start | bytes 12296 | tf_op jit(solution)/shard_map/ppermute | solution.py:22
  46.8 8.5 %collective-permute-start.10 = (bf16[160,128]{1,0:T(8,128)(2,1)S(1)}, bf16[160,128]{1,0:T(8,128)(2,1)S(1)}, u32[]{:S(2)}, u32[]{:S(2)}) collective-permute-start(bf16[160,128]{1,0:T(8,128)(2,1)S(1)} %get-tuple-element.79), channel_id=1, source_target_pairs={{0,64},{64,0},{128,192},{192,128},{1,65},{65,1},{129,193},{193,129... | collective-permute-start | bytes 122888 | tf_op jit(solution)/shard_map/ppermute | solution.py:22
  47.3 8.1 %collective-permute-start.11 = (bf16[160,128]{1,0:T(8,128)(2,1)S(1)}, bf16[160,128]{1,0:T(8,128)(2,1)S(1)}, u32[]{:S(2)}, u32[]{:S(2)}) collective-permute-start(bf16[160,128]{1,0:T(8,128)(2,1)S(1)} %get-tuple-element.79), channel_id=1, source_target_pairs={{0,128},{64,192},{128,0},{192,64},{1,129},{65,193},{129,1},{193,65... | collective-permute-start | bytes 122888 | tf_op jit(solution)/shard_map/ppermute | solution.py:22
  51.4 5.2 %collective-permute-start.12 = (bf16[160,128]{1,0:T(8,128)(2,1)S(1)}, bf16[160,128]{1,0:T(8,128)(2,1)S(1)}, u32[]{:S(2)}, u32[]{:S(2)}) collective-permute-start(bf16[160,128]{1,0:T(8,128)(2,1)S(1)} %get-tuple-element.79), channel_id=1, source_target_pairs={{0,192},{64,128},{128,64},{192,0},{1,193},{65,129},{129,65},{193,1... | collective-permute-start | bytes 122888 | tf_op jit(solution)/shard_map/ppermute | solution.py:22
  51.7 4.9 %collective-permute-start.13 = (f32[160,64]{1,0:T(8,128)S(1)}, f32[160,64]{1,0:T(8,128)S(1)}, u32[]{:S(2)}, u32[]{:S(2)}) collective-permute-start(f32[160,64]{1,0:T(8,128)S(1)} %get-tuple-element.112), channel_id=1, source_target_pairs={{0,16},{16,0},{1,17},{17,1},{2,18},{18,2},{3,19},{19,3},{4,20},{20... | collective-permute-start | bytes 122888 | tf_op jit(solution)/shard_map/ppermute | solution.py:22
  56.7 51.0 %collective-permute-start.16 = (bf16[160,512]{1,0:T(8,128)(2,1)S(1)}, bf16[160,512]{1,0:T(8,128)(2,1)}, u32[]{:S(2)}, u32[]{:S(2)}) collective-permute-start(bf16[160,512]{1,0:T(8,128)(2,1)S(1)} %constant_dynamic-update-slice_fusion), channel_id=1, source_target_pairs={{0,32},{32,0},{1,33},{33,1},{2,34},{34,2},{3,35},{35,3},{4,36},{36... | collective-permute-start | bytes 491528 | tf_op jit(solution)/shard_map/ppermute | solution.py:22
  60.0 12.7 %copy-start.4 = (bf16[256,2560]{1,0:T(8,128)(2,1)S(1)}, bf16[256,2560]{1,0:T(8,128)(2,1)}, u32[]{:S(2)}) copy-start(bf16[256,2560]{1,0:T(8,128)(2,1)} %dynamic-slice_bitcast_fusion) | copy-start | bytes 3932164
  72.6 19.5 %copy-start.9 = (bf16[256,3584]{1,0:T(8,128)(2,1)}, bf16[256,3584]{1,0:T(8,128)(2,1)S(1)}, u32[]{:S(2)}) copy-start(bf16[256,3584]{1,0:T(8,128)(2,1)S(1)} %collective-permute-done.1) | copy-start | bytes 5505028
  75.7 3.9 %copy-start.2 = (f32[2560,1024]{1,0:T(8,128)}, f32[2560,1024]{1,0:T(8,128)S(1)}, u32[]{:S(2)}) copy-start(f32[2560,1024]{1,0:T(8,128)S(1)} %fusion.3) | copy-start | bytes 31457284
  80.6 14.1 %collective-permute-start.17 = (f16[160,1024]{1,0:T(8,128)(2,1)}, f16[160,1024]{1,0:T(8,128)(2,1)S(1)}, u32[]{:S(2)}, u32[]{:S(2)}) collective-permute-start(f16[160,1024]{1,0:T(8,128)(2,1)} %get-tuple-element.90), channel_id=1, source_target_pairs={{0,1},{1,0},{2,3},{3,2},{4,5},{5,4},{6,7},{7,6},{8,9},{9,8},{10,11... | collective-permute-start | bytes 983048 | tf_op jit(solution)/shard_map/ppermute | solution.py:170
  82.6 17.2 %collective-permute-start.18 = (f16[160,1024]{1,0:T(8,128)(2,1)}, f16[160,1024]{1,0:T(8,128)(2,1)S(1)}, u32[]{:S(2)}, u32[]{:S(2)}) collective-permute-start(f16[160,1024]{1,0:T(8,128)(2,1)} %get-tuple-element.89), channel_id=1, source_target_pairs={{0,7},{1,2},{2,1},{3,4},{4,3},{5,6},{6,5},{7,0},{8,15},{9,10},{10,... | collective-permute-start | bytes 983048 | tf_op jit(solution)/shard_map/ppermute | solution.py:170
  87.5 4.6 %copy-start = (bf16[2560,768]{1,0:T(8,128)(2,1)S(1)}, bf16[2560,768]{1,0:T(8,128)(2,1)}, u32[]{:S(2)}) copy-start(bf16[2560,768]{1,0:T(8,128)(2,1)} %all-gather.3.cloned.1.call-done) | copy-start | bytes 11796484
  91.8 27.4 %collective-permute-start.15 = (f32[256,768]{1,0:T(8,128)}, f32[256,768]{1,0:T(8,128)}, u32[]{:S(2)}, u32[]{:S(2)}) collective-permute-start(f32[256,768]{1,0:T(8,128)} %fusion.54), channel_id=1, source_target_pairs={{0,8},{8,0},{1,9},{9,1},{2,10},{10,2},{3,11},{11,3},{4,12},{12,4},... | collective-permute-start | bytes 2359304 | tf_op jit(solution)/shard_map/ppermute | solution.py:22
  103.3 17.2 %collective-permute-start.21 = (f16[320,1024]{1,0:T(8,128)(2,1)}, f16[320,1024]{1,0:T(8,128)(2,1)}, u32[]{:S(2)}, u32[]{:S(2)}) collective-permute-start(f16[320,1024]{1,0:T(8,128)(2,1)} %fusion.27), channel_id=1, source_target_pairs={{0,1},{1,0},{2,3},{3,2},{4,5},{5,4},{6,7},{7,6},{8,9},{9,8},{10,11... | collective-permute-start | bytes 1966088 | tf_op jit(solution)/shard_map/ppermute | solution.py:170
  104.3 16.2 %collective-permute-start.22 = (f16[320,1024]{1,0:T(8,128)(2,1)}, f16[320,1024]{1,0:T(8,128)(2,1)}, u32[]{:S(2)}, u32[]{:S(2)}) collective-permute-start(f16[320,1024]{1,0:T(8,128)(2,1)} %fusion.28), channel_id=1, source_target_pairs={{0,7},{1,2},{2,1},{3,4},{4,3},{5,6},{6,5},{7,0},{8,15},{9,10},{10,... | collective-permute-start | bytes 1966088 | tf_op jit(solution)/shard_map/ppermute | solution.py:170
  108.8 1.6 copy-start.5
  108.8 19.9 %collective-permute-start.25 = (bf16[160,1024]{1,0:T(8,128)(2,1)S(1)}, bf16[160,1024]{1,0:T(8,128)(2,1)}, u32[]{:S(2)}, u32[]{:S(2)}) collective-permute-start(bf16[160,1024]{1,0:T(8,128)(2,1)S(1)} %slice_dynamic-update-slice_fusion), channel_id=1, source_target_pairs={{0,16},{16,0},{1,17},{17,1},{2,18},{18,2},{3,19},{19,3},{4,20},{20... | collective-permute-start | bytes 983048 | tf_op jit(solution)/shard_map/ppermute | solution.py:22
  112.5 4.0 %copy-start.1 = (bf16[2560,256]{1,0:T(8,128)(2,1)S(1)}, bf16[2560,256]{1,0:T(8,128)(2,1)}, u32[]{:S(2)}) copy-start(bf16[2560,256]{1,0:T(8,128)(2,1)} %all-gather.5.cloned.1.call-done) | copy-start | bytes 3932164
  112.5 4.0 %copy-start.10 = (bf16[256,3584]{1,0:T(8,128)(2,1)S(1)}, bf16[256,3584]{1,0:T(8,128)(2,1)}, u32[]{:S(2)}) copy-start(bf16[256,3584]{1,0:T(8,128)(2,1)} %copy-done.9) | copy-start | bytes 5505028
  117.6 1.6 copy-start.12
  117.6 50.5 %collective-permute-start.20 = (bf16[256,2560]{1,0:T(8,128)(2,1)}, bf16[256,2560]{1,0:T(8,128)(2,1)}, u32[]{:S(2)}, u32[]{:S(2)}) collective-permute-start(bf16[256,2560]{1,0:T(8,128)(2,1)} %fusion), channel_id=1, source_target_pairs={{0,8},{8,0},{1,9},{9,1},{2,10},{10,2},{3,11},{11,3},{4,12},{12,4},... | collective-permute-start | bytes 3932168 | tf_op jit(solution)/shard_map/ppermute | solution.py:22
  120.5 7.6 %copy-start.6 = (bf16[256,2560]{1,0:T(8,128)(2,1)S(1)}, bf16[256,2560]{1,0:T(8,128)(2,1)}, u32[]{:S(2)}) copy-start(bf16[256,2560]{1,0:T(8,128)(2,1)} %dynamic-slice_bitcast_fusion) | copy-start | bytes 3932164
  124.6 17.2 %collective-permute-start.23 = (f16[320,1024]{1,0:T(8,128)(2,1)S(1)}, f16[320,1024]{1,0:T(8,128)(2,1)S(1)}, u32[]{:S(2)}, u32[]{:S(2)}) collective-permute-start(f16[320,1024]{1,0:T(8,128)(2,1)S(1)} %get-tuple-element.84), channel_id=1, source_target_pairs={{0,1},{1,0},{2,3},{3,2},{4,5},{5,4},{6,7},{7,6},{8,9},{9,8},{10,11... | collective-permute-start | bytes 1966088 | tf_op jit(solution)/shard_map/ppermute | solution.py:170
  125.1 18.1 %collective-permute-start.24 = (f16[320,1024]{1,0:T(8,128)(2,1)S(1)}, f16[320,1024]{1,0:T(8,128)(2,1)S(1)}, u32[]{:S(2)}, u32[]{:S(2)}) collective-permute-start(f16[320,1024]{1,0:T(8,128)(2,1)S(1)} %get-tuple-element.83), channel_id=1, source_target_pairs={{0,7},{1,2},{2,1},{3,4},{4,3},{5,6},{6,5},{7,0},{8,15},{9,10},{10,... | collective-permute-start | bytes 1966088 | tf_op jit(solution)/shard_map/ppermute | solution.py:170
  130.7 19.0 %copy-start.13 = (f32[320,64]{1,0:T(8,128)S(1)}, f32[320,64]{1,0:T(8,128)}, u32[]{:S(2)}) copy-start(f32[320,64]{1,0:T(8,128)} %pad_maximum_fusion.3) | copy-start | bytes 245764
  146.8 16.1 %collective-permute-start.26 = (f16[320,1024]{1,0:T(8,128)(2,1)S(1)}, f16[320,1024]{1,0:T(8,128)(2,1)S(1)}, u32[]{:S(2)}, u32[]{:S(2)}) collective-permute-start(f16[320,1024]{1,0:T(8,128)(2,1)S(1)} %get-tuple-element.82), channel_id=1, source_target_pairs={{0,1},{1,0},{2,3},{3,2},{4,5},{5,4},{6,7},{7,6},{8,9},{9,8},{10,11... | collective-permute-start | bytes 1966088 | tf_op jit(solution)/shard_map/ppermute | solution.py:170
  147.3 17.1 %collective-permute-start.27 = (f16[320,1024]{1,0:T(8,128)(2,1)S(1)}, f16[320,1024]{1,0:T(8,128)(2,1)S(1)}, u32[]{:S(2)}, u32[]{:S(2)}) collective-permute-start(f16[320,1024]{1,0:T(8,128)(2,1)S(1)} %get-tuple-element.81), channel_id=1, source_target_pairs={{0,7},{1,2},{2,1},{3,4},{4,3},{5,6},{6,5},{7,0},{8,15},{9,10},{10,... | collective-permute-start | bytes 1966088 | tf_op jit(solution)/shard_map/ppermute | solution.py:170
  150.6 17.6 %collective-permute-start.19 = (f32[256,256]{1,0:T(8,128)}, f32[256,256]{1,0:T(8,128)S(1)}, u32[]{:S(2)}, u32[]{:S(2)}) collective-permute-start(f32[256,256]{1,0:T(8,128)} %fusion.52), channel_id=1, source_target_pairs={{0,8},{8,0},{1,9},{9,1},{2,10},{10,2},{3,11},{11,3},{4,12},{12,4},... | collective-permute-start | bytes 786440 | tf_op jit(solution)/shard_map/ppermute | solution.py:22
  (3 other events, 3.4 us)
Sparse Core Ops, SparseCore 0:
  10.4 55.4 all-gather.2
  67.7 39.4 all-gather.4
where the time goes:
time: 182 us; the launch traced here: 180 us
  starting transfers between devices  46.5 us (26%)
  waiting for transfers between devices  45.2 us (25%)
  other arithmetic  35.5 us (20%)
  matrix products  20.7 us (11%)
  between operations  16.6 us (9%)
  local copies, waits for them, and re-layouts  15.3 us (8%)
    ppermute x8, waiting for transfers between devices, send(): return (lax.ppermute(even, 'z', EVEN), lax.ppermute(odd, 'z', ODD))  29.9 us
    ppermute x20, starting transfers between devices, swap(): lax.ppermute(value, axis, [(i, i ^ mask) for i in range(SIZES[axis])])  29.8 us
    ppermute x8, starting transfers between devices, send(): return (lax.ppermute(even, 'z', EVEN), lax.ppermute(odd, 'z', ODD))  16.6 us
    ppermute x20, waiting for transfers between devices, swap(): lax.ppermute(value, axis, [(i, i ^ mask) for i in range(SIZES[axis])])  15.3 us
    convert_element_type x5, other arithmetic, encode(): return (scaled * jnp.abs(scaled)).astype(F16)  10.8 us
    dot_general x4, matrix products, grads(): lax.dot_general(left, right, (((1,), (1,)), ((), ())), preferred_element_...  9.49 us
    dot_general x4, matrix products, keys(): return jnp.dot(left, right, preferred_element_type=F32)  8.25 us
    unnamed x51, local copies, waits for them, and re-layouts  6.62 us
  transfers between devices with their start and end apart: 30, of which 8 were waited for; matrix products, arithmetic and copies ran while one was open for 33% of the time, Pallas kernels for 0%

commit v1 on v0

v1 whole, which is shorter than its diff:
```python
import jax
import jax.numpy as jnp
from jax import lax
from jax.experimental import pallas as pl
from jax.experimental.pallas import tpu as pltpu
from jax.sharding import Mesh
from jax.sharding import PartitionSpec as P

OUTER_RATE = 0.7
NESTEROV = 0.9
BF16 = jnp.bfloat16
F32 = jnp.float32
F16 = jnp.float16

SIZES = {"y": 4, "xh": 2, "c": 2, "xl": 2, "z": 8}
REP = ("y", "xh", "c")
FSDP = ("xl", "z")
N_Z = 8
EVEN = [(i, i ^ 1) for i in range(N_Z)]
ODD = [(i, (i - 1) % N_Z if i % 2 == 0 else (i + 1) % N_Z) for i in range(N_Z)]


def swap(value, axis, mask=1):
    return lax.ppermute(value, axis, [(i, i ^ mask) for i in range(SIZES[axis])])


class Sequence:
    def __init__(self):
        self.last = ()

    def step(self, *values):
        held = lax.optimization_barrier((*values, *self.last))[: len(values)]
        return held[0] if len(held) == 1 else held

    def did(self, *values):
        self.last = values


def rows_of(array, start, size):
    return lax.dynamic_slice_in_dim(array, start, size, 0)


def columns_of(array, start, size):
    return lax.dynamic_slice_in_dim(array, start, size, 1)


def in_order(here, mine, theirs, axis):
    first = here == 0
    return jnp.concatenate(
        [jnp.where(first, mine, theirs), jnp.where(first, theirs, mine)], axis=axis
    )


def encode(scaled):
    return (scaled * jnp.abs(scaled)).astype(F16)


def decode(sent):
    wide = sent.astype(F32)
    return jnp.sign(wide) * jnp.sqrt(jnp.abs(wide))


def column_peak(tokens):
    return jnp.max(jnp.sum(jnp.abs(tokens.astype(F32)), axis=0))


def as_tile(first, second):
    row = lax.broadcasted_iota(jnp.int32, (8, 128), 0)
    return jnp.where(row < 4, first, second)


def join_peaks(peaks, other):
    return as_tile(peaks + other, jnp.maximum(peaks, other))


def dot(left, right):
    return jnp.dot(left, right, preferred_element_type=F32)


def dot_t(left, right):
    return lax.dot_general(left, right, (((1,), (1,)), ((), ())), preferred_element_type=F32)


FREE = pl.CostEstimate(flops=0, bytes_accessed=0, transcendentals=0)
STEP = 512


def whole(array):
    return pl.BlockSpec(array.shape, lambda i, *_: (0, 0))


def rows_block(array):
    return pl.BlockSpec((STEP, array.shape[1]), lambda i, *_: (i, 0))


def columns_block(array):
    return pl.BlockSpec((array.shape[0], STEP), lambda i, *_: (0, i))


def key_part(tokens, weight):
    def body(tokens_ref, weight_ref, keys_ref):
        @pl.when(pl.program_id(0) == 0)
        def _():
            keys_ref[...] = jnp.zeros_like(keys_ref)

        keys_ref[...] += dot(tokens_ref[...], weight_ref[...])

    shape = (tokens.shape[0], weight.shape[1])
    return pl.pallas_call(
        body,
        grid=(tokens.shape[1] // STEP,),
        in_specs=[columns_block(tokens), rows_block(weight)],
        out_specs=pl.BlockSpec(shape, lambda i: (0, 0)),
        out_shape=jax.ShapeDtypeStruct(shape, F32),
        cost_estimate=FREE,
    )(tokens, weight)


def products_for_partner(tokens, cotangent, left, right):
    cut = left.shape[1]

    def body(tokens_ref, cotangent_ref, left_ref, right_ref, keys_ref, grads_ref):
        @pl.when(pl.program_id(0) == 0)
        def _():
            keys_ref[...] = jnp.zeros_like(keys_ref)

        keys_ref[...] += dot(tokens_ref[...], right_ref[...])
        grads = dot_t(cotangent_ref[:, :cut], left_ref[...])
        grads_ref[...] = (grads + dot_t(cotangent_ref[:, cut:], right_ref[...])).astype(BF16)

    keys = jax.ShapeDtypeStruct((tokens.shape[0], right.shape[1]), F32)
    return pl.pallas_call(
        body,
        grid=(tokens.shape[1] // STEP,),
        in_specs=[columns_block(tokens), whole(cotangent), rows_block(left), rows_block(right)],
        out_specs=[whole(keys), columns_block(tokens)],
        out_shape=[keys, jax.ShapeDtypeStruct(tokens.shape, BF16)],
        cost_estimate=FREE,
    )(tokens, cotangent, left, right)


def products_here(side, tokens, cotangent, left, right):
    cut = left.shape[1]
    steps = left.shape[0] // STEP

    def body(_, tokens_ref, cotangent_ref, left_ref, right_ref, keys_ref, grads_ref):
        @pl.when(pl.program_id(0) == 0)
        def _():
            keys_ref[...] = jnp.zeros_like(keys_ref)

        keys_ref[:, :cut] += dot(tokens_ref[...], left_ref[...])
        keys_ref[:, cut:] += dot(tokens_ref[...], right_ref[...])
        grads = dot_t(cotangent_ref[:, :cut], left_ref[...])
        grads_ref[...] = (grads + dot_t(cotangent_ref[:, cut:], right_ref[...])).astype(BF16)

    keys = jax.ShapeDtypeStruct(cotangent.shape, F32)
    grads = jax.ShapeDtypeStruct(tokens.shape, BF16)
    here = pl.BlockSpec((tokens.shape[0], STEP), lambda i, s: (0, s[0] * steps + i))
    return pl.pallas_call(
        body,
        grid_spec=pltpu.PrefetchScalarGridSpec(
            num_scalar_prefetch=1,
            grid=(steps,),
            in_specs=[here, whole(cotangent), rows_block(left), rows_block(right)],
            out_specs=[whole(keys), here],
        ),
        out_shape=[keys, grads],
        cost_estimate=FREE,
    )(side.reshape(1), tokens, cotangent, left, right)


def fill_other(side, grads, other):
    steps = other.shape[1] // STEP

    def body(_, __, other_ref, out_ref):
        out_ref[...] = other_ref[...]

    return pl.pallas_call(
        body,
        grid_spec=pltpu.PrefetchScalarGridSpec(
            num_scalar_prefetch=1,
            grid=(steps,),
            in_specs=[pl.BlockSpec(memory_space=pl.ANY), columns_block(other)],
            out_specs=pl.BlockSpec(
                (other.shape[0], STEP), lambda i, s: (0, (1 - s[0]) * steps + i)
            ),
        ),
        out_shape=jax.ShapeDtypeStruct(grads.shape, BF16),
        input_output_aliases={1: 0},
    )(side.reshape(1), grads, other)


def shards(activations, key_weights, key_cotangent, fragment, pseudo_grads, momentum):
    tokens, weight, cotangent, pseudo = (
        a[0] for a in (activations, key_weights, key_cotangent, pseudo_grads)
    )
    y, xh, c, x, z = (lax.axis_index(a) for a in SIZES)
    order = Sequence()
    half = tokens.shape[1] // 2
    cut = weight.shape[1] * 3 // 4
    rows = pseudo.shape[0] // 2
    mine, theirs = c * rows, (1 - c) * rows
    width = momentum.shape[1]
    pair = 2 * width
    quarter = 2 * pair
    chunk = half // N_Z
    odd_z = z % 2
    sign = 1 - 2 * odd_z
    group = z // 2
    early = [(group + 2) % 4, (group + 4 + sign) % 4]
    late = [group, (group + 4 - sign) % 4]

    def token_columns(array, side, groups):
        parts = [columns_of(array, side * half + g * 2 * chunk, 2 * chunk) for g in groups]
        return jnp.concatenate(parts, axis=1)

    weight_left = lax.all_gather(weight[:, :cut], "z", axis=0, tiled=True)
    weight_right = lax.all_gather(weight[:, cut:], "z", axis=0, tiled=True)
    cotangent_other = swap(cotangent, "xl")

    give = rows_of(pseudo, theirs, rows)
    order.did(give)
    pseudo_other = swap(give, "c")
    peak = jnp.full((8, 128), column_peak(order.step(tokens)))
    order.did(peak)
    peak_other = swap(peak, "xl")
    sent = token_columns(order.step(tokens), 1 - x, early)
    order.did(sent)
    early_other = swap(sent, "xl")
    pseudo_other, cotangent_other = order.step(pseudo_other, cotangent_other)
    total = rows_of(pseudo, mine, rows) + pseudo_other
    gives = [columns_of(total, (y ^ m) * quarter, quarter) for m in (1, 2, 3)]
    old_give = rows_of(momentum, theirs, rows)
    order.did(*gives, old_give)
    others = [swap(g, "y", m) for g, m in zip(gives, (1, 2, 3))]
    old_other = swap(old_give, "c")
    sent = token_columns(order.step(tokens), 1 - x, late)
    order.did(sent)
    late_other = swap(sent, "xl")
    peak_other = order.step(peak_other)
    peak_c = jnp.maximum(jnp.max(jnp.abs(cotangent)), jnp.max(jnp.abs(cotangent_other)))
    peaks = as_tile(peak + peak_other, peak_c.astype(F32))
    order.did(peaks)
    peaks_other = swap(peaks, "z", 1)
    early_mine = token_columns(order.step(tokens), x, early)
    order.did(early_mine)
    peaks = join_peaks(peaks, order.step(peaks_other))
    order.did(peaks)
    peaks_other = swap(peaks, "z", 2)
    *others, old_other = order.step(*others, old_other)
    summed = columns_of(total, y * quarter, quarter) + others[0] + others[1] + others[2]
    give = columns_of(summed, (1 - xh) * pair, pair)
    order.did(summed, give)
    summed_other = swap(give, "xh")
    peaks = join_peaks(peaks, order.step(peaks_other))
    order.did(peaks)
    peaks_other = swap(peaks, "z", 4)

    def product(first, second):
        return lax.dot_general(
            jnp.concatenate([first, second], axis=0),
            jnp.concatenate([cotangent, cotangent_other], axis=0),
            (((0,), (0,)), ((), ())),
            preferred_element_type=F32,
        )

    early_other = order.step(early_other)
    partial_early = product(early_mine, early_other)
    order.did(partial_early)
    peaks = join_peaks(peaks, order.step(peaks_other))
    bound = jnp.maximum(peaks[0, 0] * peaks[4, 0], 1e-32)
    scale, back = 240.0 / bound, bound / (64.0 * 240.0)
    place = {4: odd_z, -3: 1 - odd_z, 2: 2 + odd_z, 3: 3 - odd_z}
    place_late = {0: odd_z, 1: 1 - odd_z, -2: 2 + odd_z, -1: 3 - odd_z}

    def own(distance, start=0, size=chunk):
        if distance in place:
            return rows_of(partial_early, place[distance] * chunk + start, size) * scale
        return rows_of(partial_late, place_late[distance] * chunk + start, size) * scale

    def send(even, odd):
        even, odd = encode(even), encode(odd)
        order.did(even, odd)
        return lax.ppermute(even, "z", EVEN), lax.ppermute(odd, "z", ODD)

    def ring_step(distance, got):
        even_in, odd_in = order.step(*got)
        return send(own(distance) + decode(odd_in), own(-distance) + decode(even_in))

    part = chunk // 2
    far = send(own(4, 0, part), own(4, part, part))

    late_other = order.step(late_other)
    late_mine = token_columns(tokens, x, late)
    partial_late = product(late_mine, late_other)
    order.did(partial_late)

    even_in, odd_in = order.step(*far)
    even = jnp.concatenate([own(3, 0, part), own(3, part, part) + decode(odd_in)])
    odd = jnp.concatenate([own(-3, 0, part) + decode(even_in), own(-3, part, part)])
    ring = send(even, odd)

    summed_other = order.step(summed_other)
    average = (columns_of(summed, xh * pair, pair) + summed_other) / 16
    old = in_order(c, rows_of(momentum, mine, rows), old_other, 1)
    new = NESTEROV * old + average
    here = lax.dynamic_slice(fragment, (mine, (2 * y + xh) * pair), (rows, pair))
    updated = (here.astype(F32) - OUTER_RATE * (average + NESTEROV * new)).astype(BF16)
    keep = jnp.where(c == 0, new[:, :width], new[:, width:])
    give = jnp.where(c == 0, new[:, width:], new[:, :width])
    order.did(updated, keep, give)
    updated_other = swap(updated, "xh")
    new_other = swap(give, "c")

    tokens_other = jnp.zeros((tokens.shape[0], half), BF16)
    for got, groups in ((order.step(early_other), early), (late_other, late)):
        for k, g in enumerate(groups):
            piece = got[:, k * 2 * chunk : (k + 1) * 2 * chunk]
            tokens_other = lax.dynamic_update_slice(tokens_other, piece, (0, g * 2 * chunk))
    weight_left, tokens_other = lax.optimization_barrier((weight_left, tokens_other))
    keys_left = key_part(tokens_other, weight_left)
    order.did(keys_left)
    keys_left_back = swap(keys_left, "xl")

    updated_other, new_other = order.step(updated_other, new_other)
    new_momentum = in_order(c, keep, new_other, 0)
    wide = in_order(xh, updated, updated_other, 1)
    order.did(wide, new_momentum)
    wides = [swap(wide, "y", m) for m in (1, 2, 3)]

    ring = ring_step(2, ring)

    wides = order.step(*wides)
    block = jnp.zeros((rows, 4 * quarter), BF16)
    block = lax.dynamic_update_slice(block, wide, (0, y * quarter))
    for got, m in zip(wides, (1, 2, 3)):
        block = lax.dynamic_update_slice(block, got, (0, (y ^ m) * quarter))
    order.did(block)
    block_other = swap(block, "c")

    weight_right, keys_left_back = order.step(weight_right, keys_left_back)
    keys_right, grads_other = products_for_partner(
        tokens_other, cotangent_other, weight_left, weight_right
    )
    order.did(keys_right, grads_other)
    grads_back = swap(grads_other, "xl")
    keys_right_back = swap(keys_right, "xl")

    ring = ring_step(1, ring)

    keys_mine, grads_mine = products_here(
        order.step(x), tokens, cotangent, weight_left, weight_right
    )
    order.did(keys_mine, grads_mine)
    new_fragment = in_order(c, block, order.step(block_other), 0)
    key_left = (keys_mine[:, :cut] + keys_left_back).astype(BF16)
    order.did(new_fragment, key_left)
    even_in, odd_in = order.step(*ring)
    weight_grad = ((own(0) + decode(even_in) + decode(odd_in)) * back).astype(BF16)
    order.did(weight_grad)
    keys_right_back, grads_back = order.step(keys_right_back, grads_back)
    key_right = (keys_mine[:, cut:] + keys_right_back).astype(BF16)
    return (
        jnp.concatenate([key_left, key_right], axis=1)[None],
        fill_other(x, grads_mine, grads_back)[None],
        weight_grad[None],
        new_fragment,
        new_momentum,
    )


def solution(mesh):
    fine = Mesh(mesh.devices.reshape(tuple(SIZES.values())), tuple(SIZES))
    return jax.shard_map(
        shards,
        mesh=fine,
        in_specs=(
            P(REP, FSDP, None),
            P(REP, FSDP, None),
            P(REP, FSDP, None),
            P(FSDP, None),
            P(REP, FSDP, None),
            P(FSDP, REP),
        ),
        out_specs=(
            P(REP, FSDP, None),
            P(REP, FSDP, None),
            P(REP, FSDP, None),
            P(FSDP, None),
            P(FSDP, REP),
        ),
        check_vma=False,
    )
```

time: 182 us -> 167 us (0.918)
  waiting for transfers between devices: 45.2 us -> 21 us
  Pallas kernels: 0 us -> 23.9 us
  matrix products: 20.7 us -> 7.75 us
  other arithmetic: 35.5 us -> 30.9 us
  starting transfers between devices: 46.5 us -> 49.4 us
    pallas_call x0 -> x4, Pallas kernels: none -> 23.9 us  [the longest x1 7.45 us: products_here(): pl.pallas_call(body, grid_spec=pltpu.PrefetchScalarGridSpec(num_scalar_pr...]
    ppermute x8, waiting for transfers between devices: 29.9 us -> 10.2 us  [send(): return (lax.ppermute(even, 'z', EVEN), lax.ppermute(odd, 'z', ODD))]
    dot_general x9 -> x2, matrix products: 20.7 us -> 7.75 us  [product(): lax.dot_general(jnp.concatenate([first, second], axis=0), jnp.concatenate...]
    ppermute x20 -> x22, starting transfers between devices: 29.8 us -> 36.7 us  [swap(): lax.ppermute(value, axis, [(i, i ^ mask) for i in range(SIZES[axis])])]
    ppermute x20 -> x22, waiting for transfers between devices: 15.3 us -> 10.7 us  [swap(): lax.ppermute(value, axis, [(i, i ^ mask) for i in range(SIZES[axis])])]
    ppermute x8, starting transfers between devices: 16.6 us -> 12.6 us  [send(): return (lax.ppermute(even, 'z', EVEN), lax.ppermute(odd, 'z', ODD))]
    unnamed x51 -> x27, local copies, waits for them, and re-layouts: 6.62 us -> 2.89 us
    add x3, other arithmetic: 4.75 us -> 2.08 us  [the longest x1 1.16 us: shards(): total = rows_of(pseudo, mine, rows) + pseudo_other]
  transfers between devices with their start and end apart: 30 -> 32, of which waited for: 8 -> 11; matrix products, arithmetic and copies ran while one was open for 33% -> 29% of each run, Pallas kernels for 0% -> 12%
where the time goes in v1:
time: 167 us; the launch traced here: 164 us
  starting transfers between devices  49.4 us (30%)
  other arithmetic  30.9 us (19%)
  Pallas kernels  23.9 us (14%)
  waiting for transfers between devices  21 us (13%)
  between operations  17.4 us (10%)
  local copies, waits for them, and re-layouts  13.9 us (8%)
  matrix products  7.75 us (5%)
    ppermute x22, starting transfers between devices, swap(): lax.ppermute(value, axis, [(i, i ^ mask) for i in range(SIZES[axis])])  36.7 us
    convert_element_type x6, other arithmetic, encode(): return (scaled * jnp.abs(scaled)).astype(F16)  12.7 us
    ppermute x8, starting transfers between devices, send(): return (lax.ppermute(even, 'z', EVEN), lax.ppermute(odd, 'z', ODD))  12.6 us
    ppermute x22, waiting for transfers between devices, swap(): lax.ppermute(value, axis, [(i, i ^ mask) for i in range(SIZES[axis])])  10.7 us
    ppermute x8, waiting for transfers between devices, send(): return (lax.ppermute(even, 'z', EVEN), lax.ppermute(odd, 'z', ODD))  10.2 us
    dot_general x2, matrix products, product(): lax.dot_general(jnp.concatenate([first, second], axis=0), jnp.concatenate...  7.75 us
    pallas_call x1, Pallas kernels, products_here(): pl.pallas_call(body, grid_spec=pltpu.PrefetchScalarGridSpec(num_scalar_pr...  7.45 us
    pallas_call x1, Pallas kernels, products_for_partner(): pl.pallas_call(body, grid=(tokens.shape[1] // STEP,), in_specs=[columns_b...  6.8 us
  transfers between devices with their start and end apart: 32, of which 11 were waited for; matrix products, arithmetic and copies ran while one was open for 29% of the time, Pallas kernels for 12%

profile of v1, /device:TPU:2, one launch (start us, length us, event | category | flops | bytes accessed | tf_op | source)
XLA Modules:
  0.0 164.3 jit_solution(601374074226535650)
XLA Ops:
  7.2 2.0 %slice.52 = bf16[320,768]{1,0:T(8,128)(2,1)} slice(bf16[320,1024]{1,0:T(8,128)(2,1)} %bitcast.31), slice={[0:320], [0:768]} | slice | bytes 983040 | tf_op jit(solution)/shard_map/slice | solution.py:217
  9.3 2.0 %dynamic-slice_bitcast_fusion = f32[160,1024]{1,0:T(8,128)} fusion(f32[1,320,1024]{2,1,0:T(8,128)} %param.10, s32[]{:T(128)S(6)} %select_n.190), kind=kLoop, calls=%fused_computation.79 | loop fusion | bytes 1310724 | tf_op jit(solution)/shard_map/dynamic_slice | solution.py:40
  11.3 2.3 %collective-permute-start.1 = (bf16[256,1024]{1,0:T(8,128)(2,1)}, bf16[256,1024]{1,0:T(8,128)(2,1)}, u32[]{:S(2)}, u32[]{:S(2)}) collective-permute-start(bf16[256,1024]{1,0:T(8,128)(2,1)} %bitcast.26), channel_id=1, source_target_pairs={{0,8},{8,0},{1,9},{9,1},{2,10},{10,2},{3,11},{11,3},{4,12},{12,4},... | collective-permute-start | bytes 1572872 | tf_op jit(solution)/shard_map/ppermute | solution.py:24
  17.5 1.8 %collective-permute-start.4 = (bf16[256,1280]{1,0:T(8,128)(2,1)}, bf16[256,1280]{1,0:T(8,128)(2,1)}, u32[]{:S(2)}, u32[]{:S(2)}) collective-permute-start(bf16[256,1280]{1,0:T(8,128)(2,1)} %pad_maximum_fusion.3), channel_id=1, source_target_pairs={{0,8},{8,0},{1,9},{9,1},{2,10},{10,2},{3,11},{11,3},{4,12},{12,4},... | collective-permute-start | bytes 1966088 | tf_op jit(solution)/shard_map/ppermute | solution.py:24
  19.3 1.6 slice.53
  23.0 3.7 %collective-permute-done.1.cotangent_ref = bf16[256,1024]{1,0:T(8,128)(2,1)} collective-permute-done((bf16[256,1024]{1,0:T(8,128)(2,1)}, bf16[256,1024]{1,0:T(8,128)(2,1)}, u32[]{:S(2)}, u32[]{:S(2)}) %collective-permute-start.1) | collective-permute-done | bytes 524320 | tf_op jit(solution)/shard_map/ppermute | solution.py:24
  26.7 1.2 bitcast_add_fusion
  29.6 1.7 %abs_reduce_fusion.1 = bf16[]{:T(256)} fusion(bf16[256,1024]{1,0:T(8,128)(2,1)} %collective-permute-done.1.cotangent_ref), kind=kLoop, calls=%fused_computation.81 | loop fusion | flops 524287 | bytes 524290 | tf_op jit(solution)/shard_map/reduce_max | solution.py:241
  33.4 1.6 collective-permute-start.5
  35.0 1.6 collective-permute-start.7
  36.6 2.9 %collective-permute-start.8 = (f32[160,256]{1,0:T(8,128)}, f32[160,256]{1,0:T(8,128)S(1)}, u32[]{:S(2)}, u32[]{:S(2)}) collective-permute-start(f32[160,256]{1,0:T(8,128)} %get-tuple-element.117), channel_id=1, source_target_pairs={{0,128},{64,192},{128,0},{192,64},{1,129},{65,193},{129,1},{193,65... | collective-permute-start | bytes 491528 | tf_op jit(solution)/shard_map/ppermute | solution.py:24
  41.9 3.3 %collective-permute-start.6 = (f32[8,128]{1,0:T(8,128)S(1)}, f32[8,128]{1,0:T(8,128)S(1)}, u32[]{:S(2)}, u32[]{:S(2)}) collective-permute-start(f32[8,128]{1,0:T(8,128)S(1)} %maximum_select_fusion.2), channel_id=1, source_target_pairs={{0,2},{1,3},{2,0},{3,1},{4,6},{5,7},{6,4},{7,5},{8,10},{9,11},{10,... | collective-permute-start | bytes 12296 | tf_op jit(solution)/shard_map/ppermute | solution.py:24
  45.2 1.2 collective-permute-done.8
  46.4 2.0 %collective-permute-done.9 = f32[160,256]{1,0:T(8,128)S(1)} collective-permute-done((f32[160,256]{1,0:T(8,128)S(1)}, f32[160,256]{1,0:T(8,128)S(1)}, u32[]{:S(2)}, u32[]{:S(2)}) %collective-permute-start.9) | collective-permute-done | bytes 163872 | tf_op jit(solution)/shard_map/ppermute | solution.py:24
  48.5 2.2 %collective-permute-start.16 = (f32[160,128]{1,0:T(8,128)S(1)}, f32[160,128]{1,0:T(8,128)S(1)}, u32[]{:S(2)}, u32[]{:S(2)}) collective-permute-start(f32[160,128]{1,0:T(8,128)S(1)} %constant_dynamic-slice_fusion.1), channel_id=1, source_target_pairs={{0,32},{32,0},{1,33},{33,1},{2,34},{34,2},{3,35},{35,3},{4,36},{36... | collective-permute-start | bytes 245768 | tf_op jit(solution)/shard_map/ppermute | solution.py:24
  50.8 6.3 %collective-permute-start.11 = (f32[8,128]{1,0:T(8,128)S(1)}, f32[8,128]{1,0:T(8,128)S(1)}, u32[]{:S(2)}, u32[]{:S(2)}) collective-permute-start(f32[8,128]{1,0:T(8,128)S(1)} %maximum_select_fusion.1), channel_id=1, source_target_pairs={{0,4},{1,5},{2,6},{3,7},{4,0},{5,1},{6,2},{7,3},{8,12},{9,13},{10,... | collective-permute-start | bytes 12296 | tf_op jit(solution)/shard_map/ppermute | solution.py:24
  57.1 2.8 %fusion.26 = f32[1280,1024]{1,0:T(8,128)S(1)} fusion(bf16[256,1280]{1,0:T(8,128)(2,1)} %collective-permute-done.4, bf16[256,640]{1,0:T(8,128)(2,1)S(1)} %get-tuple-element.109, bf16[256,640]{1,0:T(8,128)(2,1)S(1)} %get-tuple-element.108, bf16[256,1024]{1,0:T(8,128)(2,1)} %collective-permute-done.1.cotangent_ref, bf16[256,1024]{1,0:T(8,128)(2,1)S(1)} %bitcast.28), kind=kOutput, calls=%fused_computation.45 | convolution fusion | flops 1348206592 | bytes 7602176 | tf_op jit(solution)/shard_map/dot_general | solution.py:260
  62.3 1.1 collective-permute-start.12
  63.4 3.3 %collective-permute-start.13 = (f16[160,1024]{1,0:T(8,128)(2,1)S(1)}, f16[160,1024]{1,0:T(8,128)(2,1)S(1)}, u32[]{:S(2)}, u32[]{:S(2)}) collective-permute-start(f16[160,1024]{1,0:T(8,128)(2,1)S(1)} %get-tuple-element.104), channel_id=1, source_target_pairs={{0,7},{1,2},{2,1},{3,4},{4,3},{5,6},{6,5},{7,0},{8,15},{9,10},{10,... | collective-permute-start | bytes 983048 | tf_op jit(solution)/shard_map/ppermute | solution.py:284
  67.6 4.9 %fusion.32 = f32[1280,1024]{1,0:T(8,128)} fusion(bf16[256,1280]{1,0:T(8,128)(2,1)S(1)} %collective-permute-done.2, bf16[256,640]{1,0:T(8,128)(2,1)S(1)} %copy-done.10, bf16[256,640]{1,0:T(8,128)(2,1)S(1)} %copy-done.9, bf16[256,1024]{1,0:T(8,128)(2,1)} %collective-permute-done.1.cotangent_ref, bf16[256,1024]{1,0:T(8,128)(2,1)S(1)} %bitcast.29), kind=kOutput, calls=%fused_computation.51 | convolution fusion | flops 1348206592 | bytes 7602176 | tf_op jit(solution)/shard_map/dot_general | solution.py:260
  73.6 2.5 %collective-permute-start.15 = (f16[320,1024]{1,0:T(8,128)(2,1)S(1)}, f16[320,1024]{1,0:T(8,128)(2,1)S(1)}, u32[]{:S(2)}, u32[]{:S(2)}) collective-permute-start(f16[320,1024]{1,0:T(8,128)(2,1)S(1)} %fusion.21), channel_id=1, source_target_pairs={{0,7},{1,2},{2,1},{3,4},{4,3},{5,6},{6,5},{7,0},{8,15},{9,10},{10,... | collective-permute-start | bytes 1966088 | tf_op jit(solution)/shard_map/ppermute | solution.py:284
  76.0 1.0 fusion.20
  78.1 1.5 collective-permute-start.17
  79.7 1.0 slice_dynamic-update-slice_fusion.3
  80.8 1.0 slice_dynamic-update-slice_fusion.2
  81.9 1.0 copy-done.1
  82.9 5.7 %shard_map.101 = f32[256,768]{1,0:T(8,128)} custom-call(bf16[256,2560]{1,0:T(8,128)(2,1)} %copy-done.1, bf16[2560,768]{1,0:T(8,128)(2,1)} %all-gather.3.cloned.1.call-done.weight_ref.left_ref), custom_call_target="tpu_custom_call" | custom-call | tf_op jit(solution)/shard_map/pallas_call | solution.py:109
  88.7 1.3 collective-permute-start.21
  90.3 4.9 %collective-permute-done.14 = f16[320,1024]{1,0:T(8,128)(2,1)} collective-permute-done((f16[320,1024]{1,0:T(8,128)(2,1)}, f16[320,1024]{1,0:T(8,128)(2,1)}, u32[]{:S(2)}, u32[]{:S(2)}) %collective-permute-start.14) | collective-permute-done | bytes 655392 | tf_op jit(solution)/shard_map/ppermute | solution.py:284
  95.2 3.3 %fusion.23 = f16[320,1024]{1,0:T(8,128)(2,1)} fusion(f16[320,1024]{1,0:T(8,128)(2,1)} %collective-permute-done.14, f32[1280,1024]{1,0:T(8,128)} %fusion.32, s32[]{:T(128)S(6)} %select_n.211, f32[]{:T(128)} %bitcast.6), kind=kLoop, calls=%fused_computation.42 | loop fusion | flops 2949120 | bytes 2621448 | tf_op jit(solution)/shard_map/convert_element_type | solution.py:55
  98.5 3.1 %fusion.22 = f16[320,1024]{1,0:T(8,128)(2,1)} fusion(f16[320,1024]{1,0:T(8,128)(2,1)S(1)} %collective-permute-done.15, f32[1280,1024]{1,0:T(8,128)} %copy-done.2, s32[]{:T(128)S(6)} %select_n.211, f32[]{:T(128)} %bitcast.6), kind=kLoop, calls=%fused_computation.41 | loop fusion | flops 2949120 | bytes 2621448 | tf_op jit(solution)/shard_map/convert_element_type | solution.py:55
  101.6 1.5 collective-permute-start.20
  103.6 3.2 %collective-permute-start.22 = (bf16[160,256]{1,0:T(8,128)(2,1)S(1)}, bf16[160,256]{1,0:T(8,128)(2,1)S(1)}, u32[]{:S(2)}, u32[]{:S(2)}) collective-permute-start(bf16[160,256]{1,0:T(8,128)(2,1)S(1)} %get-tuple-element.125), channel_id=1, source_target_pairs={{0,64},{64,0},{128,192},{192,128},{1,65},{65,1},{129,193},{193,129... | collective-permute-start | bytes 245768 | tf_op jit(solution)/shard_map/ppermute | solution.py:24
  106.9 2.4 %collective-permute-start.23 = (bf16[160,256]{1,0:T(8,128)(2,1)S(1)}, bf16[160,256]{1,0:T(8,128)(2,1)S(1)}, u32[]{:S(2)}, u32[]{:S(2)}) collective-permute-start(bf16[160,256]{1,0:T(8,128)(2,1)S(1)} %get-tuple-element.125), channel_id=1, source_target_pairs={{0,128},{64,192},{128,0},{192,64},{1,129},{65,193},{129,1},{193,65... | collective-permute-start | bytes 245768 | tf_op jit(solution)/shard_map/ppermute | solution.py:24
  109.3 3.0 %collective-permute-start.24 = (bf16[160,256]{1,0:T(8,128)(2,1)S(1)}, bf16[160,256]{1,0:T(8,128)(2,1)S(1)}, u32[]{:S(2)}, u32[]{:S(2)}) collective-permute-start(bf16[160,256]{1,0:T(8,128)(2,1)S(1)} %get-tuple-element.125), channel_id=1, source_target_pairs={{0,192},{64,128},{128,64},{192,0},{1,193},{65,129},{129,65},{193,1... | collective-permute-start | bytes 245768 | tf_op jit(solution)/shard_map/ppermute | solution.py:24
  112.8 2.1 %collective-permute-done.24 = bf16[160,256]{1,0:T(8,128)(2,1)S(1)} collective-permute-done((bf16[160,256]{1,0:T(8,128)(2,1)S(1)}, bf16[160,256]{1,0:T(8,128)(2,1)S(1)}, u32[]{:S(2)}, u32[]{:S(2)}) %collective-permute-start.24) | collective-permute-done | bytes 81952 | tf_op jit(solution)/shard_map/ppermute | solution.py:24
  115.0 6.8 %shard_map.102 = (f32[256,256]{1,0:T(8,128)}, bf16[256,2560]{1,0:T(8,128)(2,1)}) custom-call(bf16[256,2560]{1,0:T(8,128)(2,1)} %copy-done.1, bf16[256,1024]{1,0:T(8,128)(2,1)} %collective-permute-done.1.cotangent_ref, bf16[2560,768]{1,0:T(8,128)(2,1)} %all-gather.3.cloned.1.call-done.weight_ref.left_ref, bf16[2560,256]{1,0:T(8,128)(2,1)} %all-gather.5.cloned.1.call-done.right_ref), custom_call_target="tpu_custom_call" | custom-call | tf_op jit(solution)/shard_map/pallas_call | solution.py:132
  122.6 4.9 %fusion.25 = (f16[320,1024]{1,0:T(8,128)(2,1)}, f16[320,1024]{1,0:T(8,128)(2,1)}) fusion(f16[320,1024]{1,0:T(8,128)(2,1)} %collective-permute-done.19, f32[1280,1024]{1,0:T(8,128)} %fusion.32, s32[]{:T(128)S(6)} %select_n.212, f32[]{:T(128)} %bitcast.6, f16[320,1024]{1,0:T(8,128)(2,1)S(1)} %collective-permute-done.20, s32[]{:T(128)S(6)} %select_n.210), kind=kLoop, calls=%fused_computation.44 | loop fusion | flops 5898240 | bytes 5242892 | tf_op jit(solution)/shard_map/convert_element_type | solution.py:55
  127.5 2.0 %collective-permute-start.27 = (f16[320,1024]{1,0:T(8,128)(2,1)}, f16[320,1024]{1,0:T(8,128)(2,1)S(1)}, u32[]{:S(2)}, u32[]{:S(2)}) collective-permute-start(f16[320,1024]{1,0:T(8,128)(2,1)} %get-tuple-element.99), channel_id=1, source_target_pairs={{0,1},{1,0},{2,3},{3,2},{4,5},{5,4},{6,7},{7,6},{8,9},{9,8},{10,11... | collective-permute-start | bytes 1966088 | tf_op jit(solution)/shard_map/ppermute | solution.py:284
  129.5 1.7 %collective-permute-start.28 = (f16[320,1024]{1,0:T(8,128)(2,1)}, f16[320,1024]{1,0:T(8,128)(2,1)}, u32[]{:S(2)}, u32[]{:S(2)}) collective-permute-start(f16[320,1024]{1,0:T(8,128)(2,1)} %get-tuple-element.98), channel_id=1, source_target_pairs={{0,7},{1,2},{2,1},{3,4},{4,3},{5,6},{6,5},{7,0},{8,15},{9,10},{10,... | collective-permute-start | bytes 1966088 | tf_op jit(solution)/shard_map/ppermute | solution.py:284
  131.3 2.0 %collective-permute-start.25 = (f32[256,256]{1,0:T(8,128)}, f32[256,256]{1,0:T(8,128)S(1)}, u32[]{:S(2)}, u32[]{:S(2)}) collective-permute-start(f32[256,256]{1,0:T(8,128)} %get-tuple-element.78), channel_id=1, source_target_pairs={{0,8},{8,0},{1,9},{9,1},{2,10},{10,2},{3,11},{11,3},{4,12},{12,4},... | collective-permute-start | bytes 786440 | tf_op jit(solution)/shard_map/ppermute | solution.py:24
  133.3 7.4 %shard_map.103 = (f32[256,1024]{1,0:T(8,128)}, bf16[256,5120]{1,0:T(8,128)(2,1)}) custom-call(s32[1]{0:T(128)} %bitcast.8._, bf16[256,5120]{1,0:T(8,128)(2,1)} %bitcast.20, bf16[256,1024]{1,0:T(8,128)(2,1)} %bitcast.27, bf16[2560,768]{1,0:T(8,128)(2,1)} %all-gather.3.cloned.1.call-done.weight_ref.left_ref, ...), custom_call_target="tpu_custom_call" | custom-call | tf_op jit(solution)/shard_map/pallas_call | solution.py:159
  140.7 1.1 broadcast_select_fusion.1
  142.9 2.3 %collective-permute-done.27 = f16[320,1024]{1,0:T(8,128)(2,1)S(1)} collective-permute-done((f16[320,1024]{1,0:T(8,128)(2,1)}, f16[320,1024]{1,0:T(8,128)(2,1)S(1)}, u32[]{:S(2)}, u32[]{:S(2)}) %collective-permute-start.27) | collective-permute-done | bytes 655392 | tf_op jit(solution)/shard_map/ppermute | solution.py:284
  145.1 2.8 %collective-permute-done.28 = f16[320,1024]{1,0:T(8,128)(2,1)} collective-permute-done((f16[320,1024]{1,0:T(8,128)(2,1)}, f16[320,1024]{1,0:T(8,128)(2,1)}, u32[]{:S(2)}, u32[]{:S(2)}) %collective-permute-start.28) | collective-permute-done | bytes 655392 | tf_op jit(solution)/shard_map/ppermute | solution.py:284
  147.9 4.0 %fusion.16 = bf16[320,1024]{1,0:T(8,128)(2,1)} fusion(f16[320,1024]{1,0:T(8,128)(2,1)S(1)} %collective-permute-done.27, f16[320,1024]{1,0:T(8,128)(2,1)} %collective-permute-done.28, f32[1280,1024]{1,0:T(8,128)} %fusion.32, s32[]{:T(128)S(6)} %select_n.207, f32[]{:T(128)} %bitcast.9, f32[]{:T(128)} %bitcast.6), kind=kLoop, calls=%fused_computation.35 | loop fusion | flops 4259840 | bytes 3276812 | tf_op jit(solution)/shard_map/convert_element_type | solution.py:359
  152.3 1.0 maximum_bitcast_fusion
  153.6 4.0 %shard_map.104 = bf16[256,5120]{1,0:T(8,128)(2,1)} custom-call(s32[1]{0:T(128)} %bitcast.11._, bf16[256,5120]{1,0:T(8,128)(2,1)} %get-tuple-element.85.__, bf16[256,2560]{1,0:T(8,128)(2,1)} %copy-done.6), custom_call_target="tpu_custom_call", output_to_operand_aliasing={{}: (1, {})} | custom-call | tf_op jit(solution)/shard_map/pallas_call | solution.py:178
  (105 shorter events, 18.9 us)
Async XLA Ops:
  7.2 74.8 %all-gather.3.cloned.1.call-start = ((), (), s32[]{:S(2)}) async-start(), calls=%async_computation | async-start | bytes 4423680 | tf_op jit(solution)/shard_map/all_gather | solution.py:217
  7.2 6.4 %copy-start = (bf16[1,256,5120]{2,1,0:T(8,128)(2,1)S(1)}, bf16[1,256,5120]{2,1,0:T(8,128)(2,1)}, u32[]{:S(2)}) copy-start(bf16[1,256,5120]{2,1,0:T(8,128)(2,1)} %param.6) | copy-start | bytes 7864324
  9.2 105.8 %all-gather.5.cloned.1.call-start = ((), (), s32[]{:S(2)}) async-start(), calls=%async_computation.1 | async-start | bytes 1474560 | tf_op jit(solution)/shard_map/all_gather | solution.py:218
  11.3 15.4 %collective-permute-start = (f32[160,1024]{1,0:T(8,128)}, f32[160,1024]{1,0:T(8,128)}, u32[]{:S(2)}, u32[]{:S(2)}) collective-permute-start(f32[160,1024]{1,0:T(8,128)} %dynamic-slice_bitcast_fusion), channel_id=1, source_target_pairs={{0,16},{16,0},{1,17},{17,1},{2,18},{18,2},{3,19},{19,3},{4,20},{20... | collective-permute-start | bytes 1966088 | tf_op jit(solution)/shard_map/ppermute | solution.py:24
  11.3 15.4 %collective-permute-start.1 = (bf16[256,1024]{1,0:T(8,128)(2,1)}, bf16[256,1024]{1,0:T(8,128)(2,1)}, u32[]{:S(2)}, u32[]{:S(2)}) collective-permute-start(bf16[256,1024]{1,0:T(8,128)(2,1)} %bitcast.26), channel_id=1, source_target_pairs={{0,8},{8,0},{1,9},{9,1},{2,10},{10,2},{3,11},{11,3},{4,12},{12,4},... | collective-permute-start | bytes 1572872 | tf_op jit(solution)/shard_map/ppermute | solution.py:24
  13.6 1.9 %copy-start.11 = (f32[320,64]{0,1:T(8,128)S(1)}, f32[320,64]{0,1:T(8,128)}, u32[]{:S(2)}) copy-start(f32[320,64]{0,1:T(8,128)} %param.11) | copy-start | bytes 245764
  15.4 14.2 %collective-permute-start.3 = (f32[8,128]{1,0:T(8,128)S(1)}, f32[8,128]{1,0:T(8,128)S(1)}, u32[]{:S(2)}, u32[]{:S(2)}) collective-permute-start(f32[8,128]{1,0:T(8,128)S(1)} %broadcast_in_dim.22), channel_id=1, source_target_pairs={{0,8},{8,0},{1,9},{9,1},{2,10},{10,2},{3,11},{11,3},{4,12},{12,4},... | collective-permute-start | bytes 12296 | tf_op jit(solution)/shard_map/ppermute | solution.py:24
  16.3 24.2 %collective-permute-start.10 = (f32[160,64]{1,0:T(8,128)}, f32[160,64]{1,0:T(8,128)}, u32[]{:S(2)}, u32[]{:S(2)}) collective-permute-start(f32[160,64]{1,0:T(8,128)} %copy.22), channel_id=1, source_target_pairs={{0,16},{16,0},{1,17},{17,1},{2,18},{18,2},{3,19},{19,3},{4,20},{20... | collective-permute-start | bytes 122888 | tf_op jit(solution)/shard_map/ppermute | solution.py:24
  17.5 4.7 %copy-start.3 = (bf16[1,256,1024]{2,1,0:T(8,128)(2,1)S(1)}, bf16[1,256,1024]{2,1,0:T(8,128)(2,1)}, u32[]{:S(2)}) copy-start(bf16[1,256,1024]{2,1,0:T(8,128)(2,1)} %param.8) | copy-start | bytes 1572868
  17.5 39.6 %collective-permute-start.4 = (bf16[256,1280]{1,0:T(8,128)(2,1)}, bf16[256,1280]{1,0:T(8,128)(2,1)}, u32[]{:S(2)}, u32[]{:S(2)}) collective-permute-start(bf16[256,1280]{1,0:T(8,128)(2,1)} %pad_maximum_fusion.3), channel_id=1, source_target_pairs={{0,8},{8,0},{1,9},{9,1},{2,10},{10,2},{3,11},{11,3},{4,12},{12,4},... | collective-permute-start | bytes 1966088 | tf_op jit(solution)/shard_map/ppermute | solution.py:24
  21.2 5.4 %copy-start.5 = (f32[1,320,1024]{2,1,0:T(8,128)S(1)}, f32[1,320,1024]{2,1,0:T(8,128)}, u32[]{:S(2)}) copy-start(f32[1,320,1024]{2,1,0:T(8,128)} %param.10) | copy-start | bytes 3932164
  32.5 8.0 %copy-start.8 = (bf16[256,1280]{1,0:T(8,128)(2,1)S(1)}, bf16[256,1280]{1,0:T(8,128)(2,1)}, u32[]{:S(2)}) copy-start(bf16[256,1280]{1,0:T(8,128)(2,1)} %pad_maximum_fusion.4) | copy-start | bytes 1966084
  32.6 24.6 %copy-start.4 = (bf16[1,256,1024]{2,1,0:T(8,128)(2,1)S(1)}, bf16[1,256,1024]{2,1,0:T(8,128)(2,1)}, u32[]{:S(2)}) copy-start(bf16[1,256,1024]{2,1,0:T(8,128)(2,1)} %param.8) | copy-start | bytes 1572868
  33.4 6.2 %collective-permute-start.5 = (f32[8,128]{1,0:T(8,128)S(1)}, f32[8,128]{1,0:T(8,128)S(1)}, u32[]{:S(2)}, u32[]{:S(2)}) collective-permute-start(f32[8,128]{1,0:T(8,128)S(1)} %add_select_fusion), channel_id=1, source_target_pairs={{0,1},{1,0},{2,3},{3,2},{4,5},{5,4},{6,7},{7,6},{8,9},{9,8},{10,11... | collective-permute-start | bytes 12296 | tf_op jit(solution)/shard_map/ppermute | solution.py:24
  35.0 7.0 %collective-permute-start.7 = (f32[160,256]{1,0:T(8,128)}, f32[160,256]{1,0:T(8,128)S(1)}, u32[]{:S(2)}, u32[]{:S(2)}) collective-permute-start(f32[160,256]{1,0:T(8,128)} %get-tuple-element.118), channel_id=1, source_target_pairs={{0,64},{64,0},{128,192},{192,128},{1,65},{65,1},{129,193},{193,129... | collective-permute-start | bytes 491528 | tf_op jit(solution)/shard_map/ppermute | solution.py:24
  36.6 9.9 %collective-permute-start.8 = (f32[160,256]{1,0:T(8,128)}, f32[160,256]{1,0:T(8,128)S(1)}, u32[]{:S(2)}, u32[]{:S(2)}) collective-permute-start(f32[160,256]{1,0:T(8,128)} %get-tuple-element.117), channel_id=1, source_target_pairs={{0,128},{64,192},{128,0},{192,64},{1,129},{65,193},{129,1},{193,65... | collective-permute-start | bytes 491528 | tf_op jit(solution)/shard_map/ppermute | solution.py:24
  39.6 8.8 %collective-permute-start.9 = (f32[160,256]{1,0:T(8,128)S(1)}, f32[160,256]{1,0:T(8,128)S(1)}, u32[]{:S(2)}, u32[]{:S(2)}) collective-permute-start(f32[160,256]{1,0:T(8,128)S(1)} %get-tuple-element.116), channel_id=1, source_target_pairs={{0,192},{64,128},{128,64},{192,0},{1,193},{65,129},{129,65},{193,1... | collective-permute-start | bytes 491528 | tf_op jit(solution)/shard_map/ppermute | solution.py:24
  40.6 27.0 %collective-permute-start.2 = (bf16[256,1280]{1,0:T(8,128)(2,1)S(1)}, bf16[256,1280]{1,0:T(8,128)(2,1)S(1)}, u32[]{:S(2)}, u32[]{:S(2)}) collective-permute-start(bf16[256,1280]{1,0:T(8,128)(2,1)S(1)} %copy-done.8), channel_id=1, source_target_pairs={{0,8},{8,0},{1,9},{9,1},{2,10},{10,2},{3,11},{11,3},{4,12},{12,4},... | collective-permute-start | bytes 1966088 | tf_op jit(solution)/shard_map/ppermute | solution.py:24
  41.9 8.8 %collective-permute-start.6 = (f32[8,128]{1,0:T(8,128)S(1)}, f32[8,128]{1,0:T(8,128)S(1)}, u32[]{:S(2)}, u32[]{:S(2)}) collective-permute-start(f32[8,128]{1,0:T(8,128)S(1)} %maximum_select_fusion.2), channel_id=1, source_target_pairs={{0,2},{1,3},{2,0},{3,1},{4,6},{5,7},{6,4},{7,5},{8,10},{9,11},{10,... | collective-permute-start | bytes 12296 | tf_op jit(solution)/shard_map/ppermute | solution.py:24
  48.5 28.6 %collective-permute-start.16 = (f32[160,128]{1,0:T(8,128)S(1)}, f32[160,128]{1,0:T(8,128)S(1)}, u32[]{:S(2)}, u32[]{:S(2)}) collective-permute-start(f32[160,128]{1,0:T(8,128)S(1)} %constant_dynamic-slice_fusion.1), channel_id=1, source_target_pairs={{0,32},{32,0},{1,33},{33,1},{2,34},{34,2},{3,35},{35,3},{4,36},{36... | collective-permute-start | bytes 245768 | tf_op jit(solution)/shard_map/ppermute | solution.py:24
  50.8 9.2 %collective-permute-start.11 = (f32[8,128]{1,0:T(8,128)S(1)}, f32[8,128]{1,0:T(8,128)S(1)}, u32[]{:S(2)}, u32[]{:S(2)}) collective-permute-start(f32[8,128]{1,0:T(8,128)S(1)} %maximum_select_fusion.1), channel_id=1, source_target_pairs={{0,4},{1,5},{2,6},{3,7},{4,0},{5,1},{6,2},{7,3},{8,12},{9,13},{10,... | collective-permute-start | bytes 12296 | tf_op jit(solution)/shard_map/ppermute | solution.py:24
  59.9 12.6 %copy-start.2 = (f32[1280,1024]{1,0:T(8,128)}, f32[1280,1024]{1,0:T(8,128)S(1)}, u32[]{:S(2)}) copy-start(f32[1280,1024]{1,0:T(8,128)S(1)} %fusion.26) | copy-start | bytes 15728644
  59.9 7.6 %copy-start.9 = (bf16[256,640]{1,0:T(8,128)(2,1)S(1)}, bf16[256,640]{1,0:T(8,128)(2,1)}, u32[]{:S(2)}) copy-start(bf16[256,640]{1,0:T(8,128)(2,1)} %get-tuple-element.106) | copy-start | bytes 983044
  60.0 7.6 %copy-start.10 = (bf16[256,640]{1,0:T(8,128)(2,1)S(1)}, bf16[256,640]{1,0:T(8,128)(2,1)}, u32[]{:S(2)}) copy-start(bf16[256,640]{1,0:T(8,128)(2,1)} %get-tuple-element.107) | copy-start | bytes 983044
  62.3 10.3 %collective-permute-start.12 = (f16[160,1024]{1,0:T(8,128)(2,1)S(1)}, f16[160,1024]{1,0:T(8,128)(2,1)S(1)}, u32[]{:S(2)}, u32[]{:S(2)}) collective-permute-start(f16[160,1024]{1,0:T(8,128)(2,1)S(1)} %get-tuple-element.105), channel_id=1, source_target_pairs={{0,1},{1,0},{2,3},{3,2},{4,5},{5,4},{6,7},{7,6},{8,9},{9,8},{10,11... | collective-permute-start | bytes 983048 | tf_op jit(solution)/shard_map/ppermute | solution.py:284
  63.4 9.1 %collective-permute-start.13 = (f16[160,1024]{1,0:T(8,128)(2,1)S(1)}, f16[160,1024]{1,0:T(8,128)(2,1)S(1)}, u32[]{:S(2)}, u32[]{:S(2)}) collective-permute-start(f16[160,1024]{1,0:T(8,128)(2,1)S(1)} %get-tuple-element.104), channel_id=1, source_target_pairs={{0,7},{1,2},{2,1},{3,4},{4,3},{5,6},{6,5},{7,0},{8,15},{9,10},{10,... | collective-permute-start | bytes 983048 | tf_op jit(solution)/shard_map/ppermute | solution.py:284
  73.6 16.8 %collective-permute-start.15 = (f16[320,1024]{1,0:T(8,128)(2,1)S(1)}, f16[320,1024]{1,0:T(8,128)(2,1)S(1)}, u32[]{:S(2)}, u32[]{:S(2)}) collective-permute-start(f16[320,1024]{1,0:T(8,128)(2,1)S(1)} %fusion.21), channel_id=1, source_target_pairs={{0,7},{1,2},{2,1},{3,4},{4,3},{5,6},{6,5},{7,0},{8,15},{9,10},{10,... | collective-permute-start | bytes 1966088 | tf_op jit(solution)/shard_map/ppermute | solution.py:284
  77.0 18.1 %collective-permute-start.14 = (f16[320,1024]{1,0:T(8,128)(2,1)}, f16[320,1024]{1,0:T(8,128)(2,1)}, u32[]{:S(2)}, u32[]{:S(2)}) collective-permute-start(f16[320,1024]{1,0:T(8,128)(2,1)} %fusion.20), channel_id=1, source_target_pairs={{0,1},{1,0},{2,3},{3,2},{4,5},{5,4},{6,7},{7,6},{8,9},{9,8},{10,11... | collective-permute-start | bytes 1966088 | tf_op jit(solution)/shard_map/ppermute | solution.py:284
  78.0 11.9 %collective-permute-start.18 = (f32[160,64]{1,0:T(8,128)S(1)}, f32[160,64]{1,0:T(8,128)S(1)}, u32[]{:S(2)}, u32[]{:S(2)}) collective-permute-start(f32[160,64]{1,0:T(8,128)S(1)} %get-tuple-element.129), channel_id=1, source_target_pairs={{0,16},{16,0},{1,17},{17,1},{2,18},{18,2},{3,19},{19,3},{4,20},{20... | collective-permute-start | bytes 122888 | tf_op jit(solution)/shard_map/ppermute | solution.py:24
  78.1 11.8 %collective-permute-start.17 = (bf16[160,128]{1,0:T(8,128)(2,1)S(1)}, bf16[160,128]{1,0:T(8,128)(2,1)S(1)}, u32[]{:S(2)}, u32[]{:S(2)}) collective-permute-start(bf16[160,128]{1,0:T(8,128)(2,1)S(1)} %get-tuple-element.96), channel_id=1, source_target_pairs={{0,32},{32,0},{1,33},{33,1},{2,34},{34,2},{3,35},{35,3},{4,36},{36... | collective-permute-start | bytes 122888 | tf_op jit(solution)/shard_map/ppermute | solution.py:24
  81.9 1.1 copy-start.1
  88.7 26.3 %collective-permute-start.21 = (f32[256,768]{1,0:T(8,128)}, f32[256,768]{1,0:T(8,128)S(1)}, u32[]{:S(2)}, u32[]{:S(2)}) collective-permute-start(f32[256,768]{1,0:T(8,128)} %shard_map.101), channel_id=1, source_target_pairs={{0,8},{8,0},{1,9},{9,1},{2,10},{10,2},{3,11},{11,3},{4,12},{12,4},... | collective-permute-start | bytes 2359304 | tf_op jit(solution)/shard_map/ppermute | solution.py:24
  101.6 21.0 %collective-permute-start.20 = (f16[320,1024]{1,0:T(8,128)(2,1)}, f16[320,1024]{1,0:T(8,128)(2,1)S(1)}, u32[]{:S(2)}, u32[]{:S(2)}) collective-permute-start(f16[320,1024]{1,0:T(8,128)(2,1)} %fusion.23), channel_id=1, source_target_pairs={{0,7},{1,2},{2,1},{3,4},{4,3},{5,6},{6,5},{7,0},{8,15},{9,10},{10,... | collective-permute-start | bytes 1966088 | tf_op jit(solution)/shard_map/ppermute | solution.py:284
  103.2 19.5 %collective-permute-start.19 = (f16[320,1024]{1,0:T(8,128)(2,1)}, f16[320,1024]{1,0:T(8,128)(2,1)}, u32[]{:S(2)}, u32[]{:S(2)}) collective-permute-start(f16[320,1024]{1,0:T(8,128)(2,1)} %fusion.22), channel_id=1, source_target_pairs={{0,1},{1,0},{2,3},{3,2},{4,5},{5,4},{6,7},{7,6},{8,9},{9,8},{10,11... | collective-permute-start | bytes 1966088 | tf_op jit(solution)/shard_map/ppermute | solution.py:284
  103.6 5.7 %collective-permute-start.22 = (bf16[160,256]{1,0:T(8,128)(2,1)S(1)}, bf16[160,256]{1,0:T(8,128)(2,1)S(1)}, u32[]{:S(2)}, u32[]{:S(2)}) collective-permute-start(bf16[160,256]{1,0:T(8,128)(2,1)S(1)} %get-tuple-element.125), channel_id=1, source_target_pairs={{0,64},{64,0},{128,192},{192,128},{1,65},{65,1},{129,193},{193,129... | collective-permute-start | bytes 245768 | tf_op jit(solution)/shard_map/ppermute | solution.py:24
  106.9 5.9 %collective-permute-start.23 = (bf16[160,256]{1,0:T(8,128)(2,1)S(1)}, bf16[160,256]{1,0:T(8,128)(2,1)S(1)}, u32[]{:S(2)}, u32[]{:S(2)}) collective-permute-start(bf16[160,256]{1,0:T(8,128)(2,1)S(1)} %get-tuple-element.125), channel_id=1, source_target_pairs={{0,128},{64,192},{128,0},{192,64},{1,129},{65,193},{129,1},{193,65... | collective-permute-start | bytes 245768 | tf_op jit(solution)/shard_map/ppermute | solution.py:24
  109.3 5.7 %collective-permute-start.24 = (bf16[160,256]{1,0:T(8,128)(2,1)S(1)}, bf16[160,256]{1,0:T(8,128)(2,1)S(1)}, u32[]{:S(2)}, u32[]{:S(2)}) collective-permute-start(bf16[160,256]{1,0:T(8,128)(2,1)S(1)} %get-tuple-element.125), channel_id=1, source_target_pairs={{0,192},{64,128},{128,64},{192,0},{1,193},{65,129},{129,65},{193,1... | collective-permute-start | bytes 245768 | tf_op jit(solution)/shard_map/ppermute | solution.py:24
  121.8 30.4 %collective-permute-start.26 = (bf16[256,2560]{1,0:T(8,128)(2,1)}, bf16[256,2560]{1,0:T(8,128)(2,1)S(1)}, u32[]{:S(2)}, u32[]{:S(2)}) collective-permute-start(bf16[256,2560]{1,0:T(8,128)(2,1)} %get-tuple-element.79), channel_id=1, source_target_pairs={{0,8},{8,0},{1,9},{9,1},{2,10},{10,2},{3,11},{11,3},{4,12},{12,4},... | collective-permute-start | bytes 3932168 | tf_op jit(solution)/shard_map/ppermute | solution.py:24
  121.9 18.8 %collective-permute-start.29 = (bf16[160,1024]{1,0:T(8,128)(2,1)S(1)}, bf16[160,1024]{1,0:T(8,128)(2,1)}, u32[]{:S(2)}, u32[]{:S(2)}) collective-permute-start(bf16[160,1024]{1,0:T(8,128)(2,1)S(1)} %constant_dynamic-update-slice_fusion), channel_id=1, source_target_pairs={{0,16},{16,0},{1,17},{17,1},{2,18},{18,2},{3,19},{19,3},{4,20},{20... | collective-permute-start | bytes 983048 | tf_op jit(solution)/shard_map/ppermute | solution.py:24
  127.5 17.6 %collective-permute-start.27 = (f16[320,1024]{1,0:T(8,128)(2,1)}, f16[320,1024]{1,0:T(8,128)(2,1)S(1)}, u32[]{:S(2)}, u32[]{:S(2)}) collective-permute-start(f16[320,1024]{1,0:T(8,128)(2,1)} %get-tuple-element.99), channel_id=1, source_target_pairs={{0,1},{1,0},{2,3},{3,2},{4,5},{5,4},{6,7},{7,6},{8,9},{9,8},{10,11... | collective-permute-start | bytes 1966088 | tf_op jit(solution)/shard_map/ppermute | solution.py:284
  129.5 18.4 %collective-permute-start.28 = (f16[320,1024]{1,0:T(8,128)(2,1)}, f16[320,1024]{1,0:T(8,128)(2,1)}, u32[]{:S(2)}, u32[]{:S(2)}) collective-permute-start(f16[320,1024]{1,0:T(8,128)(2,1)} %get-tuple-element.98), channel_id=1, source_target_pairs={{0,7},{1,2},{2,1},{3,4},{4,3},{5,6},{6,5},{7,0},{8,15},{9,10},{10,... | collective-permute-start | bytes 1966088 | tf_op jit(solution)/shard_map/ppermute | solution.py:284
  131.3 21.0 %collective-permute-start.25 = (f32[256,256]{1,0:T(8,128)}, f32[256,256]{1,0:T(8,128)S(1)}, u32[]{:S(2)}, u32[]{:S(2)}) collective-permute-start(f32[256,256]{1,0:T(8,128)} %get-tuple-element.78), channel_id=1, source_target_pairs={{0,8},{8,0},{1,9},{9,1},{2,10},{10,2},{3,11},{11,3},{4,12},{12,4},... | collective-permute-start | bytes 786440 | tf_op jit(solution)/shard_map/ppermute | solution.py:24
  140.7 2.0 %copy-start.7 = (f32[256,1024]{1,0:T(8,128)S(1)}, f32[256,1024]{1,0:T(8,128)}, u32[]{:S(2)}) copy-start(f32[256,1024]{1,0:T(8,128)} %get-tuple-element.83) | copy-start | bytes 3145732
  152.3 1.3 copy-start.6
Sparse Core Ops, SparseCore 0:
  10.4 55.6 all-gather.2
  67.8 44.9 all-gather.4

commit v2 on v1

v2 whole, which is shorter than its diff:
```python
import jax
import jax.numpy as jnp
from jax import lax
from jax.experimental import pallas as pl
from jax.experimental.pallas import tpu as pltpu
from jax.sharding import Mesh
from jax.sharding import PartitionSpec as P

OUTER_RATE = 0.7
NESTEROV = 0.9
BF16 = jnp.bfloat16
F32 = jnp.float32
F16 = jnp.float16

SIZES = {"y": 4, "xh": 2, "c": 2, "xl": 2, "z": 8}
REP = ("y", "xh", "c")
FSDP = ("xl", "z")
N_Z = 8
EVEN = [(i, i ^ 1) for i in range(N_Z)]
ODD = [(i, (i - 1) % N_Z if i % 2 == 0 else (i + 1) % N_Z) for i in range(N_Z)]


def swap(value, axis, mask=1):
    return lax.ppermute(value, axis, [(i, i ^ mask) for i in range(SIZES[axis])])


class Sequence:
    def __init__(self):
        self.last = ()

    def step(self, *values):
        held = lax.optimization_barrier((*values, *self.last))[: len(values)]
        return held[0] if len(held) == 1 else held

    def did(self, *values):
        self.last = values


def rows_of(array, start, size):
    return lax.dynamic_slice_in_dim(array, start, size, 0)


def columns_of(array, start, size):
    return lax.dynamic_slice_in_dim(array, start, size, 1)


def in_order(here, mine, theirs, axis):
    first = here == 0
    return jnp.concatenate(
        [jnp.where(first, mine, theirs), jnp.where(first, theirs, mine)], axis=axis
    )


def encode(scaled):
    return (scaled * jnp.abs(scaled)).astype(F16)


def decode(sent):
    wide = sent.astype(F32)
    return jnp.sign(wide) * jnp.sqrt(jnp.abs(wide))


def column_peak(tokens):
    return jnp.max(jnp.sum(jnp.abs(tokens.astype(F32)), axis=0))


def as_tile(first, second):
    row = lax.broadcasted_iota(jnp.int32, (8, 128), 0)
    return jnp.where(row < 4, first, second)


def join_peaks(peaks, other):
    return as_tile(peaks + other, jnp.maximum(peaks, other))


def dot(left, right):
    return jnp.dot(left, right, preferred_element_type=F32)


def dot_t(left, right):
    return lax.dot_general(left, right, (((1,), (1,)), ((), ())), preferred_element_type=F32)


FREE = pl.CostEstimate(flops=0, bytes_accessed=0, transcendentals=0)


def whole(array):
    return pl.BlockSpec(array.shape, lambda i, *_: (0, 0))


def assemble(here, places, pieces, axis):
    size = pieces[0].shape[axis]

    def body(here_ref, *refs):
        out_ref = refs[-1]
        for place, piece_ref in zip(places(here_ref[0]), refs[:-1]):
            at = pl.ds(pl.multiple_of(place * size, 32 if axis == 0 else 128), size)
            if axis == 0:
                out_ref[at, :] = piece_ref[...]
            else:
                out_ref[:, at] = piece_ref[...]

    shape = list(pieces[0].shape)
    shape[axis] *= len(pieces)
    out = jax.ShapeDtypeStruct(tuple(shape), pieces[0].dtype)
    return pl.pallas_call(
        body,
        grid_spec=pltpu.PrefetchScalarGridSpec(
            num_scalar_prefetch=1,
            grid=(1,),
            in_specs=[whole(p) for p in pieces],
            out_specs=whole(out),
        ),
        out_shape=out,
        cost_estimate=FREE,
    )(here.reshape(1), *pieces)


def products_for_partner(z, early, late, cotangent, weight):
    count = 4
    wide = weight.shape[0] // count

    def group(i, z_ref):
        step = 1 - 2 * (z_ref[0] % 2)
        return (z_ref[0] // 2 + jnp.where(i % 2 == 1, 4 + step * (2 - i), 2 - i)) % 4

    def body(_, early_ref, late_ref, cotangent_ref, weight_ref, keys_ref, grads_ref):
        i = pl.program_id(0)

        @pl.when(i == 0)
        def _():
            keys_ref[...] = jnp.zeros_like(keys_ref)

        tokens = jnp.where(i < count // 2, early_ref[...], late_ref[...])
        keys_ref[...] += dot(tokens, weight_ref[...])
        grads_ref[...] = dot_t(cotangent_ref[...], weight_ref[...]).astype(BF16)

    rows = cotangent.shape[0]
    keys = jax.ShapeDtypeStruct(cotangent.shape, F32)
    return pl.pallas_call(
        body,
        grid_spec=pltpu.PrefetchScalarGridSpec(
            num_scalar_prefetch=1,
            grid=(count,),
            in_specs=[
                pl.BlockSpec((rows, wide), lambda i, g: (0, jnp.minimum(i, count // 2 - 1))),
                pl.BlockSpec((rows, wide), lambda i, g: (0, jnp.maximum(i - count // 2, 0))),
                whole(cotangent),
                pl.BlockSpec((wide, weight.shape[1]), lambda i, r: (group(i, r), 0)),
            ],
            out_specs=[whole(keys), pl.BlockSpec((rows, wide), lambda i, r: (0, group(i, r)))],
        ),
        out_shape=[keys, jax.ShapeDtypeStruct((rows, weight.shape[0]), BF16)],
        cost_estimate=FREE,
    )(z.reshape(1), early, late, cotangent, weight)


def products_here(side, tokens, cotangent, weight, keys_back):
    count = 4
    wide = weight.shape[0] // count

    def body(_, tokens_ref, cotangent_ref, weight_ref, back_ref, keys_ref, grads_ref, sum_ref):
        @pl.when(pl.program_id(0) == 0)
        def _():
            sum_ref[...] = back_ref[...]

        sum_ref[...] += dot(tokens_ref[...], weight_ref[...])
        grads_ref[...] = dot_t(cotangent_ref[...], weight_ref[...]).astype(BF16)

        @pl.when(pl.program_id(0) == count - 1)
        def _():
            keys_ref[...] = sum_ref[...].astype(BF16)

    keys = jax.ShapeDtypeStruct(cotangent.shape, BF16)
    here = pl.BlockSpec((tokens.shape[0], wide), lambda i, s: (0, s[0] * count + i))
    return pl.pallas_call(
        body,
        grid_spec=pltpu.PrefetchScalarGridSpec(
            num_scalar_prefetch=1,
            grid=(count,),
            in_specs=[
                here,
                whole(cotangent),
                pl.BlockSpec((wide, weight.shape[1]), lambda i, s: (i, 0)),
                whole(keys_back),
            ],
            out_specs=[whole(keys), here],
            scratch_shapes=[pltpu.VMEM(keys_back.shape, F32)],
        ),
        out_shape=[keys, jax.ShapeDtypeStruct(tokens.shape, BF16)],
        cost_estimate=FREE,
    )(side.reshape(1), tokens, cotangent, weight, keys_back)


def shards(activations, key_weights, key_cotangent, fragment, pseudo_grads, momentum):
    tokens, weight, cotangent, pseudo = (
        a[0] for a in (activations, key_weights, key_cotangent, pseudo_grads)
    )
    y, xh, c, x, z = (lax.axis_index(a) for a in SIZES)
    order = Sequence()
    half = tokens.shape[1] // 2
    rows = pseudo.shape[0] // 2
    mine, theirs = c * rows, (1 - c) * rows
    width = momentum.shape[1]
    pair = 2 * width
    quarter = 2 * pair
    chunk = half // N_Z
    odd_z = z % 2
    sign = 1 - 2 * odd_z
    group = z // 2
    early = [(group + 2) % 4, (group + 4 + sign) % 4]
    late = [group, (group + 4 - sign) % 4]

    def token_columns(array, side, groups):
        parts = [columns_of(array, side * half + g * 2 * chunk, 2 * chunk) for g in groups]
        return jnp.concatenate(parts, axis=1)

    weight_half = lax.all_gather(weight, "z", axis=0, tiled=True)
    cotangent_other = swap(cotangent, "xl")

    give = rows_of(pseudo, theirs, rows)
    order.did(give)
    pseudo_other = swap(give, "c")
    peak = jnp.full((8, 128), column_peak(order.step(tokens)))
    order.did(peak)
    peak_other = swap(peak, "xl")
    sent = token_columns(order.step(tokens), 1 - x, early)
    order.did(sent)
    early_other = swap(sent, "xl")
    pseudo_other, cotangent_other = order.step(pseudo_other, cotangent_other)
    total = rows_of(pseudo, mine, rows) + pseudo_other
    gives = [columns_of(total, (y ^ m) * quarter, quarter) for m in (1, 2, 3)]
    old_give = rows_of(momentum, theirs, rows)
    order.did(*gives, old_give)
    others = [swap(g, "y", m) for g, m in zip(gives, (1, 2, 3))]
    old_other = swap(old_give, "c")
    sent = token_columns(order.step(tokens), 1 - x, late)
    order.did(sent)
    late_other = swap(sent, "xl")
    peak_other = order.step(peak_other)
    peak_c = jnp.maximum(jnp.max(jnp.abs(cotangent)), jnp.max(jnp.abs(cotangent_other)))
    peaks = as_tile(peak + peak_other, peak_c.astype(F32))
    order.did(peaks)
    peaks_other = swap(peaks, "z", 1)
    early_mine = token_columns(order.step(tokens), x, early)
    order.did(early_mine)
    peaks = join_peaks(peaks, order.step(peaks_other))
    order.did(peaks)
    peaks_other = swap(peaks, "z", 2)
    *others, old_other = order.step(*others, old_other)
    summed = columns_of(total, y * quarter, quarter) + others[0] + others[1] + others[2]
    give = columns_of(summed, (1 - xh) * pair, pair)
    order.did(summed, give)
    summed_other = swap(give, "xh")
    peaks = join_peaks(peaks, order.step(peaks_other))
    order.did(peaks)
    peaks_other = swap(peaks, "z", 4)

    def product(first, second):
        return lax.dot_general(
            jnp.concatenate([first, second], axis=0),
            jnp.concatenate([cotangent, cotangent_other], axis=0),
            (((0,), (0,)), ((), ())),
            preferred_element_type=F32,
        )

    early_other = order.step(early_other)
    partial_early = product(early_mine, early_other)
    order.did(partial_early)
    peaks = join_peaks(peaks, order.step(peaks_other))
    bound = jnp.maximum(peaks[0, 0] * peaks[4, 0], 1e-32)
    scale, back = 240.0 / bound, bound / (64.0 * 240.0)
    place = {4: odd_z, -3: 1 - odd_z, 2: 2 + odd_z, 3: 3 - odd_z}
    place_late = {0: odd_z, 1: 1 - odd_z, -2: 2 + odd_z, -1: 3 - odd_z}

    def own(distance, start=0, size=chunk):
        if distance in place:
            return rows_of(partial_early, place[distance] * chunk + start, size) * scale
        return rows_of(partial_late, place_late[distance] * chunk + start, size) * scale

    def send(value, pairs):
        message = encode(value)
        order.did(message)
        return lax.ppermute(message, "z", pairs)

    def ring_step(distance, even_in, odd_in):
        odd_out = send(own(-distance) + decode(order.step(even_in)), ODD)
        even_out = send(own(distance) + decode(order.step(odd_in)), EVEN)
        return even_out, odd_out

    part = chunk // 2
    far_even = send(own(4, 0, part), EVEN)
    far_odd = send(own(4, part, part), ODD)

    late_other = order.step(late_other)
    late_mine = token_columns(tokens, x, late)
    partial_late = product(late_mine, late_other)
    order.did(partial_late)

    far_even, far_odd = order.step(far_even, far_odd)
    odd = jnp.concatenate([own(-3, 0, part) + decode(far_even), own(-3, part, part)])
    odd = send(odd, ODD)
    even = jnp.concatenate([own(3, 0, part), own(3, part, part) + decode(far_odd)])
    even = send(even, EVEN)

    summed_other = order.step(summed_other)
    average = (columns_of(summed, xh * pair, pair) + summed_other) / 16
    old = in_order(c, rows_of(momentum, mine, rows), old_other, 1)
    new = NESTEROV * old + average
    here = lax.dynamic_slice(fragment, (mine, (2 * y + xh) * pair), (rows, pair))
    updated = (here.astype(F32) - OUTER_RATE * (average + NESTEROV * new)).astype(BF16)
    keep = jnp.where(c == 0, new[:, :width], new[:, width:])
    give = jnp.where(c == 0, new[:, width:], new[:, :width])
    order.did(updated, keep, give)
    updated_other = swap(updated, "xh")
    new_other = swap(give, "c")

    weight_half = order.step(weight_half)
    keys_other, grads_other = products_for_partner(
        z,
        early_other,
        late_other,
        cotangent_other,
        weight_half,
    )
    order.did(keys_other, grads_other)
    keys_back = swap(keys_other, "xl")
    grads_back = swap(grads_other, "xl")

    updated_other, new_other = order.step(updated_other, new_other)
    new_momentum = assemble(c, lambda i: (i, 1 - i), (keep, new_other), 0)
    wide = assemble(xh, lambda i: (i, 1 - i), (updated, updated_other), 1)
    order.did(wide, new_momentum)
    wides = [swap(wide, "y", m) for m in (1, 2, 3)]

    even, odd = ring_step(2, even, odd)

    wides = order.step(*wides)
    block = assemble(y, lambda i: (i, i ^ 1, i ^ 2, i ^ 3), (wide, *wides), 1)
    order.did(block)
    block_other = swap(block, "c")

    keys_back, even = order.step(keys_back, even)
    even, odd = ring_step(1, even, odd)

    key_out, grads_mine = products_here(
        order.step(x), tokens, cotangent, weight_half, keys_back
    )
    order.did(key_out, grads_mine)
    new_fragment = assemble(c, lambda i: (i, 1 - i), (block, order.step(block_other)), 0)
    order.did(new_fragment)
    even, odd = order.step(even, odd)
    weight_grad = ((own(0) + decode(even) + decode(odd)) * back).astype(BF16)
    order.did(weight_grad)
    act_grad = lax.dynamic_update_slice(grads_mine, order.step(grads_back), (0, (1 - x) * half))
    return (
        key_out[None],
        act_grad[None],
        weight_grad[None],
        new_fragment,
        new_momentum,
    )


def solution(mesh):
    fine = Mesh(mesh.devices.reshape(tuple(SIZES.values())), tuple(SIZES))
    return jax.shard_map(
        shards,
        mesh=fine,
        in_specs=(
            P(REP, FSDP, None),
            P(REP, FSDP, None),
            P(REP, FSDP, None),
            P(FSDP, None),
            P(REP, FSDP, None),
            P(FSDP, REP),
        ),
        out_specs=(
            P(REP, FSDP, None),
            P(REP, FSDP, None),
            P(REP, FSDP, None),
            P(FSDP, None),
            P(FSDP, REP),
        ),
        check_vma=False,
    )
```

time: 167 us -> 161 us (0.964)
  local copies, waits for them, and re-layouts: 13.9 us -> 10.8 us
  Pallas kernels: 23.9 us -> 21.5 us
    slice x2 -> x0, local copies, waits for them, and re-layouts: 3.58 us -> none  [the longest x1 1.99 us: shards(): weight_left = lax.all_gather(weight[:, :cut], 'z', axis=0, tiled=True)]
    unnamed x27 -> x43, local copies, waits for them, and re-layouts: 2.89 us -> 6.19 us
    pallas_call x3 -> x5, Pallas kernels: 16.5 us -> 13.9 us  [the longest x1 7.17 us: products_for_partner(): pl.pallas_call(body, grid_spec=pltpu.PrefetchScalarGridSpec(num_scalar_pr...]
    dynamic_update_slice x7 -> x1, local copies, waits for them, and re-layouts: 2.17 us -> 0.14 us  [shards(): lax.dynamic_update_slice(grads_mine, order.step(grads_back), (0, (1 - x)...]
    ppermute x8, waiting for transfers between devices: 10.2 us -> 12.1 us  [send(): return lax.ppermute(message, 'z', pairs)]
    reduce_sum x1, other arithmetic: 0.54 us -> 2.44 us  [column_peak(): return jnp.max(jnp.sum(jnp.abs(tokens.astype(F32)), axis=0))]
    ppermute x22 -> x21, starting transfers between devices: 36.7 us -> 35 us  [swap(): lax.ppermute(value, axis, [(i, i ^ mask) for i in range(SIZES[axis])])]
    ppermute x22 -> x21, waiting for transfers between devices: 10.7 us -> 9.65 us  [swap(): lax.ppermute(value, axis, [(i, i ^ mask) for i in range(SIZES[axis])])]
  transfers between devices with their start and end apart: 32 -> 30, of which waited for: 11 -> 12; matrix products, arithmetic and copies ran while one was open for 29% -> 28% of each run, Pallas kernels for 12% -> 13%
where the time goes in v2:
time: 161 us; the launch traced here: 160 us
  starting transfers between devices  48.6 us (30%)
  other arithmetic  31.4 us (20%)
  waiting for transfers between devices  22.4 us (14%)
  Pallas kernels  21.5 us (13%)
  between operations  17.2 us (11%)
  local copies, waits for them, and re-layouts  10.8 us (7%)
  matrix products  8.05 us (5%)
    ppermute x21, starting transfers between devices, swap(): lax.ppermute(value, axis, [(i, i ^ mask) for i in range(SIZES[axis])])  35 us
    convert_element_type x7, other arithmetic, encode(): return (scaled * jnp.abs(scaled)).astype(F16)  13.7 us
    ppermute x8, starting transfers between devices, send(): return lax.ppermute(message, 'z', pairs)  13.6 us
    ppermute x8, waiting for transfers between devices, send(): return lax.ppermute(message, 'z', pairs)  12.1 us
    ppermute x21, waiting for transfers between devices, swap(): lax.ppermute(value, axis, [(i, i ^ mask) for i in range(SIZES[axis])])  9.65 us
    dot_general x2, matrix products, product(): lax.dot_general(jnp.concatenate([first, second], axis=0), jnp.concatenate...  8.05 us
    pallas_call x1, Pallas kernels, products_here(): pl.pallas_call(body, grid_spec=pltpu.PrefetchScalarGridSpec(num_scalar_pr...  7.53 us
    pallas_call x1, Pallas kernels, products_for_partner(): pl.pallas_call(body, grid_spec=pltpu.PrefetchScalarGridSpec(num_scalar_pr...  7.17 us
  transfers between devices with their start and end apart: 30, of which 12 were waited for; matrix products, arithmetic and copies ran while one was open for 28% of the time, Pallas kernels for 13%

profile of v2, /device:TPU:2, one launch (start us, length us, event | category | flops | bytes accessed | tf_op | source)
XLA Modules:
  0.0 160.0 jit_solution(14980353112497746599)
XLA Ops:
  7.9 2.0 %dynamic-slice_bitcast_fusion = f32[160,1024]{1,0:T(8,128)} fusion(f32[1,320,1024]{2,1,0:T(8,128)} %param.10, s32[]{:T(128)S(6)} %select_n.145), kind=kLoop, calls=%fused_computation.78 | loop fusion | bytes 1310724 | tf_op jit(solution)/shard_map/dynamic_slice | solution.py:40
  9.9 2.3 %collective-permute-start.1 = (bf16[256,1024]{1,0:T(8,128)(2,1)}, bf16[256,1024]{1,0:T(8,128)(2,1)S(1)}, u32[]{:S(2)}, u32[]{:S(2)}) collective-permute-start(bf16[256,1024]{1,0:T(8,128)(2,1)} %bitcast.5.cotangent_ref), channel_id=1, source_target_pairs={{0,8},{8,0},{1,9},{9,1},{2,10},{10,2},{3,11},{11,3},{4,12},{12,4},... | collective-permute-start | bytes 1572872 | tf_op jit(solution)/shard_map/ppermute | solution.py:24
  12.2 2.4 %abs_reduce_fusion = f32[5120]{0:T(1024)S(1)} fusion(bf16[256,5120]{1,0:T(8,128)(2,1)} %bitcast.24), kind=kLoop, calls=%fused_computation | loop fusion | flops 3927040 | bytes 2641920 | tf_op jit(solution)/shard_map/reduce_sum | solution.py:64
  18.1 1.8 %collective-permute-start.4 = (bf16[256,1280]{1,0:T(8,128)(2,1)}, bf16[256,1280]{1,0:T(8,128)(2,1)}, u32[]{:S(2)}, u32[]{:S(2)}) collective-permute-start(bf16[256,1280]{1,0:T(8,128)(2,1)} %pad_maximum_fusion.3), channel_id=1, source_target_pairs={{0,8},{8,0},{1,9},{9,1},{2,10},{10,2},{3,11},{11,3},{4,12},{12,4},... | collective-permute-start | bytes 1966088 | tf_op jit(solution)/shard_map/ppermute | solution.py:24
  20.0 1.8 %abs_reduce_fusion.2 = bf16[]{:T(256)} fusion(bf16[1,256,1024]{2,1,0:T(8,128)(2,1)} %param.8), kind=kLoop, calls=%fused_computation.80 | loop fusion | flops 524287 | bytes 524290 | tf_op jit(solution)/shard_map/reduce_max | solution.py:241
  21.8 3.4 %collective-permute-done.1.cotangent_ref = bf16[256,1024]{1,0:T(8,128)(2,1)S(1)} collective-permute-done((bf16[256,1024]{1,0:T(8,128)(2,1)}, bf16[256,1024]{1,0:T(8,128)(2,1)S(1)}, u32[]{:S(2)}, u32[]{:S(2)}) %collective-permute-start.1) | collective-permute-done | bytes 524320 | tf_op jit(solution)/shard_map/ppermute | solution.py:24
  26.0 1.4 bitcast_add_fusion
  32.1 1.6 %collective-permute-start.5 = (f32[8,128]{1,0:T(8,128)S(1)}, f32[8,128]{1,0:T(8,128)S(1)}, u32[]{:S(2)}, u32[]{:S(2)}) collective-permute-start(f32[8,128]{1,0:T(8,128)S(1)} %add_select_fusion), channel_id=1, source_target_pairs={{0,1},{1,0},{2,3},{3,2},{4,5},{5,4},{6,7},{7,6},{8,9},{9,8},{10,11... | collective-permute-start | bytes 12296 | tf_op jit(solution)/shard_map/ppermute | solution.py:24
  33.7 1.6 collective-permute-start.7
  35.3 2.9 %collective-permute-start.8 = (f32[160,256]{1,0:T(8,128)}, f32[160,256]{1,0:T(8,128)S(1)}, u32[]{:S(2)}, u32[]{:S(2)}) collective-permute-start(f32[160,256]{1,0:T(8,128)} %get-tuple-element.107), channel_id=1, source_target_pairs={{0,128},{64,192},{128,0},{192,64},{1,129},{65,193},{129,1},{193,65... | collective-permute-start | bytes 491528 | tf_op jit(solution)/shard_map/ppermute | solution.py:24
  40.7 3.1 %collective-permute-start.6 = (f32[8,128]{1,0:T(8,128)S(1)}, f32[8,128]{1,0:T(8,128)S(1)}, u32[]{:S(2)}, u32[]{:S(2)}) collective-permute-start(f32[8,128]{1,0:T(8,128)S(1)} %maximum_select_fusion.2), channel_id=1, source_target_pairs={{0,2},{1,3},{2,0},{3,1},{4,6},{5,7},{6,4},{7,5},{8,10},{9,11},{10,... | collective-permute-start | bytes 12296 | tf_op jit(solution)/shard_map/ppermute | solution.py:24
  43.9 1.3 collective-permute-done.8
  45.2 2.0 %collective-permute-done.9 = f32[160,256]{1,0:T(8,128)S(1)} collective-permute-done((f32[160,256]{1,0:T(8,128)S(1)}, f32[160,256]{1,0:T(8,128)S(1)}, u32[]{:S(2)}, u32[]{:S(2)}) %collective-permute-start.9) | collective-permute-done | bytes 163872 | tf_op jit(solution)/shard_map/ppermute | solution.py:24
  47.3 6.5 %collective-permute-start.11 = (f32[8,128]{1,0:T(8,128)S(1)}, f32[8,128]{1,0:T(8,128)S(1)}, u32[]{:S(2)}, u32[]{:S(2)}) collective-permute-start(f32[8,128]{1,0:T(8,128)S(1)} %maximum_select_fusion.1), channel_id=1, source_target_pairs={{0,4},{1,5},{2,6},{3,7},{4,0},{5,1},{6,2},{7,3},{8,12},{9,13},{10,... | collective-permute-start | bytes 12296 | tf_op jit(solution)/shard_map/ppermute | solution.py:24
  53.8 2.8 %fusion.26 = f32[1280,1024]{1,0:T(8,128)S(1)} fusion(bf16[256,1280]{1,0:T(8,128)(2,1)} %collective-permute-done.4.early_ref, bf16[256,640]{1,0:T(8,128)(2,1)S(1)} %get-tuple-element.101, bf16[256,640]{1,0:T(8,128)(2,1)S(1)} %get-tuple-element.100, bf16[256,1024]{1,0:T(8,128)(2,1)S(1)} %copy-done.4, bf16[256,1024]{1,0:T(8,128)(2,1)} %bitcast.5.cotangent_ref), kind=kOutput, calls=%fused_computation.45 | convolution fusion | flops 1348206592 | bytes 7602176 | tf_op jit(solution)/shard_map/dot_general | solution.py:260
  58.9 1.2 collective-permute-start.12
  60.1 3.3 %collective-permute-start.13 = (f16[160,1024]{1,0:T(8,128)(2,1)S(1)}, f16[160,1024]{1,0:T(8,128)(2,1)S(1)}, u32[]{:S(2)}, u32[]{:S(2)}) collective-permute-start(f16[160,1024]{1,0:T(8,128)(2,1)S(1)} %get-tuple-element.96), channel_id=1, source_target_pairs={{0,7},{1,2},{2,1},{3,4},{4,3},{5,6},{6,5},{7,0},{8,15},{9,10},{10,... | collective-permute-start | bytes 983048 | tf_op jit(solution)/shard_map/ppermute | solution.py:284
  63.5 2.4 %collective-permute-start.15 = (f32[160,128]{1,0:T(8,128)S(1)}, f32[160,128]{1,0:T(8,128)S(1)}, u32[]{:S(2)}, u32[]{:S(2)}) collective-permute-start(f32[160,128]{1,0:T(8,128)S(1)} %constant_dynamic-slice_fusion.1), channel_id=1, source_target_pairs={{0,32},{32,0},{1,33},{33,1},{2,34},{34,2},{3,35},{35,3},{4,36},{36... | collective-permute-start | bytes 245768 | tf_op jit(solution)/shard_map/ppermute | solution.py:24
  65.9 5.2 %fusion.32 = f32[1280,1024]{1,0:T(8,128)} fusion(bf16[256,1280]{1,0:T(8,128)(2,1)S(1)} %collective-permute-done.2.late_ref, bf16[256,640]{1,0:T(8,128)(2,1)S(1)} %get-tuple-element.99, bf16[256,640]{1,0:T(8,128)(2,1)S(1)} %get-tuple-element.98, bf16[256,1024]{1,0:T(8,128)(2,1)S(1)} %copy-done.4, bf16[256,1024]{1,0:T(8,128)(2,1)} %bitcast.5.cotangent_ref), kind=kOutput, calls=%fused_computation.51 | convolution fusion | flops 1348206592 | bytes 7602176 | tf_op jit(solution)/shard_map/dot_general | solution.py:260
  71.2 4.7 %collective-permute-done.12 = f16[160,1024]{1,0:T(8,128)(2,1)S(1)} collective-permute-done((f16[160,1024]{1,0:T(8,128)(2,1)S(1)}, f16[160,1024]{1,0:T(8,128)(2,1)S(1)}, u32[]{:S(2)}, u32[]{:S(2)}) %collective-permute-start.12) | collective-permute-done | bytes 327712 | tf_op jit(solution)/shard_map/ppermute | solution.py:284
  75.8 2.2 %collective-permute-done.13 = f16[160,1024]{1,0:T(8,128)(2,1)S(1)} collective-permute-done((f16[160,1024]{1,0:T(8,128)(2,1)S(1)}, f16[160,1024]{1,0:T(8,128)(2,1)S(1)}, u32[]{:S(2)}, u32[]{:S(2)}) %collective-permute-start.13) | collective-permute-done | bytes 327712 | tf_op jit(solution)/shard_map/ppermute | solution.py:284
  80.1 1.0 fusion.22
  81.1 3.0 %collective-permute-start.20 = (f16[320,1024]{1,0:T(8,128)(2,1)}, f16[320,1024]{1,0:T(8,128)(2,1)S(1)}, u32[]{:S(2)}, u32[]{:S(2)}) collective-permute-start(f16[320,1024]{1,0:T(8,128)(2,1)} %fusion.22), channel_id=1, source_target_pairs={{0,7},{1,2},{2,1},{3,4},{4,3},{5,6},{6,5},{7,0},{8,15},{9,10},{10,... | collective-permute-start | bytes 1966088 | tf_op jit(solution)/shard_map/ppermute | solution.py:284
  85.7 2.1 %collective-permute-start.16 = (bf16[160,128]{1,0:T(8,128)(2,1)S(1)}, bf16[160,128]{1,0:T(8,128)(2,1)S(1)}, u32[]{:S(2)}, u32[]{:S(2)}) collective-permute-start(bf16[160,128]{1,0:T(8,128)(2,1)S(1)} %get-tuple-element.90.refs_0_), channel_id=1, source_target_pairs={{0,32},{32,0},{1,33},{33,1},{2,34},{34,2},{3,35},{35,3},{4,36},{36... | collective-permute-start | bytes 122888 | tf_op jit(solution)/shard_map/ppermute | solution.py:24
  87.8 7.2 %shard_map.101 = (f32[256,1024]{1,0:T(8,128)}, bf16[256,2560]{1,0:T(8,128)(2,1)}) custom-call(s32[1]{0:T(128)} %bitcast.8._, bf16[256,1280]{1,0:T(8,128)(2,1)} %collective-permute-done.4.early_ref, bf16[256,1280]{1,0:T(8,128)(2,1)} %copy-done.7, bf16[256,1024]{1,0:T(8,128)(2,1)} %copy-done.2, bf16[2560,1024]{1,0:T(8,128)(2,1)} %bitcast.29), custom_call_target="tpu_custom_call" | custom-call | tf_op jit(solution)/shard_map/pallas_call | solution.py:140
  95.0 1.4 collective-permute-start.19
  97.1 1.6 %shard_map.103 = f32[320,64]{1,0:T(8,128)} custom-call(s32[1]{0:T(128)} %bitcast.10.here_ref, f32[160,64]{1,0:T(8,128)} %get-tuple-element.113.refs_0_, f32[160,64]{1,0:T(8,128)} %copy-done.13), custom_call_target="tpu_custom_call" | custom-call | tf_op jit(solution)/shard_map/pallas_call | solution.py:106
  98.7 1.4 shard_map.102.refs_0_
  100.1 2.5 %fusion.21 = f16[320,1024]{1,0:T(8,128)(2,1)S(1)} fusion(f16[320,1024]{1,0:T(8,128)(2,1)} %collective-permute-done.14, f32[1280,1024]{1,0:T(8,128)} %fusion.32, s32[]{:T(128)S(6)} %select_n.165, f32[]{:T(128)} %bitcast.6), kind=kLoop, calls=%fused_computation.40 | loop fusion | flops 2949120 | bytes 2621448 | tf_op jit(solution)/shard_map/convert_element_type | solution.py:55
  102.6 3.1 %fusion.23 = f16[320,1024]{1,0:T(8,128)(2,1)} fusion(f16[320,1024]{1,0:T(8,128)(2,1)S(1)} %collective-permute-done.20, f32[1280,1024]{1,0:T(8,128)} %copy-done.1, s32[]{:T(128)S(6)} %select_n.165, f32[]{:T(128)} %bitcast.6), kind=kLoop, calls=%fused_computation.42 | loop fusion | flops 2949120 | bytes 2621448 | tf_op jit(solution)/shard_map/convert_element_type | solution.py:55
  106.1 2.7 %collective-permute-start.18 = (f16[320,1024]{1,0:T(8,128)(2,1)S(1)}, f16[320,1024]{1,0:T(8,128)(2,1)}, u32[]{:S(2)}, u32[]{:S(2)}) collective-permute-start(f16[320,1024]{1,0:T(8,128)(2,1)S(1)} %fusion.21), channel_id=1, source_target_pairs={{0,7},{1,2},{2,1},{3,4},{4,3},{5,6},{6,5},{7,0},{8,15},{9,10},{10,... | collective-permute-start | bytes 1966088 | tf_op jit(solution)/shard_map/ppermute | solution.py:284
  108.8 2.0 %collective-permute-start.22 = (bf16[160,256]{1,0:T(8,128)(2,1)S(1)}, bf16[160,256]{1,0:T(8,128)(2,1)S(1)}, u32[]{:S(2)}, u32[]{:S(2)}) collective-permute-start(bf16[160,256]{1,0:T(8,128)(2,1)S(1)} %copy-done.10), channel_id=1, source_target_pairs={{0,64},{64,0},{128,192},{192,128},{1,65},{65,1},{129,193},{193,129... | collective-permute-start | bytes 245768 | tf_op jit(solution)/shard_map/ppermute | solution.py:24
  110.9 2.1 %collective-permute-start.23 = (bf16[160,256]{1,0:T(8,128)(2,1)S(1)}, bf16[160,256]{1,0:T(8,128)(2,1)S(1)}, u32[]{:S(2)}, u32[]{:S(2)}) collective-permute-start(bf16[160,256]{1,0:T(8,128)(2,1)S(1)} %copy-done.10), channel_id=1, source_target_pairs={{0,128},{64,192},{128,0},{192,64},{1,129},{65,193},{129,1},{193,65... | collective-permute-start | bytes 245768 | tf_op jit(solution)/shard_map/ppermute | solution.py:24
  113.4 2.5 %collective-permute-start.24 = (bf16[160,256]{1,0:T(8,128)(2,1)S(1)}, bf16[160,256]{1,0:T(8,128)(2,1)S(1)}, u32[]{:S(2)}, u32[]{:S(2)}) collective-permute-start(bf16[160,256]{1,0:T(8,128)(2,1)S(1)} %copy-done.10), channel_id=1, source_target_pairs={{0,192},{64,128},{128,64},{192,0},{1,193},{65,129},{129,65},{193,1... | collective-permute-start | bytes 245768 | tf_op jit(solution)/shard_map/ppermute | solution.py:24
  115.9 1.0 collective-permute-done.23.refs_2_
  116.9 1.5 collective-permute-start.25
  119.7 1.8 %shard_map.104.refs_0_ = bf16[160,1024]{1,0:T(8,128)(2,1)} custom-call(s32[1]{0:T(128)} %bitcast.11.here_ref, bf16[160,256]{1,0:T(8,128)(2,1)} %shard_map.102.refs_0_, bf16[160,256]{1,0:T(8,128)(2,1)} %copy-done.14, bf16[160,256]{1,0:T(8,128)(2,1)} %copy-done.15, bf16[160,256]{1,0:T(8,128)(2,1)} %copy-done.16), custom_call_target="tpu_custom_call" | custom-call | tf_op jit(solution)/shard_map/pallas_call | solution.py:106
  121.4 1.2 collective-permute-done.21
  122.7 1.0 copy-done.6
  123.7 3.3 %fusion.24 = f16[320,1024]{1,0:T(8,128)(2,1)} fusion(f16[320,1024]{1,0:T(8,128)(2,1)} %collective-permute-done.21, f32[1280,1024]{1,0:T(8,128)} %fusion.32, s32[]{:T(128)S(6)} %select_n.166, f32[]{:T(128)} %bitcast.6), kind=kLoop, calls=%fused_computation.43 | loop fusion | flops 2949120 | bytes 2621448 | tf_op jit(solution)/shard_map/convert_element_type | solution.py:55
  127.0 3.4 %fusion.25 = f16[320,1024]{1,0:T(8,128)(2,1)} fusion(f16[320,1024]{1,0:T(8,128)(2,1)} %collective-permute-done.18, f32[1280,1024]{1,0:T(8,128)} %fusion.32, s32[]{:T(128)S(6)} %select_n.164, f32[]{:T(128)} %bitcast.6), kind=kLoop, calls=%fused_computation.44 | loop fusion | flops 2949120 | bytes 2621448 | tf_op jit(solution)/shard_map/convert_element_type | solution.py:55
  130.7 2.7 %collective-permute-start.27 = (f16[320,1024]{1,0:T(8,128)(2,1)}, f16[320,1024]{1,0:T(8,128)(2,1)S(1)}, u32[]{:S(2)}, u32[]{:S(2)}) collective-permute-start(f16[320,1024]{1,0:T(8,128)(2,1)} %fusion.24), channel_id=1, source_target_pairs={{0,7},{1,2},{2,1},{3,4},{4,3},{5,6},{6,5},{7,0},{8,15},{9,10},{10,... | collective-permute-start | bytes 1966088 | tf_op jit(solution)/shard_map/ppermute | solution.py:284
  134.2 7.5 %shard_map.105 = (bf16[256,1024]{1,0:T(8,128)(2,1)}, bf16[256,5120]{1,0:T(8,128)(2,1)}) custom-call(s32[1]{0:T(128)} %bitcast.12._, bf16[256,5120]{1,0:T(8,128)(2,1)} %bitcast.25, bf16[256,1024]{1,0:T(8,128)(2,1)} %bitcast.5.cotangent_ref, bf16[2560,1024]{1,0:T(8,128)(2,1)} %bitcast.30, f32[256,1024]{1,0:T(8,128)} %copy-done.6), custom_call_target="tpu_custom_call" | custom-call | tf_op jit(solution)/shard_map/pallas_call | solution.py:176
  141.7 2.0 %shard_map.106 = bf16[320,1024]{1,0:T(8,128)(2,1)} custom-call(s32[1]{0:T(128)} %bitcast.10.here_ref, bf16[160,1024]{1,0:T(8,128)(2,1)} %shard_map.104.refs_0_, bf16[160,1024]{1,0:T(8,128)(2,1)} %collective-permute-done.28.refs_1_), custom_call_target="tpu_custom_call" | custom-call | tf_op jit(solution)/shard_map/pallas_call | solution.py:106
  143.7 2.7 %collective-permute-done.26 = f16[320,1024]{1,0:T(8,128)(2,1)S(1)} collective-permute-done((f16[320,1024]{1,0:T(8,128)(2,1)}, f16[320,1024]{1,0:T(8,128)(2,1)S(1)}, u32[]{:S(2)}, u32[]{:S(2)}) %collective-permute-start.26) | collective-permute-done | bytes 655392 | tf_op jit(solution)/shard_map/ppermute | solution.py:284
  146.3 1.3 collective-permute-done.27
  147.6 3.9 %fusion.16 = bf16[320,1024]{1,0:T(8,128)(2,1)} fusion(f16[320,1024]{1,0:T(8,128)(2,1)S(1)} %collective-permute-done.26, f16[320,1024]{1,0:T(8,128)(2,1)S(1)} %collective-permute-done.27, f32[1280,1024]{1,0:T(8,128)} %fusion.32, s32[]{:T(128)S(6)} %select_n.168, f32[]{:T(128)} %bitcast.15, f32[]{:T(128)} %bitcast.6), kind=kLoop, calls=%fused_computation.35 | loop fusion | flops 4259840 | bytes 3276812 | tf_op jit(solution)/shard_map/convert_element_type | solution.py:353
  151.7 1.5 copy-done.19
  (100 shorter events, 19.6 us)
Async XLA Ops:
  7.2 80.7 %all-gather.3.cloned.1.call-start = ((), (), s32[]{:S(2)}) async-start(), calls=%async_computation | async-start | bytes 5898240 | tf_op jit(solution)/shard_map/all_gather | solution.py:218
  7.9 8.1 %copy-start.11 = (f32[320,64]{0,1:T(8,128)S(1)}, f32[320,64]{0,1:T(8,128)}, u32[]{:S(2)}) copy-start(f32[320,64]{0,1:T(8,128)} %param.11) | copy-start | bytes 245764
  9.9 16.1 %collective-permute-start = (f32[160,1024]{1,0:T(8,128)}, f32[160,1024]{1,0:T(8,128)}, u32[]{:S(2)}, u32[]{:S(2)}) collective-permute-start(f32[160,1024]{1,0:T(8,128)} %dynamic-slice_bitcast_fusion), channel_id=1, source_target_pairs={{0,16},{16,0},{1,17},{17,1},{2,18},{18,2},{3,19},{19,3},{4,20},{20... | collective-permute-start | bytes 1966088 | tf_op jit(solution)/shard_map/ppermute | solution.py:24
  9.9 15.3 %collective-permute-start.1 = (bf16[256,1024]{1,0:T(8,128)(2,1)}, bf16[256,1024]{1,0:T(8,128)(2,1)S(1)}, u32[]{:S(2)}, u32[]{:S(2)}) collective-permute-start(bf16[256,1024]{1,0:T(8,128)(2,1)} %bitcast.5.cotangent_ref), channel_id=1, source_target_pairs={{0,8},{8,0},{1,9},{9,1},{2,10},{10,2},{3,11},{11,3},{4,12},{12,4},... | collective-permute-start | bytes 1572872 | tf_op jit(solution)/shard_map/ppermute | solution.py:24
  12.2 4.9 %copy-start = (bf16[1,256,5120]{2,1,0:T(8,128)(2,1)S(1)}, bf16[1,256,5120]{2,1,0:T(8,128)(2,1)}, u32[]{:S(2)}) copy-start(bf16[1,256,5120]{2,1,0:T(8,128)(2,1)} %param.6) | copy-start | bytes 7864324
  15.9 13.2 %collective-permute-start.3 = (f32[8,128]{1,0:T(8,128)S(1)}, f32[8,128]{1,0:T(8,128)S(1)}, u32[]{:S(2)}, u32[]{:S(2)}) collective-permute-start(f32[8,128]{1,0:T(8,128)S(1)} %broadcast_in_dim.18), channel_id=1, source_target_pairs={{0,8},{8,0},{1,9},{9,1},{2,10},{10,2},{3,11},{11,3},{4,12},{12,4},... | collective-permute-start | bytes 12296 | tf_op jit(solution)/shard_map/ppermute | solution.py:24
  16.9 22.5 %collective-permute-start.10 = (f32[160,64]{1,0:T(8,128)}, f32[160,64]{1,0:T(8,128)}, u32[]{:S(2)}, u32[]{:S(2)}) collective-permute-start(f32[160,64]{1,0:T(8,128)} %copy.14), channel_id=1, source_target_pairs={{0,16},{16,0},{1,17},{17,1},{2,18},{18,2},{3,19},{19,3},{4,20},{20... | collective-permute-start | bytes 122888 | tf_op jit(solution)/shard_map/ppermute | solution.py:24
  18.1 35.7 %collective-permute-start.4 = (bf16[256,1280]{1,0:T(8,128)(2,1)}, bf16[256,1280]{1,0:T(8,128)(2,1)}, u32[]{:S(2)}, u32[]{:S(2)}) collective-permute-start(bf16[256,1280]{1,0:T(8,128)(2,1)} %pad_maximum_fusion.3), channel_id=1, source_target_pairs={{0,8},{8,0},{1,9},{9,1},{2,10},{10,2},{3,11},{11,3},{4,12},{12,4},... | collective-permute-start | bytes 1966088 | tf_op jit(solution)/shard_map/ppermute | solution.py:24
  25.2 0.8 copy-start.2
  28.1 1.0 copy-start.3
  31.3 8.0 %copy-start.8 = (bf16[256,1280]{1,0:T(8,128)(2,1)S(1)}, bf16[256,1280]{1,0:T(8,128)(2,1)}, u32[]{:S(2)}) copy-start(bf16[256,1280]{1,0:T(8,128)(2,1)} %pad_maximum_fusion.4) | copy-start | bytes 1966084
  31.3 22.5 %copy-start.4 = (bf16[256,1024]{1,0:T(8,128)(2,1)S(1)}, bf16[256,1024]{1,0:T(8,128)(2,1)}, u32[]{:S(2)}) copy-start(bf16[256,1024]{1,0:T(8,128)(2,1)} %copy-done.2) | copy-start | bytes 1572868
  32.1 6.2 %collective-permute-start.5 = (f32[8,128]{1,0:T(8,128)S(1)}, f32[8,128]{1,0:T(8,128)S(1)}, u32[]{:S(2)}, u32[]{:S(2)}) collective-permute-start(f32[8,128]{1,0:T(8,128)S(1)} %add_select_fusion), channel_id=1, source_target_pairs={{0,1},{1,0},{2,3},{3,2},{4,5},{5,4},{6,7},{7,6},{8,9},{9,8},{10,11... | collective-permute-start | bytes 12296 | tf_op jit(solution)/shard_map/ppermute | solution.py:24
  33.7 7.0 %collective-permute-start.7 = (f32[160,256]{1,0:T(8,128)}, f32[160,256]{1,0:T(8,128)S(1)}, u32[]{:S(2)}, u32[]{:S(2)}) collective-permute-start(f32[160,256]{1,0:T(8,128)} %get-tuple-element.108), channel_id=1, source_target_pairs={{0,64},{64,0},{128,192},{192,128},{1,65},{65,1},{129,193},{193,129... | collective-permute-start | bytes 491528 | tf_op jit(solution)/shard_map/ppermute | solution.py:24
  35.3 9.9 %collective-permute-start.8 = (f32[160,256]{1,0:T(8,128)}, f32[160,256]{1,0:T(8,128)S(1)}, u32[]{:S(2)}, u32[]{:S(2)}) collective-permute-start(f32[160,256]{1,0:T(8,128)} %get-tuple-element.107), channel_id=1, source_target_pairs={{0,128},{64,192},{128,0},{192,64},{1,129},{65,193},{129,1},{193,65... | collective-permute-start | bytes 491528 | tf_op jit(solution)/shard_map/ppermute | solution.py:24
  38.4 8.8 %collective-permute-start.9 = (f32[160,256]{1,0:T(8,128)S(1)}, f32[160,256]{1,0:T(8,128)S(1)}, u32[]{:S(2)}, u32[]{:S(2)}) collective-permute-start(f32[160,256]{1,0:T(8,128)S(1)} %get-tuple-element.106), channel_id=1, source_target_pairs={{0,192},{64,128},{128,64},{192,0},{1,193},{65,129},{129,65},{193,1... | collective-permute-start | bytes 491528 | tf_op jit(solution)/shard_map/ppermute | solution.py:24
  39.3 26.6 %collective-permute-start.2 = (bf16[256,1280]{1,0:T(8,128)(2,1)S(1)}, bf16[256,1280]{1,0:T(8,128)(2,1)S(1)}, u32[]{:S(2)}, u32[]{:S(2)}) collective-permute-start(bf16[256,1280]{1,0:T(8,128)(2,1)S(1)} %copy-done.8), channel_id=1, source_target_pairs={{0,8},{8,0},{1,9},{9,1},{2,10},{10,2},{3,11},{11,3},{4,12},{12,4},... | collective-permute-start | bytes 1966088 | tf_op jit(solution)/shard_map/ppermute | solution.py:24
  40.7 6.5 %collective-permute-start.6 = (f32[8,128]{1,0:T(8,128)S(1)}, f32[8,128]{1,0:T(8,128)S(1)}, u32[]{:S(2)}, u32[]{:S(2)}) collective-permute-start(f32[8,128]{1,0:T(8,128)S(1)} %maximum_select_fusion.2), channel_id=1, source_target_pairs={{0,2},{1,3},{2,0},{3,1},{4,6},{5,7},{6,4},{7,5},{8,10},{9,11},{10,... | collective-permute-start | bytes 12296 | tf_op jit(solution)/shard_map/ppermute | solution.py:24
  47.3 9.3 %collective-permute-start.11 = (f32[8,128]{1,0:T(8,128)S(1)}, f32[8,128]{1,0:T(8,128)S(1)}, u32[]{:S(2)}, u32[]{:S(2)}) collective-permute-start(f32[8,128]{1,0:T(8,128)S(1)} %maximum_select_fusion.1), channel_id=1, source_target_pairs={{0,4},{1,5},{2,6},{3,7},{4,0},{5,1},{6,2},{7,3},{8,12},{9,13},{10,... | collective-permute-start | bytes 12296 | tf_op jit(solution)/shard_map/ppermute | solution.py:24
  56.6 21.4 %copy-start.1 = (f32[1280,1024]{1,0:T(8,128)}, f32[1280,1024]{1,0:T(8,128)S(1)}, u32[]{:S(2)}) copy-start(f32[1280,1024]{1,0:T(8,128)S(1)} %fusion.26) | copy-start | bytes 15728644
  58.9 16.9 %collective-permute-start.12 = (f16[160,1024]{1,0:T(8,128)(2,1)S(1)}, f16[160,1024]{1,0:T(8,128)(2,1)S(1)}, u32[]{:S(2)}, u32[]{:S(2)}) collective-permute-start(f16[160,1024]{1,0:T(8,128)(2,1)S(1)} %get-tuple-element.97), channel_id=1, source_target_pairs={{0,1},{1,0},{2,3},{3,2},{4,5},{5,4},{6,7},{7,6},{8,9},{9,8},{10,11... | collective-permute-start | bytes 983048 | tf_op jit(solution)/shard_map/ppermute | solution.py:284
  60.1 17.9 %collective-permute-start.13 = (f16[160,1024]{1,0:T(8,128)(2,1)S(1)}, f16[160,1024]{1,0:T(8,128)(2,1)S(1)}, u32[]{:S(2)}, u32[]{:S(2)}) collective-permute-start(f16[160,1024]{1,0:T(8,128)(2,1)S(1)} %get-tuple-element.96), channel_id=1, source_target_pairs={{0,7},{1,2},{2,1},{3,4},{4,3},{5,6},{6,5},{7,0},{8,15},{9,10},{10,... | collective-permute-start | bytes 983048 | tf_op jit(solution)/shard_map/ppermute | solution.py:284
  63.5 20.6 %collective-permute-start.15 = (f32[160,128]{1,0:T(8,128)S(1)}, f32[160,128]{1,0:T(8,128)S(1)}, u32[]{:S(2)}, u32[]{:S(2)}) collective-permute-start(f32[160,128]{1,0:T(8,128)S(1)} %constant_dynamic-slice_fusion.1), channel_id=1, source_target_pairs={{0,32},{32,0},{1,33},{33,1},{2,34},{34,2},{3,35},{35,3},{4,36},{36... | collective-permute-start | bytes 245768 | tf_op jit(solution)/shard_map/ppermute | solution.py:24
  65.9 5.2 %copy-start.7 = (bf16[256,1280]{1,0:T(8,128)(2,1)}, bf16[256,1280]{1,0:T(8,128)(2,1)S(1)}, u32[]{:S(2)}) copy-start(bf16[256,1280]{1,0:T(8,128)(2,1)S(1)} %collective-permute-done.2.late_ref) | copy-start | bytes 1966084
  79.1 21.0 %collective-permute-start.14 = (f16[320,1024]{1,0:T(8,128)(2,1)S(1)}, f16[320,1024]{1,0:T(8,128)(2,1)}, u32[]{:S(2)}, u32[]{:S(2)}) collective-permute-start(f16[320,1024]{1,0:T(8,128)(2,1)S(1)} %fusion.20), channel_id=1, source_target_pairs={{0,1},{1,0},{2,3},{3,2},{4,5},{5,4},{6,7},{7,6},{8,9},{9,8},{10,11... | collective-permute-start | bytes 1966088 | tf_op jit(solution)/shard_map/ppermute | solution.py:284
  81.1 21.5 %collective-permute-start.20 = (f16[320,1024]{1,0:T(8,128)(2,1)}, f16[320,1024]{1,0:T(8,128)(2,1)S(1)}, u32[]{:S(2)}, u32[]{:S(2)}) collective-permute-start(f16[320,1024]{1,0:T(8,128)(2,1)} %fusion.22), channel_id=1, source_target_pairs={{0,7},{1,2},{2,1},{3,4},{4,3},{5,6},{6,5},{7,0},{8,15},{9,10},{10,... | collective-permute-start | bytes 1966088 | tf_op jit(solution)/shard_map/ppermute | solution.py:284
  85.0 10.1 %copy-start.12 = (bf16[160,128]{1,0:T(8,128)(2,1)}, bf16[160,128]{1,0:T(8,128)(2,1)S(1)}, u32[]{:S(2)}) copy-start(bf16[160,128]{1,0:T(8,128)(2,1)S(1)} %get-tuple-element.90.refs_0_) | copy-start | bytes 122884
  85.7 10.7 %collective-permute-start.17 = (f32[160,64]{1,0:T(8,128)S(1)}, f32[160,64]{1,0:T(8,128)S(1)}, u32[]{:S(2)}, u32[]{:S(2)}) collective-permute-start(f32[160,64]{1,0:T(8,128)S(1)} %get-tuple-element.114), channel_id=1, source_target_pairs={{0,16},{16,0},{1,17},{17,1},{2,18},{18,2},{3,19},{19,3},{4,20},{20... | collective-permute-start | bytes 122888 | tf_op jit(solution)/shard_map/ppermute | solution.py:24
  85.7 10.7 %collective-permute-start.16 = (bf16[160,128]{1,0:T(8,128)(2,1)S(1)}, bf16[160,128]{1,0:T(8,128)(2,1)S(1)}, u32[]{:S(2)}, u32[]{:S(2)}) collective-permute-start(bf16[160,128]{1,0:T(8,128)(2,1)S(1)} %get-tuple-element.90.refs_0_), channel_id=1, source_target_pairs={{0,32},{32,0},{1,33},{33,1},{2,34},{34,2},{3,35},{35,3},{4,36},{36... | collective-permute-start | bytes 122888 | tf_op jit(solution)/shard_map/ppermute | solution.py:24
  95.0 27.7 %collective-permute-start.19 = (f32[256,1024]{1,0:T(8,128)}, f32[256,1024]{1,0:T(8,128)S(1)}, u32[]{:S(2)}, u32[]{:S(2)}) collective-permute-start(f32[256,1024]{1,0:T(8,128)} %get-tuple-element.64), channel_id=1, source_target_pairs={{0,8},{8,0},{1,9},{9,1},{2,10},{10,2},{3,11},{11,3},{4,12},{12,4},... | collective-permute-start | bytes 3145736 | tf_op jit(solution)/shard_map/ppermute | solution.py:24
  96.5 2.2 %copy-start.17 = (bf16[160,128]{1,0:T(8,128)(2,1)}, bf16[160,128]{1,0:T(8,128)(2,1)S(1)}, u32[]{:S(2)}) copy-start(bf16[160,128]{1,0:T(8,128)(2,1)S(1)} %collective-permute-done.16.refs_1_) | copy-start | bytes 122884
  102.6 6.2 %copy-start.10 = (bf16[160,256]{1,0:T(8,128)(2,1)S(1)}, bf16[160,256]{1,0:T(8,128)(2,1)}, u32[]{:S(2)}) copy-start(bf16[160,256]{1,0:T(8,128)(2,1)} %shard_map.102.refs_0_) | copy-start | bytes 245764
  105.8 16.9 %collective-permute-start.21 = (f16[320,1024]{1,0:T(8,128)(2,1)}, f16[320,1024]{1,0:T(8,128)(2,1)}, u32[]{:S(2)}, u32[]{:S(2)}) collective-permute-start(f16[320,1024]{1,0:T(8,128)(2,1)} %fusion.23), channel_id=1, source_target_pairs={{0,1},{1,0},{2,3},{3,2},{4,5},{5,4},{6,7},{7,6},{8,9},{9,8},{10,11... | collective-permute-start | bytes 1966088 | tf_op jit(solution)/shard_map/ppermute | solution.py:284
  106.1 20.9 %collective-permute-start.18 = (f16[320,1024]{1,0:T(8,128)(2,1)S(1)}, f16[320,1024]{1,0:T(8,128)(2,1)}, u32[]{:S(2)}, u32[]{:S(2)}) collective-permute-start(f16[320,1024]{1,0:T(8,128)(2,1)S(1)} %fusion.21), channel_id=1, source_target_pairs={{0,7},{1,2},{2,1},{3,4},{4,3},{5,6},{6,5},{7,0},{8,15},{9,10},{10,... | collective-permute-start | bytes 1966088 | tf_op jit(solution)/shard_map/ppermute | solution.py:284
  108.8 4.6 %collective-permute-start.22 = (bf16[160,256]{1,0:T(8,128)(2,1)S(1)}, bf16[160,256]{1,0:T(8,128)(2,1)S(1)}, u32[]{:S(2)}, u32[]{:S(2)}) collective-permute-start(bf16[160,256]{1,0:T(8,128)(2,1)S(1)} %copy-done.10), channel_id=1, source_target_pairs={{0,64},{64,0},{128,192},{192,128},{1,65},{65,1},{129,193},{193,129... | collective-permute-start | bytes 245768 | tf_op jit(solution)/shard_map/ppermute | solution.py:24
  110.9 6.1 %collective-permute-start.23 = (bf16[160,256]{1,0:T(8,128)(2,1)S(1)}, bf16[160,256]{1,0:T(8,128)(2,1)S(1)}, u32[]{:S(2)}, u32[]{:S(2)}) collective-permute-start(bf16[160,256]{1,0:T(8,128)(2,1)S(1)} %copy-done.10), channel_id=1, source_target_pairs={{0,128},{64,192},{128,0},{192,64},{1,129},{65,193},{129,1},{193,65... | collective-permute-start | bytes 245768 | tf_op jit(solution)/shard_map/ppermute | solution.py:24
  113.4 5.7 %copy-start.14 = (bf16[160,256]{1,0:T(8,128)(2,1)}, bf16[160,256]{1,0:T(8,128)(2,1)S(1)}, u32[]{:S(2)}) copy-start(bf16[160,256]{1,0:T(8,128)(2,1)S(1)} %collective-permute-done.22.refs_1_) | copy-start | bytes 245764
  113.4 5.7 %collective-permute-start.24 = (bf16[160,256]{1,0:T(8,128)(2,1)S(1)}, bf16[160,256]{1,0:T(8,128)(2,1)S(1)}, u32[]{:S(2)}, u32[]{:S(2)}) collective-permute-start(bf16[160,256]{1,0:T(8,128)(2,1)S(1)} %copy-done.10), channel_id=1, source_target_pairs={{0,192},{64,128},{128,64},{192,0},{1,193},{65,129},{129,65},{193,1... | collective-permute-start | bytes 245768 | tf_op jit(solution)/shard_map/ppermute | solution.py:24
  116.9 2.2 %copy-start.15 = (bf16[160,256]{1,0:T(8,128)(2,1)}, bf16[160,256]{1,0:T(8,128)(2,1)S(1)}, u32[]{:S(2)}) copy-start(bf16[160,256]{1,0:T(8,128)(2,1)S(1)} %collective-permute-done.23.refs_2_) | copy-start | bytes 245764
  116.9 34.6 %collective-permute-start.25 = (bf16[256,2560]{1,0:T(8,128)(2,1)}, bf16[256,2560]{1,0:T(8,128)(2,1)S(1)}, u32[]{:S(2)}, u32[]{:S(2)}) collective-permute-start(bf16[256,2560]{1,0:T(8,128)(2,1)} %get-tuple-element.65), channel_id=1, source_target_pairs={{0,8},{8,0},{1,9},{9,1},{2,10},{10,2},{3,11},{11,3},{4,12},{12,4},... | collective-permute-start | bytes 3932168 | tf_op jit(solution)/shard_map/ppermute | solution.py:24
  122.7 1.0 copy-start.6
  127.0 6.4 %copy-start.5 = (bf16[160,1024]{1,0:T(8,128)(2,1)S(1)}, bf16[160,1024]{1,0:T(8,128)(2,1)}, u32[]{:S(2)}) copy-start(bf16[160,1024]{1,0:T(8,128)(2,1)} %shard_map.104.refs_0_) | copy-start | bytes 983044
  127.0 6.4 %copy-start.9 = (f32[320,64]{1,0:T(8,128)S(1)}, f32[320,64]{1,0:T(8,128)}, u32[]{:S(2)}) copy-start(f32[320,64]{1,0:T(8,128)} %shard_map.103) | copy-start | bytes 245764
  130.4 15.9 %collective-permute-start.26 = (f16[320,1024]{1,0:T(8,128)(2,1)}, f16[320,1024]{1,0:T(8,128)(2,1)S(1)}, u32[]{:S(2)}, u32[]{:S(2)}) collective-permute-start(f16[320,1024]{1,0:T(8,128)(2,1)} %fusion.25), channel_id=1, source_target_pairs={{0,1},{1,0},{2,3},{3,2},{4,5},{5,4},{6,7},{7,6},{8,9},{9,8},{10,11... | collective-permute-start | bytes 1966088 | tf_op jit(solution)/shard_map/ppermute | solution.py:284
  130.7 16.9 %collective-permute-start.27 = (f16[320,1024]{1,0:T(8,128)(2,1)}, f16[320,1024]{1,0:T(8,128)(2,1)S(1)}, u32[]{:S(2)}, u32[]{:S(2)}) collective-permute-start(f16[320,1024]{1,0:T(8,128)(2,1)} %fusion.24), channel_id=1, source_target_pairs={{0,7},{1,2},{2,1},{3,4},{4,3},{5,6},{6,5},{7,0},{8,15},{9,10},{10,... | collective-permute-start | bytes 1966088 | tf_op jit(solution)/shard_map/ppermute | solution.py:284
  133.4 8.3 %collective-permute-start.28 = (bf16[160,1024]{1,0:T(8,128)(2,1)S(1)}, bf16[160,1024]{1,0:T(8,128)(2,1)}, u32[]{:S(2)}, u32[]{:S(2)}) collective-permute-start(bf16[160,1024]{1,0:T(8,128)(2,1)S(1)} %copy-done.5), channel_id=1, source_target_pairs={{0,16},{16,0},{1,17},{17,1},{2,18},{18,2},{3,19},{19,3},{4,20},{20... | collective-permute-start | bytes 983048 | tf_op jit(solution)/shard_map/ppermute | solution.py:24
  147.6 3.9 %copy-start.18 = (bf16[256,5120]{1,0:T(8,128)(2,1)S(1)}, bf16[256,5120]{1,0:T(8,128)(2,1)}, u32[]{:S(2)}) copy-start(bf16[256,5120]{1,0:T(8,128)(2,1)} %get-tuple-element.80) | copy-start | bytes 7864324
  151.7 1.5 copy-start.19
  (2 other events, 1.3 us)
Sparse Core Ops, SparseCore 0:
  9.8 75.5 all-gather.2

commit v3 on v2

--- a/solution.py
+++ b/solution.py
@@ -60,17 +60,48 @@
     return jnp.sign(wide) * jnp.sqrt(jnp.abs(wide))
 
 
-def column_peak(tokens):
-    return jnp.max(jnp.sum(jnp.abs(tokens.astype(F32)), axis=0))
-
-
-def as_tile(first, second):
-    row = lax.broadcasted_iota(jnp.int32, (8, 128), 0)
-    return jnp.where(row < 4, first, second)
+def tile_rows():
+    return lax.broadcasted_iota(jnp.int32, (8, 128), 0)
+
+
+def local_peaks(tokens, cotangent):
+    def body(tokens_ref, cotangent_ref, out_ref):
+        peak = jnp.max(jnp.sum(jnp.abs(tokens_ref[...].astype(F32)), axis=0, keepdims=True))
+
+        @pl.when(pl.program_id(0) == 0)
+        def _():
+            other = jnp.max(jnp.abs(cotangent_ref[...].astype(F32)))
+            out_ref[...] = jnp.where(tile_rows() < 4, peak, other)
+
+        @pl.when(pl.program_id(0) > 0)
+        def _():
+            held = out_ref[...]
+            out_ref[...] = jnp.where(tile_rows() < 4, jnp.maximum(held, peak), held)
+
+    return pl.pallas_call(
+        body,
+        grid=(5,),
+        in_specs=[
+            pl.BlockSpec((tokens.shape[0], tokens.shape[1] // 5), lambda i: (0, i)),
+            whole(cotangent),
+        ],
+        out_specs=pl.BlockSpec((8, 128), lambda i: (0, 0)),
+        out_shape=jax.ShapeDtypeStruct((8, 128), F32),
+    )(tokens, cotangent)
 
 
 def join_peaks(peaks, other):
-    return as_tile(peaks + other, jnp.maximum(peaks, other))
+    return jnp.where(tile_rows() < 4, peaks + other, jnp.maximum(peaks, other))
+
+
+def link_scales(peaks, other):
+    def body(peaks_ref, other_ref, out_ref):
+        joined = join_peaks(peaks_ref[...], other_ref[...])
+        bound = jnp.maximum(joined[:4] * joined[4:], 1e-32)
+        out_ref[:4, :] = 240.0 / bound
+        out_ref[4:, :] = bound * (1.0 / (64.0 * 240.0))
+
+    return pl.pallas_call(body, out_shape=jax.ShapeDtypeStruct((8, 128), F32))(peaks, other)
 
 
 def dot(left, right):
@@ -116,80 +147,95 @@
     )(here.reshape(1), *pieces)
 
 
-def products_for_partner(z, early, late, cotangent, weight):
+TOP = 220.0
+
+
+def products(z, x, tokens, early, late, cotangent, cotangent_other, weight):
     count = 4
-    wide = weight.shape[0] // count
+    rows, features = cotangent.shape
+    total = weight.shape[0]
+    wide = total // count
 
     def group(i, z_ref):
         step = 1 - 2 * (z_ref[0] % 2)
         return (z_ref[0] // 2 + jnp.where(i % 2 == 1, 4 + step * (2 - i), 2 - i)) % 4
 
-    def body(_, early_ref, late_ref, cotangent_ref, weight_ref, keys_ref, grads_ref):
+    def body(
+        z_ref, _, tokens_ref, early_ref, late_ref, own_ref, other_ref, weight_ref,
+        keys_ref, grads_ref, sent_ref, sum_ref, both_ref,
+    ):
         i = pl.program_id(0)
 
         @pl.when(i == 0)
         def _():
-            keys_ref[...] = jnp.zeros_like(keys_ref)
-
-        tokens = jnp.where(i < count // 2, early_ref[...], late_ref[...])
-        keys_ref[...] += dot(tokens, weight_ref[...])
-        grads_ref[...] = dot_t(cotangent_ref[...], weight_ref[...]).astype(BF16)
-
-    rows = cotangent.shape[0]
-    keys = jax.ShapeDtypeStruct(cotangent.shape, F32)
+            sum_ref[...] = jnp.zeros_like(sum_ref)
+            both_ref[:rows, :] = own_ref[...]
+            both_ref[rows:, :] = other_ref[...]
+
+        partner = jnp.where(i < count // 2, early_ref[...], late_ref[...])
+        sum_ref[...] += dot(jnp.concatenate([tokens_ref[...], partner], axis=0), weight_ref[...])
+        grads = dot_t(both_ref[...], weight_ref[...]).astype(BF16)
+        grads_ref[...] = grads[:rows]
+        place = pl.multiple_of(group(i, z_ref) * wide, 128)
+        sent_ref[:rows, pl.ds(place, wide)] = grads[rows:]
+
+        @pl.when(i == count - 1)
+        def _():
+            keys_ref[...] = sum_ref[:rows, :]
+            keys = sum_ref[rows:, :]
+            largest = jnp.maximum(jnp.max(jnp.abs(keys)) * 1.01, 1e-30)
+            sent = jnp.full((16, features), largest, F32).astype(BF16)
+            sent_ref[rows:, :total] = jnp.zeros((16, total), BF16)
+            sent_ref[rows:, total:] = sent
+            scaled = keys * (TOP / sent[:1, :].astype(F32))
+            power = scaled * scaled
+            power = power * power
+            power = power * power
+            power = power * power
+            sent_ref[:rows, total:] = jnp.where(scaled < 0, -power, power).astype(BF16)
+
+    columns = tokens.shape[1] // (2 * count)
+    mine = pl.BlockSpec((rows, columns), lambda i, z, x: (0, x[0] * count + group(i, z)))
+    sent = jax.ShapeDtypeStruct((rows + 16, total + features), BF16)
     return pl.pallas_call(
         body,
         grid_spec=pltpu.PrefetchScalarGridSpec(
-            num_scalar_prefetch=1,
+            num_scalar_prefetch=2,
             grid=(count,),
             in_specs=[
-                pl.BlockSpec((rows, wide), lambda i, g: (0, jnp.minimum(i, count // 2 - 1))),
-                pl.BlockSpec((rows, wide), lambda i, g: (0, jnp.maximum(i - count // 2, 0))),
+                mine,
+                pl.BlockSpec((rows, wide), lambda i, *_: (0, jnp.minimum(i, count // 2 - 1))),
+                pl.BlockSpec((rows, wide), lambda i, *_: (0, jnp.maximum(i - count // 2, 0))),
                 whole(cotangent),
-                pl.BlockSpec((wide, weight.shape[1]), lambda i, r: (group(i, r), 0)),
+                whole(cotangent_other),
+                pl.BlockSpec((wide, features), lambda i, z, x: (group(i, z), 0)),
             ],
-            out_specs=[whole(keys), pl.BlockSpec((rows, wide), lambda i, r: (0, group(i, r)))],
+            out_specs=[
+                whole(cotangent),
+                mine,
+                whole(sent),
+            ],
+            scratch_shapes=[
+                pltpu.VMEM((2 * rows, features), F32),
+                pltpu.VMEM((2 * rows, features), BF16),
+            ],
         ),
-        out_shape=[keys, jax.ShapeDtypeStruct((rows, weight.shape[0]), BF16)],
+        out_shape=[
+            jax.ShapeDtypeStruct(cotangent.shape, F32),
+            jax.ShapeDtypeStruct(tokens.shape, BF16),
+            sent,
+        ],
+        compiler_params=pltpu.CompilerParams(vmem_limit_bytes=40 * 1024 * 1024),
         cost_estimate=FREE,
-    )(z.reshape(1), early, late, cotangent, weight)
-
-
-def products_here(side, tokens, cotangent, weight, keys_back):
-    count = 4
-    wide = weight.shape[0] // count
-
-    def body(_, tokens_ref, cotangent_ref, weight_ref, back_ref, keys_ref, grads_ref, sum_ref):
-        @pl.when(pl.program_id(0) == 0)
-        def _():
-            sum_ref[...] = back_ref[...]
-
-        sum_ref[...] += dot(tokens_ref[...], weight_ref[...])
-        grads_ref[...] = dot_t(cotangent_ref[...], weight_ref[...]).astype(BF16)
-
-        @pl.when(pl.program_id(0) == count - 1)
-        def _():
-            keys_ref[...] = sum_ref[...].astype(BF16)
-
-    keys = jax.ShapeDtypeStruct(cotangent.shape, BF16)
-    here = pl.BlockSpec((tokens.shape[0], wide), lambda i, s: (0, s[0] * count + i))
-    return pl.pallas_call(
-        body,
-        grid_spec=pltpu.PrefetchScalarGridSpec(
-            num_scalar_prefetch=1,
-            grid=(count,),
-            in_specs=[
-                here,
-                whole(cotangent),
-                pl.BlockSpec((wide, weight.shape[1]), lambda i, s: (i, 0)),
-                whole(keys_back),
-            ],
-            out_specs=[whole(keys), here],
-            scratch_shapes=[pltpu.VMEM(keys_back.shape, F32)],
-        ),
-        out_shape=[keys, jax.ShapeDtypeStruct(tokens.shape, BF16)],
-        cost_estimate=FREE,
-    )(side.reshape(1), tokens, cotangent, weight, keys_back)
+    )(z.reshape(1), x.reshape(1), tokens, early, late, cotangent, cotangent_other, weight)
+
+
+def decode_keys(coded):
+    rows = coded.shape[0] - 16
+    power = coded[:rows].astype(F32)
+    size = jnp.exp2(jnp.log2(jnp.abs(power)) * (1.0 / 16.0))
+    size = jnp.where(power == 0, 0.0, size) * (coded[rows : rows + 1, :1].astype(F32) / TOP)
+    return jnp.where(power < 0, -size, size)
 
 
 def shards(activations, key_weights, key_cotangent, fragment, pseudo_grads, momentum):
@@ -221,13 +267,13 @@
     give = rows_of(pseudo, theirs, rows)
     order.did(give)
     pseudo_other = swap(give, "c")
-    peak = jnp.full((8, 128), column_peak(order.step(tokens)))
-    order.did(peak)
-    peak_other = swap(peak, "xl")
+    peaks = local_peaks(order.step(tokens), cotangent)
+    order.did(peaks)
+    peaks_other = swap(peaks, "xl")
     sent = token_columns(order.step(tokens), 1 - x, early)
     order.did(sent)
     early_other = swap(sent, "xl")
-    pseudo_other, cotangent_other = order.step(pseudo_other, cotangent_other)
+    pseudo_other = order.step(pseudo_other)
     total = rows_of(pseudo, mine, rows) + pseudo_other
     gives = [columns_of(total, (y ^ m) * quarter, quarter) for m in (1, 2, 3)]
     old_give = rows_of(momentum, theirs, rows)
@@ -237,9 +283,7 @@
     sent = token_columns(order.step(tokens), 1 - x, late)
     order.did(sent)
     late_other = swap(sent, "xl")
-    peak_other = order.step(peak_other)
-    peak_c = jnp.maximum(jnp.max(jnp.abs(cotangent)), jnp.max(jnp.abs(cotangent_other)))
-    peaks = as_tile(peak + peak_other, peak_c.astype(F32))
+    peaks = join_peaks(peaks, order.step(peaks_other))
     order.did(peaks)
     peaks_other = swap(peaks, "z", 1)
     early_mine = token_columns(order.step(tokens), x, early)
@@ -264,12 +308,11 @@
             preferred_element_type=F32,
         )
 
-    early_other = order.step(early_other)
+    early_other, cotangent_other = order.step(early_other, cotangent_other)
     partial_early = product(early_mine, early_other)
     order.did(partial_early)
-    peaks = join_peaks(peaks, order.step(peaks_other))
-    bound = jnp.maximum(peaks[0, 0] * peaks[4, 0], 1e-32)
-    scale, back = 240.0 / bound, bound / (64.0 * 240.0)
+    scales = link_scales(peaks, order.step(peaks_other))
+    scale, back = scales[:1, :1], scales[4:5, :1]
     place = {4: odd_z, -3: 1 - odd_z, 2: 2 + odd_z, 3: 3 - odd_z}
     place_late = {0: odd_z, 1: 1 - odd_z, -2: 2 + odd_z, -1: 3 - odd_z}
 
@@ -316,16 +359,11 @@
     new_other = swap(give, "c")
 
     weight_half = order.step(weight_half)
-    keys_other, grads_other = products_for_partner(
-        z,
-        early_other,
-        late_other,
-        cotangent_other,
-        weight_half,
+    keys_mine, grads_mine, sent = products(
+        z, x, tokens, early_other, late_other, cotangent, cotangent_other, weight_half
     )
-    order.did(keys_other, grads_other)
-    keys_back = swap(keys_other, "xl")
-    grads_back = swap(grads_other, "xl")
+    order.did(sent)
+    products_back = swap(sent, "xl")
 
     updated_other, new_other = order.step(updated_other, new_other)
     new_momentum = assemble(c, lambda i: (i, 1 - i), (keep, new_other), 0)
@@ -340,19 +378,20 @@
     order.did(block)
     block_other = swap(block, "c")
 
-    keys_back, even = order.step(keys_back, even)
-    even, odd = ring_step(1, even, odd)
-
-    key_out, grads_mine = products_here(
-        order.step(x), tokens, cotangent, weight_half, keys_back
-    )
-    order.did(key_out, grads_mine)
+    even, odd = order.step(even, odd)
+    even, odd = encode(own(1) + decode(odd)), encode(own(-1) + decode(even))
+    order.did(even, odd)
+    even, odd = lax.ppermute(even, "z", EVEN), lax.ppermute(odd, "z", ODD)
+
     new_fragment = assemble(c, lambda i: (i, 1 - i), (block, order.step(block_other)), 0)
     order.did(new_fragment)
     even, odd = order.step(even, odd)
     weight_grad = ((own(0) + decode(even) + decode(odd)) * back).astype(BF16)
     order.did(weight_grad)
-    act_grad = lax.dynamic_update_slice(grads_mine, order.step(grads_back), (0, (1 - x) * half))
+    products_back = order.step(products_back)
+    key_out = (keys_mine + decode_keys(products_back[:, half:])).astype(BF16)
+    grads_back = products_back[: tokens.shape[0], :half]
+    act_grad = lax.dynamic_update_slice(grads_mine, grads_back, (0, (1 - x) * half))
     return (
         key_out[None],
         act_grad[None],

time: 161 us -> 178 us (1.11)
  waiting for transfers between devices: 22.4 us -> 38 us
  local copies, waits for them, and re-layouts: 10.8 us -> 17.2 us
  starting transfers between devices: 48.6 us -> 42.8 us
  Pallas kernels: 21.5 us -> 24.1 us
  matrix products: 8.05 us -> 10.4 us
  other arithmetic: 31.4 us -> 29.1 us
  between operations: 17.2 us -> 15 us
    ppermute x0 -> x2, waiting for transfers between devices: none -> 11.2 us  [shards(): even, odd = (lax.ppermute(even, 'z', EVEN), lax.ppermute(odd, 'z', ODD))]
    ppermute x21 -> x20, waiting for transfers between devices: 9.65 us -> 16.8 us  [swap(): lax.ppermute(value, axis, [(i, i ^ mask) for i in range(SIZES[axis])])]
    ppermute x21 -> x20, starting transfers between devices: 35 us -> 30.4 us  [swap(): lax.ppermute(value, axis, [(i, i ^ mask) for i in range(SIZES[axis])])]
    ppermute x8 -> x6, starting transfers between devices: 13.6 us -> 9.45 us  [send(): return lax.ppermute(message, 'z', pairs)]
    unnamed x43 -> x57, local copies, waits for them, and re-layouts: 6.19 us -> 10.2 us
    reduce_max x3 -> x0, other arithmetic: 3.17 us -> none  [the longest x1 1.81 us: shards(): jnp.max(jnp.abs(cotangent))]
    ppermute x0 -> x2, starting transfers between devices: none -> 2.94 us  [shards(): even, odd = (lax.ppermute(even, 'z', EVEN), lax.ppermute(odd, 'z', ODD))]
    ppermute x8 -> x6, waiting for transfers between devices: 12.1 us -> 9.26 us  [send(): return lax.ppermute(message, 'z', pairs)]
  transfers between devices with their start and end apart: 30 -> 29, of which waited for: 12 -> 13; matrix products, arithmetic and copies ran while one was open for 28% -> 24% of each run, Pallas kernels for 13% -> 14%
where the time goes in v3:
time: 178 us; the launch traced here: 177 us
  starting transfers between devices  42.8 us (24%)
  waiting for transfers between devices  38 us (21%)
  other arithmetic  29.1 us (16%)
  Pallas kernels  24.1 us (14%)
  local copies, waits for them, and re-layouts  17.2 us (10%)
  between operations  15 us (8%)
  matrix products  10.4 us (6%)
    ppermute x20, starting transfers between devices, swap(): lax.ppermute(value, axis, [(i, i ^ mask) for i in range(SIZES[axis])])  30.4 us
    ppermute x20, waiting for transfers between devices, swap(): lax.ppermute(value, axis, [(i, i ^ mask) for i in range(SIZES[axis])])  16.8 us
    convert_element_type x6, other arithmetic, encode(): return (scaled * jnp.abs(scaled)).astype(F16)  15.1 us
    ppermute x2, waiting for transfers between devices, shards(): even, odd = (lax.ppermute(even, 'z', EVEN), lax.ppermute(odd, 'z', ODD))  11.2 us
    pallas_call x1, Pallas kernels, products(): pl.pallas_call(body, grid_spec=pltpu.PrefetchScalarGridSpec(num_scalar_pr...  11 us
    dot_general x2, matrix products, product(): lax.dot_general(jnp.concatenate([first, second], axis=0), jnp.concatenate...  10.4 us
    unnamed x57, local copies, waits for them, and re-layouts  10.2 us
    ppermute x6, starting transfers between devices, send(): return lax.ppermute(message, 'z', pairs)  9.45 us
  transfers between devices with their start and end apart: 29, of which 13 were waited for; matrix products, arithmetic and copies ran while one was open for 24% of the time, Pallas kernels for 14%

profile of v3, /device:TPU:2, one launch (start us, length us, event | category | flops | bytes accessed | tf_op | source)
XLA Modules:
  0.0 176.6 jit_solution(13952625421347316759)
XLA Ops:
  7.9 2.0 %dynamic-slice_bitcast_fusion = f32[160,1024]{1,0:T(8,128)} fusion(f32[1,320,1024]{2,1,0:T(8,128)} %param.10, s32[]{:T(128)S(6)} %select_n.143), kind=kLoop, calls=%fused_computation.88 | loop fusion | bytes 1310724 | tf_op jit(solution)/shard_map/dynamic_slice | solution.py:40
  11.3 5.0 %shard_map.101 = f32[8,128]{1,0:T(8,128)} custom-call(bf16[256,5120]{1,0:T(8,128)(2,1)} %bitcast.25, bf16[256,1024]{1,0:T(8,128)(2,1)} %bitcast.31), custom_call_target="tpu_custom_call" | custom-call | tf_op jit(solution)/shard_map/pallas_call | solution.py:81
  16.2 2.3 %collective-permute-start.2 = (f32[8,128]{1,0:T(8,128)}, f32[8,128]{1,0:T(8,128)S(1)}, u32[]{:S(2)}, u32[]{:S(2)}) collective-permute-start(f32[8,128]{1,0:T(8,128)} %shard_map.101), channel_id=1, source_target_pairs={{0,8},{8,0},{1,9},{9,1},{2,10},{10,2},{3,11},{11,3},{4,12},{12,4},... | collective-permute-start | bytes 12296 | tf_op jit(solution)/shard_map/ppermute | solution.py:24
  19.7 1.2 bitcast_add_fusion
  20.9 2.9 %collective-permute-start.8 = (f32[160,256]{1,0:T(8,128)S(1)}, f32[160,256]{1,0:T(8,128)S(1)}, u32[]{:S(2)}, u32[]{:S(2)}) collective-permute-start(f32[160,256]{1,0:T(8,128)S(1)} %get-tuple-element.100), channel_id=1, source_target_pairs={{0,192},{64,128},{128,64},{192,0},{1,193},{65,129},{129,65},{193,1... | collective-permute-start | bytes 491528 | tf_op jit(solution)/shard_map/ppermute | solution.py:24
  25.5 1.9 %collective-permute-start.4 = (f32[8,128]{1,0:T(8,128)S(1)}, f32[8,128]{1,0:T(8,128)S(1)}, u32[]{:S(2)}, u32[]{:S(2)}) collective-permute-start(f32[8,128]{1,0:T(8,128)S(1)} %maximum_select_fusion.2), channel_id=1, source_target_pairs={{0,1},{1,0},{2,3},{3,2},{4,5},{5,4},{6,7},{7,6},{8,9},{9,8},{10,11... | collective-permute-start | bytes 12296 | tf_op jit(solution)/shard_map/ppermute | solution.py:24
  27.5 1.7 collective-permute-done.4
  29.9 2.1 %collective-permute-start.1 = (bf16[256,1024]{1,0:T(8,128)(2,1)S(1)}, bf16[256,1024]{1,0:T(8,128)(2,1)S(1)}, u32[]{:S(2)}, u32[]{:S(2)}) collective-permute-start(bf16[256,1024]{1,0:T(8,128)(2,1)S(1)} %bitcast.32), channel_id=1, source_target_pairs={{0,8},{8,0},{1,9},{9,1},{2,10},{10,2},{3,11},{11,3},{4,12},{12,4},... | collective-permute-start | bytes 1572872 | tf_op jit(solution)/shard_map/ppermute | solution.py:24
  32.0 1.3 collective-permute-start.10
  33.3 1.7 collective-permute-start.5
  35.7 2.2 %collective-permute-done.5 = f32[8,128]{1,0:T(8,128)S(1)} collective-permute-done((f32[8,128]{1,0:T(8,128)S(1)}, f32[8,128]{1,0:T(8,128)S(1)}, u32[]{:S(2)}, u32[]{:S(2)}) %collective-permute-start.5) | collective-permute-done | bytes 4128 | tf_op jit(solution)/shard_map/ppermute | solution.py:24
  38.0 5.7 %collective-permute-start.11 = (f32[8,128]{1,0:T(8,128)S(1)}, f32[8,128]{1,0:T(8,128)S(1)}, u32[]{:S(2)}, u32[]{:S(2)}) collective-permute-start(f32[8,128]{1,0:T(8,128)S(1)} %maximum_select_fusion.peaks_ref), channel_id=1, source_target_pairs={{0,4},{1,5},{2,6},{3,7},{4,0},{5,1},{6,2},{7,3},{8,12},{9,13},{10,... | collective-permute-start | bytes 12296 | tf_op jit(solution)/shard_map/ppermute | solution.py:24
  43.6 4.9 %collective-permute-done.1.other_ref = bf16[256,1024]{1,0:T(8,128)(2,1)S(1)} collective-permute-done((bf16[256,1024]{1,0:T(8,128)(2,1)S(1)}, bf16[256,1024]{1,0:T(8,128)(2,1)S(1)}, u32[]{:S(2)}, u32[]{:S(2)}) %collective-permute-start.1) | collective-permute-done | bytes 524320 | tf_op jit(solution)/shard_map/ppermute | solution.py:24
  48.6 5.2 %fusion.26 = f32[1280,1024]{1,0:T(8,128)} fusion(bf16[256,1280]{1,0:T(8,128)(2,1)} %collective-permute-done.early_ref, bf16[256,640]{1,0:T(8,128)(2,1)S(1)} %get-tuple-element.95, bf16[256,640]{1,0:T(8,128)(2,1)S(1)} %get-tuple-element.94, bf16[256,1024]{1,0:T(8,128)(2,1)S(1)} %collective-permute-done.1.other_ref, bf16[256,1024]{1,0:T(8,128)(2,1)S(1)} %bitcast.33), kind=kOutput, calls=%fused_computation.48 | convolution fusion | flops 1348206592 | bytes 7602176 | tf_op jit(solution)/shard_map/dot_general | solution.py:304
  54.4 1.3 shard_map.102
  55.7 1.3 fusion.58
  57.1 2.1 %fusion.52 = (f16[160,1024]{1,0:T(8,128)(2,1)S(1)}, f16[160,1024]{1,0:T(8,128)(2,1)S(1)}) fusion(f32[1280,1024]{1,0:T(8,128)} %fusion.26, s32[]{:T(128)S(6)} %select_n.169, f32[]{:T(128)} %bitcast.6, s32[]{:T(128)S(6)} %select_n.164), kind=kLoop, calls=%fused_computation.82 | loop fusion | flops 1310720 | bytes 1966092 | tf_op jit(solution)/shard_map/convert_element_type | solution.py:55
  59.4 4.9 %collective-permute-start.14 = (f16[160,1024]{1,0:T(8,128)(2,1)S(1)}, f16[160,1024]{1,0:T(8,128)(2,1)S(1)}, u32[]{:S(2)}, u32[]{:S(2)}) collective-permute-start(f16[160,1024]{1,0:T(8,128)(2,1)S(1)} %get-tuple-element.91), channel_id=1, source_target_pairs={{0,7},{1,2},{2,1},{3,4},{4,3},{5,6},{6,5},{7,0},{8,15},{9,10},{10,... | collective-permute-start | bytes 983048 | tf_op jit(solution)/shard_map/ppermute | solution.py:327
  64.5 2.7 %collective-permute-start.12 = (f32[160,128]{1,0:T(8,128)S(1)}, f32[160,128]{1,0:T(8,128)S(1)}, u32[]{:S(2)}, u32[]{:S(2)}) collective-permute-start(f32[160,128]{1,0:T(8,128)S(1)} %copy-done.18), channel_id=1, source_target_pairs={{0,32},{32,0},{1,33},{33,1},{2,34},{34,2},{3,35},{35,3},{4,36},{36... | collective-permute-start | bytes 245768 | tf_op jit(solution)/shard_map/ppermute | solution.py:24
  67.2 5.2 %fusion.32 = f32[1280,1024]{1,0:T(8,128)} fusion(bf16[256,1280]{1,0:T(8,128)(2,1)} %collective-permute-done.10.late_ref, bf16[256,640]{1,0:T(8,128)(2,1)S(1)} %get-tuple-element.93, bf16[256,640]{1,0:T(8,128)(2,1)S(1)} %get-tuple-element.92, bf16[256,1024]{1,0:T(8,128)(2,1)S(1)} %copy-done.6, bf16[256,1024]{1,0:T(8,128)(2,1)S(1)} %bitcast.34), kind=kOutput, calls=%fused_computation.54 | convolution fusion | flops 1348206592 | bytes 7602176 | tf_op jit(solution)/shard_map/dot_general | solution.py:304
  72.4 3.3 %collective-permute-done.13 = f16[160,1024]{1,0:T(8,128)(2,1)S(1)} collective-permute-done((f16[160,1024]{1,0:T(8,128)(2,1)S(1)}, f16[160,1024]{1,0:T(8,128)(2,1)S(1)}, u32[]{:S(2)}, u32[]{:S(2)}) %collective-permute-start.13) | collective-permute-done | bytes 327712 | tf_op jit(solution)/shard_map/ppermute | solution.py:327
  75.7 3.1 %collective-permute-done.14 = f16[160,1024]{1,0:T(8,128)(2,1)S(1)} collective-permute-done((f16[160,1024]{1,0:T(8,128)(2,1)S(1)}, f16[160,1024]{1,0:T(8,128)(2,1)S(1)}, u32[]{:S(2)}, u32[]{:S(2)}) %collective-permute-start.14) | collective-permute-done | bytes 327712 | tf_op jit(solution)/shard_map/ppermute | solution.py:327
  78.8 1.4 fusion.49
  82.3 3.1 %collective-permute-start.16 = (f16[320,1024]{1,0:T(8,128)(2,1)}, f16[320,1024]{1,0:T(8,128)(2,1)}, u32[]{:S(2)}, u32[]{:S(2)}) collective-permute-start(f16[320,1024]{1,0:T(8,128)(2,1)} %fusion.21), channel_id=1, source_target_pairs={{0,7},{1,2},{2,1},{3,4},{4,3},{5,6},{6,5},{7,0},{8,15},{9,10},{10,... | collective-permute-start | bytes 1966088 | tf_op jit(solution)/shard_map/ppermute | solution.py:327
  86.3 2.5 %collective-permute-start.18 = (bf16[160,128]{1,0:T(8,128)(2,1)S(1)}, bf16[160,128]{1,0:T(8,128)(2,1)S(1)}, u32[]{:S(2)}, u32[]{:S(2)}) collective-permute-start(bf16[160,128]{1,0:T(8,128)(2,1)S(1)} %get-tuple-element.82.refs_0_), channel_id=1, source_target_pairs={{0,32},{32,0},{1,33},{33,1},{2,34},{34,2},{3,35},{35,3},{4,36},{36... | collective-permute-start | bytes 122888 | tf_op jit(solution)/shard_map/ppermute | solution.py:24
  89.6 2.5 %copy-done.1 = bf16[1,2560,1024]{2,1,0:T(8,128)(2,1)S(1)} copy-done((bf16[1,2560,1024]{2,1,0:T(8,128)(2,1)S(1)}, bf16[1,2560,1024]{2,1,0:T(8,128)(2,1)}, u32[]{:S(2)}) %copy-start.1) | copy-done | bytes 5242904
  92.1 1.0 copy-done.7
  93.1 11.0 %shard_map.103 = (f32[256,1024]{1,0:T(8,128)S(1)}, bf16[256,5120]{1,0:T(8,128)(2,1)}, bf16[272,3584]{1,0:T(8,128)(2,1)}) custom-call(s32[1]{0:T(128)} %bitcast.z_ref, s32[1]{0:T(128)} %bitcast.1._, bf16[256,5120]{1,0:T(8,128)(2,1)S(1)} %bitcast.29, bf16[256,1280]{1,0:T(8,128)(2,1)} %collective-permute-done.early_ref, ...), custom_call_target="tpu_custom_call" | custom-call | tf_op jit(solution)/shard_map/pallas_call | solution.py:200
  105.2 1.8 %collective-permute-start.15 = (bf16[272,3584]{1,0:T(8,128)(2,1)}, bf16[272,3584]{1,0:T(8,128)(2,1)}, u32[]{:S(2)}, u32[]{:S(2)}) collective-permute-start(bf16[272,3584]{1,0:T(8,128)(2,1)} %get-tuple-element.61), channel_id=1, source_target_pairs={{0,8},{8,0},{1,9},{9,1},{2,10},{10,2},{3,11},{11,3},{4,12},{12,4},... | collective-permute-start | bytes 5849096 | tf_op jit(solution)/shard_map/ppermute | solution.py:24
  107.6 1.4 shard_map.104.refs_0_
  109.0 1.6 shard_map.105
  110.7 3.0 %fusion.22 = f16[320,1024]{1,0:T(8,128)(2,1)S(1)} fusion(f16[320,1024]{1,0:T(8,128)(2,1)} %collective-permute-done.17, f32[1280,1024]{1,0:T(8,128)} %fusion.32, s32[]{:T(128)S(6)} %select_n.178, f32[]{:T(128)} %bitcast.6), kind=kLoop, calls=%fused_computation.44 | loop fusion | flops 2949120 | bytes 2621448 | tf_op jit(solution)/shard_map/convert_element_type | solution.py:55
  113.9 3.0 %fusion.23 = f16[320,1024]{1,0:T(8,128)(2,1)S(1)} fusion(f16[320,1024]{1,0:T(8,128)(2,1)} %collective-permute-done.16, f32[1280,1024]{1,0:T(8,128)} %fusion.26, s32[]{:T(128)S(6)} %select_n.178, f32[]{:T(128)} %bitcast.6), kind=kLoop, calls=%fused_computation.45 | loop fusion | flops 2949120 | bytes 2621448 | tf_op jit(solution)/shard_map/convert_element_type | solution.py:55
  117.8 3.0 %collective-permute-start.24 = (bf16[160,256]{1,0:T(8,128)(2,1)S(1)}, bf16[160,256]{1,0:T(8,128)(2,1)S(1)}, u32[]{:S(2)}, u32[]{:S(2)}) collective-permute-start(bf16[160,256]{1,0:T(8,128)(2,1)S(1)} %copy-done.10), channel_id=1, source_target_pairs={{0,192},{64,128},{128,64},{192,0},{1,193},{65,129},{129,65},{193,1... | collective-permute-start | bytes 245768 | tf_op jit(solution)/shard_map/ppermute | solution.py:24
  121.4 2.7 %collective-permute-done.24.refs_3_ = bf16[160,256]{1,0:T(8,128)(2,1)S(1)} collective-permute-done((bf16[160,256]{1,0:T(8,128)(2,1)S(1)}, bf16[160,256]{1,0:T(8,128)(2,1)S(1)}, u32[]{:S(2)}, u32[]{:S(2)}) %collective-permute-start.24) | collective-permute-done | bytes 81952 | tf_op jit(solution)/shard_map/ppermute | solution.py:24
  124.1 2.6 %collective-permute-done.23.refs_2_ = bf16[160,256]{1,0:T(8,128)(2,1)S(1)} collective-permute-done((bf16[160,256]{1,0:T(8,128)(2,1)S(1)}, bf16[160,256]{1,0:T(8,128)(2,1)S(1)}, u32[]{:S(2)}, u32[]{:S(2)}) %collective-permute-start.23) | collective-permute-done | bytes 81952 | tf_op jit(solution)/shard_map/ppermute | solution.py:24
  126.7 1.8 %collective-permute-done.22.refs_1_ = bf16[160,256]{1,0:T(8,128)(2,1)S(1)} collective-permute-done((bf16[160,256]{1,0:T(8,128)(2,1)S(1)}, bf16[160,256]{1,0:T(8,128)(2,1)S(1)}, u32[]{:S(2)}, u32[]{:S(2)}) %collective-permute-start.22) | collective-permute-done | bytes 81952 | tf_op jit(solution)/shard_map/ppermute | solution.py:24
  129.2 1.8 %shard_map.106.refs_0_ = bf16[160,1024]{1,0:T(8,128)(2,1)} custom-call(s32[1]{0:T(128)} %bitcast.12.here_ref, bf16[160,256]{1,0:T(8,128)(2,1)} %shard_map.104.refs_0_, bf16[160,256]{1,0:T(8,128)(2,1)} %copy-done.17, bf16[160,256]{1,0:T(8,128)(2,1)} %copy-done.16, bf16[160,256]{1,0:T(8,128)(2,1)} %copy-done.15), custom_call_target="tpu_custom_call" | custom-call | tf_op jit(solution)/shard_map/pallas_call | solution.py:137
  131.9 1.9 %collective-permute-done.20 = f16[320,1024]{1,0:T(8,128)(2,1)S(1)} collective-permute-done((f16[320,1024]{1,0:T(8,128)(2,1)S(1)}, f16[320,1024]{1,0:T(8,128)(2,1)S(1)}, u32[]{:S(2)}, u32[]{:S(2)}) %collective-permute-start.20) | collective-permute-done | bytes 655392 | tf_op jit(solution)/shard_map/ppermute | solution.py:327
  133.8 5.0 %fusion.25 = (f16[320,1024]{1,0:T(8,128)(2,1)}, f16[320,1024]{1,0:T(8,128)(2,1)S(1)}) fusion(f16[320,1024]{1,0:T(8,128)(2,1)S(1)} %collective-permute-done.20, f32[1280,1024]{1,0:T(8,128)} %fusion.32, s32[]{:T(128)S(6)} %select_n.167, f32[]{:T(128)} %bitcast.6, f16[320,1024]{1,0:T(8,128)(2,1)S(1)} %collective-permute-done.21, s32[]{:T(128)S(6)} %select_n.177), kind=kLoop, calls=%fused_computation.47 | loop fusion | flops 5898240 | bytes 5242892 | tf_op jit(solution)/shard_map/convert_element_type | solution.py:55
  138.8 2.9 %collective-permute-start.26 = (f16[320,1024]{1,0:T(8,128)(2,1)}, f16[320,1024]{1,0:T(8,128)(2,1)S(1)}, u32[]{:S(2)}, u32[]{:S(2)}) collective-permute-start(f16[320,1024]{1,0:T(8,128)(2,1)} %get-tuple-element.84), channel_id=1, source_target_pairs={{0,7},{1,2},{2,1},{3,4},{4,3},{5,6},{6,5},{7,0},{8,15},{9,10},{10,... | collective-permute-start | bytes 1966088 | tf_op jit(solution)/shard_map/ppermute | solution.py:384
  144.1 2.0 %shard_map.107 = bf16[320,1024]{1,0:T(8,128)(2,1)} custom-call(s32[1]{0:T(128)} %bitcast.11.here_ref, bf16[160,1024]{1,0:T(8,128)(2,1)} %shard_map.106.refs_0_, bf16[160,1024]{1,0:T(8,128)(2,1)} %copy-done.11), custom_call_target="tpu_custom_call" | custom-call | tf_op jit(solution)/shard_map/pallas_call | solution.py:137
  146.0 10.2 %collective-permute-done.26 = f16[320,1024]{1,0:T(8,128)(2,1)S(1)} collective-permute-done((f16[320,1024]{1,0:T(8,128)(2,1)}, f16[320,1024]{1,0:T(8,128)(2,1)S(1)}, u32[]{:S(2)}, u32[]{:S(2)}) %collective-permute-start.26) | collective-permute-done | bytes 655392 | tf_op jit(solution)/shard_map/ppermute | solution.py:384
  157.3 5.4 %fusion.16 = bf16[320,1024]{1,0:T(8,128)(2,1)} fusion(f16[320,1024]{1,0:T(8,128)(2,1)S(1)} %collective-permute-done.25, f16[320,1024]{1,0:T(8,128)(2,1)S(1)} %collective-permute-done.26, f32[1280,1024]{1,0:T(8,128)} %fusion.32, s32[]{:T(128)S(6)} %select_n.169, f32[]{:T(128)} %bitcast.13, f32[]{:T(128)} %bitcast.6), kind=kLoop, calls=%fused_computation.38 | loop fusion | flops 4259840 | bytes 3276812 | tf_op jit(solution)/shard_map/convert_element_type | solution.py:389
  162.7 1.1 slice.31
  164.5 2.3 %fusion.53 = bf16[1,256,1024]{2,1,0:T(8,128)(2,1)} fusion(f32[256,1024]{1,0:T(8,128)S(1)} %copy-done.4, f32[]{:T(128)} %bitcast.14, bf16[272,3584]{1,0:T(8,128)(2,1)} %collective-permute-done.15), kind=kLoop, calls=%fused_computation.89 | loop fusion | flops 2883584 | bytes 2097156 | tf_op jit(solution)/shard_map/broadcast_in_dim | solution.py:396
  166.8 1.5 bitcast_dynamic-update-slice_fusion
  168.3 1.5 copy-done.24
  (109 shorter events, 19.4 us)
Async XLA Ops:
  7.2 2.7 %copy-start.12 = (f32[320,64]{0,1:T(8,128)S(1)}, f32[320,64]{0,1:T(8,128)}, u32[]{:S(2)}) copy-start(f32[320,64]{0,1:T(8,128)} %param.11) | copy-start | bytes 245764
  7.2 82.4 %all-gather.3.cloned.1.call-start = ((), (), s32[]{:S(2)}) async-start(), calls=%async_computation | async-start | bytes 5898240 | tf_op jit(solution)/shard_map/all_gather | solution.py:264
  9.9 9.8 %collective-permute-start.3 = (f32[160,1024]{1,0:T(8,128)}, f32[160,1024]{1,0:T(8,128)S(1)}, u32[]{:S(2)}, u32[]{:S(2)}) collective-permute-start(f32[160,1024]{1,0:T(8,128)} %dynamic-slice_bitcast_fusion), channel_id=1, source_target_pairs={{0,16},{16,0},{1,17},{17,1},{2,18},{18,2},{3,19},{19,3},{4,20},{20... | collective-permute-start | bytes 1966088 | tf_op jit(solution)/shard_map/ppermute | solution.py:24
  10.8 19.2 %collective-permute-start.9 = (f32[160,64]{1,0:T(8,128)}, f32[160,64]{1,0:T(8,128)S(1)}, u32[]{:S(2)}, u32[]{:S(2)}) collective-permute-start(f32[160,64]{1,0:T(8,128)} %copy.14), channel_id=1, source_target_pairs={{0,16},{16,0},{1,17},{17,1},{2,18},{18,2},{3,19},{19,3},{4,20},{20... | collective-permute-start | bytes 122888 | tf_op jit(solution)/shard_map/ppermute | solution.py:24
  11.3 7.2 %copy-start = (bf16[1,256,5120]{2,1,0:T(8,128)(2,1)S(1)}, bf16[1,256,5120]{2,1,0:T(8,128)(2,1)}, u32[]{:S(2)}) copy-start(bf16[1,256,5120]{2,1,0:T(8,128)(2,1)} %param.6) | copy-start | bytes 7864324
  16.2 9.1 %collective-permute-start.2 = (f32[8,128]{1,0:T(8,128)}, f32[8,128]{1,0:T(8,128)S(1)}, u32[]{:S(2)}, u32[]{:S(2)}) collective-permute-start(f32[8,128]{1,0:T(8,128)} %shard_map.101), channel_id=1, source_target_pairs={{0,8},{8,0},{1,9},{9,1},{2,10},{10,2},{3,11},{11,3},{4,12},{12,4},... | collective-permute-start | bytes 12296 | tf_op jit(solution)/shard_map/ppermute | solution.py:24
  19.5 29.1 %collective-permute-start = (bf16[256,1280]{1,0:T(8,128)(2,1)}, bf16[256,1280]{1,0:T(8,128)(2,1)}, u32[]{:S(2)}, u32[]{:S(2)}) collective-permute-start(bf16[256,1280]{1,0:T(8,128)(2,1)} %pad_maximum_fusion.3), channel_id=1, source_target_pairs={{0,8},{8,0},{1,9},{9,1},{2,10},{10,2},{3,11},{11,3},{4,12},{12,4},... | collective-permute-start | bytes 1966088 | tf_op jit(solution)/shard_map/ppermute | solution.py:24
  20.9 11.1 %collective-permute-start.8 = (f32[160,256]{1,0:T(8,128)S(1)}, f32[160,256]{1,0:T(8,128)S(1)}, u32[]{:S(2)}, u32[]{:S(2)}) collective-permute-start(f32[160,256]{1,0:T(8,128)S(1)} %get-tuple-element.100), channel_id=1, source_target_pairs={{0,192},{64,128},{128,64},{192,0},{1,193},{65,129},{129,65},{193,1... | collective-permute-start | bytes 491528 | tf_op jit(solution)/shard_map/ppermute | solution.py:24
  23.8 9.5 %collective-permute-start.7 = (f32[160,256]{1,0:T(8,128)S(1)}, f32[160,256]{1,0:T(8,128)S(1)}, u32[]{:S(2)}, u32[]{:S(2)}) collective-permute-start(f32[160,256]{1,0:T(8,128)S(1)} %get-tuple-element.101), channel_id=1, source_target_pairs={{0,128},{64,192},{128,0},{192,64},{1,129},{65,193},{129,1},{193,65... | collective-permute-start | bytes 491528 | tf_op jit(solution)/shard_map/ppermute | solution.py:24
  24.5 5.4 %copy-start.2 = (bf16[1,256,1024]{2,1,0:T(8,128)(2,1)S(1)}, bf16[1,256,1024]{2,1,0:T(8,128)(2,1)}, u32[]{:S(2)}) copy-start(bf16[1,256,1024]{2,1,0:T(8,128)(2,1)} %param.8) | copy-start | bytes 1572868
  25.5 3.7 %collective-permute-start.4 = (f32[8,128]{1,0:T(8,128)S(1)}, f32[8,128]{1,0:T(8,128)S(1)}, u32[]{:S(2)}, u32[]{:S(2)}) collective-permute-start(f32[8,128]{1,0:T(8,128)S(1)} %maximum_select_fusion.2), channel_id=1, source_target_pairs={{0,1},{1,0},{2,3},{3,2},{4,5},{5,4},{6,7},{7,6},{8,9},{9,8},{10,11... | collective-permute-start | bytes 12296 | tf_op jit(solution)/shard_map/ppermute | solution.py:24
  29.1 5.9 %collective-permute-start.6 = (f32[160,256]{1,0:T(8,128)S(1)}, f32[160,256]{1,0:T(8,128)S(1)}, u32[]{:S(2)}, u32[]{:S(2)}) collective-permute-start(f32[160,256]{1,0:T(8,128)S(1)} %get-tuple-element.102), channel_id=1, source_target_pairs={{0,64},{64,0},{128,192},{192,128},{1,65},{65,1},{129,193},{193,129... | collective-permute-start | bytes 491528 | tf_op jit(solution)/shard_map/ppermute | solution.py:24
  29.9 18.6 %collective-permute-start.1 = (bf16[256,1024]{1,0:T(8,128)(2,1)S(1)}, bf16[256,1024]{1,0:T(8,128)(2,1)S(1)}, u32[]{:S(2)}, u32[]{:S(2)}) collective-permute-start(bf16[256,1024]{1,0:T(8,128)(2,1)S(1)} %bitcast.32), channel_id=1, source_target_pairs={{0,8},{8,0},{1,9},{9,1},{2,10},{10,2},{3,11},{11,3},{4,12},{12,4},... | collective-permute-start | bytes 1572872 | tf_op jit(solution)/shard_map/ppermute | solution.py:24
  32.0 35.2 %collective-permute-start.10 = (bf16[256,1280]{1,0:T(8,128)(2,1)}, bf16[256,1280]{1,0:T(8,128)(2,1)}, u32[]{:S(2)}, u32[]{:S(2)}) collective-permute-start(bf16[256,1280]{1,0:T(8,128)(2,1)} %pad_maximum_fusion.4), channel_id=1, source_target_pairs={{0,8},{8,0},{1,9},{9,1},{2,10},{10,2},{3,11},{11,3},{4,12},{12,4},... | collective-permute-start | bytes 1966088 | tf_op jit(solution)/shard_map/ppermute | solution.py:24
  33.3 4.6 %collective-permute-start.5 = (f32[8,128]{1,0:T(8,128)S(1)}, f32[8,128]{1,0:T(8,128)S(1)}, u32[]{:S(2)}, u32[]{:S(2)}) collective-permute-start(f32[8,128]{1,0:T(8,128)S(1)} %maximum_select_fusion.1), channel_id=1, source_target_pairs={{0,2},{1,3},{2,0},{3,1},{4,6},{5,7},{6,4},{7,5},{8,10},{9,11},{10,... | collective-permute-start | bytes 12296 | tf_op jit(solution)/shard_map/ppermute | solution.py:24
  38.0 15.8 %copy-start.21 = (f32[8,128]{1,0:T(8,128)}, f32[8,128]{1,0:T(8,128)S(1)}, u32[]{:S(2)}) copy-start(f32[8,128]{1,0:T(8,128)S(1)} %maximum_select_fusion.peaks_ref) | copy-start | bytes 12292
  38.0 15.8 %collective-permute-start.11 = (f32[8,128]{1,0:T(8,128)S(1)}, f32[8,128]{1,0:T(8,128)S(1)}, u32[]{:S(2)}, u32[]{:S(2)}) collective-permute-start(f32[8,128]{1,0:T(8,128)S(1)} %maximum_select_fusion.peaks_ref), channel_id=1, source_target_pairs={{0,4},{1,5},{2,6},{3,7},{4,0},{5,1},{6,2},{7,3},{8,12},{9,13},{10,... | collective-permute-start | bytes 12296 | tf_op jit(solution)/shard_map/ppermute | solution.py:24
  48.6 5.2 %copy-start.5 = (bf16[256,1024]{1,0:T(8,128)(2,1)}, bf16[256,1024]{1,0:T(8,128)(2,1)S(1)}, u32[]{:S(2)}) copy-start(bf16[256,1024]{1,0:T(8,128)(2,1)S(1)} %collective-permute-done.1.other_ref) | copy-start | bytes 1572868
  57.1 7.4 %copy-start.18 = (f32[160,128]{1,0:T(8,128)S(1)}, f32[160,128]{1,0:T(8,128)}, u32[]{:S(2)}) copy-start(f32[160,128]{1,0:T(8,128)} %constant_dynamic-slice_fusion.1) | copy-start | bytes 245764
  57.1 10.1 %copy-start.6 = (bf16[256,1024]{1,0:T(8,128)(2,1)S(1)}, bf16[256,1024]{1,0:T(8,128)(2,1)}, u32[]{:S(2)}) copy-start(bf16[256,1024]{1,0:T(8,128)(2,1)} %copy-done.5) | copy-start | bytes 1572868
  59.2 16.6 %collective-permute-start.13 = (f16[160,1024]{1,0:T(8,128)(2,1)S(1)}, f16[160,1024]{1,0:T(8,128)(2,1)S(1)}, u32[]{:S(2)}, u32[]{:S(2)}) collective-permute-start(f16[160,1024]{1,0:T(8,128)(2,1)S(1)} %get-tuple-element.90), channel_id=1, source_target_pairs={{0,1},{1,0},{2,3},{3,2},{4,5},{5,4},{6,7},{7,6},{8,9},{9,8},{10,11... | collective-permute-start | bytes 983048 | tf_op jit(solution)/shard_map/ppermute | solution.py:327
  59.4 19.4 %collective-permute-start.14 = (f16[160,1024]{1,0:T(8,128)(2,1)S(1)}, f16[160,1024]{1,0:T(8,128)(2,1)S(1)}, u32[]{:S(2)}, u32[]{:S(2)}) collective-permute-start(f16[160,1024]{1,0:T(8,128)(2,1)S(1)} %get-tuple-element.91), channel_id=1, source_target_pairs={{0,7},{1,2},{2,1},{3,4},{4,3},{5,6},{6,5},{7,0},{8,15},{9,10},{10,... | collective-permute-start | bytes 983048 | tf_op jit(solution)/shard_map/ppermute | solution.py:327
  64.5 16.8 %collective-permute-start.12 = (f32[160,128]{1,0:T(8,128)S(1)}, f32[160,128]{1,0:T(8,128)S(1)}, u32[]{:S(2)}, u32[]{:S(2)}) collective-permute-start(f32[160,128]{1,0:T(8,128)S(1)} %copy-done.18), channel_id=1, source_target_pairs={{0,32},{32,0},{1,33},{33,1},{2,34},{34,2},{3,35},{35,3},{4,36},{36... | collective-permute-start | bytes 245768 | tf_op jit(solution)/shard_map/ppermute | solution.py:24
  67.2 11.6 %slice-start = ((s8[5242880]{0:T(1024)(128)(4,1)}), s8[4194304]{0:T(1024)(128)(4,1)S(1)}, s32[]{:S(2)}) async-start(s8[5242880]{0:T(1024)(128)(4,1)} %bitcast.36), calls=%async_computation.1 | async-start | bytes 8388608
  67.2 11.6 %slice-start.1 = ((s8[5242880]{0:T(1024)(128)(4,1)}), s8[1048576]{0:T(1024)(128)(4,1)S(1)}, s32[]{:S(2)}) async-start(s8[5242880]{0:T(1024)(128)(4,1)} %bitcast.36), calls=%async_computation.2 | async-start | bytes 2097152
  81.2 29.4 %collective-permute-start.17 = (f16[320,1024]{1,0:T(8,128)(2,1)}, f16[320,1024]{1,0:T(8,128)(2,1)}, u32[]{:S(2)}, u32[]{:S(2)}) collective-permute-start(f16[320,1024]{1,0:T(8,128)(2,1)} %fusion.20), channel_id=1, source_target_pairs={{0,1},{1,0},{2,3},{3,2},{4,5},{5,4},{6,7},{7,6},{8,9},{9,8},{10,11... | collective-permute-start | bytes 1966088 | tf_op jit(solution)/shard_map/ppermute | solution.py:327
  82.3 31.6 %collective-permute-start.16 = (f16[320,1024]{1,0:T(8,128)(2,1)}, f16[320,1024]{1,0:T(8,128)(2,1)}, u32[]{:S(2)}, u32[]{:S(2)}) collective-permute-start(f16[320,1024]{1,0:T(8,128)(2,1)} %fusion.21), channel_id=1, source_target_pairs={{0,7},{1,2},{2,1},{3,4},{4,3},{5,6},{6,5},{7,0},{8,15},{9,10},{10,... | collective-permute-start | bytes 1966088 | tf_op jit(solution)/shard_map/ppermute | solution.py:327
  86.3 17.8 %copy-start.13 = (bf16[160,128]{1,0:T(8,128)(2,1)}, bf16[160,128]{1,0:T(8,128)(2,1)S(1)}, u32[]{:S(2)}) copy-start(bf16[160,128]{1,0:T(8,128)(2,1)S(1)} %get-tuple-element.82.refs_0_) | copy-start | bytes 122884
  86.3 20.7 %collective-permute-start.18 = (bf16[160,128]{1,0:T(8,128)(2,1)S(1)}, bf16[160,128]{1,0:T(8,128)(2,1)S(1)}, u32[]{:S(2)}, u32[]{:S(2)}) collective-permute-start(bf16[160,128]{1,0:T(8,128)(2,1)S(1)} %get-tuple-element.82.refs_0_), channel_id=1, source_target_pairs={{0,32},{32,0},{1,33},{33,1},{2,34},{34,2},{3,35},{35,3},{4,36},{36... | collective-permute-start | bytes 122888 | tf_op jit(solution)/shard_map/ppermute | solution.py:24
  89.6 17.4 %collective-permute-start.19 = (f32[160,64]{1,0:T(8,128)S(1)}, f32[160,64]{1,0:T(8,128)S(1)}, u32[]{:S(2)}, u32[]{:S(2)}) collective-permute-start(f32[160,64]{1,0:T(8,128)S(1)} %get-tuple-element.107), channel_id=1, source_target_pairs={{0,16},{16,0},{1,17},{17,1},{2,18},{18,2},{3,19},{19,3},{4,20},{20... | collective-permute-start | bytes 122888 | tf_op jit(solution)/shard_map/ppermute | solution.py:24
  89.6 2.5 %copy-start.1 = (bf16[1,2560,1024]{2,1,0:T(8,128)(2,1)S(1)}, bf16[1,2560,1024]{2,1,0:T(8,128)(2,1)}, u32[]{:S(2)}) copy-start(bf16[1,2560,1024]{2,1,0:T(8,128)(2,1)} %all-gather.3.cloned.1.call-done) | copy-start | bytes 15728644
  105.2 57.5 %collective-permute-start.15 = (bf16[272,3584]{1,0:T(8,128)(2,1)}, bf16[272,3584]{1,0:T(8,128)(2,1)}, u32[]{:S(2)}, u32[]{:S(2)}) collective-permute-start(bf16[272,3584]{1,0:T(8,128)(2,1)} %get-tuple-element.61), channel_id=1, source_target_pairs={{0,8},{8,0},{1,9},{9,1},{2,10},{10,2},{3,11},{11,3},{4,12},{12,4},... | collective-permute-start | bytes 5849096 | tf_op jit(solution)/shard_map/ppermute | solution.py:24
  107.0 2.1 %copy-start.14 = (f32[160,64]{1,0:T(8,128)}, f32[160,64]{1,0:T(8,128)S(1)}, u32[]{:S(2)}) copy-start(f32[160,64]{1,0:T(8,128)S(1)} %collective-permute-done.19.refs_1_) | copy-start | bytes 122884
  113.7 4.1 %copy-start.10 = (bf16[160,256]{1,0:T(8,128)(2,1)S(1)}, bf16[160,256]{1,0:T(8,128)(2,1)}, u32[]{:S(2)}) copy-start(bf16[160,256]{1,0:T(8,128)(2,1)} %shard_map.104.refs_0_) | copy-start | bytes 245764
  113.7 18.2 %collective-permute-start.21 = (f16[320,1024]{1,0:T(8,128)(2,1)S(1)}, f16[320,1024]{1,0:T(8,128)(2,1)S(1)}, u32[]{:S(2)}, u32[]{:S(2)}) collective-permute-start(f16[320,1024]{1,0:T(8,128)(2,1)S(1)} %fusion.22), channel_id=1, source_target_pairs={{0,7},{1,2},{2,1},{3,4},{4,3},{5,6},{6,5},{7,0},{8,15},{9,10},{10,... | collective-permute-start | bytes 1966088 | tf_op jit(solution)/shard_map/ppermute | solution.py:327
  116.9 16.9 %collective-permute-start.20 = (f16[320,1024]{1,0:T(8,128)(2,1)S(1)}, f16[320,1024]{1,0:T(8,128)(2,1)S(1)}, u32[]{:S(2)}, u32[]{:S(2)}) collective-permute-start(f16[320,1024]{1,0:T(8,128)(2,1)S(1)} %fusion.23), channel_id=1, source_target_pairs={{0,1},{1,0},{2,3},{3,2},{4,5},{5,4},{6,7},{7,6},{8,9},{9,8},{10,11... | collective-permute-start | bytes 1966088 | tf_op jit(solution)/shard_map/ppermute | solution.py:327
  117.8 6.3 %collective-permute-start.24 = (bf16[160,256]{1,0:T(8,128)(2,1)S(1)}, bf16[160,256]{1,0:T(8,128)(2,1)S(1)}, u32[]{:S(2)}, u32[]{:S(2)}) collective-permute-start(bf16[160,256]{1,0:T(8,128)(2,1)S(1)} %copy-done.10), channel_id=1, source_target_pairs={{0,192},{64,128},{128,64},{192,0},{1,193},{65,129},{129,65},{193,1... | collective-permute-start | bytes 245768 | tf_op jit(solution)/shard_map/ppermute | solution.py:24
  120.8 5.9 %collective-permute-start.23 = (bf16[160,256]{1,0:T(8,128)(2,1)S(1)}, bf16[160,256]{1,0:T(8,128)(2,1)S(1)}, u32[]{:S(2)}, u32[]{:S(2)}) collective-permute-start(bf16[160,256]{1,0:T(8,128)(2,1)S(1)} %copy-done.10), channel_id=1, source_target_pairs={{0,128},{64,192},{128,0},{192,64},{1,129},{65,193},{129,1},{193,65... | collective-permute-start | bytes 245768 | tf_op jit(solution)/shard_map/ppermute | solution.py:24
  124.1 4.4 %copy-start.15 = (bf16[160,256]{1,0:T(8,128)(2,1)}, bf16[160,256]{1,0:T(8,128)(2,1)S(1)}, u32[]{:S(2)}) copy-start(bf16[160,256]{1,0:T(8,128)(2,1)S(1)} %collective-permute-done.24.refs_3_) | copy-start | bytes 245764
  124.1 4.4 %collective-permute-start.22 = (bf16[160,256]{1,0:T(8,128)(2,1)S(1)}, bf16[160,256]{1,0:T(8,128)(2,1)S(1)}, u32[]{:S(2)}, u32[]{:S(2)}) collective-permute-start(bf16[160,256]{1,0:T(8,128)(2,1)S(1)} %copy-done.10), channel_id=1, source_target_pairs={{0,64},{64,0},{128,192},{192,128},{1,65},{65,1},{129,193},{193,129... | collective-permute-start | bytes 245768 | tf_op jit(solution)/shard_map/ppermute | solution.py:24
  126.7 1.8 %copy-start.16 = (bf16[160,256]{1,0:T(8,128)(2,1)}, bf16[160,256]{1,0:T(8,128)(2,1)S(1)}, u32[]{:S(2)}) copy-start(bf16[160,256]{1,0:T(8,128)(2,1)S(1)} %collective-permute-done.23.refs_2_) | copy-start | bytes 245764
  131.0 10.7 %copy-start.8 = (bf16[160,1024]{1,0:T(8,128)(2,1)S(1)}, bf16[160,1024]{1,0:T(8,128)(2,1)}, u32[]{:S(2)}) copy-start(bf16[160,1024]{1,0:T(8,128)(2,1)} %shard_map.106.refs_0_) | copy-start | bytes 983044
  131.0 10.8 %copy-start.9 = (f32[320,64]{1,0:T(8,128)S(1)}, f32[320,64]{1,0:T(8,128)}, u32[]{:S(2)}) copy-start(f32[320,64]{1,0:T(8,128)} %shard_map.105) | copy-start | bytes 245764
  138.8 17.5 %collective-permute-start.26 = (f16[320,1024]{1,0:T(8,128)(2,1)}, f16[320,1024]{1,0:T(8,128)(2,1)S(1)}, u32[]{:S(2)}, u32[]{:S(2)}) collective-permute-start(f16[320,1024]{1,0:T(8,128)(2,1)} %get-tuple-element.84), channel_id=1, source_target_pairs={{0,7},{1,2},{2,1},{3,4},{4,3},{5,6},{6,5},{7,0},{8,15},{9,10},{10,... | collective-permute-start | bytes 1966088 | tf_op jit(solution)/shard_map/ppermute | solution.py:384
  141.7 15.6 %collective-permute-start.25 = (f16[320,1024]{1,0:T(8,128)(2,1)S(1)}, f16[320,1024]{1,0:T(8,128)(2,1)S(1)}, u32[]{:S(2)}, u32[]{:S(2)}) collective-permute-start(f16[320,1024]{1,0:T(8,128)(2,1)S(1)} %get-tuple-element.85), channel_id=1, source_target_pairs={{0,1},{1,0},{2,3},{3,2},{4,5},{5,4},{6,7},{7,6},{8,9},{9,8},{10,11... | collective-permute-start | bytes 1966088 | tf_op jit(solution)/shard_map/ppermute | solution.py:384
  141.7 1.6 collective-permute-start.27
  157.3 7.2 %copy-start.4 = (f32[256,1024]{1,0:T(8,128)S(1)}, f32[256,1024]{1,0:T(8,128)}, u32[]{:S(2)}) copy-start(f32[256,1024]{1,0:T(8,128)} %copy-done.3) | copy-start | bytes 3145732
  157.3 9.6 %copy-start.23 = (bf16[256,5120]{1,0:T(8,128)(2,1)S(1)}, bf16[256,5120]{1,0:T(8,128)(2,1)}, u32[]{:S(2)}) copy-start(bf16[256,5120]{1,0:T(8,128)(2,1)} %get-tuple-element.76) | copy-start | bytes 7864324
  (8 other events, 7.1 us)
Sparse Core Ops, SparseCore 0:
  9.8 75.3 all-gather.2

commit v4 on v2

--- a/solution.py
+++ b/solution.py
@@ -60,17 +60,17 @@
     return jnp.sign(wide) * jnp.sqrt(jnp.abs(wide))
 
 
-def column_peak(tokens):
-    return jnp.max(jnp.sum(jnp.abs(tokens.astype(F32)), axis=0))
-
-
-def as_tile(first, second):
-    row = lax.broadcasted_iota(jnp.int32, (8, 128), 0)
-    return jnp.where(row < 4, first, second)
+def tile_rows():
+    return lax.broadcasted_iota(jnp.int32, (8, 128), 0)
+
+
+def local_peaks(tokens, cotangent):
+    peak = jnp.max(jnp.sum(jnp.abs(tokens.astype(F32)), axis=0))
+    return jnp.where(tile_rows() < 4, peak, jnp.max(jnp.abs(cotangent)).astype(F32))
 
 
 def join_peaks(peaks, other):
-    return as_tile(peaks + other, jnp.maximum(peaks, other))
+    return jnp.where(tile_rows() < 4, peaks + other, jnp.maximum(peaks, other))
 
 
 def dot(left, right):
@@ -116,15 +116,19 @@
     )(here.reshape(1), *pieces)
 
 
+TOP = 220.0
+
+
 def products_for_partner(z, early, late, cotangent, weight):
     count = 4
+    rows, features = cotangent.shape
     wide = weight.shape[0] // count
 
     def group(i, z_ref):
         step = 1 - 2 * (z_ref[0] % 2)
         return (z_ref[0] // 2 + jnp.where(i % 2 == 1, 4 + step * (2 - i), 2 - i)) % 4
 
-    def body(_, early_ref, late_ref, cotangent_ref, weight_ref, keys_ref, grads_ref):
+    def body(z_ref, early_ref, late_ref, cotangent_ref, weight_ref, sent_ref, keys_ref):
         i = pl.program_id(0)
 
         @pl.when(i == 0)
@@ -133,63 +137,103 @@
 
         tokens = jnp.where(i < count // 2, early_ref[...], late_ref[...])
         keys_ref[...] += dot(tokens, weight_ref[...])
-        grads_ref[...] = dot_t(cotangent_ref[...], weight_ref[...]).astype(BF16)
-
-    rows = cotangent.shape[0]
-    keys = jax.ShapeDtypeStruct(cotangent.shape, F32)
+        place = pl.multiple_of(features + group(i, z_ref) * wide, 128)
+        grads = dot_t(cotangent_ref[...], weight_ref[...]).astype(BF16)
+        sent_ref[:rows, pl.ds(place, wide)] = grads
+
+        @pl.when(i == count - 1)
+        def _():
+            keys = keys_ref[...]
+            largest = jnp.maximum(jnp.max(jnp.abs(keys)) * 1.01, 1e-30)
+            sent = jnp.full((16, features), largest, F32).astype(BF16)
+            sent_ref[rows:, :features] = sent
+            sent_ref[rows:, features:] = jnp.zeros((16, weight.shape[0]), BF16)
+            scaled = keys * (TOP / sent[:1, :].astype(F32))
+            power = scaled * scaled
+            power = power * power
+            power = power * power
+            power = power * power
+            sent_ref[:rows, :features] = jnp.where(scaled < 0, -power, power).astype(BF16)
+
+    sent = jax.ShapeDtypeStruct((rows + 16, features + weight.shape[0]), BF16)
     return pl.pallas_call(
         body,
         grid_spec=pltpu.PrefetchScalarGridSpec(
             num_scalar_prefetch=1,
             grid=(count,),
             in_specs=[
-                pl.BlockSpec((rows, wide), lambda i, g: (0, jnp.minimum(i, count // 2 - 1))),
-                pl.BlockSpec((rows, wide), lambda i, g: (0, jnp.maximum(i - count // 2, 0))),
+                pl.BlockSpec((rows, wide), lambda i, z: (0, jnp.minimum(i, count // 2 - 1))),
+                pl.BlockSpec((rows, wide), lambda i, z: (0, jnp.maximum(i - count // 2, 0))),
                 whole(cotangent),
-                pl.BlockSpec((wide, weight.shape[1]), lambda i, r: (group(i, r), 0)),
+                pl.BlockSpec((wide, features), lambda i, z: (group(i, z), 0)),
             ],
-            out_specs=[whole(keys), pl.BlockSpec((rows, wide), lambda i, r: (0, group(i, r)))],
+            out_specs=whole(sent),
+            scratch_shapes=[pltpu.VMEM(cotangent.shape, F32)],
         ),
-        out_shape=[keys, jax.ShapeDtypeStruct((rows, weight.shape[0]), BF16)],
+        out_shape=sent,
         cost_estimate=FREE,
     )(z.reshape(1), early, late, cotangent, weight)
 
 
-def products_here(side, tokens, cotangent, weight, keys_back):
-    count = 4
+def products_here(x, tokens, cotangent, weight, back):
+    count = 5
+    rows, features = cotangent.shape
     wide = weight.shape[0] // count
 
-    def body(_, tokens_ref, cotangent_ref, weight_ref, back_ref, keys_ref, grads_ref, sum_ref):
-        @pl.when(pl.program_id(0) == 0)
-        def _():
-            sum_ref[...] = back_ref[...]
-
-        sum_ref[...] += dot(tokens_ref[...], weight_ref[...])
-        grads_ref[...] = dot_t(cotangent_ref[...], weight_ref[...]).astype(BF16)
-
-        @pl.when(pl.program_id(0) == count - 1)
+    def body(
+        _, tokens_ref, cotangent_ref, weight_ref, coded_ref, back_ref, keys_ref, grads_ref, sum_ref
+    ):
+        i = pl.program_id(0)
+
+        @pl.when(i == 0)
+        def _():
+            power = coded_ref[:rows, :].astype(F32)
+            size = jnp.exp2(jnp.log2(jnp.abs(power)) * (1.0 / 16.0))
+            size = jnp.where(power == 0, 0.0, size) * (coded_ref[rows:, :].astype(F32)[:1] / TOP)
+            sum_ref[...] = jnp.where(power < 0, -size, size)
+
+        @pl.when(i < count)
+        def _():
+            sum_ref[...] += dot(tokens_ref[...], weight_ref[...])
+            grads_ref[...] = dot_t(cotangent_ref[...], weight_ref[...]).astype(BF16)
+
+        @pl.when(i >= count)
+        def _():
+            grads_ref[...] = back_ref[...]
+
+        @pl.when(i == count - 1)
         def _():
             keys_ref[...] = sum_ref[...].astype(BF16)
 
-    keys = jax.ShapeDtypeStruct(cotangent.shape, BF16)
-    here = pl.BlockSpec((tokens.shape[0], wide), lambda i, s: (0, s[0] * count + i))
+    def block(i):
+        return jnp.minimum(i, count - 1)
+
     return pl.pallas_call(
         body,
         grid_spec=pltpu.PrefetchScalarGridSpec(
             num_scalar_prefetch=1,
-            grid=(count,),
+            grid=(2 * count,),
             in_specs=[
-                here,
+                pl.BlockSpec((rows, wide), lambda i, x: (0, x[0] * count + block(i))),
                 whole(cotangent),
-                pl.BlockSpec((wide, weight.shape[1]), lambda i, s: (i, 0)),
-                whole(keys_back),
+                pl.BlockSpec((wide, features), lambda i, x: (block(i), 0)),
+                pl.BlockSpec((rows + 16, features), lambda i, x: (0, 0)),
+                pl.BlockSpec(
+                    (rows, wide), lambda i, x: (0, features // wide + jnp.maximum(i - count, 0))
+                ),
             ],
-            out_specs=[whole(keys), here],
-            scratch_shapes=[pltpu.VMEM(keys_back.shape, F32)],
+            out_specs=[
+                whole(cotangent),
+                pl.BlockSpec((rows, wide), lambda i, x: (0, (x[0] * count + i) % (2 * count))),
+            ],
+            scratch_shapes=[pltpu.VMEM(cotangent.shape, F32)],
         ),
-        out_shape=[keys, jax.ShapeDtypeStruct(tokens.shape, BF16)],
+        out_shape=[
+            jax.ShapeDtypeStruct(cotangent.shape, BF16),
+            jax.ShapeDtypeStruct(tokens.shape, BF16),
+        ],
         cost_estimate=FREE,
-    )(side.reshape(1), tokens, cotangent, weight, keys_back)
+    )(x.reshape(1), tokens, cotangent, weight, back, back)
 
 
 def shards(activations, key_weights, key_cotangent, fragment, pseudo_grads, momentum):
@@ -221,25 +265,24 @@
     give = rows_of(pseudo, theirs, rows)
     order.did(give)
     pseudo_other = swap(give, "c")
-    peak = jnp.full((8, 128), column_peak(order.step(tokens)))
-    order.did(peak)
-    peak_other = swap(peak, "xl")
+    peaks = local_peaks(order.step(tokens), cotangent)
+    order.did(peaks)
+    peaks_other = swap(peaks, "xl")
     sent = token_columns(order.step(tokens), 1 - x, early)
     order.did(sent)
     early_other = swap(sent, "xl")
-    pseudo_other, cotangent_other = order.step(pseudo_other, cotangent_other)
+    pseudo_other = order.step(pseudo_other)
     total = rows_of(pseudo, mine, rows) + pseudo_other
     gives = [columns_of(total, (y ^ m) * quarter, quarter) for m in (1, 2, 3)]
     old_give = rows_of(momentum, theirs, rows)
     order.did(*gives, old_give)
     others = [swap(g, "y", m) for g, m in zip(gives, (1, 2, 3))]
     old_other = swap(old_give, "c")
-    sent = token_columns(order.step(tokens), 1 - x, late)
+    tokens_held, cotangent_other = order.step(tokens, cotangent_other)
+    sent = token_columns(tokens_held, 1 - x, late)
     order.did(sent)
     late_other = swap(sent, "xl")
-    peak_other = order.step(peak_other)
-    peak_c = jnp.maximum(jnp.max(jnp.abs(cotangent)), jnp.max(jnp.abs(cotangent_other)))
-    peaks = as_tile(peak + peak_other, peak_c.astype(F32))
+    peaks = join_peaks(peaks, order.step(peaks_other))
     order.did(peaks)
     peaks_other = swap(peaks, "z", 1)
     early_mine = token_columns(order.step(tokens), x, early)
@@ -297,12 +340,6 @@
     partial_late = product(late_mine, late_other)
     order.did(partial_late)
 
-    far_even, far_odd = order.step(far_even, far_odd)
-    odd = jnp.concatenate([own(-3, 0, part) + decode(far_even), own(-3, part, part)])
-    odd = send(odd, ODD)
-    even = jnp.concatenate([own(3, 0, part), own(3, part, part) + decode(far_odd)])
-    even = send(even, EVEN)
-
     summed_other = order.step(summed_other)
     average = (columns_of(summed, xh * pair, pair) + summed_other) / 16
     old = in_order(c, rows_of(momentum, mine, rows), old_other, 1)
@@ -315,23 +352,21 @@
     updated_other = swap(updated, "xh")
     new_other = swap(give, "c")
 
+    far_even, far_odd = order.step(far_even, far_odd)
+    odd = jnp.concatenate([own(-3, 0, part) + decode(far_even), own(-3, part, part)])
+    odd = send(odd, ODD)
+    even = jnp.concatenate([own(3, 0, part), own(3, part, part) + decode(far_odd)])
+    even = send(even, EVEN)
+
+    updated_other = order.step(updated_other)
+    wide = assemble(xh, lambda i: (i, 1 - i), (updated, updated_other), 1)
+    order.did(wide)
+    wides = [swap(wide, "y", m) for m in (1, 2, 3)]
+
     weight_half = order.step(weight_half)
-    keys_other, grads_other = products_for_partner(
-        z,
-        early_other,
-        late_other,
-        cotangent_other,
-        weight_half,
-    )
-    order.did(keys_other, grads_other)
-    keys_back = swap(keys_other, "xl")
-    grads_back = swap(grads_other, "xl")
-
-    updated_other, new_other = order.step(updated_other, new_other)
-    new_momentum = assemble(c, lambda i: (i, 1 - i), (keep, new_other), 0)
-    wide = assemble(xh, lambda i: (i, 1 - i), (updated, updated_other), 1)
-    order.did(wide, new_momentum)
-    wides = [swap(wide, "y", m) for m in (1, 2, 3)]
+    sent = products_for_partner(z, early_other, late_other, cotangent_other, weight_half)
+    order.did(sent)
+    products_back = swap(sent, "xl")
 
     even, odd = ring_step(2, even, odd)
 
@@ -340,19 +375,22 @@
     order.did(block)
     block_other = swap(block, "c")
 
-    keys_back, even = order.step(keys_back, even)
-    even, odd = ring_step(1, even, odd)
-
-    key_out, grads_mine = products_here(
-        order.step(x), tokens, cotangent, weight_half, keys_back
-    )
-    order.did(key_out, grads_mine)
+    even, odd = order.step(even, odd)
+    even, odd = encode(own(1) + decode(odd)), encode(own(-1) + decode(even))
+    order.did(even, odd)
+    even, odd = lax.ppermute(even, "z", EVEN), lax.ppermute(odd, "z", ODD)
+
+    new_momentum = assemble(c, lambda i: (i, 1 - i), (keep, order.step(new_other)), 0)
+    order.did(new_momentum)
     new_fragment = assemble(c, lambda i: (i, 1 - i), (block, order.step(block_other)), 0)
     order.did(new_fragment)
+    key_out, act_grad = products_here(
+        x, tokens, cotangent, weight_half, order.step(products_back)
+    )
+    order.did(key_out, act_grad)
     even, odd = order.step(even, odd)
     weight_grad = ((own(0) + decode(even) + decode(odd)) * back).astype(BF16)
     order.did(weight_grad)
-    act_grad = lax.dynamic_update_slice(grads_mine, order.step(grads_back), (0, (1 - x) * half))
     return (
         key_out[None],
         act_grad[None],

time: 161 us -> 174 us (1.081); the launches traced: 160 us -> 171 us
  waiting for transfers between devices: 22.4 us -> 42.4 us
  other arithmetic: 31.4 us -> 24.5 us
  starting transfers between devices: 48.6 us -> 41.7 us
  Pallas kernels: 21.5 us -> 26.1 us
    all_gather x1, waiting for transfers between devices: 0.01 us -> 13.2 us  [shards(): weight_half = lax.all_gather(weight, 'z', axis=0, tiled=True)]
    ppermute x21 -> x20, waiting for transfers between devices: 9.65 us -> 19 us  [swap(): lax.ppermute(value, axis, [(i, i ^ mask) for i in range(SIZES[axis])])]
    ppermute x21 -> x20, starting transfers between devices: 35 us -> 28.8 us  [swap(): lax.ppermute(value, axis, [(i, i ^ mask) for i in range(SIZES[axis])])]
    broadcast_in_dim x0 -> x1, other arithmetic: none -> 4 us  [shards(): weight_grad[None]]
    convert_element_type x1 -> x0, other arithmetic: 3.93 us -> none  [shards(): weight_grad = ((own(0) + decode(even) + decode(odd)) * back).astype(BF16)]
    pallas_call x1, Pallas kernels: 7.53 us -> 11.2 us  [products_here(): pl.pallas_call(body, grid_spec=pltpu.PrefetchScalarGridSpec(num_scalar_pr...]
    ppermute x8 -> x6, starting transfers between devices: 13.6 us -> 10.5 us  [send(): return lax.ppermute(message, 'z', pairs)]
    ppermute x8 -> x6, waiting for transfers between devices: 12.1 us -> 9.47 us  [send(): return lax.ppermute(message, 'z', pairs)]
  transfers between devices with their start and end apart: 30 -> 29, of which waited for: 12 -> 13; matrix products, arithmetic and copies ran while one was open for 28% -> 21% of each run, Pallas kernels for 13% -> 15%
where the time goes in v4:
time: 174 us; the launch traced here: 171 us
  waiting for transfers between devices  42.4 us (24%)
  starting transfers between devices  41.7 us (24%)
  Pallas kernels  26.1 us (15%)
  other arithmetic  24.5 us (14%)
  between operations  16.5 us (9%)
  local copies, waits for them, and re-layouts  11.8 us (7%)
  matrix products  8.05 us (5%)
    ppermute x20, starting transfers between devices, swap(): lax.ppermute(value, axis, [(i, i ^ mask) for i in range(SIZES[axis])])  28.8 us
    ppermute x20, waiting for transfers between devices, swap(): lax.ppermute(value, axis, [(i, i ^ mask) for i in range(SIZES[axis])])  19 us
    all_gather x1, waiting for transfers between devices, shards(): weight_half = lax.all_gather(weight, 'z', axis=0, tiled=True)  13.2 us
    convert_element_type x6, other arithmetic, encode(): return (scaled * jnp.abs(scaled)).astype(F16)  12 us
    pallas_call x1, Pallas kernels, products_here(): pl.pallas_call(body, grid_spec=pltpu.PrefetchScalarGridSpec(num_scalar_pr...  11.2 us
    ppermute x6, starting transfers between devices, send(): return lax.ppermute(message, 'z', pairs)  10.5 us
    ppermute x6, waiting for transfers between devices, send(): return lax.ppermute(message, 'z', pairs)  9.47 us
    pallas_call x1, Pallas kernels, products_for_partner(): pl.pallas_call(body, grid_spec=pltpu.PrefetchScalarGridSpec(num_scalar_pr...  8.17 us
  transfers between devices with their start and end apart: 29, of which 13 were waited for; matrix products, arithmetic and copies ran while one was open for 21% of the time, Pallas kernels for 15%

profile of v4, /device:TPU:2, one launch (start us, length us, event | category | flops | bytes accessed | tf_op | source)
XLA Modules:
  0.0 171.0 jit_solution(16202517582695544145)
XLA Ops:
  7.9 1.0 constant_dynamic-slice_fusion
  9.7 2.3 %collective-permute-start.6 = (bf16[256,1024]{1,0:T(8,128)(2,1)}, bf16[256,1024]{1,0:T(8,128)(2,1)}, u32[]{:S(2)}, u32[]{:S(2)}) collective-permute-start(bf16[256,1024]{1,0:T(8,128)(2,1)} %bitcast.30), channel_id=1, source_target_pairs={{0,8},{8,0},{1,9},{9,1},{2,10},{10,2},{3,11},{11,3},{4,12},{12,4},... | collective-permute-start | bytes 1572872 | tf_op jit(solution)/shard_map/ppermute | solution.py:24
  12.0 2.0 %dynamic-slice_bitcast_fusion = f32[160,1024]{1,0:T(8,128)} fusion(f32[1,320,1024]{2,1,0:T(8,128)} %param.10, s32[]{:T(128)S(6)} %select_n.142), kind=kLoop, calls=%fused_computation.77 | loop fusion | bytes 1310724 | tf_op jit(solution)/shard_map/dynamic_slice | solution.py:40
  14.2 1.7 %abs_reduce_fusion.1 = bf16[]{:T(256)} fusion(bf16[1,256,1024]{2,1,0:T(8,128)(2,1)} %param.8), kind=kLoop, calls=%fused_computation.79 | loop fusion | flops 524287 | bytes 524290 | tf_op jit(solution)/shard_map/reduce_max | solution.py:69
  18.9 0.9 pad_maximum_fusion.3
  19.7 1.7 %collective-permute-start.10 = (bf16[256,1280]{1,0:T(8,128)(2,1)}, bf16[256,1280]{1,0:T(8,128)(2,1)S(1)}, u32[]{:S(2)}, u32[]{:S(2)}) collective-permute-start(bf16[256,1280]{1,0:T(8,128)(2,1)} %pad_maximum_fusion.3), channel_id=1, source_target_pairs={{0,8},{8,0},{1,9},{9,1},{2,10},{10,2},{3,11},{11,3},{4,12},{12,4},... | collective-permute-start | bytes 1966088 | tf_op jit(solution)/shard_map/ppermute | solution.py:24
  21.8 1.2 copy-done.4
  23.0 1.2 bitcast_add_fusion
  24.2 1.4 collective-permute-start.3
  25.6 2.3 %collective-permute-start.2 = (f32[160,256]{1,0:T(8,128)S(1)}, f32[160,256]{1,0:T(8,128)S(1)}, u32[]{:S(2)}, u32[]{:S(2)}) collective-permute-start(f32[160,256]{1,0:T(8,128)S(1)} %get-tuple-element.99), channel_id=1, source_target_pairs={{0,128},{64,192},{128,0},{192,64},{1,129},{65,193},{129,1},{193,65... | collective-permute-start | bytes 491528 | tf_op jit(solution)/shard_map/ppermute | solution.py:24
  28.2 1.9 %collective-permute-start.7 = (f32[8,128]{1,0:T(8,128)S(1)}, f32[8,128]{1,0:T(8,128)S(1)}, u32[]{:S(2)}, u32[]{:S(2)}) collective-permute-start(f32[8,128]{1,0:T(8,128)S(1)} %maximum_select_fusion.3), channel_id=1, source_target_pairs={{0,1},{1,0},{2,3},{3,2},{4,5},{5,4},{6,7},{7,6},{8,9},{9,8},{10,11... | collective-permute-start | bytes 12296 | tf_op jit(solution)/shard_map/ppermute | solution.py:24
  30.2 1.7 collective-permute-done.7
  33.2 1.7 collective-permute-done.3
  34.9 1.6 collective-permute-start.11
  37.3 2.2 %collective-permute-start.8 = (f32[160,128]{1,0:T(8,128)S(1)}, f32[160,128]{1,0:T(8,128)S(1)}, u32[]{:S(2)}, u32[]{:S(2)}) collective-permute-start(f32[160,128]{1,0:T(8,128)S(1)} %constant_dynamic-slice_fusion.1), channel_id=1, source_target_pairs={{0,32},{32,0},{1,33},{33,1},{2,34},{34,2},{3,35},{35,3},{4,36},{36... | collective-permute-start | bytes 245768 | tf_op jit(solution)/shard_map/ppermute | solution.py:24
  39.6 7.2 %collective-permute-start.12 = (f32[8,128]{1,0:T(8,128)S(1)}, f32[8,128]{1,0:T(8,128)S(1)}, u32[]{:S(2)}, u32[]{:S(2)}) collective-permute-start(f32[8,128]{1,0:T(8,128)S(1)} %maximum_select_fusion.1), channel_id=1, source_target_pairs={{0,4},{1,5},{2,6},{3,7},{4,0},{5,1},{6,2},{7,3},{8,12},{9,13},{10,... | collective-permute-start | bytes 12296 | tf_op jit(solution)/shard_map/ppermute | solution.py:24
  46.8 2.8 %fusion.26 = f32[1280,1024]{1,0:T(8,128)S(1)} fusion(bf16[256,1280]{1,0:T(8,128)(2,1)S(1)} %collective-permute-done.10.early_ref, bf16[256,640]{1,0:T(8,128)(2,1)S(1)} %get-tuple-element.93, bf16[256,640]{1,0:T(8,128)(2,1)S(1)} %get-tuple-element.92, bf16[256,1024]{1,0:T(8,128)(2,1)} %collective-permute-done.6.cotangent_ref, bf16[256,1024]{1,0:T(8,128)(2,1)S(1)} %bitcast.32), kind=kOutput, calls=%fused_computation.45 | convolution fusion | flops 1348206592 | bytes 7602176 | tf_op jit(solution)/shard_map/dot_general | solution.py:303
  52.0 1.1 collective-permute-start.14
  53.1 3.2 %collective-permute-start.15 = (f16[160,1024]{1,0:T(8,128)(2,1)S(1)}, f16[160,1024]{1,0:T(8,128)(2,1)S(1)}, u32[]{:S(2)}, u32[]{:S(2)}) collective-permute-start(f16[160,1024]{1,0:T(8,128)(2,1)S(1)} %get-tuple-element.89), channel_id=1, source_target_pairs={{0,7},{1,2},{2,1},{3,4},{4,3},{5,6},{6,5},{7,0},{8,15},{9,10},{10,... | collective-permute-start | bytes 983048 | tf_op jit(solution)/shard_map/ppermute | solution.py:327
  56.3 5.2 %fusion.32 = f32[1280,1024]{1,0:T(8,128)} fusion(bf16[256,1280]{1,0:T(8,128)(2,1)S(1)} %collective-permute-done.9.late_ref, bf16[256,640]{1,0:T(8,128)(2,1)S(1)} %get-tuple-element.91, bf16[256,640]{1,0:T(8,128)(2,1)S(1)} %get-tuple-element.90, bf16[256,1024]{1,0:T(8,128)(2,1)} %collective-permute-done.6.cotangent_ref, bf16[256,1024]{1,0:T(8,128)(2,1)S(1)} %bitcast.33), kind=kOutput, calls=%fused_computation.51 | convolution fusion | flops 1348206592 | bytes 7602176 | tf_op jit(solution)/shard_map/dot_general | solution.py:303
  63.2 5.2 %collective-permute-done.14 = f16[160,1024]{1,0:T(8,128)(2,1)S(1)} collective-permute-done((f16[160,1024]{1,0:T(8,128)(2,1)S(1)}, f16[160,1024]{1,0:T(8,128)(2,1)S(1)}, u32[]{:S(2)}, u32[]{:S(2)}) %collective-permute-start.14) | collective-permute-done | bytes 327712 | tf_op jit(solution)/shard_map/ppermute | solution.py:327
  68.4 2.1 %collective-permute-done.15 = f16[160,1024]{1,0:T(8,128)(2,1)S(1)} collective-permute-done((f16[160,1024]{1,0:T(8,128)(2,1)S(1)}, f16[160,1024]{1,0:T(8,128)(2,1)S(1)}, u32[]{:S(2)}, u32[]{:S(2)}) %collective-permute-start.15) | collective-permute-done | bytes 327712 | tf_op jit(solution)/shard_map/ppermute | solution.py:327
  71.8 3.0 %collective-permute-start.20 = (f16[320,1024]{1,0:T(8,128)(2,1)S(1)}, f16[320,1024]{1,0:T(8,128)(2,1)}, u32[]{:S(2)}, u32[]{:S(2)}) collective-permute-start(f16[320,1024]{1,0:T(8,128)(2,1)S(1)} %fusion.21), channel_id=1, source_target_pairs={{0,7},{1,2},{2,1},{3,4},{4,3},{5,6},{6,5},{7,0},{8,15},{9,10},{10,... | collective-permute-start | bytes 1966088 | tf_op jit(solution)/shard_map/ppermute | solution.py:327
  74.8 1.4 collective-permute-start.13
  76.2 4.1 %collective-permute-done.13.refs_1_ = bf16[160,128]{1,0:T(8,128)(2,1)S(1)} collective-permute-done((bf16[160,128]{1,0:T(8,128)(2,1)S(1)}, bf16[160,128]{1,0:T(8,128)(2,1)S(1)}, u32[]{:S(2)}, u32[]{:S(2)}) %collective-permute-start.13) | collective-permute-done | bytes 40992 | tf_op jit(solution)/shard_map/ppermute | solution.py:24
  80.9 1.4 shard_map.101.refs_0_
  82.3 13.2 %all-gather.3.cloned.1.call-done = bf16[1,2560,1024]{2,1,0:T(8,128)(2,1)} async-done(((bf16[1,320,1024]{2,1,0:T(8,128)(2,1)}), bf16[1,2560,1024]{2,1,0:T(8,128)(2,1)}) %all-gather.3.cloned.1.call-update) | async-done | bytes 5242896 | tf_op jit(solution)/shard_map/all_gather | solution.py:262
  95.5 8.2 %shard_map.102 = bf16[272,3584]{1,0:T(8,128)(2,1)} custom-call(s32[1]{0:T(128)} %bitcast.10.z_ref, bf16[256,1280]{1,0:T(8,128)(2,1)} %copy-done.6, bf16[256,1280]{1,0:T(8,128)(2,1)} %copy-done.7, bf16[256,1024]{1,0:T(8,128)(2,1)} %collective-permute-done.6.cotangent_ref, bf16[2560,1024]{1,0:T(8,128)(2,1)} %bitcast.28), custom_call_target="tpu_custom_call" | custom-call | tf_op jit(solution)/shard_map/pallas_call | solution.py:159
  103.7 3.3 %fusion.22 = f16[320,1024]{1,0:T(8,128)(2,1)} fusion(f16[320,1024]{1,0:T(8,128)(2,1)} %collective-permute-done.21, f32[1280,1024]{1,0:T(8,128)} %fusion.32, s32[]{:T(128)S(6)} %select_n.176, f32[]{:T(128)} %bitcast.9), kind=kLoop, calls=%fused_computation.41 | loop fusion | flops 2949120 | bytes 2621448 | tf_op jit(solution)/shard_map/convert_element_type | solution.py:55
  107.0 2.3 %collective-permute-start.25 = (f16[320,1024]{1,0:T(8,128)(2,1)}, f16[320,1024]{1,0:T(8,128)(2,1)S(1)}, u32[]{:S(2)}, u32[]{:S(2)}) collective-permute-start(f16[320,1024]{1,0:T(8,128)(2,1)} %fusion.22), channel_id=1, source_target_pairs={{0,7},{1,2},{2,1},{3,4},{4,3},{5,6},{6,5},{7,0},{8,15},{9,10},{10,... | collective-permute-start | bytes 1966088 | tf_op jit(solution)/shard_map/ppermute | solution.py:327
  109.3 3.3 %fusion.23 = f16[320,1024]{1,0:T(8,128)(2,1)} fusion(f16[320,1024]{1,0:T(8,128)(2,1)} %collective-permute-done.20, f32[1280,1024]{1,0:T(8,128)} %copy-done.2, s32[]{:T(128)S(6)} %select_n.176, f32[]{:T(128)} %bitcast.9), kind=kLoop, calls=%fused_computation.42 | loop fusion | flops 2949120 | bytes 2621448 | tf_op jit(solution)/shard_map/convert_element_type | solution.py:55
  112.6 0.9 collective-permute-start.24
  113.5 3.3 %collective-permute-start.19 = (bf16[160,256]{1,0:T(8,128)(2,1)S(1)}, bf16[160,256]{1,0:T(8,128)(2,1)S(1)}, u32[]{:S(2)}, u32[]{:S(2)}) collective-permute-start(bf16[160,256]{1,0:T(8,128)(2,1)S(1)} %copy-done.8), channel_id=1, source_target_pairs={{0,192},{64,128},{128,64},{192,0},{1,193},{65,129},{129,65},{193,1... | collective-permute-start | bytes 245768 | tf_op jit(solution)/shard_map/ppermute | solution.py:24
  117.6 2.1 %collective-permute-done.19.refs_3_ = bf16[160,256]{1,0:T(8,128)(2,1)S(1)} collective-permute-done((bf16[160,256]{1,0:T(8,128)(2,1)S(1)}, bf16[160,256]{1,0:T(8,128)(2,1)S(1)}, u32[]{:S(2)}, u32[]{:S(2)}) %collective-permute-start.19) | collective-permute-done | bytes 81952 | tf_op jit(solution)/shard_map/ppermute | solution.py:24
  120.0 2.8 %collective-permute-done.18.refs_2_ = bf16[160,256]{1,0:T(8,128)(2,1)S(1)} collective-permute-done((bf16[160,256]{1,0:T(8,128)(2,1)S(1)}, bf16[160,256]{1,0:T(8,128)(2,1)S(1)}, u32[]{:S(2)}, u32[]{:S(2)}) %collective-permute-start.18) | collective-permute-done | bytes 81952 | tf_op jit(solution)/shard_map/ppermute | solution.py:24
  122.7 1.4 collective-permute-done.17.refs_1_
  124.7 1.8 %shard_map.103.refs_0_ = bf16[160,1024]{1,0:T(8,128)(2,1)} custom-call(s32[1]{0:T(128)} %bitcast.12.here_ref, bf16[160,256]{1,0:T(8,128)(2,1)} %shard_map.101.refs_0_, bf16[160,256]{1,0:T(8,128)(2,1)} %copy-done.13, bf16[160,256]{1,0:T(8,128)(2,1)} %copy-done.12, bf16[160,256]{1,0:T(8,128)(2,1)} %copy-done.11), custom_call_target="tpu_custom_call" | custom-call | tf_op jit(solution)/shard_map/pallas_call | solution.py:106
  126.5 2.1 %collective-permute-done.24 = f16[320,1024]{1,0:T(8,128)(2,1)} collective-permute-done((f16[320,1024]{1,0:T(8,128)(2,1)}, f16[320,1024]{1,0:T(8,128)(2,1)}, u32[]{:S(2)}, u32[]{:S(2)}) %collective-permute-start.24) | collective-permute-done | bytes 655392 | tf_op jit(solution)/shard_map/ppermute | solution.py:327
  128.7 4.9 %fusion.25 = (f16[320,1024]{1,0:T(8,128)(2,1)}, f16[320,1024]{1,0:T(8,128)(2,1)}) fusion(f16[320,1024]{1,0:T(8,128)(2,1)} %collective-permute-done.24, f32[1280,1024]{1,0:T(8,128)} %fusion.32, s32[]{:T(128)S(6)} %select_n.171, f32[]{:T(128)} %bitcast.9, f16[320,1024]{1,0:T(8,128)(2,1)S(1)} %collective-permute-done.25, s32[]{:T(128)S(6)} %select_n.177), kind=kLoop, calls=%fused_computation.44 | loop fusion | flops 5898240 | bytes 5242892 | tf_op jit(solution)/shard_map/convert_element_type | solution.py:55
  133.5 2.3 %collective-permute-start.27 = (f16[320,1024]{1,0:T(8,128)(2,1)}, f16[320,1024]{1,0:T(8,128)(2,1)S(1)}, u32[]{:S(2)}, u32[]{:S(2)}) collective-permute-start(f16[320,1024]{1,0:T(8,128)(2,1)} %get-tuple-element.82), channel_id=1, source_target_pairs={{0,7},{1,2},{2,1},{3,4},{4,3},{5,6},{6,5},{7,0},{8,15},{9,10},{10,... | collective-permute-start | bytes 1966088 | tf_op jit(solution)/shard_map/ppermute | solution.py:381
  136.4 1.2 collective-permute-done.23.refs_1_
  138.2 1.6 shard_map.104
  139.8 1.7 copy.13
  142.2 2.0 %shard_map.105 = bf16[320,1024]{1,0:T(8,128)(2,1)} custom-call(s32[1]{0:T(128)} %bitcast.11.here_ref, bf16[160,1024]{1,0:T(8,128)(2,1)} %shard_map.103.refs_0_, bf16[160,1024]{1,0:T(8,128)(2,1)} %copy-done.9), custom_call_target="tpu_custom_call" | custom-call | tf_op jit(solution)/shard_map/pallas_call | solution.py:106
  144.2 3.5 %collective-permute-done.16.coded_ref.back_ref = bf16[272,3584]{1,0:T(8,128)(2,1)S(1)} collective-permute-done((bf16[272,3584]{1,0:T(8,128)(2,1)}, bf16[272,3584]{1,0:T(8,128)(2,1)S(1)}, u32[]{:S(2)}, u32[]{:S(2)}) %collective-permute-start.16) | collective-permute-done | bytes 1949728 | tf_op jit(solution)/shard_map/ppermute | solution.py:24
  147.7 1.3 copy-done.1
  149.0 11.2 %shard_map.106 = (bf16[256,1024]{1,0:T(8,128)(2,1)}, bf16[256,5120]{1,0:T(8,128)(2,1)}) custom-call(s32[1]{0:T(128)} %bitcast._, bf16[256,5120]{1,0:T(8,128)(2,1)} %bitcast.23, bf16[256,1024]{1,0:T(8,128)(2,1)} %bitcast.31, bf16[2560,1024]{1,0:T(8,128)(2,1)} %bitcast.29, bf16[272,3584]{1,0:T(8,128)(2,1)} %copy-done.1, bf16[272,3584]{1,0:T(8,128)(2,1)} %copy-done.1), custom_call_target="tpu_custom_call" | custom-call | tf_op jit(solution)/shard_map/pallas_call | solution.py:211
  160.2 4.0 %fusion.46 = bf16[1,320,1024]{2,1,0:T(8,128)(2,1)} fusion(f32[]{:T(128)} %bitcast.15, f16[320,1024]{1,0:T(8,128)(2,1)S(1)} %collective-permute-done.27, f16[320,1024]{1,0:T(8,128)(2,1)} %collective-permute-done.26, f32[]{:T(128)} %bitcast.9, f32[1280,1024]{1,0:T(8,128)} %fusion.32, s32[]{:T(128)S(6)} %select_n.173), kind=kLoop, calls=%fused_computation.78 | loop fusion | flops 4259840 | bytes 3276812 | tf_op jit(solution)/shard_map/broadcast_in_dim | solution.py:397
  (88 shorter events, 14.8 us)
Async XLA Ops:
  7.2 9.4 %copy-start = (bf16[1,256,5120]{2,1,0:T(8,128)(2,1)S(1)}, bf16[1,256,5120]{2,1,0:T(8,128)(2,1)}, u32[]{:S(2)}) copy-start(bf16[1,256,5120]{2,1,0:T(8,128)(2,1)} %param.6) | copy-start | bytes 7864324
  7.2 88.4 %all-gather.3.cloned.1.call-start = ((), (), s32[]{:S(2)}) async-start(), calls=%async_computation | async-start | bytes 5898240 | tf_op jit(solution)/shard_map/all_gather | solution.py:262
  9.7 22.9 %collective-permute-start.4 = (f32[160,64]{1,0:T(8,128)}, f32[160,64]{1,0:T(8,128)S(1)}, u32[]{:S(2)}, u32[]{:S(2)}) collective-permute-start(f32[160,64]{1,0:T(8,128)} %copy.14), channel_id=1, source_target_pairs={{0,16},{16,0},{1,17},{17,1},{2,18},{18,2},{3,19},{19,3},{4,20},{20... | collective-permute-start | bytes 122888 | tf_op jit(solution)/shard_map/ppermute | solution.py:24
  9.7 15.9 %collective-permute-start.6 = (bf16[256,1024]{1,0:T(8,128)(2,1)}, bf16[256,1024]{1,0:T(8,128)(2,1)}, u32[]{:S(2)}, u32[]{:S(2)}) collective-permute-start(bf16[256,1024]{1,0:T(8,128)(2,1)} %bitcast.30), channel_id=1, source_target_pairs={{0,8},{8,0},{1,9},{9,1},{2,10},{10,2},{3,11},{11,3},{4,12},{12,4},... | collective-permute-start | bytes 1572872 | tf_op jit(solution)/shard_map/ppermute | solution.py:24
  14.0 7.8 %collective-permute-start = (f32[160,1024]{1,0:T(8,128)}, f32[160,1024]{1,0:T(8,128)}, u32[]{:S(2)}, u32[]{:S(2)}) collective-permute-start(f32[160,1024]{1,0:T(8,128)} %dynamic-slice_bitcast_fusion), channel_id=1, source_target_pairs={{0,16},{16,0},{1,17},{17,1},{2,18},{18,2},{3,19},{19,3},{4,20},{20... | collective-permute-start | bytes 1966088 | tf_op jit(solution)/shard_map/ppermute | solution.py:24
  18.5 9.6 %collective-permute-start.5 = (f32[8,128]{1,0:T(8,128)S(1)}, f32[8,128]{1,0:T(8,128)S(1)}, u32[]{:S(2)}, u32[]{:S(2)}) collective-permute-start(f32[8,128]{1,0:T(8,128)S(1)} %iota.31), channel_id=1, source_target_pairs={{0,8},{8,0},{1,9},{9,1},{2,10},{10,2},{3,11},{11,3},{4,12},{12,4},... | collective-permute-start | bytes 12296 | tf_op jit(solution)/shard_map/ppermute | solution.py:24
  19.7 27.0 %collective-permute-start.10 = (bf16[256,1280]{1,0:T(8,128)(2,1)}, bf16[256,1280]{1,0:T(8,128)(2,1)S(1)}, u32[]{:S(2)}, u32[]{:S(2)}) collective-permute-start(bf16[256,1280]{1,0:T(8,128)(2,1)} %pad_maximum_fusion.3), channel_id=1, source_target_pairs={{0,8},{8,0},{1,9},{9,1},{2,10},{10,2},{3,11},{11,3},{4,12},{12,4},... | collective-permute-start | bytes 1966088 | tf_op jit(solution)/shard_map/ppermute | solution.py:24
  21.7 1.3 copy-start.4
  24.2 10.6 %collective-permute-start.3 = (f32[160,256]{1,0:T(8,128)S(1)}, f32[160,256]{1,0:T(8,128)S(1)}, u32[]{:S(2)}, u32[]{:S(2)}) collective-permute-start(f32[160,256]{1,0:T(8,128)S(1)} %get-tuple-element.98), channel_id=1, source_target_pairs={{0,192},{64,128},{128,64},{192,0},{1,193},{65,129},{129,65},{193,1... | collective-permute-start | bytes 491528 | tf_op jit(solution)/shard_map/ppermute | solution.py:24
  25.6 10.9 %collective-permute-start.2 = (f32[160,256]{1,0:T(8,128)S(1)}, f32[160,256]{1,0:T(8,128)S(1)}, u32[]{:S(2)}, u32[]{:S(2)}) collective-permute-start(f32[160,256]{1,0:T(8,128)S(1)} %get-tuple-element.99), channel_id=1, source_target_pairs={{0,128},{64,192},{128,0},{192,64},{1,129},{65,193},{129,1},{193,65... | collective-permute-start | bytes 491528 | tf_op jit(solution)/shard_map/ppermute | solution.py:24
  28.1 18.7 %copy-start.3 = (bf16[1,256,1024]{2,1,0:T(8,128)(2,1)S(1)}, bf16[1,256,1024]{2,1,0:T(8,128)(2,1)}, u32[]{:S(2)}) copy-start(bf16[1,256,1024]{2,1,0:T(8,128)(2,1)} %param.8) | copy-start | bytes 1572868
  28.2 3.7 %collective-permute-start.7 = (f32[8,128]{1,0:T(8,128)S(1)}, f32[8,128]{1,0:T(8,128)S(1)}, u32[]{:S(2)}, u32[]{:S(2)}) collective-permute-start(f32[8,128]{1,0:T(8,128)S(1)} %maximum_select_fusion.3), channel_id=1, source_target_pairs={{0,1},{1,0},{2,3},{3,2},{4,5},{5,4},{6,7},{7,6},{8,9},{9,8},{10,11... | collective-permute-start | bytes 12296 | tf_op jit(solution)/shard_map/ppermute | solution.py:24
  31.9 5.3 %collective-permute-start.1 = (f32[160,256]{1,0:T(8,128)S(1)}, f32[160,256]{1,0:T(8,128)S(1)}, u32[]{:S(2)}, u32[]{:S(2)}) collective-permute-start(f32[160,256]{1,0:T(8,128)S(1)} %get-tuple-element.100), channel_id=1, source_target_pairs={{0,64},{64,0},{128,192},{192,128},{1,65},{65,1},{129,193},{193,129... | collective-permute-start | bytes 491528 | tf_op jit(solution)/shard_map/ppermute | solution.py:24
  32.6 23.7 %collective-permute-start.9 = (bf16[256,1280]{1,0:T(8,128)(2,1)S(1)}, bf16[256,1280]{1,0:T(8,128)(2,1)S(1)}, u32[]{:S(2)}, u32[]{:S(2)}) collective-permute-start(bf16[256,1280]{1,0:T(8,128)(2,1)S(1)} %pad_maximum_fusion.4), channel_id=1, source_target_pairs={{0,8},{8,0},{1,9},{9,1},{2,10},{10,2},{3,11},{11,3},{4,12},{12,4},... | collective-permute-start | bytes 1966088 | tf_op jit(solution)/shard_map/ppermute | solution.py:24
  34.9 4.6 %collective-permute-start.11 = (f32[8,128]{1,0:T(8,128)S(1)}, f32[8,128]{1,0:T(8,128)S(1)}, u32[]{:S(2)}, u32[]{:S(2)}) collective-permute-start(f32[8,128]{1,0:T(8,128)S(1)} %maximum_select_fusion.2), channel_id=1, source_target_pairs={{0,2},{1,3},{2,0},{3,1},{4,6},{5,7},{6,4},{7,5},{8,10},{9,11},{10,... | collective-permute-start | bytes 12296 | tf_op jit(solution)/shard_map/ppermute | solution.py:24
  37.3 24.3 %collective-permute-start.8 = (f32[160,128]{1,0:T(8,128)S(1)}, f32[160,128]{1,0:T(8,128)S(1)}, u32[]{:S(2)}, u32[]{:S(2)}) collective-permute-start(f32[160,128]{1,0:T(8,128)S(1)} %constant_dynamic-slice_fusion.1), channel_id=1, source_target_pairs={{0,32},{32,0},{1,33},{33,1},{2,34},{34,2},{3,35},{35,3},{4,36},{36... | collective-permute-start | bytes 245768 | tf_op jit(solution)/shard_map/ppermute | solution.py:24
  39.6 10.1 %collective-permute-start.12 = (f32[8,128]{1,0:T(8,128)S(1)}, f32[8,128]{1,0:T(8,128)S(1)}, u32[]{:S(2)}, u32[]{:S(2)}) collective-permute-start(f32[8,128]{1,0:T(8,128)S(1)} %maximum_select_fusion.1), channel_id=1, source_target_pairs={{0,4},{1,5},{2,6},{3,7},{4,0},{5,1},{6,2},{7,3},{8,12},{9,13},{10,... | collective-permute-start | bytes 12296 | tf_op jit(solution)/shard_map/ppermute | solution.py:24
  46.8 2.9 %copy-start.6 = (bf16[256,1280]{1,0:T(8,128)(2,1)}, bf16[256,1280]{1,0:T(8,128)(2,1)S(1)}, u32[]{:S(2)}) copy-start(bf16[256,1280]{1,0:T(8,128)(2,1)S(1)} %collective-permute-done.10.early_ref) | copy-start | bytes 1966084
  49.6 20.9 %copy-start.2 = (f32[1280,1024]{1,0:T(8,128)}, f32[1280,1024]{1,0:T(8,128)S(1)}, u32[]{:S(2)}) copy-start(f32[1280,1024]{1,0:T(8,128)S(1)} %fusion.26) | copy-start | bytes 15728644
  52.0 16.3 %collective-permute-start.14 = (f16[160,1024]{1,0:T(8,128)(2,1)S(1)}, f16[160,1024]{1,0:T(8,128)(2,1)S(1)}, u32[]{:S(2)}, u32[]{:S(2)}) collective-permute-start(f16[160,1024]{1,0:T(8,128)(2,1)S(1)} %get-tuple-element.88), channel_id=1, source_target_pairs={{0,1},{1,0},{2,3},{3,2},{4,5},{5,4},{6,7},{7,6},{8,9},{9,8},{10,11... | collective-permute-start | bytes 983048 | tf_op jit(solution)/shard_map/ppermute | solution.py:327
  53.1 17.4 %collective-permute-start.15 = (f16[160,1024]{1,0:T(8,128)(2,1)S(1)}, f16[160,1024]{1,0:T(8,128)(2,1)S(1)}, u32[]{:S(2)}, u32[]{:S(2)}) collective-permute-start(f16[160,1024]{1,0:T(8,128)(2,1)S(1)} %get-tuple-element.89), channel_id=1, source_target_pairs={{0,7},{1,2},{2,1},{3,4},{4,3},{5,6},{6,5},{7,0},{8,15},{9,10},{10,... | collective-permute-start | bytes 983048 | tf_op jit(solution)/shard_map/ppermute | solution.py:327
  56.3 5.2 %copy-start.7 = (bf16[256,1280]{1,0:T(8,128)(2,1)}, bf16[256,1280]{1,0:T(8,128)(2,1)S(1)}, u32[]{:S(2)}) copy-start(bf16[256,1280]{1,0:T(8,128)(2,1)S(1)} %collective-permute-done.9.late_ref) | copy-start | bytes 1966084
  62.4 12.4 %copy-start.10 = (bf16[160,128]{1,0:T(8,128)(2,1)}, bf16[160,128]{1,0:T(8,128)(2,1)S(1)}, u32[]{:S(2)}) copy-start(bf16[160,128]{1,0:T(8,128)(2,1)S(1)} %get-tuple-element.80.refs_0_) | copy-start | bytes 122884
  71.5 32.2 %collective-permute-start.21 = (f16[320,1024]{1,0:T(8,128)(2,1)S(1)}, f16[320,1024]{1,0:T(8,128)(2,1)}, u32[]{:S(2)}, u32[]{:S(2)}) collective-permute-start(f16[320,1024]{1,0:T(8,128)(2,1)S(1)} %fusion.20), channel_id=1, source_target_pairs={{0,1},{1,0},{2,3},{3,2},{4,5},{5,4},{6,7},{7,6},{8,9},{9,8},{10,11... | collective-permute-start | bytes 1966088 | tf_op jit(solution)/shard_map/ppermute | solution.py:327
  71.8 37.5 %collective-permute-start.20 = (f16[320,1024]{1,0:T(8,128)(2,1)S(1)}, f16[320,1024]{1,0:T(8,128)(2,1)}, u32[]{:S(2)}, u32[]{:S(2)}) collective-permute-start(f16[320,1024]{1,0:T(8,128)(2,1)S(1)} %fusion.21), channel_id=1, source_target_pairs={{0,7},{1,2},{2,1},{3,4},{4,3},{5,6},{6,5},{7,0},{8,15},{9,10},{10,... | collective-permute-start | bytes 1966088 | tf_op jit(solution)/shard_map/ppermute | solution.py:327
  74.8 5.5 %collective-permute-start.13 = (bf16[160,128]{1,0:T(8,128)(2,1)S(1)}, bf16[160,128]{1,0:T(8,128)(2,1)S(1)}, u32[]{:S(2)}, u32[]{:S(2)}) collective-permute-start(bf16[160,128]{1,0:T(8,128)(2,1)S(1)} %get-tuple-element.80.refs_0_), channel_id=1, source_target_pairs={{0,32},{32,0},{1,33},{33,1},{2,34},{34,2},{3,35},{35,3},{4,36},{36... | collective-permute-start | bytes 122888 | tf_op jit(solution)/shard_map/ppermute | solution.py:24
  80.3 0.6 copy-start.15
  103.7 43.9 %collective-permute-start.16 = (bf16[272,3584]{1,0:T(8,128)(2,1)}, bf16[272,3584]{1,0:T(8,128)(2,1)S(1)}, u32[]{:S(2)}, u32[]{:S(2)}) collective-permute-start(bf16[272,3584]{1,0:T(8,128)(2,1)} %shard_map.102), channel_id=1, source_target_pairs={{0,8},{8,0},{1,9},{9,1},{2,10},{10,2},{3,11},{11,3},{4,12},{12,4},... | collective-permute-start | bytes 5849096 | tf_op jit(solution)/shard_map/ppermute | solution.py:24
  107.0 6.5 %copy-start.8 = (bf16[160,256]{1,0:T(8,128)(2,1)S(1)}, bf16[160,256]{1,0:T(8,128)(2,1)}, u32[]{:S(2)}) copy-start(bf16[160,256]{1,0:T(8,128)(2,1)} %shard_map.101.refs_0_) | copy-start | bytes 245764
  107.0 19.5 %collective-permute-start.25 = (f16[320,1024]{1,0:T(8,128)(2,1)}, f16[320,1024]{1,0:T(8,128)(2,1)S(1)}, u32[]{:S(2)}, u32[]{:S(2)}) collective-permute-start(f16[320,1024]{1,0:T(8,128)(2,1)} %fusion.22), channel_id=1, source_target_pairs={{0,7},{1,2},{2,1},{3,4},{4,3},{5,6},{6,5},{7,0},{8,15},{9,10},{10,... | collective-permute-start | bytes 1966088 | tf_op jit(solution)/shard_map/ppermute | solution.py:327
  112.6 16.0 %collective-permute-start.24 = (f16[320,1024]{1,0:T(8,128)(2,1)}, f16[320,1024]{1,0:T(8,128)(2,1)}, u32[]{:S(2)}, u32[]{:S(2)}) collective-permute-start(f16[320,1024]{1,0:T(8,128)(2,1)} %fusion.23), channel_id=1, source_target_pairs={{0,1},{1,0},{2,3},{3,2},{4,5},{5,4},{6,7},{7,6},{8,9},{9,8},{10,11... | collective-permute-start | bytes 1966088 | tf_op jit(solution)/shard_map/ppermute | solution.py:327
  113.5 6.1 %collective-permute-start.19 = (bf16[160,256]{1,0:T(8,128)(2,1)S(1)}, bf16[160,256]{1,0:T(8,128)(2,1)S(1)}, u32[]{:S(2)}, u32[]{:S(2)}) collective-permute-start(bf16[160,256]{1,0:T(8,128)(2,1)S(1)} %copy-done.8), channel_id=1, source_target_pairs={{0,192},{64,128},{128,64},{192,0},{1,193},{65,129},{129,65},{193,1... | collective-permute-start | bytes 245768 | tf_op jit(solution)/shard_map/ppermute | solution.py:24
  116.8 5.9 %collective-permute-start.18 = (bf16[160,256]{1,0:T(8,128)(2,1)S(1)}, bf16[160,256]{1,0:T(8,128)(2,1)S(1)}, u32[]{:S(2)}, u32[]{:S(2)}) collective-permute-start(bf16[160,256]{1,0:T(8,128)(2,1)S(1)} %copy-done.8), channel_id=1, source_target_pairs={{0,128},{64,192},{128,0},{192,64},{1,129},{65,193},{129,1},{193,65... | collective-permute-start | bytes 245768 | tf_op jit(solution)/shard_map/ppermute | solution.py:24
  119.7 4.4 %copy-start.11 = (bf16[160,256]{1,0:T(8,128)(2,1)}, bf16[160,256]{1,0:T(8,128)(2,1)S(1)}, u32[]{:S(2)}) copy-start(bf16[160,256]{1,0:T(8,128)(2,1)S(1)} %collective-permute-done.19.refs_3_) | copy-start | bytes 245764
  119.7 4.4 %collective-permute-start.17 = (bf16[160,256]{1,0:T(8,128)(2,1)S(1)}, bf16[160,256]{1,0:T(8,128)(2,1)S(1)}, u32[]{:S(2)}, u32[]{:S(2)}) collective-permute-start(bf16[160,256]{1,0:T(8,128)(2,1)S(1)} %copy-done.8), channel_id=1, source_target_pairs={{0,64},{64,0},{128,192},{192,128},{1,65},{65,1},{129,193},{193,129... | collective-permute-start | bytes 245768 | tf_op jit(solution)/shard_map/ppermute | solution.py:24
  122.7 1.4 copy-start.12
  124.1 0.6 copy-start.13
  126.5 9.3 %copy-start.5 = (bf16[160,1024]{1,0:T(8,128)(2,1)S(1)}, bf16[160,1024]{1,0:T(8,128)(2,1)}, u32[]{:S(2)}) copy-start(bf16[160,1024]{1,0:T(8,128)(2,1)} %shard_map.103.refs_0_) | copy-start | bytes 983044
  133.5 26.6 %collective-permute-start.27 = (f16[320,1024]{1,0:T(8,128)(2,1)}, f16[320,1024]{1,0:T(8,128)(2,1)S(1)}, u32[]{:S(2)}, u32[]{:S(2)}) collective-permute-start(f16[320,1024]{1,0:T(8,128)(2,1)} %get-tuple-element.82), channel_id=1, source_target_pairs={{0,7},{1,2},{2,1},{3,4},{4,3},{5,6},{6,5},{7,0},{8,15},{9,10},{10,... | collective-permute-start | bytes 1966088 | tf_op jit(solution)/shard_map/ppermute | solution.py:381
  135.8 24.3 %collective-permute-start.26 = (f16[320,1024]{1,0:T(8,128)(2,1)}, f16[320,1024]{1,0:T(8,128)(2,1)}, u32[]{:S(2)}, u32[]{:S(2)}) collective-permute-start(f16[320,1024]{1,0:T(8,128)(2,1)} %get-tuple-element.83), channel_id=1, source_target_pairs={{0,1},{1,0},{2,3},{3,2},{4,5},{5,4},{6,7},{7,6},{8,9},{9,8},{10,11... | collective-permute-start | bytes 1966088 | tf_op jit(solution)/shard_map/ppermute | solution.py:381
  135.8 5.7 %collective-permute-start.22 = (bf16[160,1024]{1,0:T(8,128)(2,1)S(1)}, bf16[160,1024]{1,0:T(8,128)(2,1)S(1)}, u32[]{:S(2)}, u32[]{:S(2)}) collective-permute-start(bf16[160,1024]{1,0:T(8,128)(2,1)S(1)} %copy-done.5), channel_id=1, source_target_pairs={{0,16},{16,0},{1,17},{17,1},{2,18},{18,2},{3,19},{19,3},{4,20},{20... | collective-permute-start | bytes 983048 | tf_op jit(solution)/shard_map/ppermute | solution.py:24
  135.8 1.7 %collective-permute-start.23 = (f32[160,64]{1,0:T(8,128)S(1)}, f32[160,64]{1,0:T(8,128)S(1)}, u32[]{:S(2)}, u32[]{:S(2)}) collective-permute-start(f32[160,64]{1,0:T(8,128)S(1)} %get-tuple-element.105), channel_id=1, source_target_pairs={{0,16},{16,0},{1,17},{17,1},{2,18},{18,2},{3,19},{19,3},{4,20},{20... | collective-permute-start | bytes 122888 | tf_op jit(solution)/shard_map/ppermute | solution.py:24
  137.6 0.6 copy-start.14
  141.5 0.7 copy-start.9
  147.7 1.3 copy-start.1
Sparse Core Ops, SparseCore 0:
  9.8 85.7 all-gather.2

commit v5 on v4

--- a/solution.py
+++ b/solution.py
@@ -175,65 +175,78 @@
     )(z.reshape(1), early, late, cotangent, weight)
 
 
-def products_here(x, tokens, cotangent, weight, back):
+def products_here(x, tokens, cotangent, weight):
+    count = 4
+    rows = cotangent.shape[0]
+    wide = weight.shape[0] // count
+
+    def body(_, tokens_ref, cotangent_ref, weight_ref, keys_ref, grads_ref):
+        @pl.when(pl.program_id(0) == 0)
+        def _():
+            keys_ref[...] = jnp.zeros_like(keys_ref)
+
+        keys_ref[...] += dot(tokens_ref[...], weight_ref[...])
+        grads_ref[...] = dot_t(cotangent_ref[...], weight_ref[...]).astype(BF16)
+
+    here = pl.BlockSpec((rows, wide), lambda i, x: (0, x[0] * count + i))
+    return pl.pallas_call(
+        body,
+        grid_spec=pltpu.PrefetchScalarGridSpec(
+            num_scalar_prefetch=1,
+            grid=(count,),
+            in_specs=[
+                here,
+                whole(cotangent),
+                pl.BlockSpec((wide, weight.shape[1]), lambda i, x: (i, 0)),
+            ],
+            out_specs=[whole(cotangent), here],
+        ),
+        out_shape=[
+            jax.ShapeDtypeStruct(cotangent.shape, F32),
+            jax.ShapeDtypeStruct(tokens.shape, BF16),
+        ],
+        cost_estimate=FREE,
+    )(x.reshape(1), tokens, cotangent, weight)
+
+
+def finish(x, keys, grads, back):
     count = 5
-    rows, features = cotangent.shape
-    wide = weight.shape[0] // count
-
-    def body(
-        _, tokens_ref, cotangent_ref, weight_ref, coded_ref, back_ref, keys_ref, grads_ref, sum_ref
-    ):
-        i = pl.program_id(0)
-
-        @pl.when(i == 0)
+    rows, features = keys.shape
+    wide = grads.shape[1] // (2 * count)
+
+    def body(_, __, keys_ref, coded_ref, back_ref, out_ref, grads_ref):
+        @pl.when(pl.program_id(0) == 0)
         def _():
             power = coded_ref[:rows, :].astype(F32)
             size = jnp.exp2(jnp.log2(jnp.abs(power)) * (1.0 / 16.0))
             size = jnp.where(power == 0, 0.0, size) * (coded_ref[rows:, :].astype(F32)[:1] / TOP)
-            sum_ref[...] = jnp.where(power < 0, -size, size)
-
-        @pl.when(i < count)
-        def _():
-            sum_ref[...] += dot(tokens_ref[...], weight_ref[...])
-            grads_ref[...] = dot_t(cotangent_ref[...], weight_ref[...]).astype(BF16)
-
-        @pl.when(i >= count)
-        def _():
-            grads_ref[...] = back_ref[...]
-
-        @pl.when(i == count - 1)
-        def _():
-            keys_ref[...] = sum_ref[...].astype(BF16)
-
-    def block(i):
-        return jnp.minimum(i, count - 1)
+            out_ref[...] = (keys_ref[...] + jnp.where(power < 0, -size, size)).astype(BF16)
+
+        grads_ref[...] = back_ref[...]
 
     return pl.pallas_call(
         body,
         grid_spec=pltpu.PrefetchScalarGridSpec(
             num_scalar_prefetch=1,
-            grid=(2 * count,),
+            grid=(count,),
             in_specs=[
-                pl.BlockSpec((rows, wide), lambda i, x: (0, x[0] * count + block(i))),
-                whole(cotangent),
-                pl.BlockSpec((wide, features), lambda i, x: (block(i), 0)),
+                pl.BlockSpec(memory_space=pl.ANY),
+                whole(keys),
                 pl.BlockSpec((rows + 16, features), lambda i, x: (0, 0)),
-                pl.BlockSpec(
-                    (rows, wide), lambda i, x: (0, features // wide + jnp.maximum(i - count, 0))
-                ),
+                pl.BlockSpec((rows, wide), lambda i, x: (0, features // wide + i)),
             ],
             out_specs=[
-                whole(cotangent),
-                pl.BlockSpec((rows, wide), lambda i, x: (0, (x[0] * count + i) % (2 * count))),
+                whole(keys),
+                pl.BlockSpec((rows, wide), lambda i, x: (0, (1 - x[0]) * count + i)),
             ],
-            scratch_shapes=[pltpu.VMEM(cotangent.shape, F32)],
         ),
         out_shape=[
-            jax.ShapeDtypeStruct(cotangent.shape, BF16),
-            jax.ShapeDtypeStruct(tokens.shape, BF16),
+            jax.ShapeDtypeStruct(keys.shape, BF16),
+            jax.ShapeDtypeStruct(grads.shape, BF16),
         ],
+        input_output_aliases={1: 1},
         cost_estimate=FREE,
-    )(x.reshape(1), tokens, cotangent, weight, back, back)
+    )(x.reshape(1), grads, keys, back, back)
 
 
 def shards(activations, key_weights, key_cotangent, fragment, pseudo_grads, momentum):
@@ -352,16 +365,21 @@
     updated_other = swap(updated, "xh")
     new_other = swap(give, "c")
 
+    updated_other = order.step(updated_other)
+    wide = assemble(xh, lambda i: (i, 1 - i), (updated, updated_other), 1)
+    order.did(wide)
+    wides = [swap(wide, "y", m) for m in (1, 2, 3)]
+
     far_even, far_odd = order.step(far_even, far_odd)
     odd = jnp.concatenate([own(-3, 0, part) + decode(far_even), own(-3, part, part)])
     odd = send(odd, ODD)
     even = jnp.concatenate([own(3, 0, part), own(3, part, part) + decode(far_odd)])
     even = send(even, EVEN)
 
-    updated_other = order.step(updated_other)
-    wide = assemble(xh, lambda i: (i, 1 - i), (updated, updated_other), 1)
-    order.did(wide)
-    wides = [swap(wide, "y", m) for m in (1, 2, 3)]
+    wides = order.step(*wides)
+    block = assemble(y, lambda i: (i, i ^ 1, i ^ 2, i ^ 3), (wide, *wides), 1)
+    order.did(block)
+    block_other = swap(block, "c")
 
     weight_half = order.step(weight_half)
     sent = products_for_partner(z, early_other, late_other, cotangent_other, weight_half)
@@ -370,23 +388,20 @@
 
     even, odd = ring_step(2, even, odd)
 
-    wides = order.step(*wides)
-    block = assemble(y, lambda i: (i, i ^ 1, i ^ 2, i ^ 3), (wide, *wides), 1)
-    order.did(block)
-    block_other = swap(block, "c")
+    keys_mine, grads_mine = products_here(order.step(x), tokens, cotangent, weight_half)
+    order.did(keys_mine, grads_mine)
+    new_momentum = assemble(c, lambda i: (i, 1 - i), (keep, order.step(new_other)), 0)
+    order.did(new_momentum)
+    new_fragment = assemble(c, lambda i: (i, 1 - i), (block, order.step(block_other)), 0)
+    order.did(new_fragment)
 
     even, odd = order.step(even, odd)
     even, odd = encode(own(1) + decode(odd)), encode(own(-1) + decode(even))
     order.did(even, odd)
     even, odd = lax.ppermute(even, "z", EVEN), lax.ppermute(odd, "z", ODD)
 
-    new_momentum = assemble(c, lambda i: (i, 1 - i), (keep, order.step(new_other)), 0)
-    order.did(new_momentum)
-    new_fragment = assemble(c, lambda i: (i, 1 - i), (block, order.step(block_other)), 0)
-    order.did(new_fragment)
-    key_out, act_grad = products_here(
-        x, tokens, cotangent, weight_half, order.step(products_back)
-    )
+    products_back = order.step(products_back)
+    key_out, act_grad = finish(x, keys_mine, grads_mine, products_back)
     order.did(key_out, act_grad)
     even, odd = order.step(even, odd)
     weight_grad = ((own(0) + decode(even) + decode(odd)) * back).astype(BF16)

time: 174 us -> 176 us (1.011)
  other arithmetic: 24.5 us -> 28.6 us
  local copies, waits for them, and re-layouts: 11.8 us -> 9.27 us
    ppermute x20, waiting for transfers between devices: 19 us -> 38.6 us  [swap(): lax.ppermute(value, axis, [(i, i ^ mask) for i in range(SIZES[axis])])]
    all_gather x1, waiting for transfers between devices: 13.2 us -> 0.01 us  [shards(): weight_half = lax.all_gather(weight, 'z', axis=0, tiled=True)]
    ppermute x6, waiting for transfers between devices: 9.47 us -> 0.02 us  [send(): return lax.ppermute(message, 'z', pairs)]
    pallas_call x0 -> x1, Pallas kernels: none -> 5.1 us  [finish(): pl.pallas_call(body, grid_spec=pltpu.PrefetchScalarGridSpec(num_scalar_pr...]
    pallas_call x1, Pallas kernels: 11.2 us -> 7.05 us  [products_here(): pl.pallas_call(body, grid_spec=pltpu.PrefetchScalarGridSpec(num_scalar_pr...]
    ppermute x2, waiting for transfers between devices: 0.01 us -> 3.51 us  [shards(): even, odd = (lax.ppermute(even, 'z', EVEN), lax.ppermute(odd, 'z', ODD))]
    ppermute x6, starting transfers between devices: 10.5 us -> 7.56 us  [send(): return lax.ppermute(message, 'z', pairs)]
    ppermute x20, starting transfers between devices: 28.8 us -> 31.7 us  [swap(): lax.ppermute(value, axis, [(i, i ^ mask) for i in range(SIZES[axis])])]
  transfers between devices with their start and end apart: 29 -> 29, of which waited for: 13 -> 9; matrix products, arithmetic and copies ran while one was open for 21% -> 21% of each run, Pallas kernels for 15% -> 16%
where the time goes in v5:
time: 176 us; the launch traced here: 175 us
  waiting for transfers between devices  42.9 us (24%)
  starting transfers between devices  42.3 us (24%)
  other arithmetic  28.6 us (16%)
  Pallas kernels  27.1 us (15%)
  between operations  16.6 us (9%)
  local copies, waits for them, and re-layouts  9.27 us (5%)
  matrix products  8 us (5%)
    ppermute x20, waiting for transfers between devices, swap(): lax.ppermute(value, axis, [(i, i ^ mask) for i in range(SIZES[axis])])  38.6 us
    ppermute x20, starting transfers between devices, swap(): lax.ppermute(value, axis, [(i, i ^ mask) for i in range(SIZES[axis])])  31.7 us
    convert_element_type x6, other arithmetic, encode(): return (scaled * jnp.abs(scaled)).astype(F16)  13.6 us
    pallas_call x1, Pallas kernels, products_for_partner(): pl.pallas_call(body, grid_spec=pltpu.PrefetchScalarGridSpec(num_scalar_pr...  8.2 us
    dot_general x2, matrix products, product(): lax.dot_general(jnp.concatenate([first, second], axis=0), jnp.concatenate...  8 us
    ppermute x6, starting transfers between devices, send(): return lax.ppermute(message, 'z', pairs)  7.56 us
    pallas_call x1, Pallas kernels, products_here(): pl.pallas_call(body, grid_spec=pltpu.PrefetchScalarGridSpec(num_scalar_pr...  7.05 us
    pallas_call x4, Pallas kernels, assemble(): pl.pallas_call(body, grid_spec=pltpu.PrefetchScalarGridSpec(num_scalar_pr...  6.77 us
  transfers between devices with their start and end apart: 29, of which 9 were waited for; matrix products, arithmetic and copies ran while one was open for 21% of the time, Pallas kernels for 16%

profile of v5, /device:TPU:2, one launch (start us, length us, event | category | flops | bytes accessed | tf_op | source)
XLA Modules:
  0.0 174.7 jit_solution(10313257169031109265)
XLA Ops:
  7.9 2.0 %dynamic-slice_bitcast_fusion = f32[160,1024]{1,0:T(8,128)} fusion(f32[1,320,1024]{2,1,0:T(8,128)} %param.10, s32[]{:T(128)S(6)} %select_n.140), kind=kLoop, calls=%fused_computation.77 | loop fusion | bytes 1310724 | tf_op jit(solution)/shard_map/dynamic_slice | solution.py:40
  11.3 2.4 %abs_reduce_fusion = f32[5120]{0:T(1024)S(1)} fusion(bf16[256,5120]{1,0:T(8,128)(2,1)} %bitcast.24), kind=kLoop, calls=%fused_computation | loop fusion | flops 3927040 | bytes 2641920 | tf_op jit(solution)/shard_map/reduce_sum | solution.py:68
  15.0 2.3 %collective-permute-start = (f32[8,128]{1,0:T(8,128)S(1)}, f32[8,128]{1,0:T(8,128)S(1)}, u32[]{:S(2)}, u32[]{:S(2)}) collective-permute-start(f32[8,128]{1,0:T(8,128)S(1)} %iota.32), channel_id=1, source_target_pairs={{0,8},{8,0},{1,9},{9,1},{2,10},{10,2},{3,11},{11,3},{4,12},{12,4},... | collective-permute-start | bytes 12296 | tf_op jit(solution)/shard_map/ppermute | solution.py:24
  18.4 1.9 %collective-permute-start.1 = (bf16[256,1024]{1,0:T(8,128)(2,1)S(1)}, bf16[256,1024]{1,0:T(8,128)(2,1)}, u32[]{:S(2)}, u32[]{:S(2)}) collective-permute-start(bf16[256,1024]{1,0:T(8,128)(2,1)S(1)} %bitcast.33), channel_id=1, source_target_pairs={{0,8},{8,0},{1,9},{9,1},{2,10},{10,2},{3,11},{11,3},{4,12},{12,4},... | collective-permute-start | bytes 1572872 | tf_op jit(solution)/shard_map/ppermute | solution.py:24
  21.1 1.2 copy-done.4
  22.3 1.2 bitcast_add_fusion
  23.6 23.1 %collective-permute-done.1.cotangent_ref = bf16[256,1024]{1,0:T(8,128)(2,1)} collective-permute-done((bf16[256,1024]{1,0:T(8,128)(2,1)S(1)}, bf16[256,1024]{1,0:T(8,128)(2,1)}, u32[]{:S(2)}, u32[]{:S(2)}) %collective-permute-start.1) | collective-permute-done | bytes 524320 | tf_op jit(solution)/shard_map/ppermute | solution.py:24
  46.7 1.5 collective-permute-start.7
  48.4 1.9 %collective-permute-start.4 = (f32[8,128]{1,0:T(8,128)S(1)}, f32[8,128]{1,0:T(8,128)S(1)}, u32[]{:S(2)}, u32[]{:S(2)}) collective-permute-start(f32[8,128]{1,0:T(8,128)S(1)} %maximum_select_fusion.3), channel_id=1, source_target_pairs={{0,1},{1,0},{2,3},{3,2},{4,5},{5,4},{6,7},{7,6},{8,9},{9,8},{10,11... | collective-permute-start | bytes 12296 | tf_op jit(solution)/shard_map/ppermute | solution.py:24
  50.5 1.7 collective-permute-done.4
  52.1 1.1 collective-permute-start.8
  53.2 1.5 collective-permute-start.14
  54.8 3.3 %collective-permute-start.5 = (f32[8,128]{1,0:T(8,128)S(1)}, f32[8,128]{1,0:T(8,128)S(1)}, u32[]{:S(2)}, u32[]{:S(2)}) collective-permute-start(f32[8,128]{1,0:T(8,128)S(1)} %maximum_select_fusion.2), channel_id=1, source_target_pairs={{0,2},{1,3},{2,0},{3,1},{4,6},{5,7},{6,4},{7,5},{8,10},{9,11},{10,... | collective-permute-start | bytes 12296 | tf_op jit(solution)/shard_map/ppermute | solution.py:24
  58.7 2.5 %collective-permute-start.13 = (f32[160,128]{1,0:T(8,128)S(1)}, f32[160,128]{1,0:T(8,128)S(1)}, u32[]{:S(2)}, u32[]{:S(2)}) collective-permute-start(f32[160,128]{1,0:T(8,128)S(1)} %constant_dynamic-slice_fusion.1), channel_id=1, source_target_pairs={{0,32},{32,0},{1,33},{33,1},{2,34},{34,2},{3,35},{35,3},{4,36},{36... | collective-permute-start | bytes 245768 | tf_op jit(solution)/shard_map/ppermute | solution.py:24
  61.3 7.2 %collective-permute-start.10 = (f32[8,128]{1,0:T(8,128)S(1)}, f32[8,128]{1,0:T(8,128)S(1)}, u32[]{:S(2)}, u32[]{:S(2)}) collective-permute-start(f32[8,128]{1,0:T(8,128)S(1)} %maximum_select_fusion.1), channel_id=1, source_target_pairs={{0,4},{1,5},{2,6},{3,7},{4,0},{5,1},{6,2},{7,3},{8,12},{9,13},{10,... | collective-permute-start | bytes 12296 | tf_op jit(solution)/shard_map/ppermute | solution.py:24
  68.5 2.8 %fusion.26 = f32[1280,1024]{1,0:T(8,128)S(1)} fusion(bf16[256,1280]{1,0:T(8,128)(2,1)} %collective-permute-done.3.early_ref, bf16[256,640]{1,0:T(8,128)(2,1)S(1)} %get-tuple-element.99, bf16[256,640]{1,0:T(8,128)(2,1)S(1)} %get-tuple-element.98, bf16[256,1024]{1,0:T(8,128)(2,1)} %collective-permute-done.1.cotangent_ref, bf16[256,1024]{1,0:T(8,128)(2,1)S(1)} %bitcast.34), kind=kOutput, calls=%fused_computation.45 | convolution fusion | flops 1348206592 | bytes 7602176 | tf_op jit(solution)/shard_map/dot_general | solution.py:316
  73.7 1.1 collective-permute-start.11
  74.8 3.2 %collective-permute-start.12 = (f16[160,1024]{1,0:T(8,128)(2,1)S(1)}, f16[160,1024]{1,0:T(8,128)(2,1)S(1)}, u32[]{:S(2)}, u32[]{:S(2)}) collective-permute-start(f16[160,1024]{1,0:T(8,128)(2,1)S(1)} %get-tuple-element.94), channel_id=1, source_target_pairs={{0,7},{1,2},{2,1},{3,4},{4,3},{5,6},{6,5},{7,0},{8,15},{9,10},{10,... | collective-permute-start | bytes 983048 | tf_op jit(solution)/shard_map/ppermute | solution.py:340
  78.0 5.2 %fusion.32 = f32[1280,1024]{1,0:T(8,128)} fusion(bf16[256,1280]{1,0:T(8,128)(2,1)S(1)} %collective-permute-done.14.late_ref, bf16[256,640]{1,0:T(8,128)(2,1)S(1)} %get-tuple-element.97, bf16[256,640]{1,0:T(8,128)(2,1)S(1)} %get-tuple-element.96, bf16[256,1024]{1,0:T(8,128)(2,1)} %collective-permute-done.1.cotangent_ref, bf16[256,1024]{1,0:T(8,128)(2,1)S(1)} %bitcast.35), kind=kOutput, calls=%fused_computation.51 | convolution fusion | flops 1348206592 | bytes 7602176 | tf_op jit(solution)/shard_map/dot_general | solution.py:316
  83.2 0.9 subtract_convert_fusion
  84.2 1.2 collective-permute-start.15
  86.1 3.7 %collective-permute-done.15.refs_1_ = bf16[160,128]{1,0:T(8,128)(2,1)S(1)} collective-permute-done((bf16[160,128]{1,0:T(8,128)(2,1)S(1)}, bf16[160,128]{1,0:T(8,128)(2,1)S(1)}, u32[]{:S(2)}, u32[]{:S(2)}) %collective-permute-start.15) | collective-permute-done | bytes 40992 | tf_op jit(solution)/shard_map/ppermute | solution.py:24
  90.4 1.4 shard_map.101.refs_0_
  91.8 2.5 %dynamic-slice_multiply_fusion = (f32[160,1024]{1,0:T(8,128)S(1)}, f32[160,1024]{1,0:T(8,128)S(1)}, f32[160,1024]{1,0:T(8,128)S(1)}, f32[160,1024]{1,0:T(8,128)S(1)}) fusion(f32[1280,1024]{1,0:T(8,128)} %copy-done.2, s32[]{:T(128)S(6)} %select_n.177, f32[]{:T(128)} %bitcast.5, f16[160,1024]{1,0:T(8,128)(2,1)S(1)} %collective-permute-done.12, ...), kind=kLoop, calls=%fused_computation.75 | loop fusion | flops 2293760 | bytes 5898260 | tf_op jit(solution)/shard_map/mul | solution.py:334
  94.4 1.0 fusion.21
  95.4 1.0 fusion.20
  96.4 2.0 %collective-permute-start.16 = (f16[320,1024]{1,0:T(8,128)(2,1)}, f16[320,1024]{1,0:T(8,128)(2,1)}, u32[]{:S(2)}, u32[]{:S(2)}) collective-permute-start(f16[320,1024]{1,0:T(8,128)(2,1)} %fusion.20), channel_id=1, source_target_pairs={{0,7},{1,2},{2,1},{3,4},{4,3},{5,6},{6,5},{7,0},{8,15},{9,10},{10,... | collective-permute-start | bytes 1966088 | tf_op jit(solution)/shard_map/ppermute | solution.py:340
  98.4 2.5 %collective-permute-start.19 = (bf16[160,256]{1,0:T(8,128)(2,1)S(1)}, bf16[160,256]{1,0:T(8,128)(2,1)S(1)}, u32[]{:S(2)}, u32[]{:S(2)}) collective-permute-start(bf16[160,256]{1,0:T(8,128)(2,1)S(1)} %copy-done.8), channel_id=1, source_target_pairs={{0,128},{64,192},{128,0},{192,64},{1,129},{65,193},{129,1},{193,65... | collective-permute-start | bytes 245768 | tf_op jit(solution)/shard_map/ppermute | solution.py:24
  100.9 2.2 %collective-permute-start.20 = (bf16[160,256]{1,0:T(8,128)(2,1)S(1)}, bf16[160,256]{1,0:T(8,128)(2,1)S(1)}, u32[]{:S(2)}, u32[]{:S(2)}) collective-permute-start(bf16[160,256]{1,0:T(8,128)(2,1)S(1)} %copy-done.8), channel_id=1, source_target_pairs={{0,192},{64,128},{128,64},{192,0},{1,193},{65,129},{129,65},{193,1... | collective-permute-start | bytes 245768 | tf_op jit(solution)/shard_map/ppermute | solution.py:24
  103.1 1.2 collective-permute-done.19.refs_2_
  104.3 2.2 %collective-permute-done.20.refs_3_ = bf16[160,256]{1,0:T(8,128)(2,1)S(1)} collective-permute-done((bf16[160,256]{1,0:T(8,128)(2,1)S(1)}, bf16[160,256]{1,0:T(8,128)(2,1)S(1)}, u32[]{:S(2)}, u32[]{:S(2)}) %collective-permute-start.20) | collective-permute-done | bytes 81952 | tf_op jit(solution)/shard_map/ppermute | solution.py:24
  107.2 1.8 %shard_map.102.refs_0_ = bf16[160,1024]{1,0:T(8,128)(2,1)} custom-call(s32[1]{0:T(128)} %bitcast.11.here_ref, bf16[160,256]{1,0:T(8,128)(2,1)} %shard_map.101.refs_0_, bf16[160,256]{1,0:T(8,128)(2,1)} %copy-done.12, bf16[160,256]{1,0:T(8,128)(2,1)} %copy-done.13, bf16[160,256]{1,0:T(8,128)(2,1)} %copy-done.14), custom_call_target="tpu_custom_call" | custom-call | tf_op jit(solution)/shard_map/pallas_call | solution.py:106
  109.0 8.2 %shard_map.103 = bf16[272,3584]{1,0:T(8,128)(2,1)} custom-call(s32[1]{0:T(128)} %bitcast.9.z_ref, bf16[256,1280]{1,0:T(8,128)(2,1)} %collective-permute-done.3.early_ref, bf16[256,1280]{1,0:T(8,128)(2,1)} %copy-done.6, bf16[256,1024]{1,0:T(8,128)(2,1)} %collective-permute-done.1.cotangent_ref, bf16[2560,1024]{1,0:T(8,128)(2,1)} %bitcast.29), custom_call_target="tpu_custom_call" | custom-call | tf_op jit(solution)/shard_map/pallas_call | solution.py:159
  117.2 1.8 %collective-permute-start.21 = (bf16[272,3584]{1,0:T(8,128)(2,1)}, bf16[272,3584]{1,0:T(8,128)(2,1)S(1)}, u32[]{:S(2)}, u32[]{:S(2)}) collective-permute-start(bf16[272,3584]{1,0:T(8,128)(2,1)} %shard_map.103), channel_id=1, source_target_pairs={{0,8},{8,0},{1,9},{9,1},{2,10},{10,2},{3,11},{11,3},{4,12},{12,4},... | collective-permute-start | bytes 5849096 | tf_op jit(solution)/shard_map/ppermute | solution.py:24
  119.0 3.1 %fusion.22 = f16[320,1024]{1,0:T(8,128)(2,1)} fusion(f16[320,1024]{1,0:T(8,128)(2,1)S(1)} %collective-permute-done.17, f32[1280,1024]{1,0:T(8,128)} %fusion.32, s32[]{:T(128)S(6)} %select_n.162, f32[]{:T(128)} %bitcast.5), kind=kLoop, calls=%fused_computation.41 | loop fusion | flops 2949120 | bytes 2621448 | tf_op jit(solution)/shard_map/convert_element_type | solution.py:55
  122.1 3.4 %fusion.23 = f16[320,1024]{1,0:T(8,128)(2,1)} fusion(f16[320,1024]{1,0:T(8,128)(2,1)} %collective-permute-done.16, f32[1280,1024]{1,0:T(8,128)} %copy-done.2, s32[]{:T(128)S(6)} %select_n.162, f32[]{:T(128)} %bitcast.5), kind=kLoop, calls=%fused_computation.42 | loop fusion | flops 2949120 | bytes 2621448 | tf_op jit(solution)/shard_map/convert_element_type | solution.py:55
  125.4 1.0 collective-permute-start.22
  127.2 7.0 %shard_map.104 = (f32[256,1024]{1,0:T(8,128)}, bf16[256,5120]{1,0:T(8,128)(2,1)}) custom-call(s32[1]{0:T(128)} %bitcast.12._, bf16[256,5120]{1,0:T(8,128)(2,1)} %bitcast.25, bf16[256,1024]{1,0:T(8,128)(2,1)} %bitcast.32, bf16[2560,1024]{1,0:T(8,128)(2,1)} %bitcast.30), custom_call_target="tpu_custom_call" | custom-call | tf_op jit(solution)/shard_map/pallas_call | solution.py:192
  134.9 1.6 shard_map.105
  137.2 2.0 %shard_map.106 = bf16[320,1024]{1,0:T(8,128)(2,1)} custom-call(s32[1]{0:T(128)} %bitcast.13.here_ref, bf16[160,1024]{1,0:T(8,128)(2,1)} %shard_map.102.refs_0_, bf16[160,1024]{1,0:T(8,128)(2,1)} %copy-done.9), custom_call_target="tpu_custom_call" | custom-call | tf_op jit(solution)/shard_map/pallas_call | solution.py:106
  139.2 5.0 %fusion.25 = (f16[320,1024]{1,0:T(8,128)(2,1)}, f16[320,1024]{1,0:T(8,128)(2,1)}) fusion(f16[320,1024]{1,0:T(8,128)(2,1)S(1)} %collective-permute-done.22, f32[1280,1024]{1,0:T(8,128)} %fusion.32, s32[]{:T(128)S(6)} %select_n.177, f32[]{:T(128)} %bitcast.5, f16[320,1024]{1,0:T(8,128)(2,1)} %collective-permute-done.23, s32[]{:T(128)S(6)} %select_n.164), kind=kLoop, calls=%fused_computation.44 | loop fusion | flops 5898240 | bytes 5242892 | tf_op jit(solution)/shard_map/convert_element_type | solution.py:55
  144.2 1.8 %collective-permute-start.26 = (f16[320,1024]{1,0:T(8,128)(2,1)}, f16[320,1024]{1,0:T(8,128)(2,1)S(1)}, u32[]{:S(2)}, u32[]{:S(2)}) collective-permute-start(f16[320,1024]{1,0:T(8,128)(2,1)} %get-tuple-element.89), channel_id=1, source_target_pairs={{0,1},{1,0},{2,3},{3,2},{4,5},{5,4},{6,7},{7,6},{8,9},{9,8},{10,11... | collective-permute-start | bytes 1966088 | tf_op jit(solution)/shard_map/ppermute | solution.py:401
  146.0 1.2 collective-permute-start.27
  148.0 6.1 %collective-permute-done.21.coded_ref.back_ref = bf16[272,3584]{1,0:T(8,128)(2,1)S(1)} collective-permute-done((bf16[272,3584]{1,0:T(8,128)(2,1)}, bf16[272,3584]{1,0:T(8,128)(2,1)S(1)}, u32[]{:S(2)}, u32[]{:S(2)}) %collective-permute-start.21) | collective-permute-done | bytes 1949728 | tf_op jit(solution)/shard_map/ppermute | solution.py:24
  154.0 1.3 copy-done.1
  155.3 5.1 %shard_map.107 = (bf16[256,1024]{1,0:T(8,128)(2,1)}, bf16[256,5120]{1,0:T(8,128)(2,1)}) custom-call(s32[1]{0:T(128)} %bitcast._, bf16[256,5120]{1,0:T(8,128)(2,1)} %get-tuple-element.70.__, f32[256,1024]{1,0:T(8,128)} %get-tuple-element.71.keys_ref, bf16[272,3584]{1,0:T(8,128)(2,1)} %copy-done.1, ...), custom_call_target="tpu_custom_call", output_to_operand_aliasing={{1}: (1, {})} | custom-call | tf_op jit(solution)/shard_map/pallas_call | solution.py:227
  161.1 2.8 %collective-permute-done.27 = f16[320,1024]{1,0:T(8,128)(2,1)} collective-permute-done((f16[320,1024]{1,0:T(8,128)(2,1)}, f16[320,1024]{1,0:T(8,128)(2,1)}, u32[]{:S(2)}, u32[]{:S(2)}) %collective-permute-start.27) | collective-permute-done | bytes 655392 | tf_op jit(solution)/shard_map/ppermute | solution.py:401
  163.9 4.0 %fusion.46 = bf16[1,320,1024]{2,1,0:T(8,128)(2,1)} fusion(f32[]{:T(128)} %bitcast.16, f16[320,1024]{1,0:T(8,128)(2,1)} %collective-permute-done.27, f16[320,1024]{1,0:T(8,128)(2,1)S(1)} %collective-permute-done.26, f32[]{:T(128)} %bitcast.5, f32[1280,1024]{1,0:T(8,128)} %fusion.32, s32[]{:T(128)S(6)} %select_n.165), kind=kLoop, calls=%fused_computation.78 | loop fusion | flops 4259840 | bytes 3276812 | tf_op jit(solution)/shard_map/broadcast_in_dim | solution.py:412
  (91 shorter events, 12.1 us)
Async XLA Ops:
  7.2 2.8 %copy-start.3 = (bf16[1,256,1024]{2,1,0:T(8,128)(2,1)S(1)}, bf16[1,256,1024]{2,1,0:T(8,128)(2,1)}, u32[]{:S(2)}) copy-start(bf16[1,256,1024]{2,1,0:T(8,128)(2,1)} %param.8) | copy-start | bytes 1572868
  7.2 101.8 %all-gather.3.cloned.1.call-start = ((), (), s32[]{:S(2)}) async-start(), calls=%async_computation | async-start | bytes 5898240 | tf_op jit(solution)/shard_map/all_gather | solution.py:275
  9.9 11.1 %collective-permute-start.2 = (f32[160,1024]{1,0:T(8,128)}, f32[160,1024]{1,0:T(8,128)}, u32[]{:S(2)}, u32[]{:S(2)}) collective-permute-start(f32[160,1024]{1,0:T(8,128)} %dynamic-slice_bitcast_fusion), channel_id=1, source_target_pairs={{0,16},{16,0},{1,17},{17,1},{2,18},{18,2},{3,19},{19,3},{4,20},{20... | collective-permute-start | bytes 1966088 | tf_op jit(solution)/shard_map/ppermute | solution.py:24
  11.2 6.1 %copy-start = (bf16[1,256,5120]{2,1,0:T(8,128)(2,1)S(1)}, bf16[1,256,5120]{2,1,0:T(8,128)(2,1)}, u32[]{:S(2)}) copy-start(bf16[1,256,5120]{2,1,0:T(8,128)(2,1)} %param.6) | copy-start | bytes 7864324
  15.0 33.3 %collective-permute-start = (f32[8,128]{1,0:T(8,128)S(1)}, f32[8,128]{1,0:T(8,128)S(1)}, u32[]{:S(2)}, u32[]{:S(2)}) collective-permute-start(f32[8,128]{1,0:T(8,128)S(1)} %iota.32), channel_id=1, source_target_pairs={{0,8},{8,0},{1,9},{9,1},{2,10},{10,2},{3,11},{11,3},{4,12},{12,4},... | collective-permute-start | bytes 12296 | tf_op jit(solution)/shard_map/ppermute | solution.py:24
  17.3 3.0 %copy-start.10 = (f32[320,64]{0,1:T(8,128)S(1)}, f32[320,64]{0,1:T(8,128)}, u32[]{:S(2)}) copy-start(f32[320,64]{0,1:T(8,128)} %param.11) | copy-start | bytes 245764
  18.3 50.2 %collective-permute-start.3 = (bf16[256,1280]{1,0:T(8,128)(2,1)}, bf16[256,1280]{1,0:T(8,128)(2,1)}, u32[]{:S(2)}, u32[]{:S(2)}) collective-permute-start(bf16[256,1280]{1,0:T(8,128)(2,1)} %pad_maximum_fusion.3), channel_id=1, source_target_pairs={{0,8},{8,0},{1,9},{9,1},{2,10},{10,2},{3,11},{11,3},{4,12},{12,4},... | collective-permute-start | bytes 1966088 | tf_op jit(solution)/shard_map/ppermute | solution.py:24
  18.4 28.3 %collective-permute-start.1 = (bf16[256,1024]{1,0:T(8,128)(2,1)S(1)}, bf16[256,1024]{1,0:T(8,128)(2,1)}, u32[]{:S(2)}, u32[]{:S(2)}) collective-permute-start(bf16[256,1024]{1,0:T(8,128)(2,1)S(1)} %bitcast.33), channel_id=1, source_target_pairs={{0,8},{8,0},{1,9},{9,1},{2,10},{10,2},{3,11},{11,3},{4,12},{12,4},... | collective-permute-start | bytes 1572872 | tf_op jit(solution)/shard_map/ppermute | solution.py:24
  20.5 32.7 %collective-permute-start.9 = (f32[160,64]{1,0:T(8,128)S(1)}, f32[160,64]{1,0:T(8,128)S(1)}, u32[]{:S(2)}, u32[]{:S(2)}) collective-permute-start(f32[160,64]{1,0:T(8,128)S(1)} %copy.15), channel_id=1, source_target_pairs={{0,16},{16,0},{1,17},{17,1},{2,18},{18,2},{3,19},{19,3},{4,20},{20... | collective-permute-start | bytes 122888 | tf_op jit(solution)/shard_map/ppermute | solution.py:24
  20.9 1.3 copy-start.4
  23.5 31.3 %collective-permute-start.6 = (f32[160,256]{1,0:T(8,128)S(1)}, f32[160,256]{1,0:T(8,128)S(1)}, u32[]{:S(2)}, u32[]{:S(2)}) collective-permute-start(f32[160,256]{1,0:T(8,128)S(1)} %get-tuple-element.106), channel_id=1, source_target_pairs={{0,64},{64,0},{128,192},{192,128},{1,65},{65,1},{129,193},{193,129... | collective-permute-start | bytes 491528 | tf_op jit(solution)/shard_map/ppermute | solution.py:24
  46.7 11.3 %collective-permute-start.7 = (f32[160,256]{1,0:T(8,128)S(1)}, f32[160,256]{1,0:T(8,128)S(1)}, u32[]{:S(2)}, u32[]{:S(2)}) collective-permute-start(f32[160,256]{1,0:T(8,128)S(1)} %get-tuple-element.105), channel_id=1, source_target_pairs={{0,128},{64,192},{128,0},{192,64},{1,129},{65,193},{129,1},{193,65... | collective-permute-start | bytes 491528 | tf_op jit(solution)/shard_map/ppermute | solution.py:24
  48.4 3.7 %collective-permute-start.4 = (f32[8,128]{1,0:T(8,128)S(1)}, f32[8,128]{1,0:T(8,128)S(1)}, u32[]{:S(2)}, u32[]{:S(2)}) collective-permute-start(f32[8,128]{1,0:T(8,128)S(1)} %maximum_select_fusion.3), channel_id=1, source_target_pairs={{0,1},{1,0},{2,3},{3,2},{4,5},{5,4},{6,7},{7,6},{8,9},{9,8},{10,11... | collective-permute-start | bytes 12296 | tf_op jit(solution)/shard_map/ppermute | solution.py:24
  52.1 6.5 %collective-permute-start.8 = (f32[160,256]{1,0:T(8,128)S(1)}, f32[160,256]{1,0:T(8,128)S(1)}, u32[]{:S(2)}, u32[]{:S(2)}) collective-permute-start(f32[160,256]{1,0:T(8,128)S(1)} %get-tuple-element.104), channel_id=1, source_target_pairs={{0,192},{64,128},{128,64},{192,0},{1,193},{65,129},{129,65},{193,1... | collective-permute-start | bytes 491528 | tf_op jit(solution)/shard_map/ppermute | solution.py:24
  53.2 24.8 %collective-permute-start.14 = (bf16[256,1280]{1,0:T(8,128)(2,1)S(1)}, bf16[256,1280]{1,0:T(8,128)(2,1)S(1)}, u32[]{:S(2)}, u32[]{:S(2)}) collective-permute-start(bf16[256,1280]{1,0:T(8,128)(2,1)S(1)} %pad_maximum_fusion.4), channel_id=1, source_target_pairs={{0,8},{8,0},{1,9},{9,1},{2,10},{10,2},{3,11},{11,3},{4,12},{12,4},... | collective-permute-start | bytes 1966088 | tf_op jit(solution)/shard_map/ppermute | solution.py:24
  54.8 6.5 %collective-permute-start.5 = (f32[8,128]{1,0:T(8,128)S(1)}, f32[8,128]{1,0:T(8,128)S(1)}, u32[]{:S(2)}, u32[]{:S(2)}) collective-permute-start(f32[8,128]{1,0:T(8,128)S(1)} %maximum_select_fusion.2), channel_id=1, source_target_pairs={{0,2},{1,3},{2,0},{3,1},{4,6},{5,7},{6,4},{7,5},{8,10},{9,11},{10,... | collective-permute-start | bytes 12296 | tf_op jit(solution)/shard_map/ppermute | solution.py:24
  58.7 24.5 %collective-permute-start.13 = (f32[160,128]{1,0:T(8,128)S(1)}, f32[160,128]{1,0:T(8,128)S(1)}, u32[]{:S(2)}, u32[]{:S(2)}) collective-permute-start(f32[160,128]{1,0:T(8,128)S(1)} %constant_dynamic-slice_fusion.1), channel_id=1, source_target_pairs={{0,32},{32,0},{1,33},{33,1},{2,34},{34,2},{3,35},{35,3},{4,36},{36... | collective-permute-start | bytes 245768 | tf_op jit(solution)/shard_map/ppermute | solution.py:24
  61.3 10.1 %collective-permute-start.10 = (f32[8,128]{1,0:T(8,128)S(1)}, f32[8,128]{1,0:T(8,128)S(1)}, u32[]{:S(2)}, u32[]{:S(2)}) collective-permute-start(f32[8,128]{1,0:T(8,128)S(1)} %maximum_select_fusion.1), channel_id=1, source_target_pairs={{0,4},{1,5},{2,6},{3,7},{4,0},{5,1},{6,2},{7,3},{8,12},{9,13},{10,... | collective-permute-start | bytes 12296 | tf_op jit(solution)/shard_map/ppermute | solution.py:24
  71.3 11.9 %copy-start.2 = (f32[1280,1024]{1,0:T(8,128)}, f32[1280,1024]{1,0:T(8,128)S(1)}, u32[]{:S(2)}) copy-start(f32[1280,1024]{1,0:T(8,128)S(1)} %fusion.26) | copy-start | bytes 15728644
  73.7 18.1 %collective-permute-start.11 = (f16[160,1024]{1,0:T(8,128)(2,1)S(1)}, f16[160,1024]{1,0:T(8,128)(2,1)S(1)}, u32[]{:S(2)}, u32[]{:S(2)}) collective-permute-start(f16[160,1024]{1,0:T(8,128)(2,1)S(1)} %get-tuple-element.95), channel_id=1, source_target_pairs={{0,1},{1,0},{2,3},{3,2},{4,5},{5,4},{6,7},{7,6},{8,9},{9,8},{10,11... | collective-permute-start | bytes 983048 | tf_op jit(solution)/shard_map/ppermute | solution.py:340
  74.8 17.0 %collective-permute-start.12 = (f16[160,1024]{1,0:T(8,128)(2,1)S(1)}, f16[160,1024]{1,0:T(8,128)(2,1)S(1)}, u32[]{:S(2)}, u32[]{:S(2)}) collective-permute-start(f16[160,1024]{1,0:T(8,128)(2,1)S(1)} %get-tuple-element.94), channel_id=1, source_target_pairs={{0,7},{1,2},{2,1},{3,4},{4,3},{5,6},{6,5},{7,0},{8,15},{9,10},{10,... | collective-permute-start | bytes 983048 | tf_op jit(solution)/shard_map/ppermute | solution.py:340
  78.0 5.2 %copy-start.6 = (bf16[256,1280]{1,0:T(8,128)(2,1)}, bf16[256,1280]{1,0:T(8,128)(2,1)S(1)}, u32[]{:S(2)}) copy-start(bf16[256,1280]{1,0:T(8,128)(2,1)S(1)} %collective-permute-done.14.late_ref) | copy-start | bytes 1966084
  84.1 5.6 %copy-start.11 = (bf16[160,128]{1,0:T(8,128)(2,1)}, bf16[160,128]{1,0:T(8,128)(2,1)S(1)}, u32[]{:S(2)}) copy-start(bf16[160,128]{1,0:T(8,128)(2,1)S(1)} %get-tuple-element.86.refs_0_) | copy-start | bytes 122884
  84.2 5.6 %collective-permute-start.15 = (bf16[160,128]{1,0:T(8,128)(2,1)S(1)}, bf16[160,128]{1,0:T(8,128)(2,1)S(1)}, u32[]{:S(2)}, u32[]{:S(2)}) collective-permute-start(bf16[160,128]{1,0:T(8,128)(2,1)S(1)} %get-tuple-element.86.refs_0_), channel_id=1, source_target_pairs={{0,32},{32,0},{1,33},{33,1},{2,34},{34,2},{3,35},{35,3},{4,36},{36... | collective-permute-start | bytes 122888 | tf_op jit(solution)/shard_map/ppermute | solution.py:24
  89.7 0.6 copy-start.16
  95.4 3.0 %copy-start.8 = (bf16[160,256]{1,0:T(8,128)(2,1)S(1)}, bf16[160,256]{1,0:T(8,128)(2,1)}, u32[]{:S(2)}) copy-start(bf16[160,256]{1,0:T(8,128)(2,1)} %shard_map.101.refs_0_) | copy-start | bytes 245764
  95.4 23.6 %collective-permute-start.17 = (f16[320,1024]{1,0:T(8,128)(2,1)}, f16[320,1024]{1,0:T(8,128)(2,1)S(1)}, u32[]{:S(2)}, u32[]{:S(2)}) collective-permute-start(f16[320,1024]{1,0:T(8,128)(2,1)} %fusion.21), channel_id=1, source_target_pairs={{0,1},{1,0},{2,3},{3,2},{4,5},{5,4},{6,7},{7,6},{8,9},{9,8},{10,11... | collective-permute-start | bytes 1966088 | tf_op jit(solution)/shard_map/ppermute | solution.py:340
  96.4 25.7 %collective-permute-start.16 = (f16[320,1024]{1,0:T(8,128)(2,1)}, f16[320,1024]{1,0:T(8,128)(2,1)}, u32[]{:S(2)}, u32[]{:S(2)}) collective-permute-start(f16[320,1024]{1,0:T(8,128)(2,1)} %fusion.20), channel_id=1, source_target_pairs={{0,7},{1,2},{2,1},{3,4},{4,3},{5,6},{6,5},{7,0},{8,15},{9,10},{10,... | collective-permute-start | bytes 1966088 | tf_op jit(solution)/shard_map/ppermute | solution.py:340
  98.4 4.7 %collective-permute-start.18 = (bf16[160,256]{1,0:T(8,128)(2,1)S(1)}, bf16[160,256]{1,0:T(8,128)(2,1)S(1)}, u32[]{:S(2)}, u32[]{:S(2)}) collective-permute-start(bf16[160,256]{1,0:T(8,128)(2,1)S(1)} %copy-done.8), channel_id=1, source_target_pairs={{0,64},{64,0},{128,192},{192,128},{1,65},{65,1},{129,193},{193,129... | collective-permute-start | bytes 245768 | tf_op jit(solution)/shard_map/ppermute | solution.py:24
  98.4 5.9 %collective-permute-start.19 = (bf16[160,256]{1,0:T(8,128)(2,1)S(1)}, bf16[160,256]{1,0:T(8,128)(2,1)S(1)}, u32[]{:S(2)}, u32[]{:S(2)}) collective-permute-start(bf16[160,256]{1,0:T(8,128)(2,1)S(1)} %copy-done.8), channel_id=1, source_target_pairs={{0,128},{64,192},{128,0},{192,64},{1,129},{65,193},{129,1},{193,65... | collective-permute-start | bytes 245768 | tf_op jit(solution)/shard_map/ppermute | solution.py:24
  100.9 5.7 %collective-permute-start.20 = (bf16[160,256]{1,0:T(8,128)(2,1)S(1)}, bf16[160,256]{1,0:T(8,128)(2,1)S(1)}, u32[]{:S(2)}, u32[]{:S(2)}) collective-permute-start(bf16[160,256]{1,0:T(8,128)(2,1)S(1)} %copy-done.8), channel_id=1, source_target_pairs={{0,192},{64,128},{128,64},{192,0},{1,193},{65,129},{129,65},{193,1... | collective-permute-start | bytes 245768 | tf_op jit(solution)/shard_map/ppermute | solution.py:24
  103.1 3.5 %copy-start.12 = (bf16[160,256]{1,0:T(8,128)(2,1)}, bf16[160,256]{1,0:T(8,128)(2,1)S(1)}, u32[]{:S(2)}) copy-start(bf16[160,256]{1,0:T(8,128)(2,1)S(1)} %collective-permute-done.18.refs_1_) | copy-start | bytes 245764
  104.3 2.2 %copy-start.13 = (bf16[160,256]{1,0:T(8,128)(2,1)}, bf16[160,256]{1,0:T(8,128)(2,1)S(1)}, u32[]{:S(2)}) copy-start(bf16[160,256]{1,0:T(8,128)(2,1)S(1)} %collective-permute-done.19.refs_2_) | copy-start | bytes 245764
  106.6 0.6 copy-start.14
  117.2 36.9 %collective-permute-start.21 = (bf16[272,3584]{1,0:T(8,128)(2,1)}, bf16[272,3584]{1,0:T(8,128)(2,1)S(1)}, u32[]{:S(2)}, u32[]{:S(2)}) collective-permute-start(bf16[272,3584]{1,0:T(8,128)(2,1)} %shard_map.103), channel_id=1, source_target_pairs={{0,8},{8,0},{1,9},{9,1},{2,10},{10,2},{3,11},{11,3},{4,12},{12,4},... | collective-permute-start | bytes 5849096 | tf_op jit(solution)/shard_map/ppermute | solution.py:24
  122.1 4.6 %copy-start.5 = (bf16[160,1024]{1,0:T(8,128)(2,1)S(1)}, bf16[160,1024]{1,0:T(8,128)(2,1)}, u32[]{:S(2)}) copy-start(bf16[160,1024]{1,0:T(8,128)(2,1)} %shard_map.102.refs_0_) | copy-start | bytes 983044
  125.4 13.7 %collective-permute-start.22 = (f16[320,1024]{1,0:T(8,128)(2,1)}, f16[320,1024]{1,0:T(8,128)(2,1)S(1)}, u32[]{:S(2)}, u32[]{:S(2)}) collective-permute-start(f16[320,1024]{1,0:T(8,128)(2,1)} %fusion.23), channel_id=1, source_target_pairs={{0,1},{1,0},{2,3},{3,2},{4,5},{5,4},{6,7},{7,6},{8,9},{9,8},{10,11... | collective-permute-start | bytes 1966088 | tf_op jit(solution)/shard_map/ppermute | solution.py:340
  126.5 12.7 %collective-permute-start.23 = (f16[320,1024]{1,0:T(8,128)(2,1)}, f16[320,1024]{1,0:T(8,128)(2,1)}, u32[]{:S(2)}, u32[]{:S(2)}) collective-permute-start(f16[320,1024]{1,0:T(8,128)(2,1)} %fusion.22), channel_id=1, source_target_pairs={{0,7},{1,2},{2,1},{3,4},{4,3},{5,6},{6,5},{7,0},{8,15},{9,10},{10,... | collective-permute-start | bytes 1966088 | tf_op jit(solution)/shard_map/ppermute | solution.py:340
  126.7 9.8 %collective-permute-start.24 = (bf16[160,1024]{1,0:T(8,128)(2,1)S(1)}, bf16[160,1024]{1,0:T(8,128)(2,1)S(1)}, u32[]{:S(2)}, u32[]{:S(2)}) collective-permute-start(bf16[160,1024]{1,0:T(8,128)(2,1)S(1)} %copy-done.5), channel_id=1, source_target_pairs={{0,16},{16,0},{1,17},{17,1},{2,18},{18,2},{3,19},{19,3},{4,20},{20... | collective-permute-start | bytes 983048 | tf_op jit(solution)/shard_map/ppermute | solution.py:24
  126.7 7.6 %collective-permute-start.25 = (f32[160,64]{1,0:T(8,128)S(1)}, f32[160,64]{1,0:T(8,128)S(1)}, u32[]{:S(2)}, u32[]{:S(2)}) collective-permute-start(f32[160,64]{1,0:T(8,128)S(1)} %get-tuple-element.111), channel_id=1, source_target_pairs={{0,16},{16,0},{1,17},{17,1},{2,18},{18,2},{3,19},{19,3},{4,20},{20... | collective-permute-start | bytes 122888 | tf_op jit(solution)/shard_map/ppermute | solution.py:24
  134.2 0.6 copy-start.15
  136.5 0.8 copy-start.9
  139.2 8.0 %copy-start.7 = (f32[320,64]{1,0:T(8,128)S(1)}, f32[320,64]{1,0:T(8,128)}, u32[]{:S(2)}) copy-start(f32[320,64]{1,0:T(8,128)} %shard_map.105) | copy-start | bytes 245764
  144.2 17.0 %collective-permute-start.26 = (f16[320,1024]{1,0:T(8,128)(2,1)}, f16[320,1024]{1,0:T(8,128)(2,1)S(1)}, u32[]{:S(2)}, u32[]{:S(2)}) collective-permute-start(f16[320,1024]{1,0:T(8,128)(2,1)} %get-tuple-element.89), channel_id=1, source_target_pairs={{0,1},{1,0},{2,3},{3,2},{4,5},{5,4},{6,7},{7,6},{8,9},{9,8},{10,11... | collective-permute-start | bytes 1966088 | tf_op jit(solution)/shard_map/ppermute | solution.py:401
  146.0 17.9 %collective-permute-start.27 = (f16[320,1024]{1,0:T(8,128)(2,1)}, f16[320,1024]{1,0:T(8,128)(2,1)}, u32[]{:S(2)}, u32[]{:S(2)}) collective-permute-start(f16[320,1024]{1,0:T(8,128)(2,1)} %get-tuple-element.88), channel_id=1, source_target_pairs={{0,7},{1,2},{2,1},{3,4},{4,3},{5,6},{6,5},{7,0},{8,15},{9,10},{10,... | collective-permute-start | bytes 1966088 | tf_op jit(solution)/shard_map/ppermute | solution.py:401
  154.0 1.3 copy-start.1
Sparse Core Ops, SparseCore 0:
  9.8 68.8 all-gather.2

commit v6 on v5

--- a/solution.py
+++ b/solution.py
@@ -291,8 +291,7 @@
     order.did(*gives, old_give)
     others = [swap(g, "y", m) for g, m in zip(gives, (1, 2, 3))]
     old_other = swap(old_give, "c")
-    tokens_held, cotangent_other = order.step(tokens, cotangent_other)
-    sent = token_columns(tokens_held, 1 - x, late)
+    sent = token_columns(order.step(tokens), 1 - x, late)
     order.did(sent)
     late_other = swap(sent, "xl")
     peaks = join_peaks(peaks, order.step(peaks_other))
@@ -320,7 +319,7 @@
             preferred_element_type=F32,
         )
 
-    early_other = order.step(early_other)
+    early_other, cotangent_other = order.step(early_other, cotangent_other)
     partial_early = product(early_mine, early_other)
     order.did(partial_early)
     peaks = join_peaks(peaks, order.step(peaks_other))

time: 176 us -> 164 us (0.932)
  waiting for transfers between devices: 42.9 us -> 28.5 us
  starting transfers between devices: 42.3 us -> 45.3 us
    ppermute x20, waiting for transfers between devices: 38.6 us -> 27.8 us  [swap(): lax.ppermute(value, axis, [(i, i ^ mask) for i in range(SIZES[axis])])]
    ppermute x6, starting transfers between devices: 7.56 us -> 12.4 us  [send(): return lax.ppermute(message, 'z', pairs)]
    ppermute x2, waiting for transfers between devices: 3.51 us -> 0.01 us  [shards(): even, odd = (lax.ppermute(even, 'z', EVEN), lax.ppermute(odd, 'z', ODD))]
    ppermute x2, starting transfers between devices: 3.04 us -> 1.21 us  [shards(): even, odd = (lax.ppermute(even, 'z', EVEN), lax.ppermute(odd, 'z', ODD))]
    unnamed x37 -> x39, local copies, waits for them, and re-layouts: 6.08 us -> 6.04 us
  transfers between devices with their start and end apart: 29 -> 29, of which waited for: 9 -> 9; matrix products, arithmetic and copies ran while one was open for 21% -> 22% of each run, Pallas kernels for 16% -> 17%
where the time goes in v6:
time: 164 us; the launch traced here: 162 us
  starting transfers between devices  45.3 us (28%)
  other arithmetic  28.7 us (18%)
  waiting for transfers between devices  28.5 us (17%)
  Pallas kernels  27.1 us (17%)
  between operations  16.4 us (10%)
  local copies, waits for them, and re-layouts  9.24 us (6%)
  matrix products  6.75 us (4%)
    ppermute x20, starting transfers between devices, swap(): lax.ppermute(value, axis, [(i, i ^ mask) for i in range(SIZES[axis])])  31.6 us
    ppermute x20, waiting for transfers between devices, swap(): lax.ppermute(value, axis, [(i, i ^ mask) for i in range(SIZES[axis])])  27.8 us
    convert_element_type x6, other arithmetic, encode(): return (scaled * jnp.abs(scaled)).astype(F16)  13.6 us
    ppermute x6, starting transfers between devices, send(): return lax.ppermute(message, 'z', pairs)  12.4 us
    pallas_call x1, Pallas kernels, products_for_partner(): pl.pallas_call(body, grid_spec=pltpu.PrefetchScalarGridSpec(num_scalar_pr...  8.2 us
    pallas_call x1, Pallas kernels, products_here(): pl.pallas_call(body, grid_spec=pltpu.PrefetchScalarGridSpec(num_scalar_pr...  7.05 us
    pallas_call x4, Pallas kernels, assemble(): pl.pallas_call(body, grid_spec=pltpu.PrefetchScalarGridSpec(num_scalar_pr...  6.79 us
    dot_general x2, matrix products, product(): lax.dot_general(jnp.concatenate([first, second], axis=0), jnp.concatenate...  6.75 us
  transfers between devices with their start and end apart: 29, of which 9 were waited for; matrix products, arithmetic and copies ran while one was open for 22% of the time, Pallas kernels for 17%

profile of v6, /device:TPU:2, one launch (start us, length us, event | category | flops | bytes accessed | tf_op | source)
XLA Modules:
  0.0 162.0 jit_solution(15847214631351901130)
XLA Ops:
  7.9 2.0 %dynamic-slice_bitcast_fusion = f32[160,1024]{1,0:T(8,128)} fusion(f32[1,320,1024]{2,1,0:T(8,128)} %param.10, s32[]{:T(128)S(6)} %select_n.140), kind=kLoop, calls=%fused_computation.77 | loop fusion | bytes 1310724 | tf_op jit(solution)/shard_map/dynamic_slice | solution.py:40
  11.3 2.4 %abs_reduce_fusion = f32[5120]{0:T(1024)S(1)} fusion(bf16[256,5120]{1,0:T(8,128)(2,1)} %bitcast.24), kind=kLoop, calls=%fused_computation | loop fusion | flops 3927040 | bytes 2641920 | tf_op jit(solution)/shard_map/reduce_sum | solution.py:68
  15.0 2.3 %collective-permute-start = (f32[8,128]{1,0:T(8,128)S(1)}, f32[8,128]{1,0:T(8,128)S(1)}, u32[]{:S(2)}, u32[]{:S(2)}) collective-permute-start(f32[8,128]{1,0:T(8,128)S(1)} %iota.32), channel_id=1, source_target_pairs={{0,8},{8,0},{1,9},{9,1},{2,10},{10,2},{3,11},{11,3},{4,12},{12,4},... | collective-permute-start | bytes 12296 | tf_op jit(solution)/shard_map/ppermute | solution.py:24
  17.4 0.9 pad_maximum_fusion.3
  19.2 1.2 copy-done.4
  20.4 1.2 bitcast_add_fusion
  21.7 1.2 collective-permute-start.6
  22.9 2.9 %collective-permute-start.7 = (f32[160,256]{1,0:T(8,128)S(1)}, f32[160,256]{1,0:T(8,128)S(1)}, u32[]{:S(2)}, u32[]{:S(2)}) collective-permute-start(f32[160,256]{1,0:T(8,128)S(1)} %get-tuple-element.105), channel_id=1, source_target_pairs={{0,128},{64,192},{128,0},{192,64},{1,129},{65,193},{129,1},{193,65... | collective-permute-start | bytes 491528 | tf_op jit(solution)/shard_map/ppermute | solution.py:24
  26.0 1.9 %collective-permute-start.4 = (f32[8,128]{1,0:T(8,128)S(1)}, f32[8,128]{1,0:T(8,128)S(1)}, u32[]{:S(2)}, u32[]{:S(2)}) collective-permute-start(f32[8,128]{1,0:T(8,128)S(1)} %maximum_select_fusion.3), channel_id=1, source_target_pairs={{0,1},{1,0},{2,3},{3,2},{4,5},{5,4},{6,7},{7,6},{8,9},{9,8},{10,11... | collective-permute-start | bytes 12296 | tf_op jit(solution)/shard_map/ppermute | solution.py:24
  28.1 1.7 %collective-permute-done.4 = f32[8,128]{1,0:T(8,128)S(1)} collective-permute-done((f32[8,128]{1,0:T(8,128)S(1)}, f32[8,128]{1,0:T(8,128)S(1)}, u32[]{:S(2)}, u32[]{:S(2)}) %collective-permute-start.4) | collective-permute-done | bytes 4128 | tf_op jit(solution)/shard_map/ppermute | solution.py:24
  30.4 1.9 %collective-permute-start.3 = (bf16[256,1024]{1,0:T(8,128)(2,1)S(1)}, bf16[256,1024]{1,0:T(8,128)(2,1)S(1)}, u32[]{:S(2)}, u32[]{:S(2)}) collective-permute-start(bf16[256,1024]{1,0:T(8,128)(2,1)S(1)} %bitcast.33), channel_id=1, source_target_pairs={{0,8},{8,0},{1,9},{9,1},{2,10},{10,2},{3,11},{11,3},{4,12},{12,4},... | collective-permute-start | bytes 1572872 | tf_op jit(solution)/shard_map/ppermute | solution.py:24
  32.5 1.4 collective-permute-done.7
  33.8 3.3 %collective-permute-start.5 = (f32[8,128]{1,0:T(8,128)S(1)}, f32[8,128]{1,0:T(8,128)S(1)}, u32[]{:S(2)}, u32[]{:S(2)}) collective-permute-start(f32[8,128]{1,0:T(8,128)S(1)} %maximum_select_fusion.2), channel_id=1, source_target_pairs={{0,2},{1,3},{2,0},{3,1},{4,6},{5,7},{6,4},{7,5},{8,10},{9,11},{10,... | collective-permute-start | bytes 12296 | tf_op jit(solution)/shard_map/ppermute | solution.py:24
  37.3 2.2 %collective-permute-start.13 = (f32[160,128]{1,0:T(8,128)S(1)}, f32[160,128]{1,0:T(8,128)S(1)}, u32[]{:S(2)}, u32[]{:S(2)}) collective-permute-start(f32[160,128]{1,0:T(8,128)S(1)} %constant_dynamic-slice_fusion.1), channel_id=1, source_target_pairs={{0,32},{32,0},{1,33},{33,1},{2,34},{34,2},{3,35},{35,3},{4,36},{36... | collective-permute-start | bytes 245768 | tf_op jit(solution)/shard_map/ppermute | solution.py:24
  39.6 7.2 %collective-permute-start.10 = (f32[8,128]{1,0:T(8,128)S(1)}, f32[8,128]{1,0:T(8,128)S(1)}, u32[]{:S(2)}, u32[]{:S(2)}) collective-permute-start(f32[8,128]{1,0:T(8,128)S(1)} %maximum_select_fusion.1), channel_id=1, source_target_pairs={{0,4},{1,5},{2,6},{3,7},{4,0},{5,1},{6,2},{7,3},{8,12},{9,13},{10,... | collective-permute-start | bytes 12296 | tf_op jit(solution)/shard_map/ppermute | solution.py:24
  47.3 2.9 %fusion.26 = f32[1280,1024]{1,0:T(8,128)S(1)} fusion(bf16[256,1280]{1,0:T(8,128)(2,1)} %collective-permute-done.2.early_ref, bf16[256,640]{1,0:T(8,128)(2,1)S(1)} %get-tuple-element.99, bf16[256,640]{1,0:T(8,128)(2,1)S(1)} %get-tuple-element.98, bf16[256,1024]{1,0:T(8,128)(2,1)S(1)} %collective-permute-done.3.cotangent_ref, bf16[256,1024]{1,0:T(8,128)(2,1)S(1)} %bitcast.34), kind=kOutput, calls=%fused_computation.45 | convolution fusion | flops 1348206592 | bytes 7602176 | tf_op jit(solution)/shard_map/dot_general | solution.py:315
  53.2 4.6 %collective-permute-start.12 = (f16[160,1024]{1,0:T(8,128)(2,1)S(1)}, f16[160,1024]{1,0:T(8,128)(2,1)}, u32[]{:S(2)}, u32[]{:S(2)}) collective-permute-start(f16[160,1024]{1,0:T(8,128)(2,1)S(1)} %get-tuple-element.94), channel_id=1, source_target_pairs={{0,7},{1,2},{2,1},{3,4},{4,3},{5,6},{6,5},{7,0},{8,15},{9,10},{10,... | collective-permute-start | bytes 983048 | tf_op jit(solution)/shard_map/ppermute | solution.py:339
  57.8 3.6 %collective-permute-done.14.late_ref = bf16[256,1280]{1,0:T(8,128)(2,1)S(1)} collective-permute-done((bf16[256,1280]{1,0:T(8,128)(2,1)S(1)}, bf16[256,1280]{1,0:T(8,128)(2,1)S(1)}, u32[]{:S(2)}, u32[]{:S(2)}) %collective-permute-start.14) | collective-permute-done | bytes 655392 | tf_op jit(solution)/shard_map/ppermute | solution.py:24
  61.4 3.9 %fusion.32 = f32[1280,1024]{1,0:T(8,128)} fusion(bf16[256,1280]{1,0:T(8,128)(2,1)S(1)} %collective-permute-done.14.late_ref, bf16[256,640]{1,0:T(8,128)(2,1)S(1)} %get-tuple-element.97, bf16[256,640]{1,0:T(8,128)(2,1)S(1)} %get-tuple-element.96, bf16[256,1024]{1,0:T(8,128)(2,1)S(1)} %collective-permute-done.3.cotangent_ref, bf16[256,1024]{1,0:T(8,128)(2,1)S(1)} %bitcast.35), kind=kOutput, calls=%fused_computation.51 | convolution fusion | flops 1348206592 | bytes 7602176 | tf_op jit(solution)/shard_map/dot_general | solution.py:315
  65.3 0.9 subtract_convert_fusion
  66.2 0.8 collective-permute-start.15
  67.7 4.1 %collective-permute-done.15.refs_1_ = bf16[160,128]{1,0:T(8,128)(2,1)S(1)} collective-permute-done((bf16[160,128]{1,0:T(8,128)(2,1)S(1)}, bf16[160,128]{1,0:T(8,128)(2,1)S(1)}, u32[]{:S(2)}, u32[]{:S(2)}) %collective-permute-start.15) | collective-permute-done | bytes 40992 | tf_op jit(solution)/shard_map/ppermute | solution.py:24
  72.4 1.4 shard_map.101.refs_0_
  73.9 2.7 %dynamic-slice_multiply_fusion = (f32[160,1024]{1,0:T(8,128)S(1)}, f32[160,1024]{1,0:T(8,128)S(1)}, f32[160,1024]{1,0:T(8,128)S(1)}, f32[160,1024]{1,0:T(8,128)S(1)}) fusion(f32[1280,1024]{1,0:T(8,128)} %copy-done.2, s32[]{:T(128)S(6)} %select_n.177, f32[]{:T(128)} %bitcast.5, f16[160,1024]{1,0:T(8,128)(2,1)} %collective-permute-done.12, s32[]{:T(128)S(6)} %select_n.178, ...), kind=kLoop, calls=%fused_computation.75 | loop fusion | flops 2293760 | bytes 5898260 | tf_op jit(solution)/shard_map/mul | solution.py:333
  76.5 1.0 fusion.21
  77.7 1.0 fusion.20
  78.7 5.0 %collective-permute-start.16 = (f16[320,1024]{1,0:T(8,128)(2,1)}, f16[320,1024]{1,0:T(8,128)(2,1)}, u32[]{:S(2)}, u32[]{:S(2)}) collective-permute-start(f16[320,1024]{1,0:T(8,128)(2,1)} %fusion.20), channel_id=1, source_target_pairs={{0,7},{1,2},{2,1},{3,4},{4,3},{5,6},{6,5},{7,0},{8,15},{9,10},{10,... | collective-permute-start | bytes 1966088 | tf_op jit(solution)/shard_map/ppermute | solution.py:339
  83.7 1.6 collective-permute-start.18
  85.2 2.9 %collective-permute-start.19 = (bf16[160,256]{1,0:T(8,128)(2,1)S(1)}, bf16[160,256]{1,0:T(8,128)(2,1)S(1)}, u32[]{:S(2)}, u32[]{:S(2)}) collective-permute-start(bf16[160,256]{1,0:T(8,128)(2,1)S(1)} %copy-done.9), channel_id=1, source_target_pairs={{0,128},{64,192},{128,0},{192,64},{1,129},{65,193},{129,1},{193,65... | collective-permute-start | bytes 245768 | tf_op jit(solution)/shard_map/ppermute | solution.py:24
  88.4 3.0 %collective-permute-done.19.refs_2_ = bf16[160,256]{1,0:T(8,128)(2,1)S(1)} collective-permute-done((bf16[160,256]{1,0:T(8,128)(2,1)S(1)}, bf16[160,256]{1,0:T(8,128)(2,1)S(1)}, u32[]{:S(2)}, u32[]{:S(2)}) %collective-permute-start.19) | collective-permute-done | bytes 81952 | tf_op jit(solution)/shard_map/ppermute | solution.py:24
  91.4 2.4 %collective-permute-done.20.refs_3_ = bf16[160,256]{1,0:T(8,128)(2,1)S(1)} collective-permute-done((bf16[160,256]{1,0:T(8,128)(2,1)S(1)}, bf16[160,256]{1,0:T(8,128)(2,1)S(1)}, u32[]{:S(2)}, u32[]{:S(2)}) %collective-permute-start.20) | collective-permute-done | bytes 81952 | tf_op jit(solution)/shard_map/ppermute | solution.py:24
  94.4 1.8 %shard_map.102.refs_0_ = bf16[160,1024]{1,0:T(8,128)(2,1)} custom-call(s32[1]{0:T(128)} %bitcast.11.here_ref, bf16[160,256]{1,0:T(8,128)(2,1)} %shard_map.101.refs_0_, bf16[160,256]{1,0:T(8,128)(2,1)} %copy-done.13, bf16[160,256]{1,0:T(8,128)(2,1)} %copy-done.14, bf16[160,256]{1,0:T(8,128)(2,1)} %copy-done.15), custom_call_target="tpu_custom_call" | custom-call | tf_op jit(solution)/shard_map/pallas_call | solution.py:106
  96.2 8.2 %shard_map.103 = bf16[272,3584]{1,0:T(8,128)(2,1)} custom-call(s32[1]{0:T(128)} %bitcast.9.z_ref, bf16[256,1280]{1,0:T(8,128)(2,1)} %collective-permute-done.2.early_ref, bf16[256,1280]{1,0:T(8,128)(2,1)} %copy-done.6, bf16[256,1024]{1,0:T(8,128)(2,1)} %copy-done.8, bf16[2560,1024]{1,0:T(8,128)(2,1)} %bitcast.29), custom_call_target="tpu_custom_call" | custom-call | tf_op jit(solution)/shard_map/pallas_call | solution.py:159
  104.4 1.5 collective-permute-start.21
  105.9 3.1 %fusion.22 = f16[320,1024]{1,0:T(8,128)(2,1)} fusion(f16[320,1024]{1,0:T(8,128)(2,1)S(1)} %collective-permute-done.17, f32[1280,1024]{1,0:T(8,128)} %fusion.32, s32[]{:T(128)S(6)} %select_n.162, f32[]{:T(128)} %bitcast.5), kind=kLoop, calls=%fused_computation.41 | loop fusion | flops 2949120 | bytes 2621448 | tf_op jit(solution)/shard_map/convert_element_type | solution.py:55
  109.0 3.4 %fusion.23 = f16[320,1024]{1,0:T(8,128)(2,1)} fusion(f16[320,1024]{1,0:T(8,128)(2,1)} %collective-permute-done.16, f32[1280,1024]{1,0:T(8,128)} %copy-done.2, s32[]{:T(128)S(6)} %select_n.162, f32[]{:T(128)} %bitcast.5), kind=kLoop, calls=%fused_computation.42 | loop fusion | flops 2949120 | bytes 2621448 | tf_op jit(solution)/shard_map/convert_element_type | solution.py:55
  112.4 2.0 %collective-permute-start.23 = (f16[320,1024]{1,0:T(8,128)(2,1)}, f16[320,1024]{1,0:T(8,128)(2,1)}, u32[]{:S(2)}, u32[]{:S(2)}) collective-permute-start(f16[320,1024]{1,0:T(8,128)(2,1)} %fusion.22), channel_id=1, source_target_pairs={{0,7},{1,2},{2,1},{3,4},{4,3},{5,6},{6,5},{7,0},{8,15},{9,10},{10,... | collective-permute-start | bytes 1966088 | tf_op jit(solution)/shard_map/ppermute | solution.py:339
  114.9 7.0 %shard_map.104 = (f32[256,1024]{1,0:T(8,128)}, bf16[256,5120]{1,0:T(8,128)(2,1)}) custom-call(s32[1]{0:T(128)} %bitcast.12._, bf16[256,5120]{1,0:T(8,128)(2,1)} %bitcast.25, bf16[256,1024]{1,0:T(8,128)(2,1)} %bitcast.32, bf16[2560,1024]{1,0:T(8,128)(2,1)} %bitcast.30), custom_call_target="tpu_custom_call" | custom-call | tf_op jit(solution)/shard_map/pallas_call | solution.py:192
  122.6 1.6 shard_map.105
  124.2 0.7 copy-done.10
  124.9 2.0 %shard_map.106 = bf16[320,1024]{1,0:T(8,128)(2,1)} custom-call(s32[1]{0:T(128)} %bitcast.13.here_ref, bf16[160,1024]{1,0:T(8,128)(2,1)} %shard_map.102.refs_0_, bf16[160,1024]{1,0:T(8,128)(2,1)} %copy-done.10), custom_call_target="tpu_custom_call" | custom-call | tf_op jit(solution)/shard_map/pallas_call | solution.py:106
  126.9 5.0 %fusion.25 = (f16[320,1024]{1,0:T(8,128)(2,1)}, f16[320,1024]{1,0:T(8,128)(2,1)}) fusion(f16[320,1024]{1,0:T(8,128)(2,1)S(1)} %collective-permute-done.22, f32[1280,1024]{1,0:T(8,128)} %fusion.32, s32[]{:T(128)S(6)} %select_n.177, f32[]{:T(128)} %bitcast.5, f16[320,1024]{1,0:T(8,128)(2,1)} %collective-permute-done.23, s32[]{:T(128)S(6)} %select_n.164), kind=kLoop, calls=%fused_computation.44 | loop fusion | flops 5898240 | bytes 5242892 | tf_op jit(solution)/shard_map/convert_element_type | solution.py:55
  131.9 1.0 collective-permute-start.26
  133.1 0.8 copy.14
  133.8 11.0 %collective-permute-done.21.coded_ref.back_ref = bf16[272,3584]{1,0:T(8,128)(2,1)S(1)} collective-permute-done((bf16[272,3584]{1,0:T(8,128)(2,1)}, bf16[272,3584]{1,0:T(8,128)(2,1)S(1)}, u32[]{:S(2)}, u32[]{:S(2)}) %collective-permute-start.21) | collective-permute-done | bytes 1949728 | tf_op jit(solution)/shard_map/ppermute | solution.py:24
  144.8 1.3 copy-done.1
  146.1 5.1 %shard_map.107 = (bf16[256,1024]{1,0:T(8,128)(2,1)}, bf16[256,5120]{1,0:T(8,128)(2,1)}) custom-call(s32[1]{0:T(128)} %bitcast._, bf16[256,5120]{1,0:T(8,128)(2,1)} %get-tuple-element.70.__, f32[256,1024]{1,0:T(8,128)} %get-tuple-element.71.keys_ref, bf16[272,3584]{1,0:T(8,128)(2,1)} %copy-done.1, ...), custom_call_target="tpu_custom_call", output_to_operand_aliasing={{1}: (1, {})} | custom-call | tf_op jit(solution)/shard_map/pallas_call | solution.py:227
  151.2 4.0 %fusion.46 = bf16[1,320,1024]{2,1,0:T(8,128)(2,1)} fusion(f32[]{:T(128)} %bitcast.16, f16[320,1024]{1,0:T(8,128)(2,1)} %collective-permute-done.27, f16[320,1024]{1,0:T(8,128)(2,1)S(1)} %collective-permute-done.26, f32[]{:T(128)} %bitcast.5, f32[1280,1024]{1,0:T(8,128)} %fusion.32, s32[]{:T(128)S(6)} %select_n.165), kind=kLoop, calls=%fused_computation.78 | loop fusion | flops 4259840 | bytes 3276812 | tf_op jit(solution)/shard_map/broadcast_in_dim | solution.py:411
  (93 shorter events, 10.9 us)
Async XLA Ops:
  7.2 2.8 %copy-start.3 = (bf16[1,256,1024]{2,1,0:T(8,128)(2,1)S(1)}, bf16[1,256,1024]{2,1,0:T(8,128)(2,1)}, u32[]{:S(2)}) copy-start(bf16[1,256,1024]{2,1,0:T(8,128)(2,1)} %param.8) | copy-start | bytes 1572868
  7.2 89.0 %all-gather.3.cloned.1.call-start = ((), (), s32[]{:S(2)}) async-start(), calls=%async_computation | async-start | bytes 5898240 | tf_op jit(solution)/shard_map/all_gather | solution.py:275
  9.9 9.3 %collective-permute-start.1 = (f32[160,1024]{1,0:T(8,128)}, f32[160,1024]{1,0:T(8,128)}, u32[]{:S(2)}, u32[]{:S(2)}) collective-permute-start(f32[160,1024]{1,0:T(8,128)} %dynamic-slice_bitcast_fusion), channel_id=1, source_target_pairs={{0,16},{16,0},{1,17},{17,1},{2,18},{18,2},{3,19},{19,3},{4,20},{20... | collective-permute-start | bytes 1966088 | tf_op jit(solution)/shard_map/ppermute | solution.py:24
  11.2 6.1 %copy-start = (bf16[1,256,5120]{2,1,0:T(8,128)(2,1)S(1)}, bf16[1,256,5120]{2,1,0:T(8,128)(2,1)}, u32[]{:S(2)}) copy-start(bf16[1,256,5120]{2,1,0:T(8,128)(2,1)} %param.6) | copy-start | bytes 7864324
  15.0 10.9 %collective-permute-start = (f32[8,128]{1,0:T(8,128)S(1)}, f32[8,128]{1,0:T(8,128)S(1)}, u32[]{:S(2)}, u32[]{:S(2)}) collective-permute-start(f32[8,128]{1,0:T(8,128)S(1)} %iota.32), channel_id=1, source_target_pairs={{0,8},{8,0},{1,9},{9,1},{2,10},{10,2},{3,11},{11,3},{4,12},{12,4},... | collective-permute-start | bytes 12296 | tf_op jit(solution)/shard_map/ppermute | solution.py:24
  17.3 1.1 copy-start.11
  18.3 29.0 %collective-permute-start.2 = (bf16[256,1280]{1,0:T(8,128)(2,1)}, bf16[256,1280]{1,0:T(8,128)(2,1)}, u32[]{:S(2)}, u32[]{:S(2)}) collective-permute-start(bf16[256,1280]{1,0:T(8,128)(2,1)} %pad_maximum_fusion.3), channel_id=1, source_target_pairs={{0,8},{8,0},{1,9},{9,1},{2,10},{10,2},{3,11},{11,3},{4,12},{12,4},... | collective-permute-start | bytes 1966088 | tf_op jit(solution)/shard_map/ppermute | solution.py:24
  18.6 11.8 %collective-permute-start.9 = (f32[160,64]{1,0:T(8,128)S(1)}, f32[160,64]{1,0:T(8,128)S(1)}, u32[]{:S(2)}, u32[]{:S(2)}) collective-permute-start(f32[160,64]{1,0:T(8,128)S(1)} %copy.15), channel_id=1, source_target_pairs={{0,16},{16,0},{1,17},{17,1},{2,18},{18,2},{3,19},{19,3},{4,20},{20... | collective-permute-start | bytes 122888 | tf_op jit(solution)/shard_map/ppermute | solution.py:24
  19.1 1.3 copy-start.4
  21.7 10.7 %collective-permute-start.6 = (f32[160,256]{1,0:T(8,128)S(1)}, f32[160,256]{1,0:T(8,128)S(1)}, u32[]{:S(2)}, u32[]{:S(2)}) collective-permute-start(f32[160,256]{1,0:T(8,128)S(1)} %get-tuple-element.106), channel_id=1, source_target_pairs={{0,64},{64,0},{128,192},{192,128},{1,65},{65,1},{129,193},{193,129... | collective-permute-start | bytes 491528 | tf_op jit(solution)/shard_map/ppermute | solution.py:24
  22.9 11.0 %collective-permute-start.7 = (f32[160,256]{1,0:T(8,128)S(1)}, f32[160,256]{1,0:T(8,128)S(1)}, u32[]{:S(2)}, u32[]{:S(2)}) collective-permute-start(f32[160,256]{1,0:T(8,128)S(1)} %get-tuple-element.105), channel_id=1, source_target_pairs={{0,128},{64,192},{128,0},{192,64},{1,129},{65,193},{129,1},{193,65... | collective-permute-start | bytes 491528 | tf_op jit(solution)/shard_map/ppermute | solution.py:24
  26.0 3.7 %collective-permute-start.4 = (f32[8,128]{1,0:T(8,128)S(1)}, f32[8,128]{1,0:T(8,128)S(1)}, u32[]{:S(2)}, u32[]{:S(2)}) collective-permute-start(f32[8,128]{1,0:T(8,128)S(1)} %maximum_select_fusion.3), channel_id=1, source_target_pairs={{0,1},{1,0},{2,3},{3,2},{4,5},{5,4},{6,7},{7,6},{8,9},{9,8},{10,11... | collective-permute-start | bytes 12296 | tf_op jit(solution)/shard_map/ppermute | solution.py:24
  29.7 7.5 %collective-permute-start.8 = (f32[160,256]{1,0:T(8,128)S(1)}, f32[160,256]{1,0:T(8,128)S(1)}, u32[]{:S(2)}, u32[]{:S(2)}) collective-permute-start(f32[160,256]{1,0:T(8,128)S(1)} %get-tuple-element.104), channel_id=1, source_target_pairs={{0,192},{64,128},{128,64},{192,0},{1,193},{65,129},{129,65},{193,1... | collective-permute-start | bytes 491528 | tf_op jit(solution)/shard_map/ppermute | solution.py:24
  30.4 16.9 %collective-permute-start.3 = (bf16[256,1024]{1,0:T(8,128)(2,1)S(1)}, bf16[256,1024]{1,0:T(8,128)(2,1)S(1)}, u32[]{:S(2)}, u32[]{:S(2)}) collective-permute-start(bf16[256,1024]{1,0:T(8,128)(2,1)S(1)} %bitcast.33), channel_id=1, source_target_pairs={{0,8},{8,0},{1,9},{9,1},{2,10},{10,2},{3,11},{11,3},{4,12},{12,4},... | collective-permute-start | bytes 1572872 | tf_op jit(solution)/shard_map/ppermute | solution.py:24
  32.3 29.1 %collective-permute-start.14 = (bf16[256,1280]{1,0:T(8,128)(2,1)S(1)}, bf16[256,1280]{1,0:T(8,128)(2,1)S(1)}, u32[]{:S(2)}, u32[]{:S(2)}) collective-permute-start(bf16[256,1280]{1,0:T(8,128)(2,1)S(1)} %pad_maximum_fusion.4), channel_id=1, source_target_pairs={{0,8},{8,0},{1,9},{9,1},{2,10},{10,2},{3,11},{11,3},{4,12},{12,4},... | collective-permute-start | bytes 1966088 | tf_op jit(solution)/shard_map/ppermute | solution.py:24
  33.8 5.7 %collective-permute-start.5 = (f32[8,128]{1,0:T(8,128)S(1)}, f32[8,128]{1,0:T(8,128)S(1)}, u32[]{:S(2)}, u32[]{:S(2)}) collective-permute-start(f32[8,128]{1,0:T(8,128)S(1)} %maximum_select_fusion.2), channel_id=1, source_target_pairs={{0,2},{1,3},{2,0},{3,1},{4,6},{5,7},{6,4},{7,5},{8,10},{9,11},{10,... | collective-permute-start | bytes 12296 | tf_op jit(solution)/shard_map/ppermute | solution.py:24
  37.3 27.9 %collective-permute-start.13 = (f32[160,128]{1,0:T(8,128)S(1)}, f32[160,128]{1,0:T(8,128)S(1)}, u32[]{:S(2)}, u32[]{:S(2)}) collective-permute-start(f32[160,128]{1,0:T(8,128)S(1)} %constant_dynamic-slice_fusion.1), channel_id=1, source_target_pairs={{0,32},{32,0},{1,33},{33,1},{2,34},{34,2},{3,35},{35,3},{4,36},{36... | collective-permute-start | bytes 245768 | tf_op jit(solution)/shard_map/ppermute | solution.py:24
  39.6 10.6 %collective-permute-start.10 = (f32[8,128]{1,0:T(8,128)S(1)}, f32[8,128]{1,0:T(8,128)S(1)}, u32[]{:S(2)}, u32[]{:S(2)}) collective-permute-start(f32[8,128]{1,0:T(8,128)S(1)} %maximum_select_fusion.1), channel_id=1, source_target_pairs={{0,4},{1,5},{2,6},{3,7},{4,0},{5,1},{6,2},{7,3},{8,12},{9,13},{10,... | collective-permute-start | bytes 12296 | tf_op jit(solution)/shard_map/ppermute | solution.py:24
  47.3 14.0 %copy-start.8 = (bf16[256,1024]{1,0:T(8,128)(2,1)}, bf16[256,1024]{1,0:T(8,128)(2,1)S(1)}, u32[]{:S(2)}) copy-start(bf16[256,1024]{1,0:T(8,128)(2,1)S(1)} %collective-permute-done.3.cotangent_ref) | copy-start | bytes 1572868
  50.2 15.1 %copy-start.2 = (f32[1280,1024]{1,0:T(8,128)}, f32[1280,1024]{1,0:T(8,128)S(1)}, u32[]{:S(2)}) copy-start(f32[1280,1024]{1,0:T(8,128)S(1)} %fusion.26) | copy-start | bytes 15728644
  52.6 21.3 %collective-permute-start.11 = (f16[160,1024]{1,0:T(8,128)(2,1)S(1)}, f16[160,1024]{1,0:T(8,128)(2,1)S(1)}, u32[]{:S(2)}, u32[]{:S(2)}) collective-permute-start(f16[160,1024]{1,0:T(8,128)(2,1)S(1)} %get-tuple-element.95), channel_id=1, source_target_pairs={{0,1},{1,0},{2,3},{3,2},{4,5},{5,4},{6,7},{7,6},{8,9},{9,8},{10,11... | collective-permute-start | bytes 983048 | tf_op jit(solution)/shard_map/ppermute | solution.py:339
  53.2 20.7 %collective-permute-start.12 = (f16[160,1024]{1,0:T(8,128)(2,1)S(1)}, f16[160,1024]{1,0:T(8,128)(2,1)}, u32[]{:S(2)}, u32[]{:S(2)}) collective-permute-start(f16[160,1024]{1,0:T(8,128)(2,1)S(1)} %get-tuple-element.94), channel_id=1, source_target_pairs={{0,7},{1,2},{2,1},{3,4},{4,3},{5,6},{6,5},{7,0},{8,15},{9,10},{10,... | collective-permute-start | bytes 983048 | tf_op jit(solution)/shard_map/ppermute | solution.py:339
  61.4 3.9 %copy-start.6 = (bf16[256,1280]{1,0:T(8,128)(2,1)}, bf16[256,1280]{1,0:T(8,128)(2,1)S(1)}, u32[]{:S(2)}) copy-start(bf16[256,1280]{1,0:T(8,128)(2,1)S(1)} %collective-permute-done.14.late_ref) | copy-start | bytes 1966084
  66.2 5.6 %copy-start.12 = (bf16[160,128]{1,0:T(8,128)(2,1)}, bf16[160,128]{1,0:T(8,128)(2,1)S(1)}, u32[]{:S(2)}) copy-start(bf16[160,128]{1,0:T(8,128)(2,1)S(1)} %get-tuple-element.86.refs_0_) | copy-start | bytes 122884
  66.2 5.6 %collective-permute-start.15 = (bf16[160,128]{1,0:T(8,128)(2,1)S(1)}, bf16[160,128]{1,0:T(8,128)(2,1)S(1)}, u32[]{:S(2)}, u32[]{:S(2)}) collective-permute-start(bf16[160,128]{1,0:T(8,128)(2,1)S(1)} %get-tuple-element.86.refs_0_), channel_id=1, source_target_pairs={{0,32},{32,0},{1,33},{33,1},{2,34},{34,2},{3,35},{35,3},{4,36},{36... | collective-permute-start | bytes 122888 | tf_op jit(solution)/shard_map/ppermute | solution.py:24
  71.8 0.6 copy-start.17
  77.5 6.1 %copy-start.9 = (bf16[160,256]{1,0:T(8,128)(2,1)S(1)}, bf16[160,256]{1,0:T(8,128)(2,1)}, u32[]{:S(2)}) copy-start(bf16[160,256]{1,0:T(8,128)(2,1)} %shard_map.101.refs_0_) | copy-start | bytes 245764
  77.5 28.4 %collective-permute-start.17 = (f16[320,1024]{1,0:T(8,128)(2,1)}, f16[320,1024]{1,0:T(8,128)(2,1)S(1)}, u32[]{:S(2)}, u32[]{:S(2)}) collective-permute-start(f16[320,1024]{1,0:T(8,128)(2,1)} %fusion.21), channel_id=1, source_target_pairs={{0,1},{1,0},{2,3},{3,2},{4,5},{5,4},{6,7},{7,6},{8,9},{9,8},{10,11... | collective-permute-start | bytes 1966088 | tf_op jit(solution)/shard_map/ppermute | solution.py:339
  78.7 30.3 %collective-permute-start.16 = (f16[320,1024]{1,0:T(8,128)(2,1)}, f16[320,1024]{1,0:T(8,128)(2,1)}, u32[]{:S(2)}, u32[]{:S(2)}) collective-permute-start(f16[320,1024]{1,0:T(8,128)(2,1)} %fusion.20), channel_id=1, source_target_pairs={{0,7},{1,2},{2,1},{3,4},{4,3},{5,6},{6,5},{7,0},{8,15},{9,10},{10,... | collective-permute-start | bytes 1966088 | tf_op jit(solution)/shard_map/ppermute | solution.py:339
  83.7 4.7 %collective-permute-start.18 = (bf16[160,256]{1,0:T(8,128)(2,1)S(1)}, bf16[160,256]{1,0:T(8,128)(2,1)S(1)}, u32[]{:S(2)}, u32[]{:S(2)}) collective-permute-start(bf16[160,256]{1,0:T(8,128)(2,1)S(1)} %copy-done.9), channel_id=1, source_target_pairs={{0,64},{64,0},{128,192},{192,128},{1,65},{65,1},{129,193},{193,129... | collective-permute-start | bytes 245768 | tf_op jit(solution)/shard_map/ppermute | solution.py:24
  85.2 6.2 %collective-permute-start.19 = (bf16[160,256]{1,0:T(8,128)(2,1)S(1)}, bf16[160,256]{1,0:T(8,128)(2,1)S(1)}, u32[]{:S(2)}, u32[]{:S(2)}) collective-permute-start(bf16[160,256]{1,0:T(8,128)(2,1)S(1)} %copy-done.9), channel_id=1, source_target_pairs={{0,128},{64,192},{128,0},{192,64},{1,129},{65,193},{129,1},{193,65... | collective-permute-start | bytes 245768 | tf_op jit(solution)/shard_map/ppermute | solution.py:24
  88.1 5.7 %collective-permute-start.20 = (bf16[160,256]{1,0:T(8,128)(2,1)S(1)}, bf16[160,256]{1,0:T(8,128)(2,1)S(1)}, u32[]{:S(2)}, u32[]{:S(2)}) collective-permute-start(bf16[160,256]{1,0:T(8,128)(2,1)S(1)} %copy-done.9), channel_id=1, source_target_pairs={{0,192},{64,128},{128,64},{192,0},{1,193},{65,129},{129,65},{193,1... | collective-permute-start | bytes 245768 | tf_op jit(solution)/shard_map/ppermute | solution.py:24
  88.4 5.4 %copy-start.13 = (bf16[160,256]{1,0:T(8,128)(2,1)}, bf16[160,256]{1,0:T(8,128)(2,1)S(1)}, u32[]{:S(2)}) copy-start(bf16[160,256]{1,0:T(8,128)(2,1)S(1)} %collective-permute-done.18.refs_1_) | copy-start | bytes 245764
  91.4 2.4 %copy-start.14 = (bf16[160,256]{1,0:T(8,128)(2,1)}, bf16[160,256]{1,0:T(8,128)(2,1)S(1)}, u32[]{:S(2)}) copy-start(bf16[160,256]{1,0:T(8,128)(2,1)S(1)} %collective-permute-done.19.refs_2_) | copy-start | bytes 245764
  93.8 0.6 copy-start.15
  104.4 40.4 %collective-permute-start.21 = (bf16[272,3584]{1,0:T(8,128)(2,1)}, bf16[272,3584]{1,0:T(8,128)(2,1)S(1)}, u32[]{:S(2)}, u32[]{:S(2)}) collective-permute-start(bf16[272,3584]{1,0:T(8,128)(2,1)} %shard_map.103), channel_id=1, source_target_pairs={{0,8},{8,0},{1,9},{9,1},{2,10},{10,2},{3,11},{11,3},{4,12},{12,4},... | collective-permute-start | bytes 5849096 | tf_op jit(solution)/shard_map/ppermute | solution.py:24
  109.0 5.4 %copy-start.5 = (bf16[160,1024]{1,0:T(8,128)(2,1)S(1)}, bf16[160,1024]{1,0:T(8,128)(2,1)}, u32[]{:S(2)}) copy-start(bf16[160,1024]{1,0:T(8,128)(2,1)} %shard_map.102.refs_0_) | copy-start | bytes 983044
  112.4 14.5 %collective-permute-start.22 = (f16[320,1024]{1,0:T(8,128)(2,1)}, f16[320,1024]{1,0:T(8,128)(2,1)S(1)}, u32[]{:S(2)}, u32[]{:S(2)}) collective-permute-start(f16[320,1024]{1,0:T(8,128)(2,1)} %fusion.23), channel_id=1, source_target_pairs={{0,1},{1,0},{2,3},{3,2},{4,5},{5,4},{6,7},{7,6},{8,9},{9,8},{10,11... | collective-permute-start | bytes 1966088 | tf_op jit(solution)/shard_map/ppermute | solution.py:339
  112.4 14.5 %collective-permute-start.23 = (f16[320,1024]{1,0:T(8,128)(2,1)}, f16[320,1024]{1,0:T(8,128)(2,1)}, u32[]{:S(2)}, u32[]{:S(2)}) collective-permute-start(f16[320,1024]{1,0:T(8,128)(2,1)} %fusion.22), channel_id=1, source_target_pairs={{0,7},{1,2},{2,1},{3,4},{4,3},{5,6},{6,5},{7,0},{8,15},{9,10},{10,... | collective-permute-start | bytes 1966088 | tf_op jit(solution)/shard_map/ppermute | solution.py:339
  114.4 9.8 %collective-permute-start.24 = (bf16[160,1024]{1,0:T(8,128)(2,1)S(1)}, bf16[160,1024]{1,0:T(8,128)(2,1)S(1)}, u32[]{:S(2)}, u32[]{:S(2)}) collective-permute-start(bf16[160,1024]{1,0:T(8,128)(2,1)S(1)} %copy-done.5), channel_id=1, source_target_pairs={{0,16},{16,0},{1,17},{17,1},{2,18},{18,2},{3,19},{19,3},{4,20},{20... | collective-permute-start | bytes 983048 | tf_op jit(solution)/shard_map/ppermute | solution.py:24
  114.4 7.6 %collective-permute-start.25 = (f32[160,64]{1,0:T(8,128)S(1)}, f32[160,64]{1,0:T(8,128)S(1)}, u32[]{:S(2)}, u32[]{:S(2)}) collective-permute-start(f32[160,64]{1,0:T(8,128)S(1)} %get-tuple-element.111), channel_id=1, source_target_pairs={{0,16},{16,0},{1,17},{17,1},{2,18},{18,2},{3,19},{19,3},{4,20},{20... | collective-permute-start | bytes 122888 | tf_op jit(solution)/shard_map/ppermute | solution.py:24
  122.0 0.6 copy-start.16
  124.2 0.7 copy-start.10
  126.9 6.2 %copy-start.7 = (f32[320,64]{1,0:T(8,128)S(1)}, f32[320,64]{1,0:T(8,128)}, u32[]{:S(2)}) copy-start(f32[320,64]{1,0:T(8,128)} %shard_map.105) | copy-start | bytes 245764
  131.9 19.3 %collective-permute-start.26 = (f16[320,1024]{1,0:T(8,128)(2,1)}, f16[320,1024]{1,0:T(8,128)(2,1)S(1)}, u32[]{:S(2)}, u32[]{:S(2)}) collective-permute-start(f16[320,1024]{1,0:T(8,128)(2,1)} %get-tuple-element.89), channel_id=1, source_target_pairs={{0,1},{1,0},{2,3},{3,2},{4,5},{5,4},{6,7},{7,6},{8,9},{9,8},{10,11... | collective-permute-start | bytes 1966088 | tf_op jit(solution)/shard_map/ppermute | solution.py:400
  132.8 18.4 %collective-permute-start.27 = (f16[320,1024]{1,0:T(8,128)(2,1)}, f16[320,1024]{1,0:T(8,128)(2,1)}, u32[]{:S(2)}, u32[]{:S(2)}) collective-permute-start(f16[320,1024]{1,0:T(8,128)(2,1)} %get-tuple-element.88), channel_id=1, source_target_pairs={{0,7},{1,2},{2,1},{3,4},{4,3},{5,6},{6,5},{7,0},{8,15},{9,10},{10,... | collective-permute-start | bytes 1966088 | tf_op jit(solution)/shard_map/ppermute | solution.py:400
  144.8 1.3 copy-start.1
Sparse Core Ops, SparseCore 0:
  9.8 76.4 all-gather.2

commit v7 on v6

--- a/solution.py
+++ b/solution.py
@@ -117,6 +117,42 @@
 
 
 TOP = 220.0
+
+
+def lay_chunks(z, chunks, halves):
+    size = chunks[0][0].shape[0]
+    count = N_Z
+    pieces = [(c, d, 0) for c, d in chunks]
+    pieces += [(h, 4, k * (size // 2)) for k, h in enumerate(halves)]
+
+    def body(z_ref, *refs):
+        *piece_refs, out_ref, sems = refs
+        here = z_ref[0]
+        sign = 1 - 2 * (here % 2)
+        copies = []
+        for k, (ref, (piece, distance, offset)) in enumerate(zip(piece_refs, pieces)):
+            start = (here + count + distance * sign) % count * size + offset
+            at = pl.ds(pl.multiple_of(start, 32), piece.shape[0])
+            copies.append(pltpu.make_async_copy(ref, out_ref.at[at, :], sems.at[k]))
+        for copy in copies:
+            copy.start()
+        for copy in copies:
+            copy.wait()
+
+    hbm = pl.BlockSpec(memory_space=pl.ANY)
+    first = chunks[0][0]
+    return pl.pallas_call(
+        body,
+        grid_spec=pltpu.PrefetchScalarGridSpec(
+            num_scalar_prefetch=1,
+            grid=(1,),
+            in_specs=[hbm] * len(pieces),
+            out_specs=hbm,
+            scratch_shapes=[pltpu.SemaphoreType.DMA((len(pieces),))],
+        ),
+        out_shape=jax.ShapeDtypeStruct((count * size, first.shape[1]), first.dtype),
+        cost_estimate=FREE,
+    )(z.reshape(1), *(p for p, _, _ in pieces))
 
 
 def products_for_partner(z, early, late, cotangent, weight):
@@ -272,7 +308,18 @@
         parts = [columns_of(array, side * half + g * 2 * chunk, 2 * chunk) for g in groups]
         return jnp.concatenate(parts, axis=1)
 
-    weight_half = lax.all_gather(weight, "z", axis=0, tiled=True)
+    def pass_on(even, odd):
+        return lax.ppermute(odd, "z", EVEN), lax.ppermute(even, "z", ODD)
+
+    chunks = [(weight, 0)]
+    weight_even, weight_odd = pass_on(weight, weight)
+
+    def arrived(distance, even, odd):
+        even, odd = order.step(even, odd)
+        order.did(even, odd)
+        chunks.extend([(even, distance), (odd, -distance)])
+        return even, odd
+
     cotangent_other = swap(cotangent, "xl")
 
     give = rows_of(pseudo, theirs, rows)
@@ -284,6 +331,7 @@
     sent = token_columns(order.step(tokens), 1 - x, early)
     order.did(sent)
     early_other = swap(sent, "xl")
+    weight_even, weight_odd = pass_on(*arrived(1, weight_even, weight_odd))
     pseudo_other = order.step(pseudo_other)
     total = rows_of(pseudo, mine, rows) + pseudo_other
     gives = [columns_of(total, (y ^ m) * quarter, quarter) for m in (1, 2, 3)]
@@ -302,6 +350,7 @@
     peaks = join_peaks(peaks, order.step(peaks_other))
     order.did(peaks)
     peaks_other = swap(peaks, "z", 2)
+    weight_even, weight_odd = pass_on(*arrived(2, weight_even, weight_odd))
     *others, old_other = order.step(*others, old_other)
     summed = columns_of(total, y * quarter, quarter) + others[0] + others[1] + others[2]
     give = columns_of(summed, (1 - xh) * pair, pair)
@@ -322,6 +371,9 @@
     early_other, cotangent_other = order.step(early_other, cotangent_other)
     partial_early = product(early_mine, early_other)
     order.did(partial_early)
+    weight_even, weight_odd = arrived(3, weight_even, weight_odd)
+    top = weight.shape[0] // 2
+    halves = pass_on(weight_even[top:], weight_odd[:top])
     peaks = join_peaks(peaks, order.step(peaks_other))
     bound = jnp.maximum(peaks[0, 0] * peaks[4, 0], 1e-32)
     scale, back = 240.0 / bound, bound / (64.0 * 240.0)
@@ -351,6 +403,8 @@
     late_mine = token_columns(tokens, x, late)
     partial_late = product(late_mine, late_other)
     order.did(partial_late)
+    halves = order.step(*halves)
+    order.did(*halves)
 
     summed_other = order.step(summed_other)
     average = (columns_of(summed, xh * pair, pair) + summed_other) / 16
@@ -364,26 +418,28 @@
     updated_other = swap(updated, "xh")
     new_other = swap(give, "c")
 
-    updated_other = order.step(updated_other)
-    wide = assemble(xh, lambda i: (i, 1 - i), (updated, updated_other), 1)
-    order.did(wide)
-    wides = [swap(wide, "y", m) for m in (1, 2, 3)]
-
     far_even, far_odd = order.step(far_even, far_odd)
     odd = jnp.concatenate([own(-3, 0, part) + decode(far_even), own(-3, part, part)])
     odd = send(odd, ODD)
     even = jnp.concatenate([own(3, 0, part), own(3, part, part) + decode(far_odd)])
     even = send(even, EVEN)
 
+    weight_half = lay_chunks(z, chunks, halves)
+    order.did(weight_half)
+    updated_other = order.step(updated_other)
+    wide = assemble(xh, lambda i: (i, 1 - i), (updated, updated_other), 1)
+    order.did(wide)
+    wides = [swap(wide, "y", m) for m in (1, 2, 3)]
+
+    early_held = order.step(early_other)
+    sent = products_for_partner(z, early_held, late_other, cotangent_other, weight_half)
+    order.did(sent)
+    products_back = swap(sent, "xl")
+
     wides = order.step(*wides)
     block = assemble(y, lambda i: (i, i ^ 1, i ^ 2, i ^ 3), (wide, *wides), 1)
     order.did(block)
     block_other = swap(block, "c")
-
-    weight_half = order.step(weight_half)
-    sent = products_for_partner(z, early_other, late_other, cotangent_other, weight_half)
-    order.did(sent)
-    products_back = swap(sent, "xl")
 
     even, odd = ring_step(2, even, odd)
 

time: 164 us -> 325 us (1.98)
  Pallas kernels: 27.1 us -> 187 us
  waiting for transfers between devices: 28.5 us -> 45.4 us
  between operations: 16.4 us -> 3.16 us
    pallas_call x0 -> x1, Pallas kernels: none -> 160 us  [lay_chunks(): pl.pallas_call(body, grid_spec=pltpu.PrefetchScalarGridSpec(num_scalar_pr...]
    ppermute x0 -> x8, starting transfers between devices: none -> 13.5 us  [pass_on(): return (lax.ppermute(odd, 'z', EVEN), lax.ppermute(even, 'z', ODD))]
    ppermute x2, waiting for transfers between devices: 0.01 us -> 10 us  [shards(): even, odd = (lax.ppermute(even, 'z', EVEN), lax.ppermute(odd, 'z', ODD))]
    ppermute x0 -> x8, waiting for transfers between devices: none -> 9.08 us  [pass_on(): return (lax.ppermute(odd, 'z', EVEN), lax.ppermute(even, 'z', ODD))]
    ppermute x20, waiting for transfers between devices: 27.8 us -> 21.8 us  [swap(): lax.ppermute(value, axis, [(i, i ^ mask) for i in range(SIZES[axis])])]
    ppermute x6, starting transfers between devices: 12.4 us -> 6.83 us  [send(): return lax.ppermute(message, 'z', pairs)]
    ppermute x20, starting transfers between devices: 31.6 us -> 26.4 us  [swap(): lax.ppermute(value, axis, [(i, i ^ mask) for i in range(SIZES[axis])])]
    ppermute x6, waiting for transfers between devices: 0.02 us -> 4.58 us  [send(): return lax.ppermute(message, 'z', pairs)]
  transfers between devices with their start and end apart: 29 -> 36, of which waited for: 9 -> 11; matrix products, arithmetic and copies ran while one was open for 22% -> 9% of each run, Pallas kernels for 17% -> 58%
where the time goes in v7:
time: 325 us; the launch traced here: 324 us
  Pallas kernels  187 us (58%)
  starting transfers between devices  47.7 us (15%)
  waiting for transfers between devices  45.4 us (14%)
  other arithmetic  26.1 us (8%)
  local copies, waits for them, and re-layouts  9.02 us (3%)
  matrix products  5.48 us (2%)
    pallas_call x1, Pallas kernels, lay_chunks(): pl.pallas_call(body, grid_spec=pltpu.PrefetchScalarGridSpec(num_scalar_pr...  160 us
    ppermute x20, starting transfers between devices, swap(): lax.ppermute(value, axis, [(i, i ^ mask) for i in range(SIZES[axis])])  26.4 us
    ppermute x20, waiting for transfers between devices, swap(): lax.ppermute(value, axis, [(i, i ^ mask) for i in range(SIZES[axis])])  21.8 us
    convert_element_type x6, other arithmetic, encode(): return (scaled * jnp.abs(scaled)).astype(F16)  13.6 us
    ppermute x8, starting transfers between devices, pass_on(): return (lax.ppermute(odd, 'z', EVEN), lax.ppermute(even, 'z', ODD))  13.5 us
    ppermute x2, waiting for transfers between devices, shards(): even, odd = (lax.ppermute(even, 'z', EVEN), lax.ppermute(odd, 'z', ODD))  10 us
    ppermute x8, waiting for transfers between devices, pass_on(): return (lax.ppermute(odd, 'z', EVEN), lax.ppermute(even, 'z', ODD))  9.08 us
    pallas_call x1, Pallas kernels, products_for_partner(): pl.pallas_call(body, grid_spec=pltpu.PrefetchScalarGridSpec(num_scalar_pr...  8.17 us
  transfers between devices with their start and end apart: 36, of which 11 were waited for; matrix products, arithmetic and copies ran while one was open for 9% of the time, Pallas kernels for 58%

profile of v7, /device:TPU:2, one launch (start us, length us, event | category | flops | bytes accessed | tf_op | source)
XLA Modules:
  0.0 324.0 jit_solution(13860546472292767454)
XLA Ops:
  0.6 5.9 %collective-permute-start.3 = (bf16[320,1024]{1,0:T(8,128)(2,1)}, bf16[320,1024]{1,0:T(8,128)(2,1)}, u32[]{:S(2)}, u32[]{:S(2)}) collective-permute-start(bf16[320,1024]{1,0:T(8,128)(2,1)} %bitcast.34), channel_id=1, source_target_pairs={{0,7},{1,2},{2,1},{3,4},{4,3},{5,6},{6,5},{7,0},{8,15},{9,10},{10,... | collective-permute-start | bytes 1966088 | tf_op jit(solution)/shard_map/ppermute | solution.py:312
  6.6 1.0 constant_dynamic-slice_fusion
  7.8 2.0 dynamic-slice_bitcast_fusion
  11.6 2.4 abs_reduce_fusion
  16.4 5.2 %collective-permute-done.3.refs_2_ = bf16[320,1024]{1,0:T(8,128)(2,1)} collective-permute-done((bf16[320,1024]{1,0:T(8,128)(2,1)}, bf16[320,1024]{1,0:T(8,128)(2,1)}, u32[]{:S(2)}, u32[]{:S(2)}) %collective-permute-start.3) | collective-permute-done | bytes 655392 | tf_op jit(solution)/shard_map/ppermute | solution.py:312
  22.2 0.9 collective-permute-done.2.refs_1_
  23.1 2.0 collective-permute-start.13
  25.1 1.2 bitcast_add_fusion
  26.6 2.0 collective-permute-start.6
  28.7 11.7 %collective-permute-done.6 = f32[8,128]{1,0:T(8,128)S(1)} collective-permute-done((f32[8,128]{1,0:T(8,128)S(1)}, f32[8,128]{1,0:T(8,128)S(1)}, u32[]{:S(2)}, u32[]{:S(2)}) %collective-permute-start.6) | collective-permute-done | bytes 4128 | tf_op jit(solution)/shard_map/ppermute | solution.py:24
  40.5 3.0 collective-permute-start.10
  44.7 1.5 collective-permute-start.5
  46.2 2.1 collective-permute-done.10
  48.3 1.5 collective-permute-start.22
  51.1 1.1 collective-permute-start.16
  52.3 2.7 collective-permute-done.7
  55.3 4.2 %collective-permute-done.5.cotangent_ref = bf16[256,1024]{1,0:T(8,128)(2,1)S(1)} collective-permute-done((bf16[256,1024]{1,0:T(8,128)(2,1)S(1)}, bf16[256,1024]{1,0:T(8,128)(2,1)S(1)}, u32[]{:S(2)}, u32[]{:S(2)}) %collective-permute-start.5) | collective-permute-done | bytes 524320 | tf_op jit(solution)/shard_map/ppermute | solution.py:24
  59.5 2.4 collective-permute-start.19
  62.0 2.5 collective-permute-start.14
  64.5 1.6 fusion.26
  66.1 2.9 collective-permute-done.15.refs_5_
  69.6 1.0 collective-permute-start.20
  70.6 3.1 collective-permute-start.21
  76.2 3.9 %fusion.32 = f32[1280,1024]{1,0:T(8,128)} fusion(bf16[256,1280]{1,0:T(8,128)(2,1)S(1)} %collective-permute-done.22.late_ref, bf16[256,640]{1,0:T(8,128)(2,1)S(1)} %get-tuple-element.113, bf16[256,640]{1,0:T(8,128)(2,1)S(1)} %get-tuple-element.112, bf16[256,1024]{1,0:T(8,128)(2,1)S(1)} %collective-permute-done.5.cotangent_ref, bf16[256,1024]{1,0:T(8,128)(2,1)S(1)} %bitcast.33), kind=kOutput, calls=%fused_computation.51 | convolution fusion | flops 1348206592 | bytes 7602176 | tf_op jit(solution)/shard_map/dot_general | solution.py:364
  80.1 1.0 subtract_convert_fusion
  81.8 4.6 %collective-permute-done.17 = f16[160,1024]{1,0:T(8,128)(2,1)S(1)} collective-permute-done((f16[160,1024]{1,0:T(8,128)(2,1)S(1)}, f16[160,1024]{1,0:T(8,128)(2,1)S(1)}, u32[]{:S(2)}, u32[]{:S(2)}) %collective-permute-start.17) | collective-permute-done | bytes 327712 | tf_op jit(solution)/shard_map/ppermute | solution.py:391
  87.3 1.0 fusion.21
  88.3 1.0 fusion.20
  89.3 3.5 %collective-permute-start.23 = (f16[320,1024]{1,0:T(8,128)(2,1)}, f16[320,1024]{1,0:T(8,128)(2,1)}, u32[]{:S(2)}, u32[]{:S(2)}) collective-permute-start(f16[320,1024]{1,0:T(8,128)(2,1)} %fusion.20), channel_id=1, source_target_pairs={{0,7},{1,2},{2,1},{3,4},{4,3},{5,6},{6,5},{7,0},{8,15},{9,10},{10,... | collective-permute-start | bytes 1966088 | tf_op jit(solution)/shard_map/ppermute | solution.py:391
  92.8 2.7 collective-permute-start.25
  95.5 160.0 %shard_map.101.weight_ref = bf16[2560,1024]{1,0:T(8,128)(2,1)} custom-call(s32[1]{0:T(128)} %bitcast.11.z_ref, bf16[320,1024]{1,0:T(8,128)(2,1)} %bitcast.36, bf16[320,1024]{1,0:T(8,128)(2,1)} %collective-permute-done.2.refs_1_, bf16[320,1024]{1,0:T(8,128)(2,1)} %collective-permute-done.3.refs_2_, bf16[320,1024]{1,0:T(8,128)(2,1)} %copy-done.12, ...), custom_call_target="tpu_custom_call" | custom-call | tf_op jit(solution)/shard_map/pallas_call | solution.py:144
  256.2 1.4 shard_map.102.refs_0_
  257.6 2.6 collective-permute-start.28
  260.2 1.5 collective-permute-start.26
  261.7 8.2 %shard_map.103 = bf16[272,3584]{1,0:T(8,128)(2,1)} custom-call(s32[1]{0:T(128)} %bitcast.11.z_ref, bf16[256,1280]{1,0:T(8,128)(2,1)} %copy-done.8, bf16[256,1280]{1,0:T(8,128)(2,1)} %copy-done.9, bf16[256,1024]{1,0:T(8,128)(2,1)} %copy-done.13, bf16[2560,1024]{1,0:T(8,128)(2,1)} %shard_map.101.weight_ref), custom_call_target="tpu_custom_call" | custom-call | tf_op jit(solution)/shard_map/pallas_call | solution.py:195
  269.9 2.6 collective-permute-start.29
  273.1 1.8 shard_map.104.refs_0_
  274.9 3.1 fusion.22
  278.0 3.4 %fusion.23 = f16[320,1024]{1,0:T(8,128)(2,1)} fusion(f16[320,1024]{1,0:T(8,128)(2,1)} %collective-permute-done.23, f32[1280,1024]{1,0:T(8,128)} %copy-done.2, s32[]{:T(128)S(6)} %select_n.162, f32[]{:T(128)} %bitcast.6), kind=kLoop, calls=%fused_computation.42 | loop fusion | flops 2949120 | bytes 2621448 | tf_op jit(solution)/shard_map/convert_element_type | solution.py:55
  281.9 2.7 collective-permute-start.31
  285.1 7.0 %shard_map.105 = (f32[256,1024]{1,0:T(8,128)}, bf16[256,5120]{1,0:T(8,128)(2,1)}) custom-call(s32[1]{0:T(128)} %bitcast.12._, bf16[256,5120]{1,0:T(8,128)(2,1)} %bitcast.25, bf16[256,1024]{1,0:T(8,128)(2,1)} %bitcast.30, bf16[2560,1024]{1,0:T(8,128)(2,1)} %shard_map.101.weight_ref), custom_call_target="tpu_custom_call" | custom-call | tf_op jit(solution)/shard_map/pallas_call | solution.py:228
  292.8 1.6 shard_map.106
  295.1 2.0 shard_map.107
  297.1 4.9 %fusion.25 = (f16[320,1024]{1,0:T(8,128)(2,1)}, f16[320,1024]{1,0:T(8,128)(2,1)}) fusion(f16[320,1024]{1,0:T(8,128)(2,1)S(1)} %collective-permute-done.30, f32[1280,1024]{1,0:T(8,128)} %fusion.32, s32[]{:T(128)S(6)} %select_n.177, f32[]{:T(128)} %bitcast.6, f16[320,1024]{1,0:T(8,128)(2,1)} %collective-permute-done.31, s32[]{:T(128)S(6)} %select_n.164), kind=kLoop, calls=%fused_computation.44 | loop fusion | flops 5898240 | bytes 5242892 | tf_op jit(solution)/shard_map/convert_element_type | solution.py:55
  303.6 1.3 copy-done.1
  304.9 5.1 %shard_map.108 = (bf16[256,1024]{1,0:T(8,128)(2,1)}, bf16[256,5120]{1,0:T(8,128)(2,1)}) custom-call(s32[1]{0:T(128)} %bitcast._, bf16[256,5120]{1,0:T(8,128)(2,1)} %get-tuple-element.86.__, f32[256,1024]{1,0:T(8,128)} %get-tuple-element.87.keys_ref, bf16[272,3584]{1,0:T(8,128)(2,1)} %copy-done.1, ...), custom_call_target="tpu_custom_call", output_to_operand_aliasing={{1}: (1, {})} | custom-call | tf_op jit(solution)/shard_map/pallas_call | solution.py:263
  310.0 10.0 %collective-permute-done.35 = f16[320,1024]{1,0:T(8,128)(2,1)S(1)} collective-permute-done((f16[320,1024]{1,0:T(8,128)(2,1)}, f16[320,1024]{1,0:T(8,128)(2,1)S(1)}, u32[]{:S(2)}, u32[]{:S(2)}) %collective-permute-start.35) | collective-permute-done | bytes 655392 | tf_op jit(solution)/shard_map/ppermute | solution.py:456
  320.0 4.0 %fusion.46 = bf16[1,320,1024]{2,1,0:T(8,128)(2,1)} fusion(f32[]{:T(128)} %bitcast.16, f16[320,1024]{1,0:T(8,128)(2,1)S(1)} %collective-permute-done.35, f16[320,1024]{1,0:T(8,128)(2,1)} %collective-permute-done.34, f32[]{:T(128)} %bitcast.6, f32[1280,1024]{1,0:T(8,128)} %fusion.32, s32[]{:T(128)S(6)} %select_n.165), kind=kLoop, calls=%fused_computation.78 | loop fusion | flops 4259840 | bytes 3276812 | tf_op jit(solution)/shard_map/broadcast_in_dim | solution.py:467
  (119 shorter events, 15.9 us)
Async XLA Ops:
  0.6 9.7 %copy-start.3 = (bf16[1,256,1024]{2,1,0:T(8,128)(2,1)S(1)}, bf16[1,256,1024]{2,1,0:T(8,128)(2,1)}, u32[]{:S(2)}) copy-start(bf16[1,256,1024]{2,1,0:T(8,128)(2,1)} %param.8) | copy-start | bytes 1572868
  0.6 21.0 %collective-permute-start.3 = (bf16[320,1024]{1,0:T(8,128)(2,1)}, bf16[320,1024]{1,0:T(8,128)(2,1)}, u32[]{:S(2)}, u32[]{:S(2)}) collective-permute-start(bf16[320,1024]{1,0:T(8,128)(2,1)} %bitcast.34), channel_id=1, source_target_pairs={{0,7},{1,2},{2,1},{3,4},{4,3},{5,6},{6,5},{7,0},{8,15},{9,10},{10,... | collective-permute-start | bytes 1966088 | tf_op jit(solution)/shard_map/ppermute | solution.py:312
  6.6 16.5 %collective-permute-start.2 = (bf16[320,1024]{1,0:T(8,128)(2,1)}, bf16[320,1024]{1,0:T(8,128)(2,1)}, u32[]{:S(2)}, u32[]{:S(2)}) collective-permute-start(bf16[320,1024]{1,0:T(8,128)(2,1)} %bitcast.35), channel_id=1, source_target_pairs={{0,1},{1,0},{2,3},{3,2},{4,5},{5,4},{6,7},{7,6},{8,9},{9,8},{10,11... | collective-permute-start | bytes 1966088 | tf_op jit(solution)/shard_map/ppermute | solution.py:312
  7.7 36.9 %collective-permute-start.11 = (f32[160,64]{1,0:T(8,128)S(1)}, f32[160,64]{1,0:T(8,128)S(1)}, u32[]{:S(2)}, u32[]{:S(2)}) collective-permute-start(f32[160,64]{1,0:T(8,128)S(1)} %copy.15), channel_id=1, source_target_pairs={{0,16},{16,0},{1,17},{17,1},{2,18},{18,2},{3,19},{19,3},{4,20},{20... | collective-permute-start | bytes 122888 | tf_op jit(solution)/shard_map/ppermute | solution.py:24
  9.8 15.3 %collective-permute-start.1 = (f32[160,1024]{1,0:T(8,128)}, f32[160,1024]{1,0:T(8,128)}, u32[]{:S(2)}, u32[]{:S(2)}) collective-permute-start(f32[160,1024]{1,0:T(8,128)} %dynamic-slice_bitcast_fusion), channel_id=1, source_target_pairs={{0,16},{16,0},{1,17},{17,1},{2,18},{18,2},{3,19},{19,3},{4,20},{20... | collective-permute-start | bytes 1966088 | tf_op jit(solution)/shard_map/ppermute | solution.py:24
  15.4 11.1 %collective-permute-start = (f32[8,128]{1,0:T(8,128)S(1)}, f32[8,128]{1,0:T(8,128)S(1)}, u32[]{:S(2)}, u32[]{:S(2)}) collective-permute-start(f32[8,128]{1,0:T(8,128)S(1)} %iota.32), channel_id=1, source_target_pairs={{0,8},{8,0},{1,9},{9,1},{2,10},{10,2},{3,11},{11,3},{4,12},{12,4},... | collective-permute-start | bytes 12296 | tf_op jit(solution)/shard_map/ppermute | solution.py:24
  16.3 8.9 %copy-start.6 = (f32[1,320,1024]{2,1,0:T(8,128)S(1)}, f32[1,320,1024]{2,1,0:T(8,128)}, u32[]{:S(2)}) copy-start(f32[1,320,1024]{2,1,0:T(8,128)} %param.10) | copy-start | bytes 3932164
  21.6 40.3 %collective-permute-start.4 = (bf16[256,1280]{1,0:T(8,128)(2,1)S(1)}, bf16[256,1280]{1,0:T(8,128)(2,1)S(1)}, u32[]{:S(2)}, u32[]{:S(2)}) collective-permute-start(bf16[256,1280]{1,0:T(8,128)(2,1)S(1)} %pad_maximum_fusion.3), channel_id=1, source_target_pairs={{0,8},{8,0},{1,9},{9,1},{2,10},{10,2},{3,11},{11,3},{4,12},{12,4},... | collective-permute-start | bytes 1966088 | tf_op jit(solution)/shard_map/ppermute | solution.py:24
  23.1 20.4 %collective-permute-start.13 = (bf16[320,1024]{1,0:T(8,128)(2,1)}, bf16[320,1024]{1,0:T(8,128)(2,1)S(1)}, u32[]{:S(2)}, u32[]{:S(2)}) collective-permute-start(bf16[320,1024]{1,0:T(8,128)(2,1)} %collective-permute-done.2.refs_1_), channel_id=1, source_target_pairs={{0,7},{1,2},{2,1},{3,4},{4,3},{5,6},{6,5},{7,0},{8,15},{9,10},{10,... | collective-permute-start | bytes 1966088 | tf_op jit(solution)/shard_map/ppermute | solution.py:312
  25.1 19.0 %collective-permute-start.12 = (bf16[320,1024]{1,0:T(8,128)(2,1)}, bf16[320,1024]{1,0:T(8,128)(2,1)S(1)}, u32[]{:S(2)}, u32[]{:S(2)}) collective-permute-start(bf16[320,1024]{1,0:T(8,128)(2,1)} %collective-permute-done.3.refs_2_), channel_id=1, source_target_pairs={{0,1},{1,0},{2,3},{3,2},{4,5},{5,4},{6,7},{7,6},{8,9},{9,8},{10,11... | collective-permute-start | bytes 1966088 | tf_op jit(solution)/shard_map/ppermute | solution.py:312
  26.6 13.9 %collective-permute-start.6 = (f32[8,128]{1,0:T(8,128)S(1)}, f32[8,128]{1,0:T(8,128)S(1)}, u32[]{:S(2)}, u32[]{:S(2)}) collective-permute-start(f32[8,128]{1,0:T(8,128)S(1)} %maximum_select_fusion.3), channel_id=1, source_target_pairs={{0,1},{1,0},{2,3},{3,2},{4,5},{5,4},{6,7},{7,6},{8,9},{9,8},{10,11... | collective-permute-start | bytes 12296 | tf_op jit(solution)/shard_map/ppermute | solution.py:24
  40.5 7.8 %collective-permute-start.10 = (f32[160,256]{1,0:T(8,128)S(1)}, f32[160,256]{1,0:T(8,128)S(1)}, u32[]{:S(2)}, u32[]{:S(2)}) collective-permute-start(f32[160,256]{1,0:T(8,128)S(1)} %get-tuple-element.120), channel_id=1, source_target_pairs={{0,192},{64,128},{128,64},{192,0},{1,193},{65,129},{129,65},{193,1... | collective-permute-start | bytes 491528 | tf_op jit(solution)/shard_map/ppermute | solution.py:24
  43.5 22.6 %copy-start.11 = (bf16[320,1024]{1,0:T(8,128)(2,1)}, bf16[320,1024]{1,0:T(8,128)(2,1)S(1)}, u32[]{:S(2)}) copy-start(bf16[320,1024]{1,0:T(8,128)(2,1)S(1)} %collective-permute-done.13.refs_4_) | copy-start | bytes 1966084
  43.5 6.8 %collective-permute-start.9 = (f32[160,256]{1,0:T(8,128)S(1)}, f32[160,256]{1,0:T(8,128)S(1)}, u32[]{:S(2)}, u32[]{:S(2)}) collective-permute-start(f32[160,256]{1,0:T(8,128)S(1)} %get-tuple-element.121), channel_id=1, source_target_pairs={{0,128},{64,192},{128,0},{192,64},{1,129},{65,193},{129,1},{193,65... | collective-permute-start | bytes 491528 | tf_op jit(solution)/shard_map/ppermute | solution.py:24
  44.1 21.9 %copy-start.12 = (bf16[320,1024]{1,0:T(8,128)(2,1)}, bf16[320,1024]{1,0:T(8,128)(2,1)S(1)}, u32[]{:S(2)}) copy-start(bf16[320,1024]{1,0:T(8,128)(2,1)S(1)} %collective-permute-done.12.refs_3_) | copy-start | bytes 1966084
  44.1 6.9 %collective-permute-start.8 = (f32[160,256]{1,0:T(8,128)S(1)}, f32[160,256]{1,0:T(8,128)S(1)}, u32[]{:S(2)}, u32[]{:S(2)}) collective-permute-start(f32[160,256]{1,0:T(8,128)S(1)} %get-tuple-element.122), channel_id=1, source_target_pairs={{0,64},{64,0},{128,192},{192,128},{1,65},{65,1},{129,193},{193,129... | collective-permute-start | bytes 491528 | tf_op jit(solution)/shard_map/ppermute | solution.py:24
  44.7 14.9 %collective-permute-start.5 = (bf16[256,1024]{1,0:T(8,128)(2,1)S(1)}, bf16[256,1024]{1,0:T(8,128)(2,1)S(1)}, u32[]{:S(2)}, u32[]{:S(2)}) collective-permute-start(bf16[256,1024]{1,0:T(8,128)(2,1)S(1)} %bitcast.31), channel_id=1, source_target_pairs={{0,8},{8,0},{1,9},{9,1},{2,10},{10,2},{3,11},{11,3},{4,12},{12,4},... | collective-permute-start | bytes 1572872 | tf_op jit(solution)/shard_map/ppermute | solution.py:24
  48.3 27.8 %collective-permute-start.22 = (bf16[256,1280]{1,0:T(8,128)(2,1)S(1)}, bf16[256,1280]{1,0:T(8,128)(2,1)S(1)}, u32[]{:S(2)}, u32[]{:S(2)}) collective-permute-start(bf16[256,1280]{1,0:T(8,128)(2,1)S(1)} %pad_maximum_fusion.4), channel_id=1, source_target_pairs={{0,8},{8,0},{1,9},{9,1},{2,10},{10,2},{3,11},{11,3},{4,12},{12,4},... | collective-permute-start | bytes 1966088 | tf_op jit(solution)/shard_map/ppermute | solution.py:24
  50.3 4.6 %collective-permute-start.7 = (f32[8,128]{1,0:T(8,128)S(1)}, f32[8,128]{1,0:T(8,128)S(1)}, u32[]{:S(2)}, u32[]{:S(2)}) collective-permute-start(f32[8,128]{1,0:T(8,128)S(1)} %maximum_select_fusion.2), channel_id=1, source_target_pairs={{0,2},{1,3},{2,0},{3,1},{4,6},{5,7},{6,4},{7,5},{8,10},{9,11},{10,... | collective-permute-start | bytes 12296 | tf_op jit(solution)/shard_map/ppermute | solution.py:24
  51.1 15.1 %collective-permute-start.16 = (bf16[320,1024]{1,0:T(8,128)(2,1)S(1)}, bf16[320,1024]{1,0:T(8,128)(2,1)S(1)}, u32[]{:S(2)}, u32[]{:S(2)}) collective-permute-start(bf16[320,1024]{1,0:T(8,128)(2,1)S(1)} %collective-permute-done.12.refs_3_), channel_id=1, source_target_pairs={{0,7},{1,2},{2,1},{3,4},{4,3},{5,6},{6,5},{7,0},{8,15},{9,10},{10,... | collective-permute-start | bytes 1966088 | tf_op jit(solution)/shard_map/ppermute | solution.py:312
  54.9 14.1 %collective-permute-start.15 = (bf16[320,1024]{1,0:T(8,128)(2,1)S(1)}, bf16[320,1024]{1,0:T(8,128)(2,1)S(1)}, u32[]{:S(2)}, u32[]{:S(2)}) collective-permute-start(bf16[320,1024]{1,0:T(8,128)(2,1)S(1)} %collective-permute-done.13.refs_4_), channel_id=1, source_target_pairs={{0,1},{1,0},{2,3},{3,2},{4,5},{5,4},{6,7},{7,6},{8,9},{9,8},{10,11... | collective-permute-start | bytes 1966088 | tf_op jit(solution)/shard_map/ppermute | solution.py:312
  59.5 16.6 %copy-start.13 = (bf16[256,1024]{1,0:T(8,128)(2,1)}, bf16[256,1024]{1,0:T(8,128)(2,1)S(1)}, u32[]{:S(2)}) copy-start(bf16[256,1024]{1,0:T(8,128)(2,1)S(1)} %collective-permute-done.5.cotangent_ref) | copy-start | bytes 1572868
  59.5 20.6 %collective-permute-start.19 = (f32[160,128]{1,0:T(8,128)S(1)}, f32[160,128]{1,0:T(8,128)S(1)}, u32[]{:S(2)}, u32[]{:S(2)}) collective-permute-start(f32[160,128]{1,0:T(8,128)S(1)} %constant_dynamic-slice_fusion.1), channel_id=1, source_target_pairs={{0,32},{32,0},{1,33},{33,1},{2,34},{34,2},{3,35},{35,3},{4,36},{36... | collective-permute-start | bytes 245768 | tf_op jit(solution)/shard_map/ppermute | solution.py:24
  62.0 7.6 %collective-permute-start.14 = (f32[8,128]{1,0:T(8,128)S(1)}, f32[8,128]{1,0:T(8,128)S(1)}, u32[]{:S(2)}, u32[]{:S(2)}) collective-permute-start(f32[8,128]{1,0:T(8,128)S(1)} %maximum_select_fusion.1), channel_id=1, source_target_pairs={{0,4},{1,5},{2,6},{3,7},{4,0},{5,1},{6,2},{7,3},{8,12},{9,13},{10,... | collective-permute-start | bytes 12296 | tf_op jit(solution)/shard_map/ppermute | solution.py:24
  66.1 20.3 %copy-start.2 = (f32[1280,1024]{1,0:T(8,128)}, f32[1280,1024]{1,0:T(8,128)S(1)}, u32[]{:S(2)}) copy-start(f32[1280,1024]{1,0:T(8,128)S(1)} %fusion.26) | copy-start | bytes 15728644
  66.1 14.0 %copy-start.4 = (bf16[320,1024]{1,0:T(8,128)(2,1)}, bf16[320,1024]{1,0:T(8,128)(2,1)S(1)}, u32[]{:S(2)}) copy-start(bf16[320,1024]{1,0:T(8,128)(2,1)S(1)} %collective-permute-done.16.refs_6_) | copy-start | bytes 1966084
  69.1 11.0 %copy-start.5 = (bf16[320,1024]{1,0:T(8,128)(2,1)}, bf16[320,1024]{1,0:T(8,128)(2,1)S(1)}, u32[]{:S(2)}) copy-start(bf16[320,1024]{1,0:T(8,128)(2,1)S(1)} %collective-permute-done.15.refs_5_) | copy-start | bytes 1966084
  69.6 10.5 %collective-permute-start.20 = (bf16[160,1024]{1,0:T(8,128)(2,1)S(1)}, bf16[160,1024]{1,0:T(8,128)(2,1)S(1)}, u32[]{:S(2)}, u32[]{:S(2)}) collective-permute-start(bf16[160,1024]{1,0:T(8,128)(2,1)S(1)} %slice.22), channel_id=1, source_target_pairs={{0,1},{1,0},{2,3},{3,2},{4,5},{5,4},{6,7},{7,6},{8,9},{9,8},{10,11... | collective-permute-start | bytes 983048 | tf_op jit(solution)/shard_map/ppermute | solution.py:312
  70.6 9.5 %collective-permute-start.21 = (bf16[160,1024]{1,0:T(8,128)(2,1)S(1)}, bf16[160,1024]{1,0:T(8,128)(2,1)S(1)}, u32[]{:S(2)}, u32[]{:S(2)}) collective-permute-start(bf16[160,1024]{1,0:T(8,128)(2,1)S(1)} %slice.23), channel_id=1, source_target_pairs={{0,7},{1,2},{2,1},{3,4},{4,3},{5,6},{6,5},{7,0},{8,15},{9,10},{10,... | collective-permute-start | bytes 983048 | tf_op jit(solution)/shard_map/ppermute | solution.py:312
  75.9 10.5 %collective-permute-start.18 = (f16[160,1024]{1,0:T(8,128)(2,1)S(1)}, f16[160,1024]{1,0:T(8,128)(2,1)S(1)}, u32[]{:S(2)}, u32[]{:S(2)}) collective-permute-start(f16[160,1024]{1,0:T(8,128)(2,1)S(1)} %get-tuple-element.110), channel_id=1, source_target_pairs={{0,7},{1,2},{2,1},{3,4},{4,3},{5,6},{6,5},{7,0},{8,15},{9,10},{10,... | collective-permute-start | bytes 983048 | tf_op jit(solution)/shard_map/ppermute | solution.py:391
  76.1 10.3 %collective-permute-start.17 = (f16[160,1024]{1,0:T(8,128)(2,1)S(1)}, f16[160,1024]{1,0:T(8,128)(2,1)S(1)}, u32[]{:S(2)}, u32[]{:S(2)}) collective-permute-start(f16[160,1024]{1,0:T(8,128)(2,1)S(1)} %get-tuple-element.111), channel_id=1, source_target_pairs={{0,1},{1,0},{2,3},{3,2},{4,5},{5,4},{6,7},{7,6},{8,9},{9,8},{10,11... | collective-permute-start | bytes 983048 | tf_op jit(solution)/shard_map/ppermute | solution.py:391
  80.1 7.2 %copy-start.15 = (bf16[160,1024]{1,0:T(8,128)(2,1)}, bf16[160,1024]{1,0:T(8,128)(2,1)S(1)}, u32[]{:S(2)}) copy-start(bf16[160,1024]{1,0:T(8,128)(2,1)S(1)} %collective-permute-done.20.refs_7_) | copy-start | bytes 983044
  80.1 7.2 %copy-start.16 = (bf16[160,1024]{1,0:T(8,128)(2,1)}, bf16[160,1024]{1,0:T(8,128)(2,1)S(1)}, u32[]{:S(2)}) copy-start(bf16[160,1024]{1,0:T(8,128)(2,1)S(1)} %collective-permute-done.21.refs_8_) | copy-start | bytes 983044
  81.1 11.7 %copy-start.17 = (bf16[160,128]{1,0:T(8,128)(2,1)}, bf16[160,128]{1,0:T(8,128)(2,1)S(1)}, u32[]{:S(2)}) copy-start(bf16[160,128]{1,0:T(8,128)(2,1)S(1)} %get-tuple-element.102.refs_0_) | copy-start | bytes 122884
  88.3 186.6 %collective-permute-start.24 = (f16[320,1024]{1,0:T(8,128)(2,1)}, f16[320,1024]{1,0:T(8,128)(2,1)S(1)}, u32[]{:S(2)}, u32[]{:S(2)}) collective-permute-start(f16[320,1024]{1,0:T(8,128)(2,1)} %fusion.21), channel_id=1, source_target_pairs={{0,1},{1,0},{2,3},{3,2},{4,5},{5,4},{6,7},{7,6},{8,9},{9,8},{10,11... | collective-permute-start | bytes 1966088 | tf_op jit(solution)/shard_map/ppermute | solution.py:391
  89.3 188.7 %collective-permute-start.23 = (f16[320,1024]{1,0:T(8,128)(2,1)}, f16[320,1024]{1,0:T(8,128)(2,1)}, u32[]{:S(2)}, u32[]{:S(2)}) collective-permute-start(f16[320,1024]{1,0:T(8,128)(2,1)} %fusion.20), channel_id=1, source_target_pairs={{0,7},{1,2},{2,1},{3,4},{4,3},{5,6},{6,5},{7,0},{8,15},{9,10},{10,... | collective-permute-start | bytes 1966088 | tf_op jit(solution)/shard_map/ppermute | solution.py:391
  92.8 162.7 %collective-permute-start.25 = (bf16[160,128]{1,0:T(8,128)(2,1)S(1)}, bf16[160,128]{1,0:T(8,128)(2,1)S(1)}, u32[]{:S(2)}, u32[]{:S(2)}) collective-permute-start(bf16[160,128]{1,0:T(8,128)(2,1)S(1)} %get-tuple-element.102.refs_0_), channel_id=1, source_target_pairs={{0,32},{32,0},{1,33},{33,1},{2,34},{34,2},{3,35},{35,3},{4,36},{36... | collective-permute-start | bytes 122888 | tf_op jit(solution)/shard_map/ppermute | solution.py:24
  257.6 12.3 %collective-permute-start.28 = (bf16[160,256]{1,0:T(8,128)(2,1)}, bf16[160,256]{1,0:T(8,128)(2,1)S(1)}, u32[]{:S(2)}, u32[]{:S(2)}) collective-permute-start(bf16[160,256]{1,0:T(8,128)(2,1)} %shard_map.102.refs_0_), channel_id=1, source_target_pairs={{0,192},{64,128},{128,64},{192,0},{1,193},{65,129},{129,65},{193,1... | collective-permute-start | bytes 245768 | tf_op jit(solution)/shard_map/ppermute | solution.py:24
  260.2 12.3 %collective-permute-start.27 = (bf16[160,256]{1,0:T(8,128)(2,1)}, bf16[160,256]{1,0:T(8,128)(2,1)S(1)}, u32[]{:S(2)}, u32[]{:S(2)}) collective-permute-start(bf16[160,256]{1,0:T(8,128)(2,1)} %shard_map.102.refs_0_), channel_id=1, source_target_pairs={{0,128},{64,192},{128,0},{192,64},{1,129},{65,193},{129,1},{193,65... | collective-permute-start | bytes 245768 | tf_op jit(solution)/shard_map/ppermute | solution.py:24
  260.2 12.3 %collective-permute-start.26 = (bf16[160,256]{1,0:T(8,128)(2,1)}, bf16[160,256]{1,0:T(8,128)(2,1)S(1)}, u32[]{:S(2)}, u32[]{:S(2)}) collective-permute-start(bf16[160,256]{1,0:T(8,128)(2,1)} %shard_map.102.refs_0_), channel_id=1, source_target_pairs={{0,64},{64,0},{128,192},{192,128},{1,65},{65,1},{129,193},{193,129... | collective-permute-start | bytes 245768 | tf_op jit(solution)/shard_map/ppermute | solution.py:24
  269.9 33.7 %collective-permute-start.29 = (bf16[272,3584]{1,0:T(8,128)(2,1)}, bf16[272,3584]{1,0:T(8,128)(2,1)S(1)}, u32[]{:S(2)}, u32[]{:S(2)}) collective-permute-start(bf16[272,3584]{1,0:T(8,128)(2,1)} %shard_map.103), channel_id=1, source_target_pairs={{0,8},{8,0},{1,9},{9,1},{2,10},{10,2},{3,11},{11,3},{4,12},{12,4},... | collective-permute-start | bytes 5849096 | tf_op jit(solution)/shard_map/ppermute | solution.py:24
  278.0 6.5 %copy-start.7 = (bf16[160,1024]{1,0:T(8,128)(2,1)S(1)}, bf16[160,1024]{1,0:T(8,128)(2,1)}, u32[]{:S(2)}) copy-start(bf16[160,1024]{1,0:T(8,128)(2,1)} %shard_map.104.refs_0_) | copy-start | bytes 983044
  281.4 15.7 %collective-permute-start.30 = (f16[320,1024]{1,0:T(8,128)(2,1)}, f16[320,1024]{1,0:T(8,128)(2,1)S(1)}, u32[]{:S(2)}, u32[]{:S(2)}) collective-permute-start(f16[320,1024]{1,0:T(8,128)(2,1)} %fusion.23), channel_id=1, source_target_pairs={{0,1},{1,0},{2,3},{3,2},{4,5},{5,4},{6,7},{7,6},{8,9},{9,8},{10,11... | collective-permute-start | bytes 1966088 | tf_op jit(solution)/shard_map/ppermute | solution.py:391
  281.9 15.2 %collective-permute-start.31 = (f16[320,1024]{1,0:T(8,128)(2,1)}, f16[320,1024]{1,0:T(8,128)(2,1)}, u32[]{:S(2)}, u32[]{:S(2)}) collective-permute-start(f16[320,1024]{1,0:T(8,128)(2,1)} %fusion.22), channel_id=1, source_target_pairs={{0,7},{1,2},{2,1},{3,4},{4,3},{5,6},{6,5},{7,0},{8,15},{9,10},{10,... | collective-permute-start | bytes 1966088 | tf_op jit(solution)/shard_map/ppermute | solution.py:391
  284.6 9.8 %collective-permute-start.32 = (bf16[160,1024]{1,0:T(8,128)(2,1)S(1)}, bf16[160,1024]{1,0:T(8,128)(2,1)S(1)}, u32[]{:S(2)}, u32[]{:S(2)}) collective-permute-start(bf16[160,1024]{1,0:T(8,128)(2,1)S(1)} %copy-done.7), channel_id=1, source_target_pairs={{0,16},{16,0},{1,17},{17,1},{2,18},{18,2},{3,19},{19,3},{4,20},{20... | collective-permute-start | bytes 983048 | tf_op jit(solution)/shard_map/ppermute | solution.py:24
  284.6 7.6 %collective-permute-start.33 = (f32[160,64]{1,0:T(8,128)S(1)}, f32[160,64]{1,0:T(8,128)S(1)}, u32[]{:S(2)}, u32[]{:S(2)}) collective-permute-start(f32[160,64]{1,0:T(8,128)S(1)} %get-tuple-element.127), channel_id=1, source_target_pairs={{0,16},{16,0},{1,17},{17,1},{2,18},{18,2},{3,19},{19,3},{4,20},{20... | collective-permute-start | bytes 122888 | tf_op jit(solution)/shard_map/ppermute | solution.py:24
  301.9 18.1 %collective-permute-start.35 = (f16[320,1024]{1,0:T(8,128)(2,1)}, f16[320,1024]{1,0:T(8,128)(2,1)S(1)}, u32[]{:S(2)}, u32[]{:S(2)}) collective-permute-start(f16[320,1024]{1,0:T(8,128)(2,1)} %get-tuple-element.104), channel_id=1, source_target_pairs={{0,7},{1,2},{2,1},{3,4},{4,3},{5,6},{6,5},{7,0},{8,15},{9,10},{10,... | collective-permute-start | bytes 1966088 | tf_op jit(solution)/shard_map/ppermute | solution.py:456
  302.5 17.5 %collective-permute-start.34 = (f16[320,1024]{1,0:T(8,128)(2,1)}, f16[320,1024]{1,0:T(8,128)(2,1)}, u32[]{:S(2)}, u32[]{:S(2)}) collective-permute-start(f16[320,1024]{1,0:T(8,128)(2,1)} %get-tuple-element.105), channel_id=1, source_target_pairs={{0,1},{1,0},{2,3},{3,2},{4,5},{5,4},{6,7},{7,6},{8,9},{9,8},{10,11... | collective-permute-start | bytes 1966088 | tf_op jit(solution)/shard_map/ppermute | solution.py:456
  (11 other events, 25.6 us)

commit v8 on v6

--- a/solution.py
+++ b/solution.py
@@ -375,15 +375,15 @@
     even = jnp.concatenate([own(3, 0, part), own(3, part, part) + decode(far_odd)])
     even = send(even, EVEN)
 
+    weight_half = order.step(weight_half)
+    sent = products_for_partner(z, early_other, late_other, cotangent_other, weight_half)
+    order.did(sent)
+    products_back = swap(sent, "xl")
+
     wides = order.step(*wides)
     block = assemble(y, lambda i: (i, i ^ 1, i ^ 2, i ^ 3), (wide, *wides), 1)
     order.did(block)
     block_other = swap(block, "c")
-
-    weight_half = order.step(weight_half)
-    sent = products_for_partner(z, early_other, late_other, cotangent_other, weight_half)
-    order.did(sent)
-    products_back = swap(sent, "xl")
 
     even, odd = ring_step(2, even, odd)
 

time: 164 us -> 158 us (0.963)
  waiting for transfers between devices: 28.5 us -> 21.5 us
    ppermute x20, waiting for transfers between devices: 27.8 us -> 20.3 us  [swap(): lax.ppermute(value, axis, [(i, i ^ mask) for i in range(SIZES[axis])])]
  transfers between devices with their start and end apart: 29 -> 29, of which waited for: 9 -> 8; matrix products, arithmetic and copies ran while one was open for 22% -> 23% of each run, Pallas kernels for 17% -> 17%
where the time goes in v8:
time: 158 us; the launch traced here: 156 us
  starting transfers between devices  46.5 us (29%)
  other arithmetic  28.7 us (18%)
  Pallas kernels  27.1 us (17%)
  waiting for transfers between devices  21.5 us (14%)
  between operations  16.4 us (10%)
  local copies, waits for them, and re-layouts  9.3 us (6%)
  matrix products  6.75 us (4%)
    ppermute x20, starting transfers between devices, swap(): lax.ppermute(value, axis, [(i, i ^ mask) for i in range(SIZES[axis])])  31.7 us
    ppermute x20, waiting for transfers between devices, swap(): lax.ppermute(value, axis, [(i, i ^ mask) for i in range(SIZES[axis])])  20.3 us
    convert_element_type x6, other arithmetic, encode(): return (scaled * jnp.abs(scaled)).astype(F16)  13.6 us
    ppermute x6, starting transfers between devices, send(): return lax.ppermute(message, 'z', pairs)  12.4 us
    pallas_call x1, Pallas kernels, products_for_partner(): pl.pallas_call(body, grid_spec=pltpu.PrefetchScalarGridSpec(num_scalar_pr...  8.2 us
    pallas_call x1, Pallas kernels, products_here(): pl.pallas_call(body, grid_spec=pltpu.PrefetchScalarGridSpec(num_scalar_pr...  7.05 us
    pallas_call x4, Pallas kernels, assemble(): pl.pallas_call(body, grid_spec=pltpu.PrefetchScalarGridSpec(num_scalar_pr...  6.76 us
    dot_general x2, matrix products, product(): lax.dot_general(jnp.concatenate([first, second], axis=0), jnp.concatenate...  6.75 us
  transfers between devices with their start and end apart: 29, of which 8 were waited for; matrix products, arithmetic and copies ran while one was open for 23% of the time, Pallas kernels for 17%

profile of v8, /device:TPU:2, one launch (start us, length us, event | category | flops | bytes accessed | tf_op | source)
XLA Modules:
  0.0 156.3 jit_solution(5530077408336308862)
XLA Ops:
  7.9 2.0 %dynamic-slice_bitcast_fusion = f32[160,1024]{1,0:T(8,128)} fusion(f32[1,320,1024]{2,1,0:T(8,128)} %param.10, s32[]{:T(128)S(6)} %select_n.140), kind=kLoop, calls=%fused_computation.77 | loop fusion | bytes 1310724 | tf_op jit(solution)/shard_map/dynamic_slice | solution.py:40
  11.3 2.4 %abs_reduce_fusion = f32[5120]{0:T(1024)S(1)} fusion(bf16[256,5120]{1,0:T(8,128)(2,1)} %bitcast.24), kind=kLoop, calls=%fused_computation | loop fusion | flops 3927040 | bytes 2641920 | tf_op jit(solution)/shard_map/reduce_sum | solution.py:68
  15.0 2.3 %collective-permute-start = (f32[8,128]{1,0:T(8,128)S(1)}, f32[8,128]{1,0:T(8,128)S(1)}, u32[]{:S(2)}, u32[]{:S(2)}) collective-permute-start(f32[8,128]{1,0:T(8,128)S(1)} %iota.32), channel_id=1, source_target_pairs={{0,8},{8,0},{1,9},{9,1},{2,10},{10,2},{3,11},{11,3},{4,12},{12,4},... | collective-permute-start | bytes 12296 | tf_op jit(solution)/shard_map/ppermute | solution.py:24
  17.4 0.9 pad_maximum_fusion.3
  19.2 1.2 copy-done.4
  20.4 1.2 bitcast_add_fusion
  21.7 1.2 collective-permute-start.6
  22.9 2.9 %collective-permute-start.7 = (f32[160,256]{1,0:T(8,128)S(1)}, f32[160,256]{1,0:T(8,128)S(1)}, u32[]{:S(2)}, u32[]{:S(2)}) collective-permute-start(f32[160,256]{1,0:T(8,128)S(1)} %get-tuple-element.105), channel_id=1, source_target_pairs={{0,128},{64,192},{128,0},{192,64},{1,129},{65,193},{129,1},{193,65... | collective-permute-start | bytes 491528 | tf_op jit(solution)/shard_map/ppermute | solution.py:24
  26.0 1.9 %collective-permute-start.4 = (f32[8,128]{1,0:T(8,128)S(1)}, f32[8,128]{1,0:T(8,128)S(1)}, u32[]{:S(2)}, u32[]{:S(2)}) collective-permute-start(f32[8,128]{1,0:T(8,128)S(1)} %maximum_select_fusion.3), channel_id=1, source_target_pairs={{0,1},{1,0},{2,3},{3,2},{4,5},{5,4},{6,7},{7,6},{8,9},{9,8},{10,11... | collective-permute-start | bytes 12296 | tf_op jit(solution)/shard_map/ppermute | solution.py:24
  28.1 1.7 %collective-permute-done.4 = f32[8,128]{1,0:T(8,128)S(1)} collective-permute-done((f32[8,128]{1,0:T(8,128)S(1)}, f32[8,128]{1,0:T(8,128)S(1)}, u32[]{:S(2)}, u32[]{:S(2)}) %collective-permute-start.4) | collective-permute-done | bytes 4128 | tf_op jit(solution)/shard_map/ppermute | solution.py:24
  30.4 1.9 %collective-permute-start.3 = (bf16[256,1024]{1,0:T(8,128)(2,1)S(1)}, bf16[256,1024]{1,0:T(8,128)(2,1)S(1)}, u32[]{:S(2)}, u32[]{:S(2)}) collective-permute-start(bf16[256,1024]{1,0:T(8,128)(2,1)S(1)} %bitcast.33), channel_id=1, source_target_pairs={{0,8},{8,0},{1,9},{9,1},{2,10},{10,2},{3,11},{11,3},{4,12},{12,4},... | collective-permute-start | bytes 1572872 | tf_op jit(solution)/shard_map/ppermute | solution.py:24
  32.5 1.4 collective-permute-done.7
  33.8 3.3 %collective-permute-start.5 = (f32[8,128]{1,0:T(8,128)S(1)}, f32[8,128]{1,0:T(8,128)S(1)}, u32[]{:S(2)}, u32[]{:S(2)}) collective-permute-start(f32[8,128]{1,0:T(8,128)S(1)} %maximum_select_fusion.2), channel_id=1, source_target_pairs={{0,2},{1,3},{2,0},{3,1},{4,6},{5,7},{6,4},{7,5},{8,10},{9,11},{10,... | collective-permute-start | bytes 12296 | tf_op jit(solution)/shard_map/ppermute | solution.py:24
  37.3 2.2 %collective-permute-start.13 = (f32[160,128]{1,0:T(8,128)S(1)}, f32[160,128]{1,0:T(8,128)S(1)}, u32[]{:S(2)}, u32[]{:S(2)}) collective-permute-start(f32[160,128]{1,0:T(8,128)S(1)} %constant_dynamic-slice_fusion.1), channel_id=1, source_target_pairs={{0,32},{32,0},{1,33},{33,1},{2,34},{34,2},{3,35},{35,3},{4,36},{36... | collective-permute-start | bytes 245768 | tf_op jit(solution)/shard_map/ppermute | solution.py:24
  39.6 7.2 %collective-permute-start.10 = (f32[8,128]{1,0:T(8,128)S(1)}, f32[8,128]{1,0:T(8,128)S(1)}, u32[]{:S(2)}, u32[]{:S(2)}) collective-permute-start(f32[8,128]{1,0:T(8,128)S(1)} %maximum_select_fusion.1), channel_id=1, source_target_pairs={{0,4},{1,5},{2,6},{3,7},{4,0},{5,1},{6,2},{7,3},{8,12},{9,13},{10,... | collective-permute-start | bytes 12296 | tf_op jit(solution)/shard_map/ppermute | solution.py:24
  47.3 2.9 %fusion.26 = f32[1280,1024]{1,0:T(8,128)S(1)} fusion(bf16[256,1280]{1,0:T(8,128)(2,1)} %collective-permute-done.2.early_ref, bf16[256,640]{1,0:T(8,128)(2,1)S(1)} %get-tuple-element.99, bf16[256,640]{1,0:T(8,128)(2,1)S(1)} %get-tuple-element.98, bf16[256,1024]{1,0:T(8,128)(2,1)S(1)} %collective-permute-done.3.cotangent_ref, bf16[256,1024]{1,0:T(8,128)(2,1)S(1)} %bitcast.34), kind=kOutput, calls=%fused_computation.45 | convolution fusion | flops 1348206592 | bytes 7602176 | tf_op jit(solution)/shard_map/dot_general | solution.py:315
  53.2 4.6 %collective-permute-start.12 = (f16[160,1024]{1,0:T(8,128)(2,1)S(1)}, f16[160,1024]{1,0:T(8,128)(2,1)}, u32[]{:S(2)}, u32[]{:S(2)}) collective-permute-start(f16[160,1024]{1,0:T(8,128)(2,1)S(1)} %get-tuple-element.94), channel_id=1, source_target_pairs={{0,7},{1,2},{2,1},{3,4},{4,3},{5,6},{6,5},{7,0},{8,15},{9,10},{10,... | collective-permute-start | bytes 983048 | tf_op jit(solution)/shard_map/ppermute | solution.py:339
  57.8 3.6 %collective-permute-done.14.late_ref = bf16[256,1280]{1,0:T(8,128)(2,1)S(1)} collective-permute-done((bf16[256,1280]{1,0:T(8,128)(2,1)S(1)}, bf16[256,1280]{1,0:T(8,128)(2,1)S(1)}, u32[]{:S(2)}, u32[]{:S(2)}) %collective-permute-start.14) | collective-permute-done | bytes 655392 | tf_op jit(solution)/shard_map/ppermute | solution.py:24
  61.4 3.9 %fusion.32 = f32[1280,1024]{1,0:T(8,128)} fusion(bf16[256,1280]{1,0:T(8,128)(2,1)S(1)} %collective-permute-done.14.late_ref, bf16[256,640]{1,0:T(8,128)(2,1)S(1)} %get-tuple-element.97, bf16[256,640]{1,0:T(8,128)(2,1)S(1)} %get-tuple-element.96, bf16[256,1024]{1,0:T(8,128)(2,1)S(1)} %collective-permute-done.3.cotangent_ref, bf16[256,1024]{1,0:T(8,128)(2,1)S(1)} %bitcast.35), kind=kOutput, calls=%fused_computation.51 | convolution fusion | flops 1348206592 | bytes 7602176 | tf_op jit(solution)/shard_map/dot_general | solution.py:315
  65.3 0.9 subtract_convert_fusion
  66.2 0.8 collective-permute-start.15
  67.0 0.7 slice_select_fusion
  67.7 4.1 %collective-permute-done.15.refs_1_ = bf16[160,128]{1,0:T(8,128)(2,1)S(1)} collective-permute-done((bf16[160,128]{1,0:T(8,128)(2,1)S(1)}, bf16[160,128]{1,0:T(8,128)(2,1)S(1)}, u32[]{:S(2)}, u32[]{:S(2)}) %collective-permute-start.15) | collective-permute-done | bytes 40992 | tf_op jit(solution)/shard_map/ppermute | solution.py:24
  72.4 1.4 shard_map.101.refs_0_
  73.9 2.7 %dynamic-slice_multiply_fusion = (f32[160,1024]{1,0:T(8,128)S(1)}, f32[160,1024]{1,0:T(8,128)S(1)}, f32[160,1024]{1,0:T(8,128)S(1)}, f32[160,1024]{1,0:T(8,128)S(1)}) fusion(f32[1280,1024]{1,0:T(8,128)} %copy-done.2, s32[]{:T(128)S(6)} %select_n.177, f32[]{:T(128)} %bitcast.5, f16[160,1024]{1,0:T(8,128)(2,1)} %collective-permute-done.12, s32[]{:T(128)S(6)} %select_n.178, ...), kind=kLoop, calls=%fused_computation.75 | loop fusion | flops 2293760 | bytes 5898260 | tf_op jit(solution)/shard_map/mul | solution.py:333
  76.5 1.0 fusion.21
  77.7 1.0 fusion.20
  78.7 5.0 %collective-permute-start.16 = (f16[320,1024]{1,0:T(8,128)(2,1)}, f16[320,1024]{1,0:T(8,128)(2,1)}, u32[]{:S(2)}, u32[]{:S(2)}) collective-permute-start(f16[320,1024]{1,0:T(8,128)(2,1)} %fusion.20), channel_id=1, source_target_pairs={{0,7},{1,2},{2,1},{3,4},{4,3},{5,6},{6,5},{7,0},{8,15},{9,10},{10,... | collective-permute-start | bytes 1966088 | tf_op jit(solution)/shard_map/ppermute | solution.py:339
  83.7 1.6 %collective-permute-start.18 = (bf16[160,256]{1,0:T(8,128)(2,1)S(1)}, bf16[160,256]{1,0:T(8,128)(2,1)S(1)}, u32[]{:S(2)}, u32[]{:S(2)}) collective-permute-start(bf16[160,256]{1,0:T(8,128)(2,1)S(1)} %copy-done.9), channel_id=1, source_target_pairs={{0,64},{64,0},{128,192},{192,128},{1,65},{65,1},{129,193},{193,129... | collective-permute-start | bytes 245768 | tf_op jit(solution)/shard_map/ppermute | solution.py:24
  85.2 2.9 %collective-permute-start.19 = (bf16[160,256]{1,0:T(8,128)(2,1)S(1)}, bf16[160,256]{1,0:T(8,128)(2,1)S(1)}, u32[]{:S(2)}, u32[]{:S(2)}) collective-permute-start(bf16[160,256]{1,0:T(8,128)(2,1)S(1)} %copy-done.9), channel_id=1, source_target_pairs={{0,128},{64,192},{128,0},{192,64},{1,129},{65,193},{129,1},{193,65... | collective-permute-start | bytes 245768 | tf_op jit(solution)/shard_map/ppermute | solution.py:24
  88.4 8.2 %shard_map.102 = bf16[272,3584]{1,0:T(8,128)(2,1)} custom-call(s32[1]{0:T(128)} %bitcast.10.z_ref, bf16[256,1280]{1,0:T(8,128)(2,1)} %collective-permute-done.2.early_ref, bf16[256,1280]{1,0:T(8,128)(2,1)} %copy-done.6, bf16[256,1024]{1,0:T(8,128)(2,1)} %copy-done.8, bf16[2560,1024]{1,0:T(8,128)(2,1)} %bitcast.29), custom_call_target="tpu_custom_call" | custom-call | tf_op jit(solution)/shard_map/pallas_call | solution.py:159
  96.6 1.5 collective-permute-start.21
  98.8 1.8 %shard_map.103.refs_0_ = bf16[160,1024]{1,0:T(8,128)(2,1)} custom-call(s32[1]{0:T(128)} %bitcast.9.here_ref, bf16[160,256]{1,0:T(8,128)(2,1)} %shard_map.101.refs_0_, bf16[160,256]{1,0:T(8,128)(2,1)} %copy-done.13, bf16[160,256]{1,0:T(8,128)(2,1)} %copy-done.14, bf16[160,256]{1,0:T(8,128)(2,1)} %copy-done.15), custom_call_target="tpu_custom_call" | custom-call | tf_op jit(solution)/shard_map/pallas_call | solution.py:106
  100.6 3.1 %fusion.22 = f16[320,1024]{1,0:T(8,128)(2,1)} fusion(f16[320,1024]{1,0:T(8,128)(2,1)S(1)} %collective-permute-done.17, f32[1280,1024]{1,0:T(8,128)} %fusion.32, s32[]{:T(128)S(6)} %select_n.162, f32[]{:T(128)} %bitcast.5), kind=kLoop, calls=%fused_computation.41 | loop fusion | flops 2949120 | bytes 2621448 | tf_op jit(solution)/shard_map/convert_element_type | solution.py:55
  103.7 3.4 %fusion.23 = f16[320,1024]{1,0:T(8,128)(2,1)} fusion(f16[320,1024]{1,0:T(8,128)(2,1)} %collective-permute-done.16, f32[1280,1024]{1,0:T(8,128)} %copy-done.2, s32[]{:T(128)S(6)} %select_n.162, f32[]{:T(128)} %bitcast.5), kind=kLoop, calls=%fused_computation.42 | loop fusion | flops 2949120 | bytes 2621448 | tf_op jit(solution)/shard_map/convert_element_type | solution.py:55
  107.0 2.0 %collective-permute-start.23 = (f16[320,1024]{1,0:T(8,128)(2,1)}, f16[320,1024]{1,0:T(8,128)(2,1)}, u32[]{:S(2)}, u32[]{:S(2)}) collective-permute-start(f16[320,1024]{1,0:T(8,128)(2,1)} %fusion.22), channel_id=1, source_target_pairs={{0,7},{1,2},{2,1},{3,4},{4,3},{5,6},{6,5},{7,0},{8,15},{9,10},{10,... | collective-permute-start | bytes 1966088 | tf_op jit(solution)/shard_map/ppermute | solution.py:339
  109.6 7.0 %shard_map.104 = (f32[256,1024]{1,0:T(8,128)}, bf16[256,5120]{1,0:T(8,128)(2,1)}) custom-call(s32[1]{0:T(128)} %bitcast.12._, bf16[256,5120]{1,0:T(8,128)(2,1)} %bitcast.25, bf16[256,1024]{1,0:T(8,128)(2,1)} %bitcast.32, bf16[2560,1024]{1,0:T(8,128)(2,1)} %bitcast.30), custom_call_target="tpu_custom_call" | custom-call | tf_op jit(solution)/shard_map/pallas_call | solution.py:192
  117.3 1.6 %shard_map.105 = f32[320,64]{1,0:T(8,128)} custom-call(s32[1]{0:T(128)} %bitcast.13.here_ref, f32[160,64]{1,0:T(8,128)} %get-tuple-element.112.refs_0_, f32[160,64]{1,0:T(8,128)} %copy-done.16), custom_call_target="tpu_custom_call" | custom-call | tf_op jit(solution)/shard_map/pallas_call | solution.py:106
  118.9 0.8 copy-done.10
  119.6 2.0 %shard_map.106 = bf16[320,1024]{1,0:T(8,128)(2,1)} custom-call(s32[1]{0:T(128)} %bitcast.13.here_ref, bf16[160,1024]{1,0:T(8,128)(2,1)} %shard_map.103.refs_0_, bf16[160,1024]{1,0:T(8,128)(2,1)} %copy-done.10), custom_call_target="tpu_custom_call" | custom-call | tf_op jit(solution)/shard_map/pallas_call | solution.py:106
  121.6 5.0 %fusion.25 = (f16[320,1024]{1,0:T(8,128)(2,1)}, f16[320,1024]{1,0:T(8,128)(2,1)}) fusion(f16[320,1024]{1,0:T(8,128)(2,1)S(1)} %collective-permute-done.22, f32[1280,1024]{1,0:T(8,128)} %fusion.32, s32[]{:T(128)S(6)} %select_n.177, f32[]{:T(128)} %bitcast.5, f16[320,1024]{1,0:T(8,128)(2,1)} %collective-permute-done.23, s32[]{:T(128)S(6)} %select_n.164), kind=kLoop, calls=%fused_computation.44 | loop fusion | flops 5898240 | bytes 5242892 | tf_op jit(solution)/shard_map/convert_element_type | solution.py:55
  126.5 1.0 collective-permute-start.26
  127.5 1.4 collective-permute-start.27
  128.9 0.8 copy.14
  129.7 8.9 %collective-permute-done.21.coded_ref.back_ref = bf16[272,3584]{1,0:T(8,128)(2,1)S(1)} collective-permute-done((bf16[272,3584]{1,0:T(8,128)(2,1)}, bf16[272,3584]{1,0:T(8,128)(2,1)S(1)}, u32[]{:S(2)}, u32[]{:S(2)}) %collective-permute-start.21) | collective-permute-done | bytes 1949728 | tf_op jit(solution)/shard_map/ppermute | solution.py:24
  138.6 1.3 copy-done.1
  139.9 5.1 %shard_map.107 = (bf16[256,1024]{1,0:T(8,128)(2,1)}, bf16[256,5120]{1,0:T(8,128)(2,1)}) custom-call(s32[1]{0:T(128)} %bitcast._, bf16[256,5120]{1,0:T(8,128)(2,1)} %get-tuple-element.70.__, f32[256,1024]{1,0:T(8,128)} %get-tuple-element.71.keys_ref, bf16[272,3584]{1,0:T(8,128)(2,1)} %copy-done.1, ...), custom_call_target="tpu_custom_call", output_to_operand_aliasing={{1}: (1, {})} | custom-call | tf_op jit(solution)/shard_map/pallas_call | solution.py:227
  145.4 4.0 %fusion.46 = bf16[1,320,1024]{2,1,0:T(8,128)(2,1)} fusion(f32[]{:T(128)} %bitcast.16, f16[320,1024]{1,0:T(8,128)(2,1)} %collective-permute-done.27, f16[320,1024]{1,0:T(8,128)(2,1)S(1)} %collective-permute-done.26, f32[]{:T(128)} %bitcast.5, f32[1280,1024]{1,0:T(8,128)} %fusion.32, s32[]{:T(128)S(6)} %select_n.165), kind=kLoop, calls=%fused_computation.78 | loop fusion | flops 4259840 | bytes 3276812 | tf_op jit(solution)/shard_map/broadcast_in_dim | solution.py:411
  (93 shorter events, 10.5 us)
Async XLA Ops:
  7.2 2.8 %copy-start.3 = (bf16[1,256,1024]{2,1,0:T(8,128)(2,1)S(1)}, bf16[1,256,1024]{2,1,0:T(8,128)(2,1)}, u32[]{:S(2)}) copy-start(bf16[1,256,1024]{2,1,0:T(8,128)(2,1)} %param.8) | copy-start | bytes 1572868
  7.2 81.2 %all-gather.3.cloned.1.call-start = ((), (), s32[]{:S(2)}) async-start(), calls=%async_computation | async-start | bytes 5898240 | tf_op jit(solution)/shard_map/all_gather | solution.py:275
  9.9 9.3 %collective-permute-start.1 = (f32[160,1024]{1,0:T(8,128)}, f32[160,1024]{1,0:T(8,128)}, u32[]{:S(2)}, u32[]{:S(2)}) collective-permute-start(f32[160,1024]{1,0:T(8,128)} %dynamic-slice_bitcast_fusion), channel_id=1, source_target_pairs={{0,16},{16,0},{1,17},{17,1},{2,18},{18,2},{3,19},{19,3},{4,20},{20... | collective-permute-start | bytes 1966088 | tf_op jit(solution)/shard_map/ppermute | solution.py:24
  11.2 6.1 %copy-start = (bf16[1,256,5120]{2,1,0:T(8,128)(2,1)S(1)}, bf16[1,256,5120]{2,1,0:T(8,128)(2,1)}, u32[]{:S(2)}) copy-start(bf16[1,256,5120]{2,1,0:T(8,128)(2,1)} %param.6) | copy-start | bytes 7864324
  15.0 10.9 %collective-permute-start = (f32[8,128]{1,0:T(8,128)S(1)}, f32[8,128]{1,0:T(8,128)S(1)}, u32[]{:S(2)}, u32[]{:S(2)}) collective-permute-start(f32[8,128]{1,0:T(8,128)S(1)} %iota.32), channel_id=1, source_target_pairs={{0,8},{8,0},{1,9},{9,1},{2,10},{10,2},{3,11},{11,3},{4,12},{12,4},... | collective-permute-start | bytes 12296 | tf_op jit(solution)/shard_map/ppermute | solution.py:24
  17.3 1.1 copy-start.11
  18.3 29.0 %collective-permute-start.2 = (bf16[256,1280]{1,0:T(8,128)(2,1)}, bf16[256,1280]{1,0:T(8,128)(2,1)}, u32[]{:S(2)}, u32[]{:S(2)}) collective-permute-start(bf16[256,1280]{1,0:T(8,128)(2,1)} %pad_maximum_fusion.3), channel_id=1, source_target_pairs={{0,8},{8,0},{1,9},{9,1},{2,10},{10,2},{3,11},{11,3},{4,12},{12,4},... | collective-permute-start | bytes 1966088 | tf_op jit(solution)/shard_map/ppermute | solution.py:24
  18.6 11.8 %collective-permute-start.9 = (f32[160,64]{1,0:T(8,128)S(1)}, f32[160,64]{1,0:T(8,128)S(1)}, u32[]{:S(2)}, u32[]{:S(2)}) collective-permute-start(f32[160,64]{1,0:T(8,128)S(1)} %copy.15), channel_id=1, source_target_pairs={{0,16},{16,0},{1,17},{17,1},{2,18},{18,2},{3,19},{19,3},{4,20},{20... | collective-permute-start | bytes 122888 | tf_op jit(solution)/shard_map/ppermute | solution.py:24
  19.1 1.3 copy-start.4
  21.7 10.7 %collective-permute-start.6 = (f32[160,256]{1,0:T(8,128)S(1)}, f32[160,256]{1,0:T(8,128)S(1)}, u32[]{:S(2)}, u32[]{:S(2)}) collective-permute-start(f32[160,256]{1,0:T(8,128)S(1)} %get-tuple-element.106), channel_id=1, source_target_pairs={{0,64},{64,0},{128,192},{192,128},{1,65},{65,1},{129,193},{193,129... | collective-permute-start | bytes 491528 | tf_op jit(solution)/shard_map/ppermute | solution.py:24
  22.9 11.0 %collective-permute-start.7 = (f32[160,256]{1,0:T(8,128)S(1)}, f32[160,256]{1,0:T(8,128)S(1)}, u32[]{:S(2)}, u32[]{:S(2)}) collective-permute-start(f32[160,256]{1,0:T(8,128)S(1)} %get-tuple-element.105), channel_id=1, source_target_pairs={{0,128},{64,192},{128,0},{192,64},{1,129},{65,193},{129,1},{193,65... | collective-permute-start | bytes 491528 | tf_op jit(solution)/shard_map/ppermute | solution.py:24
  26.0 3.7 %collective-permute-start.4 = (f32[8,128]{1,0:T(8,128)S(1)}, f32[8,128]{1,0:T(8,128)S(1)}, u32[]{:S(2)}, u32[]{:S(2)}) collective-permute-start(f32[8,128]{1,0:T(8,128)S(1)} %maximum_select_fusion.3), channel_id=1, source_target_pairs={{0,1},{1,0},{2,3},{3,2},{4,5},{5,4},{6,7},{7,6},{8,9},{9,8},{10,11... | collective-permute-start | bytes 12296 | tf_op jit(solution)/shard_map/ppermute | solution.py:24
  29.7 7.5 %collective-permute-start.8 = (f32[160,256]{1,0:T(8,128)S(1)}, f32[160,256]{1,0:T(8,128)S(1)}, u32[]{:S(2)}, u32[]{:S(2)}) collective-permute-start(f32[160,256]{1,0:T(8,128)S(1)} %get-tuple-element.104), channel_id=1, source_target_pairs={{0,192},{64,128},{128,64},{192,0},{1,193},{65,129},{129,65},{193,1... | collective-permute-start | bytes 491528 | tf_op jit(solution)/shard_map/ppermute | solution.py:24
  30.4 16.9 %collective-permute-start.3 = (bf16[256,1024]{1,0:T(8,128)(2,1)S(1)}, bf16[256,1024]{1,0:T(8,128)(2,1)S(1)}, u32[]{:S(2)}, u32[]{:S(2)}) collective-permute-start(bf16[256,1024]{1,0:T(8,128)(2,1)S(1)} %bitcast.33), channel_id=1, source_target_pairs={{0,8},{8,0},{1,9},{9,1},{2,10},{10,2},{3,11},{11,3},{4,12},{12,4},... | collective-permute-start | bytes 1572872 | tf_op jit(solution)/shard_map/ppermute | solution.py:24
  32.3 29.1 %collective-permute-start.14 = (bf16[256,1280]{1,0:T(8,128)(2,1)S(1)}, bf16[256,1280]{1,0:T(8,128)(2,1)S(1)}, u32[]{:S(2)}, u32[]{:S(2)}) collective-permute-start(bf16[256,1280]{1,0:T(8,128)(2,1)S(1)} %pad_maximum_fusion.4), channel_id=1, source_target_pairs={{0,8},{8,0},{1,9},{9,1},{2,10},{10,2},{3,11},{11,3},{4,12},{12,4},... | collective-permute-start | bytes 1966088 | tf_op jit(solution)/shard_map/ppermute | solution.py:24
  33.8 5.7 %collective-permute-start.5 = (f32[8,128]{1,0:T(8,128)S(1)}, f32[8,128]{1,0:T(8,128)S(1)}, u32[]{:S(2)}, u32[]{:S(2)}) collective-permute-start(f32[8,128]{1,0:T(8,128)S(1)} %maximum_select_fusion.2), channel_id=1, source_target_pairs={{0,2},{1,3},{2,0},{3,1},{4,6},{5,7},{6,4},{7,5},{8,10},{9,11},{10,... | collective-permute-start | bytes 12296 | tf_op jit(solution)/shard_map/ppermute | solution.py:24
  37.3 27.9 %collective-permute-start.13 = (f32[160,128]{1,0:T(8,128)S(1)}, f32[160,128]{1,0:T(8,128)S(1)}, u32[]{:S(2)}, u32[]{:S(2)}) collective-permute-start(f32[160,128]{1,0:T(8,128)S(1)} %constant_dynamic-slice_fusion.1), channel_id=1, source_target_pairs={{0,32},{32,0},{1,33},{33,1},{2,34},{34,2},{3,35},{35,3},{4,36},{36... | collective-permute-start | bytes 245768 | tf_op jit(solution)/shard_map/ppermute | solution.py:24
  39.6 10.6 %collective-permute-start.10 = (f32[8,128]{1,0:T(8,128)S(1)}, f32[8,128]{1,0:T(8,128)S(1)}, u32[]{:S(2)}, u32[]{:S(2)}) collective-permute-start(f32[8,128]{1,0:T(8,128)S(1)} %maximum_select_fusion.1), channel_id=1, source_target_pairs={{0,4},{1,5},{2,6},{3,7},{4,0},{5,1},{6,2},{7,3},{8,12},{9,13},{10,... | collective-permute-start | bytes 12296 | tf_op jit(solution)/shard_map/ppermute | solution.py:24
  47.3 14.0 %copy-start.8 = (bf16[256,1024]{1,0:T(8,128)(2,1)}, bf16[256,1024]{1,0:T(8,128)(2,1)S(1)}, u32[]{:S(2)}) copy-start(bf16[256,1024]{1,0:T(8,128)(2,1)S(1)} %collective-permute-done.3.cotangent_ref) | copy-start | bytes 1572868
  50.2 15.1 %copy-start.2 = (f32[1280,1024]{1,0:T(8,128)}, f32[1280,1024]{1,0:T(8,128)S(1)}, u32[]{:S(2)}) copy-start(f32[1280,1024]{1,0:T(8,128)S(1)} %fusion.26) | copy-start | bytes 15728644
  52.6 21.3 %collective-permute-start.11 = (f16[160,1024]{1,0:T(8,128)(2,1)S(1)}, f16[160,1024]{1,0:T(8,128)(2,1)S(1)}, u32[]{:S(2)}, u32[]{:S(2)}) collective-permute-start(f16[160,1024]{1,0:T(8,128)(2,1)S(1)} %get-tuple-element.95), channel_id=1, source_target_pairs={{0,1},{1,0},{2,3},{3,2},{4,5},{5,4},{6,7},{7,6},{8,9},{9,8},{10,11... | collective-permute-start | bytes 983048 | tf_op jit(solution)/shard_map/ppermute | solution.py:339
  53.2 20.7 %collective-permute-start.12 = (f16[160,1024]{1,0:T(8,128)(2,1)S(1)}, f16[160,1024]{1,0:T(8,128)(2,1)}, u32[]{:S(2)}, u32[]{:S(2)}) collective-permute-start(f16[160,1024]{1,0:T(8,128)(2,1)S(1)} %get-tuple-element.94), channel_id=1, source_target_pairs={{0,7},{1,2},{2,1},{3,4},{4,3},{5,6},{6,5},{7,0},{8,15},{9,10},{10,... | collective-permute-start | bytes 983048 | tf_op jit(solution)/shard_map/ppermute | solution.py:339
  61.4 3.9 %copy-start.6 = (bf16[256,1280]{1,0:T(8,128)(2,1)}, bf16[256,1280]{1,0:T(8,128)(2,1)S(1)}, u32[]{:S(2)}) copy-start(bf16[256,1280]{1,0:T(8,128)(2,1)S(1)} %collective-permute-done.14.late_ref) | copy-start | bytes 1966084
  66.2 5.6 %copy-start.12 = (bf16[160,128]{1,0:T(8,128)(2,1)}, bf16[160,128]{1,0:T(8,128)(2,1)S(1)}, u32[]{:S(2)}) copy-start(bf16[160,128]{1,0:T(8,128)(2,1)S(1)} %get-tuple-element.86.refs_0_) | copy-start | bytes 122884
  66.2 5.6 %collective-permute-start.15 = (bf16[160,128]{1,0:T(8,128)(2,1)S(1)}, bf16[160,128]{1,0:T(8,128)(2,1)S(1)}, u32[]{:S(2)}, u32[]{:S(2)}) collective-permute-start(bf16[160,128]{1,0:T(8,128)(2,1)S(1)} %get-tuple-element.86.refs_0_), channel_id=1, source_target_pairs={{0,32},{32,0},{1,33},{33,1},{2,34},{34,2},{3,35},{35,3},{4,36},{36... | collective-permute-start | bytes 122888 | tf_op jit(solution)/shard_map/ppermute | solution.py:24
  71.8 0.6 copy-start.17
  77.5 6.1 %copy-start.9 = (bf16[160,256]{1,0:T(8,128)(2,1)S(1)}, bf16[160,256]{1,0:T(8,128)(2,1)}, u32[]{:S(2)}) copy-start(bf16[160,256]{1,0:T(8,128)(2,1)} %shard_map.101.refs_0_) | copy-start | bytes 245764
  77.5 23.0 %collective-permute-start.17 = (f16[320,1024]{1,0:T(8,128)(2,1)}, f16[320,1024]{1,0:T(8,128)(2,1)S(1)}, u32[]{:S(2)}, u32[]{:S(2)}) collective-permute-start(f16[320,1024]{1,0:T(8,128)(2,1)} %fusion.21), channel_id=1, source_target_pairs={{0,1},{1,0},{2,3},{3,2},{4,5},{5,4},{6,7},{7,6},{8,9},{9,8},{10,11... | collective-permute-start | bytes 1966088 | tf_op jit(solution)/shard_map/ppermute | solution.py:339
  78.7 25.0 %collective-permute-start.16 = (f16[320,1024]{1,0:T(8,128)(2,1)}, f16[320,1024]{1,0:T(8,128)(2,1)}, u32[]{:S(2)}, u32[]{:S(2)}) collective-permute-start(f16[320,1024]{1,0:T(8,128)(2,1)} %fusion.20), channel_id=1, source_target_pairs={{0,7},{1,2},{2,1},{3,4},{4,3},{5,6},{6,5},{7,0},{8,15},{9,10},{10,... | collective-permute-start | bytes 1966088 | tf_op jit(solution)/shard_map/ppermute | solution.py:339
  83.7 12.9 %collective-permute-start.18 = (bf16[160,256]{1,0:T(8,128)(2,1)S(1)}, bf16[160,256]{1,0:T(8,128)(2,1)S(1)}, u32[]{:S(2)}, u32[]{:S(2)}) collective-permute-start(bf16[160,256]{1,0:T(8,128)(2,1)S(1)} %copy-done.9), channel_id=1, source_target_pairs={{0,64},{64,0},{128,192},{192,128},{1,65},{65,1},{129,193},{193,129... | collective-permute-start | bytes 245768 | tf_op jit(solution)/shard_map/ppermute | solution.py:24
  85.2 12.9 %collective-permute-start.19 = (bf16[160,256]{1,0:T(8,128)(2,1)S(1)}, bf16[160,256]{1,0:T(8,128)(2,1)S(1)}, u32[]{:S(2)}, u32[]{:S(2)}) collective-permute-start(bf16[160,256]{1,0:T(8,128)(2,1)S(1)} %copy-done.9), channel_id=1, source_target_pairs={{0,128},{64,192},{128,0},{192,64},{1,129},{65,193},{129,1},{193,65... | collective-permute-start | bytes 245768 | tf_op jit(solution)/shard_map/ppermute | solution.py:24
  88.1 10.0 %collective-permute-start.20 = (bf16[160,256]{1,0:T(8,128)(2,1)S(1)}, bf16[160,256]{1,0:T(8,128)(2,1)S(1)}, u32[]{:S(2)}, u32[]{:S(2)}) collective-permute-start(bf16[160,256]{1,0:T(8,128)(2,1)S(1)} %copy-done.9), channel_id=1, source_target_pairs={{0,192},{64,128},{128,64},{192,0},{1,193},{65,129},{129,65},{193,1... | collective-permute-start | bytes 245768 | tf_op jit(solution)/shard_map/ppermute | solution.py:24
  96.6 1.6 copy-start.13
  96.6 42.0 %collective-permute-start.21 = (bf16[272,3584]{1,0:T(8,128)(2,1)}, bf16[272,3584]{1,0:T(8,128)(2,1)S(1)}, u32[]{:S(2)}, u32[]{:S(2)}) collective-permute-start(bf16[272,3584]{1,0:T(8,128)(2,1)} %shard_map.102), channel_id=1, source_target_pairs={{0,8},{8,0},{1,9},{9,1},{2,10},{10,2},{3,11},{11,3},{4,12},{12,4},... | collective-permute-start | bytes 5849096 | tf_op jit(solution)/shard_map/ppermute | solution.py:24
  98.1 0.6 copy-start.14
  98.1 0.7 copy-start.15
  103.7 5.4 %copy-start.5 = (bf16[160,1024]{1,0:T(8,128)(2,1)S(1)}, bf16[160,1024]{1,0:T(8,128)(2,1)}, u32[]{:S(2)}) copy-start(bf16[160,1024]{1,0:T(8,128)(2,1)} %shard_map.103.refs_0_) | copy-start | bytes 983044
  107.0 14.5 %collective-permute-start.22 = (f16[320,1024]{1,0:T(8,128)(2,1)}, f16[320,1024]{1,0:T(8,128)(2,1)S(1)}, u32[]{:S(2)}, u32[]{:S(2)}) collective-permute-start(f16[320,1024]{1,0:T(8,128)(2,1)} %fusion.23), channel_id=1, source_target_pairs={{0,1},{1,0},{2,3},{3,2},{4,5},{5,4},{6,7},{7,6},{8,9},{9,8},{10,11... | collective-permute-start | bytes 1966088 | tf_op jit(solution)/shard_map/ppermute | solution.py:339
  107.0 14.6 %collective-permute-start.23 = (f16[320,1024]{1,0:T(8,128)(2,1)}, f16[320,1024]{1,0:T(8,128)(2,1)}, u32[]{:S(2)}, u32[]{:S(2)}) collective-permute-start(f16[320,1024]{1,0:T(8,128)(2,1)} %fusion.22), channel_id=1, source_target_pairs={{0,7},{1,2},{2,1},{3,4},{4,3},{5,6},{6,5},{7,0},{8,15},{9,10},{10,... | collective-permute-start | bytes 1966088 | tf_op jit(solution)/shard_map/ppermute | solution.py:339
  109.1 9.8 %collective-permute-start.24 = (bf16[160,1024]{1,0:T(8,128)(2,1)S(1)}, bf16[160,1024]{1,0:T(8,128)(2,1)S(1)}, u32[]{:S(2)}, u32[]{:S(2)}) collective-permute-start(bf16[160,1024]{1,0:T(8,128)(2,1)S(1)} %copy-done.5), channel_id=1, source_target_pairs={{0,16},{16,0},{1,17},{17,1},{2,18},{18,2},{3,19},{19,3},{4,20},{20... | collective-permute-start | bytes 983048 | tf_op jit(solution)/shard_map/ppermute | solution.py:24
  109.1 7.6 %collective-permute-start.25 = (f32[160,64]{1,0:T(8,128)S(1)}, f32[160,64]{1,0:T(8,128)S(1)}, u32[]{:S(2)}, u32[]{:S(2)}) collective-permute-start(f32[160,64]{1,0:T(8,128)S(1)} %get-tuple-element.111), channel_id=1, source_target_pairs={{0,16},{16,0},{1,17},{17,1},{2,18},{18,2},{3,19},{19,3},{4,20},{20... | collective-permute-start | bytes 122888 | tf_op jit(solution)/shard_map/ppermute | solution.py:24
  116.6 0.6 copy-start.16
  118.9 0.8 copy-start.10
  121.6 7.4 %copy-start.7 = (f32[320,64]{1,0:T(8,128)S(1)}, f32[320,64]{1,0:T(8,128)}, u32[]{:S(2)}) copy-start(f32[320,64]{1,0:T(8,128)} %shard_map.105) | copy-start | bytes 245764
  126.5 18.4 %collective-permute-start.26 = (f16[320,1024]{1,0:T(8,128)(2,1)}, f16[320,1024]{1,0:T(8,128)(2,1)S(1)}, u32[]{:S(2)}, u32[]{:S(2)}) collective-permute-start(f16[320,1024]{1,0:T(8,128)(2,1)} %get-tuple-element.89), channel_id=1, source_target_pairs={{0,1},{1,0},{2,3},{3,2},{4,5},{5,4},{6,7},{7,6},{8,9},{9,8},{10,11... | collective-permute-start | bytes 1966088 | tf_op jit(solution)/shard_map/ppermute | solution.py:400
  127.5 17.9 %collective-permute-start.27 = (f16[320,1024]{1,0:T(8,128)(2,1)}, f16[320,1024]{1,0:T(8,128)(2,1)}, u32[]{:S(2)}, u32[]{:S(2)}) collective-permute-start(f16[320,1024]{1,0:T(8,128)(2,1)} %get-tuple-element.88), channel_id=1, source_target_pairs={{0,7},{1,2},{2,1},{3,4},{4,3},{5,6},{6,5},{7,0},{8,15},{9,10},{10,... | collective-permute-start | bytes 1966088 | tf_op jit(solution)/shard_map/ppermute | solution.py:400
  138.6 1.3 copy-start.1
Sparse Core Ops, SparseCore 0:
  9.8 76.4 all-gather.2

commit v9 on v8

--- a/solution.py
+++ b/solution.py
@@ -380,15 +380,13 @@
     order.did(sent)
     products_back = swap(sent, "xl")
 
+    even, odd = ring_step(2, even, odd)
+
     wides = order.step(*wides)
     block = assemble(y, lambda i: (i, i ^ 1, i ^ 2, i ^ 3), (wide, *wides), 1)
     order.did(block)
     block_other = swap(block, "c")
 
-    even, odd = ring_step(2, even, odd)
-
-    keys_mine, grads_mine = products_here(order.step(x), tokens, cotangent, weight_half)
-    order.did(keys_mine, grads_mine)
     new_momentum = assemble(c, lambda i: (i, 1 - i), (keep, order.step(new_other)), 0)
     order.did(new_momentum)
     new_fragment = assemble(c, lambda i: (i, 1 - i), (block, order.step(block_other)), 0)
@@ -399,6 +397,8 @@
     order.did(even, odd)
     even, odd = lax.ppermute(even, "z", EVEN), lax.ppermute(odd, "z", ODD)
 
+    keys_mine, grads_mine = products_here(order.step(x), tokens, cotangent, weight_half)
+    order.did(keys_mine, grads_mine)
     products_back = order.step(products_back)
     key_out, act_grad = finish(x, keys_mine, grads_mine, products_back)
     order.did(key_out, act_grad)

time: 158 us -> 161 us (1.019)
  starting transfers between devices: 46.5 us -> 49.6 us
    ppermute x20, waiting for transfers between devices: 20.3 us -> 16.7 us  [swap(): lax.ppermute(value, axis, [(i, i ^ mask) for i in range(SIZES[axis])])]
    all_gather x1, waiting for transfers between devices: 0.01 us -> 2.56 us  [shards(): weight_half = lax.all_gather(weight, 'z', axis=0, tiled=True)]
    ppermute x6, starting transfers between devices: 12.4 us -> 14.1 us  [send(): return lax.ppermute(message, 'z', pairs)]
    unnamed x39 -> x37, local copies, waits for them, and re-layouts: 6.11 us -> 6.08 us
  transfers between devices with their start and end apart: 29 -> 29, of which waited for: 8 -> 14; matrix products, arithmetic and copies ran while one was open for 23% -> 22% of each run, Pallas kernels for 17% -> 17%
where the time goes in v9:
time: 161 us; the launch traced here: 160 us
  starting transfers between devices  49.6 us (31%)
  other arithmetic  28.7 us (18%)
  Pallas kernels  27.1 us (17%)
  waiting for transfers between devices  22.6 us (14%)
  between operations  16.4 us (10%)
  local copies, waits for them, and re-layouts  9.27 us (6%)
  matrix products  6.8 us (4%)
    ppermute x20, starting transfers between devices, swap(): lax.ppermute(value, axis, [(i, i ^ mask) for i in range(SIZES[axis])])  32.6 us
    ppermute x20, waiting for transfers between devices, swap(): lax.ppermute(value, axis, [(i, i ^ mask) for i in range(SIZES[axis])])  16.7 us
    ppermute x6, starting transfers between devices, send(): return lax.ppermute(message, 'z', pairs)  14.1 us
    convert_element_type x6, other arithmetic, encode(): return (scaled * jnp.abs(scaled)).astype(F16)  13.6 us
    pallas_call x1, Pallas kernels, products_for_partner(): pl.pallas_call(body, grid_spec=pltpu.PrefetchScalarGridSpec(num_scalar_pr...  8.19 us
    pallas_call x1, Pallas kernels, products_here(): pl.pallas_call(body, grid_spec=pltpu.PrefetchScalarGridSpec(num_scalar_pr...  7.05 us
    dot_general x2, matrix products, product(): lax.dot_general(jnp.concatenate([first, second], axis=0), jnp.concatenate...  6.8 us
    pallas_call x4, Pallas kernels, assemble(): pl.pallas_call(body, grid_spec=pltpu.PrefetchScalarGridSpec(num_scalar_pr...  6.77 us
  transfers between devices with their start and end apart: 29, of which 14 were waited for; matrix products, arithmetic and copies ran while one was open for 22% of the time, Pallas kernels for 17%

profile of v9, /device:TPU:2, one launch (start us, length us, event | category | flops | bytes accessed | tf_op | source)
XLA Modules:
  0.0 160.5 jit_solution(8816848161182662077)
XLA Ops:
  7.9 2.0 %dynamic-slice_bitcast_fusion = f32[160,1024]{1,0:T(8,128)} fusion(f32[1,320,1024]{2,1,0:T(8,128)} %param.10, s32[]{:T(128)S(6)} %select_n.146), kind=kLoop, calls=%fused_computation.77 | loop fusion | bytes 1310724 | tf_op jit(solution)/shard_map/dynamic_slice | solution.py:40
  11.3 2.4 %abs_reduce_fusion = f32[5120]{0:T(1024)S(1)} fusion(bf16[256,5120]{1,0:T(8,128)(2,1)} %bitcast.24), kind=kLoop, calls=%fused_computation | loop fusion | flops 3927040 | bytes 2641920 | tf_op jit(solution)/shard_map/reduce_sum | solution.py:68
  15.0 2.3 %collective-permute-start.2 = (f32[8,128]{1,0:T(8,128)S(1)}, f32[8,128]{1,0:T(8,128)S(1)}, u32[]{:S(2)}, u32[]{:S(2)}) collective-permute-start(f32[8,128]{1,0:T(8,128)S(1)} %iota.31), channel_id=1, source_target_pairs={{0,8},{8,0},{1,9},{9,1},{2,10},{10,2},{3,11},{11,3},{4,12},{12,4},... | collective-permute-start | bytes 12296 | tf_op jit(solution)/shard_map/ppermute | solution.py:24
  17.4 0.9 pad_maximum_fusion.3
  19.2 1.2 copy-done.4
  20.4 1.2 bitcast_add_fusion
  21.7 1.2 collective-permute-start.7
  22.9 2.9 %collective-permute-start.8 = (f32[160,256]{1,0:T(8,128)S(1)}, f32[160,256]{1,0:T(8,128)S(1)}, u32[]{:S(2)}, u32[]{:S(2)}) collective-permute-start(f32[160,256]{1,0:T(8,128)S(1)} %get-tuple-element.105), channel_id=1, source_target_pairs={{0,128},{64,192},{128,0},{192,64},{1,129},{65,193},{129,1},{193,65... | collective-permute-start | bytes 491528 | tf_op jit(solution)/shard_map/ppermute | solution.py:24
  26.0 1.9 %collective-permute-start.5 = (f32[8,128]{1,0:T(8,128)S(1)}, f32[8,128]{1,0:T(8,128)S(1)}, u32[]{:S(2)}, u32[]{:S(2)}) collective-permute-start(f32[8,128]{1,0:T(8,128)S(1)} %maximum_select_fusion.3), channel_id=1, source_target_pairs={{0,1},{1,0},{2,3},{3,2},{4,5},{5,4},{6,7},{7,6},{8,9},{9,8},{10,11... | collective-permute-start | bytes 12296 | tf_op jit(solution)/shard_map/ppermute | solution.py:24
  28.1 1.7 %collective-permute-done.5 = f32[8,128]{1,0:T(8,128)S(1)} collective-permute-done((f32[8,128]{1,0:T(8,128)S(1)}, f32[8,128]{1,0:T(8,128)S(1)}, u32[]{:S(2)}, u32[]{:S(2)}) %collective-permute-start.5) | collective-permute-done | bytes 4128 | tf_op jit(solution)/shard_map/ppermute | solution.py:24
  30.4 1.9 %collective-permute-start.4 = (bf16[256,1024]{1,0:T(8,128)(2,1)S(1)}, bf16[256,1024]{1,0:T(8,128)(2,1)S(1)}, u32[]{:S(2)}, u32[]{:S(2)}) collective-permute-start(bf16[256,1024]{1,0:T(8,128)(2,1)S(1)} %bitcast.33), channel_id=1, source_target_pairs={{0,8},{8,0},{1,9},{9,1},{2,10},{10,2},{3,11},{11,3},{4,12},{12,4},... | collective-permute-start | bytes 1572872 | tf_op jit(solution)/shard_map/ppermute | solution.py:24
  32.5 1.4 collective-permute-done.8
  33.8 3.3 %collective-permute-start.6 = (f32[8,128]{1,0:T(8,128)S(1)}, f32[8,128]{1,0:T(8,128)S(1)}, u32[]{:S(2)}, u32[]{:S(2)}) collective-permute-start(f32[8,128]{1,0:T(8,128)S(1)} %maximum_select_fusion.2), channel_id=1, source_target_pairs={{0,2},{1,3},{2,0},{3,1},{4,6},{5,7},{6,4},{7,5},{8,10},{9,11},{10,... | collective-permute-start | bytes 12296 | tf_op jit(solution)/shard_map/ppermute | solution.py:24
  37.3 2.2 %collective-permute-start.14 = (f32[160,128]{1,0:T(8,128)S(1)}, f32[160,128]{1,0:T(8,128)S(1)}, u32[]{:S(2)}, u32[]{:S(2)}) collective-permute-start(f32[160,128]{1,0:T(8,128)S(1)} %constant_dynamic-slice_fusion.1), channel_id=1, source_target_pairs={{0,32},{32,0},{1,33},{33,1},{2,34},{34,2},{3,35},{35,3},{4,36},{36... | collective-permute-start | bytes 245768 | tf_op jit(solution)/shard_map/ppermute | solution.py:24
  39.6 7.2 %collective-permute-start.11 = (f32[8,128]{1,0:T(8,128)S(1)}, f32[8,128]{1,0:T(8,128)S(1)}, u32[]{:S(2)}, u32[]{:S(2)}) collective-permute-start(f32[8,128]{1,0:T(8,128)S(1)} %maximum_select_fusion.1), channel_id=1, source_target_pairs={{0,4},{1,5},{2,6},{3,7},{4,0},{5,1},{6,2},{7,3},{8,12},{9,13},{10,... | collective-permute-start | bytes 12296 | tf_op jit(solution)/shard_map/ppermute | solution.py:24
  47.3 2.9 %fusion.26 = f32[1280,1024]{1,0:T(8,128)S(1)} fusion(bf16[256,1280]{1,0:T(8,128)(2,1)} %collective-permute-done.3.early_ref, bf16[256,640]{1,0:T(8,128)(2,1)S(1)} %get-tuple-element.99, bf16[256,640]{1,0:T(8,128)(2,1)S(1)} %get-tuple-element.98, bf16[256,1024]{1,0:T(8,128)(2,1)S(1)} %collective-permute-done.4.cotangent_ref, bf16[256,1024]{1,0:T(8,128)(2,1)S(1)} %bitcast.34), kind=kOutput, calls=%fused_computation.45 | convolution fusion | flops 1348206592 | bytes 7602176 | tf_op jit(solution)/shard_map/dot_general | solution.py:315
  53.2 4.6 %collective-permute-start.13 = (f16[160,1024]{1,0:T(8,128)(2,1)S(1)}, f16[160,1024]{1,0:T(8,128)(2,1)}, u32[]{:S(2)}, u32[]{:S(2)}) collective-permute-start(f16[160,1024]{1,0:T(8,128)(2,1)S(1)} %get-tuple-element.94), channel_id=1, source_target_pairs={{0,7},{1,2},{2,1},{3,4},{4,3},{5,6},{6,5},{7,0},{8,15},{9,10},{10,... | collective-permute-start | bytes 983048 | tf_op jit(solution)/shard_map/ppermute | solution.py:339
  57.8 3.6 %collective-permute-done.1.late_ref = bf16[256,1280]{1,0:T(8,128)(2,1)S(1)} collective-permute-done((bf16[256,1280]{1,0:T(8,128)(2,1)S(1)}, bf16[256,1280]{1,0:T(8,128)(2,1)S(1)}, u32[]{:S(2)}, u32[]{:S(2)}) %collective-permute-start.1) | collective-permute-done | bytes 655392 | tf_op jit(solution)/shard_map/ppermute | solution.py:24
  61.4 4.0 %fusion.32 = f32[1280,1024]{1,0:T(8,128)} fusion(bf16[256,1280]{1,0:T(8,128)(2,1)S(1)} %collective-permute-done.1.late_ref, bf16[256,640]{1,0:T(8,128)(2,1)S(1)} %get-tuple-element.97, bf16[256,640]{1,0:T(8,128)(2,1)S(1)} %get-tuple-element.96, bf16[256,1024]{1,0:T(8,128)(2,1)S(1)} %collective-permute-done.4.cotangent_ref, bf16[256,1024]{1,0:T(8,128)(2,1)S(1)} %bitcast.35), kind=kOutput, calls=%fused_computation.51 | convolution fusion | flops 1348206592 | bytes 7602176 | tf_op jit(solution)/shard_map/dot_general | solution.py:315
  65.3 0.9 subtract_convert_fusion
  67.7 4.1 %collective-permute-done.15.refs_1_ = bf16[160,128]{1,0:T(8,128)(2,1)S(1)} collective-permute-done((bf16[160,128]{1,0:T(8,128)(2,1)S(1)}, bf16[160,128]{1,0:T(8,128)(2,1)S(1)}, u32[]{:S(2)}, u32[]{:S(2)}) %collective-permute-start.15) | collective-permute-done | bytes 40992 | tf_op jit(solution)/shard_map/ppermute | solution.py:24
  72.5 1.5 shard_map.101.refs_0_
  73.9 2.7 %dynamic-slice_multiply_fusion = (f32[160,1024]{1,0:T(8,128)S(1)}, f32[160,1024]{1,0:T(8,128)S(1)}, f32[160,1024]{1,0:T(8,128)S(1)}, f32[160,1024]{1,0:T(8,128)S(1)}) fusion(f32[1280,1024]{1,0:T(8,128)} %copy-done.2, s32[]{:T(128)S(6)} %select_n.177, f32[]{:T(128)} %bitcast.7, f16[160,1024]{1,0:T(8,128)(2,1)} %collective-permute-done.13, s32[]{:T(128)S(6)} %select_n.178, ...), kind=kLoop, calls=%fused_computation.75 | loop fusion | flops 2293760 | bytes 5898260 | tf_op jit(solution)/shard_map/mul | solution.py:333
  76.6 1.0 fusion.21
  77.8 1.0 fusion.20
  78.8 4.9 %collective-permute-start.16 = (f16[320,1024]{1,0:T(8,128)(2,1)}, f16[320,1024]{1,0:T(8,128)(2,1)}, u32[]{:S(2)}, u32[]{:S(2)}) collective-permute-start(f16[320,1024]{1,0:T(8,128)(2,1)} %fusion.20), channel_id=1, source_target_pairs={{0,7},{1,2},{2,1},{3,4},{4,3},{5,6},{6,5},{7,0},{8,15},{9,10},{10,... | collective-permute-start | bytes 1966088 | tf_op jit(solution)/shard_map/ppermute | solution.py:339
  83.7 2.6 %all-gather.3.cloned.1.call-done = bf16[1,2560,1024]{2,1,0:T(8,128)(2,1)} async-done(((bf16[1,320,1024]{2,1,0:T(8,128)(2,1)}), bf16[1,2560,1024]{2,1,0:T(8,128)(2,1)}) %all-gather.3.cloned.1.call-update) | async-done | bytes 5242896 | tf_op jit(solution)/shard_map/all_gather | solution.py:275
  86.3 8.2 %shard_map.102 = bf16[272,3584]{1,0:T(8,128)(2,1)} custom-call(s32[1]{0:T(128)} %bitcast.9.z_ref, bf16[256,1280]{1,0:T(8,128)(2,1)} %collective-permute-done.3.early_ref, bf16[256,1280]{1,0:T(8,128)(2,1)} %copy-done.5, bf16[256,1024]{1,0:T(8,128)(2,1)} %copy-done.7, bf16[2560,1024]{1,0:T(8,128)(2,1)} %bitcast.29), custom_call_target="tpu_custom_call" | custom-call | tf_op jit(solution)/shard_map/pallas_call | solution.py:159
  95.3 1.2 collective-permute-done.17
  96.5 3.1 %fusion.22 = f16[320,1024]{1,0:T(8,128)(2,1)} fusion(f16[320,1024]{1,0:T(8,128)(2,1)S(1)} %collective-permute-done.17, f32[1280,1024]{1,0:T(8,128)} %fusion.32, s32[]{:T(128)S(6)} %select_n.167, f32[]{:T(128)} %bitcast.7), kind=kLoop, calls=%fused_computation.41 | loop fusion | flops 2949120 | bytes 2621448 | tf_op jit(solution)/shard_map/convert_element_type | solution.py:55
  99.6 3.3 %fusion.23 = f16[320,1024]{1,0:T(8,128)(2,1)} fusion(f16[320,1024]{1,0:T(8,128)(2,1)} %collective-permute-done.16, f32[1280,1024]{1,0:T(8,128)} %copy-done.2, s32[]{:T(128)S(6)} %select_n.167, f32[]{:T(128)} %bitcast.7), kind=kLoop, calls=%fused_computation.42 | loop fusion | flops 2949120 | bytes 2621448 | tf_op jit(solution)/shard_map/convert_element_type | solution.py:55
  103.4 3.3 %collective-permute-start.19 = (f16[320,1024]{1,0:T(8,128)(2,1)}, f16[320,1024]{1,0:T(8,128)(2,1)}, u32[]{:S(2)}, u32[]{:S(2)}) collective-permute-start(f16[320,1024]{1,0:T(8,128)(2,1)} %fusion.22), channel_id=1, source_target_pairs={{0,7},{1,2},{2,1},{3,4},{4,3},{5,6},{6,5},{7,0},{8,15},{9,10},{10,... | collective-permute-start | bytes 1966088 | tf_op jit(solution)/shard_map/ppermute | solution.py:339
  106.7 1.5 collective-permute-start.20
  108.2 2.7 %collective-permute-start.21 = (bf16[160,256]{1,0:T(8,128)(2,1)S(1)}, bf16[160,256]{1,0:T(8,128)(2,1)S(1)}, u32[]{:S(2)}, u32[]{:S(2)}) collective-permute-start(bf16[160,256]{1,0:T(8,128)(2,1)S(1)} %copy-done.8), channel_id=1, source_target_pairs={{0,128},{64,192},{128,0},{192,64},{1,129},{65,193},{129,1},{193,65... | collective-permute-start | bytes 245768 | tf_op jit(solution)/shard_map/ppermute | solution.py:24
  110.9 0.8 collective-permute-done.20.refs_1_
  111.8 2.1 %collective-permute-start.22 = (bf16[160,256]{1,0:T(8,128)(2,1)S(1)}, bf16[160,256]{1,0:T(8,128)(2,1)S(1)}, u32[]{:S(2)}, u32[]{:S(2)}) collective-permute-start(bf16[160,256]{1,0:T(8,128)(2,1)S(1)} %copy-done.8), channel_id=1, source_target_pairs={{0,192},{64,128},{128,64},{192,0},{1,193},{65,129},{129,65},{193,1... | collective-permute-start | bytes 245768 | tf_op jit(solution)/shard_map/ppermute | solution.py:24
  114.3 3.1 %collective-permute-done.22.refs_3_ = bf16[160,256]{1,0:T(8,128)(2,1)S(1)} collective-permute-done((bf16[160,256]{1,0:T(8,128)(2,1)S(1)}, bf16[160,256]{1,0:T(8,128)(2,1)S(1)}, u32[]{:S(2)}, u32[]{:S(2)}) %collective-permute-start.22) | collective-permute-done | bytes 81952 | tf_op jit(solution)/shard_map/ppermute | solution.py:24
  118.0 1.8 %shard_map.103.refs_0_ = bf16[160,1024]{1,0:T(8,128)(2,1)} custom-call(s32[1]{0:T(128)} %bitcast.12.here_ref, bf16[160,256]{1,0:T(8,128)(2,1)} %shard_map.101.refs_0_, bf16[160,256]{1,0:T(8,128)(2,1)} %copy-done.12, bf16[160,256]{1,0:T(8,128)(2,1)} %copy-done.13, bf16[160,256]{1,0:T(8,128)(2,1)} %copy-done.14), custom_call_target="tpu_custom_call" | custom-call | tf_op jit(solution)/shard_map/pallas_call | solution.py:106
  120.3 0.9 collective-permute-done.24.refs_1_
  121.9 1.6 %shard_map.104 = f32[320,64]{1,0:T(8,128)} custom-call(s32[1]{0:T(128)} %bitcast.11.here_ref, f32[160,64]{1,0:T(8,128)} %get-tuple-element.112.refs_0_, f32[160,64]{1,0:T(8,128)} %copy-done.15), custom_call_target="tpu_custom_call" | custom-call | tf_op jit(solution)/shard_map/pallas_call | solution.py:106
  124.2 2.0 %shard_map.105 = bf16[320,1024]{1,0:T(8,128)(2,1)} custom-call(s32[1]{0:T(128)} %bitcast.11.here_ref, bf16[160,1024]{1,0:T(8,128)(2,1)} %shard_map.103.refs_0_, bf16[160,1024]{1,0:T(8,128)(2,1)} %copy-done.9), custom_call_target="tpu_custom_call" | custom-call | tf_op jit(solution)/shard_map/pallas_call | solution.py:106
  126.2 4.9 %fusion.25 = (f16[320,1024]{1,0:T(8,128)(2,1)}, f16[320,1024]{1,0:T(8,128)(2,1)}) fusion(f16[320,1024]{1,0:T(8,128)(2,1)S(1)} %collective-permute-done.18, f32[1280,1024]{1,0:T(8,128)} %fusion.32, s32[]{:T(128)S(6)} %select_n.177, f32[]{:T(128)} %bitcast.7, f16[320,1024]{1,0:T(8,128)(2,1)} %collective-permute-done.19, s32[]{:T(128)S(6)} %select_n.166), kind=kLoop, calls=%fused_computation.44 | loop fusion | flops 5898240 | bytes 5242892 | tf_op jit(solution)/shard_map/convert_element_type | solution.py:55
  131.1 2.9 %collective-permute-start.27 = (f16[320,1024]{1,0:T(8,128)(2,1)}, f16[320,1024]{1,0:T(8,128)(2,1)}, u32[]{:S(2)}, u32[]{:S(2)}) collective-permute-start(f16[320,1024]{1,0:T(8,128)(2,1)} %get-tuple-element.88), channel_id=1, source_target_pairs={{0,7},{1,2},{2,1},{3,4},{4,3},{5,6},{6,5},{7,0},{8,15},{9,10},{10,... | collective-permute-start | bytes 1966088 | tf_op jit(solution)/shard_map/ppermute | solution.py:398
  134.7 7.0 %shard_map.106 = (f32[256,1024]{1,0:T(8,128)}, bf16[256,5120]{1,0:T(8,128)(2,1)}) custom-call(s32[1]{0:T(128)} %bitcast.13._, bf16[256,5120]{1,0:T(8,128)(2,1)} %bitcast.25, bf16[256,1024]{1,0:T(8,128)(2,1)} %bitcast.32, bf16[2560,1024]{1,0:T(8,128)(2,1)} %bitcast.30), custom_call_target="tpu_custom_call" | custom-call | tf_op jit(solution)/shard_map/pallas_call | solution.py:192
  141.8 1.3 copy-done.1
  143.1 5.1 %shard_map.107 = (bf16[256,1024]{1,0:T(8,128)(2,1)}, bf16[256,5120]{1,0:T(8,128)(2,1)}) custom-call(s32[1]{0:T(128)} %bitcast._, bf16[256,5120]{1,0:T(8,128)(2,1)} %get-tuple-element.74.__, f32[256,1024]{1,0:T(8,128)} %get-tuple-element.75.keys_ref, bf16[272,3584]{1,0:T(8,128)(2,1)} %copy-done.1, ...), custom_call_target="tpu_custom_call", output_to_operand_aliasing={{1}: (1, {})} | custom-call | tf_op jit(solution)/shard_map/pallas_call | solution.py:227
  148.3 1.3 collective-permute-done.27
  149.6 4.0 %fusion.46 = bf16[1,320,1024]{2,1,0:T(8,128)(2,1)} fusion(f32[]{:T(128)} %bitcast.16, f16[320,1024]{1,0:T(8,128)(2,1)} %collective-permute-done.27, f16[320,1024]{1,0:T(8,128)(2,1)S(1)} %collective-permute-done.26, f32[]{:T(128)} %bitcast.7, f32[1280,1024]{1,0:T(8,128)} %fusion.32, s32[]{:T(128)S(6)} %select_n.168), kind=kLoop, calls=%fused_computation.78 | loop fusion | flops 4259840 | bytes 3276812 | tf_op jit(solution)/shard_map/broadcast_in_dim | solution.py:411
  (91 shorter events, 14.5 us)
Async XLA Ops:
  7.2 2.8 %copy-start.3 = (bf16[1,256,1024]{2,1,0:T(8,128)(2,1)S(1)}, bf16[1,256,1024]{2,1,0:T(8,128)(2,1)}, u32[]{:S(2)}) copy-start(bf16[1,256,1024]{2,1,0:T(8,128)(2,1)} %param.8) | copy-start | bytes 1572868
  7.2 79.1 %all-gather.3.cloned.1.call-start = ((), (), s32[]{:S(2)}) async-start(), calls=%async_computation | async-start | bytes 5898240 | tf_op jit(solution)/shard_map/all_gather | solution.py:275
  9.9 9.3 %collective-permute-start = (f32[160,1024]{1,0:T(8,128)}, f32[160,1024]{1,0:T(8,128)}, u32[]{:S(2)}, u32[]{:S(2)}) collective-permute-start(f32[160,1024]{1,0:T(8,128)} %dynamic-slice_bitcast_fusion), channel_id=1, source_target_pairs={{0,16},{16,0},{1,17},{17,1},{2,18},{18,2},{3,19},{19,3},{4,20},{20... | collective-permute-start | bytes 1966088 | tf_op jit(solution)/shard_map/ppermute | solution.py:24
  11.2 6.1 %copy-start = (bf16[1,256,5120]{2,1,0:T(8,128)(2,1)S(1)}, bf16[1,256,5120]{2,1,0:T(8,128)(2,1)}, u32[]{:S(2)}) copy-start(bf16[1,256,5120]{2,1,0:T(8,128)(2,1)} %param.6) | copy-start | bytes 7864324
  15.0 10.9 %collective-permute-start.2 = (f32[8,128]{1,0:T(8,128)S(1)}, f32[8,128]{1,0:T(8,128)S(1)}, u32[]{:S(2)}, u32[]{:S(2)}) collective-permute-start(f32[8,128]{1,0:T(8,128)S(1)} %iota.31), channel_id=1, source_target_pairs={{0,8},{8,0},{1,9},{9,1},{2,10},{10,2},{3,11},{11,3},{4,12},{12,4},... | collective-permute-start | bytes 12296 | tf_op jit(solution)/shard_map/ppermute | solution.py:24
  17.3 1.1 copy-start.10
  18.3 29.0 %collective-permute-start.3 = (bf16[256,1280]{1,0:T(8,128)(2,1)}, bf16[256,1280]{1,0:T(8,128)(2,1)}, u32[]{:S(2)}, u32[]{:S(2)}) collective-permute-start(bf16[256,1280]{1,0:T(8,128)(2,1)} %pad_maximum_fusion.3), channel_id=1, source_target_pairs={{0,8},{8,0},{1,9},{9,1},{2,10},{10,2},{3,11},{11,3},{4,12},{12,4},... | collective-permute-start | bytes 1966088 | tf_op jit(solution)/shard_map/ppermute | solution.py:24
  18.6 11.8 %collective-permute-start.10 = (f32[160,64]{1,0:T(8,128)S(1)}, f32[160,64]{1,0:T(8,128)S(1)}, u32[]{:S(2)}, u32[]{:S(2)}) collective-permute-start(f32[160,64]{1,0:T(8,128)S(1)} %copy.15), channel_id=1, source_target_pairs={{0,16},{16,0},{1,17},{17,1},{2,18},{18,2},{3,19},{19,3},{4,20},{20... | collective-permute-start | bytes 122888 | tf_op jit(solution)/shard_map/ppermute | solution.py:24
  19.1 1.3 copy-start.4
  21.7 10.7 %collective-permute-start.7 = (f32[160,256]{1,0:T(8,128)S(1)}, f32[160,256]{1,0:T(8,128)S(1)}, u32[]{:S(2)}, u32[]{:S(2)}) collective-permute-start(f32[160,256]{1,0:T(8,128)S(1)} %get-tuple-element.106), channel_id=1, source_target_pairs={{0,64},{64,0},{128,192},{192,128},{1,65},{65,1},{129,193},{193,129... | collective-permute-start | bytes 491528 | tf_op jit(solution)/shard_map/ppermute | solution.py:24
  22.9 11.0 %collective-permute-start.8 = (f32[160,256]{1,0:T(8,128)S(1)}, f32[160,256]{1,0:T(8,128)S(1)}, u32[]{:S(2)}, u32[]{:S(2)}) collective-permute-start(f32[160,256]{1,0:T(8,128)S(1)} %get-tuple-element.105), channel_id=1, source_target_pairs={{0,128},{64,192},{128,0},{192,64},{1,129},{65,193},{129,1},{193,65... | collective-permute-start | bytes 491528 | tf_op jit(solution)/shard_map/ppermute | solution.py:24
  26.0 3.7 %collective-permute-start.5 = (f32[8,128]{1,0:T(8,128)S(1)}, f32[8,128]{1,0:T(8,128)S(1)}, u32[]{:S(2)}, u32[]{:S(2)}) collective-permute-start(f32[8,128]{1,0:T(8,128)S(1)} %maximum_select_fusion.3), channel_id=1, source_target_pairs={{0,1},{1,0},{2,3},{3,2},{4,5},{5,4},{6,7},{7,6},{8,9},{9,8},{10,11... | collective-permute-start | bytes 12296 | tf_op jit(solution)/shard_map/ppermute | solution.py:24
  29.7 7.5 %collective-permute-start.9 = (f32[160,256]{1,0:T(8,128)S(1)}, f32[160,256]{1,0:T(8,128)S(1)}, u32[]{:S(2)}, u32[]{:S(2)}) collective-permute-start(f32[160,256]{1,0:T(8,128)S(1)} %get-tuple-element.104), channel_id=1, source_target_pairs={{0,192},{64,128},{128,64},{192,0},{1,193},{65,129},{129,65},{193,1... | collective-permute-start | bytes 491528 | tf_op jit(solution)/shard_map/ppermute | solution.py:24
  30.4 16.9 %collective-permute-start.4 = (bf16[256,1024]{1,0:T(8,128)(2,1)S(1)}, bf16[256,1024]{1,0:T(8,128)(2,1)S(1)}, u32[]{:S(2)}, u32[]{:S(2)}) collective-permute-start(bf16[256,1024]{1,0:T(8,128)(2,1)S(1)} %bitcast.33), channel_id=1, source_target_pairs={{0,8},{8,0},{1,9},{9,1},{2,10},{10,2},{3,11},{11,3},{4,12},{12,4},... | collective-permute-start | bytes 1572872 | tf_op jit(solution)/shard_map/ppermute | solution.py:24
  32.3 29.1 %collective-permute-start.1 = (bf16[256,1280]{1,0:T(8,128)(2,1)S(1)}, bf16[256,1280]{1,0:T(8,128)(2,1)S(1)}, u32[]{:S(2)}, u32[]{:S(2)}) collective-permute-start(bf16[256,1280]{1,0:T(8,128)(2,1)S(1)} %pad_maximum_fusion.4), channel_id=1, source_target_pairs={{0,8},{8,0},{1,9},{9,1},{2,10},{10,2},{3,11},{11,3},{4,12},{12,4},... | collective-permute-start | bytes 1966088 | tf_op jit(solution)/shard_map/ppermute | solution.py:24
  33.8 5.7 %collective-permute-start.6 = (f32[8,128]{1,0:T(8,128)S(1)}, f32[8,128]{1,0:T(8,128)S(1)}, u32[]{:S(2)}, u32[]{:S(2)}) collective-permute-start(f32[8,128]{1,0:T(8,128)S(1)} %maximum_select_fusion.2), channel_id=1, source_target_pairs={{0,2},{1,3},{2,0},{3,1},{4,6},{5,7},{6,4},{7,5},{8,10},{9,11},{10,... | collective-permute-start | bytes 12296 | tf_op jit(solution)/shard_map/ppermute | solution.py:24
  37.3 28.0 %collective-permute-start.14 = (f32[160,128]{1,0:T(8,128)S(1)}, f32[160,128]{1,0:T(8,128)S(1)}, u32[]{:S(2)}, u32[]{:S(2)}) collective-permute-start(f32[160,128]{1,0:T(8,128)S(1)} %constant_dynamic-slice_fusion.1), channel_id=1, source_target_pairs={{0,32},{32,0},{1,33},{33,1},{2,34},{34,2},{3,35},{35,3},{4,36},{36... | collective-permute-start | bytes 245768 | tf_op jit(solution)/shard_map/ppermute | solution.py:24
  39.6 10.6 %collective-permute-start.11 = (f32[8,128]{1,0:T(8,128)S(1)}, f32[8,128]{1,0:T(8,128)S(1)}, u32[]{:S(2)}, u32[]{:S(2)}) collective-permute-start(f32[8,128]{1,0:T(8,128)S(1)} %maximum_select_fusion.1), channel_id=1, source_target_pairs={{0,4},{1,5},{2,6},{3,7},{4,0},{5,1},{6,2},{7,3},{8,12},{9,13},{10,... | collective-permute-start | bytes 12296 | tf_op jit(solution)/shard_map/ppermute | solution.py:24
  47.3 14.0 %copy-start.7 = (bf16[256,1024]{1,0:T(8,128)(2,1)}, bf16[256,1024]{1,0:T(8,128)(2,1)S(1)}, u32[]{:S(2)}) copy-start(bf16[256,1024]{1,0:T(8,128)(2,1)S(1)} %collective-permute-done.4.cotangent_ref) | copy-start | bytes 1572868
  50.2 15.1 %copy-start.2 = (f32[1280,1024]{1,0:T(8,128)}, f32[1280,1024]{1,0:T(8,128)S(1)}, u32[]{:S(2)}) copy-start(f32[1280,1024]{1,0:T(8,128)S(1)} %fusion.26) | copy-start | bytes 15728644
  52.6 21.4 %collective-permute-start.12 = (f16[160,1024]{1,0:T(8,128)(2,1)S(1)}, f16[160,1024]{1,0:T(8,128)(2,1)S(1)}, u32[]{:S(2)}, u32[]{:S(2)}) collective-permute-start(f16[160,1024]{1,0:T(8,128)(2,1)S(1)} %get-tuple-element.95), channel_id=1, source_target_pairs={{0,1},{1,0},{2,3},{3,2},{4,5},{5,4},{6,7},{7,6},{8,9},{9,8},{10,11... | collective-permute-start | bytes 983048 | tf_op jit(solution)/shard_map/ppermute | solution.py:339
  53.2 20.8 %collective-permute-start.13 = (f16[160,1024]{1,0:T(8,128)(2,1)S(1)}, f16[160,1024]{1,0:T(8,128)(2,1)}, u32[]{:S(2)}, u32[]{:S(2)}) collective-permute-start(f16[160,1024]{1,0:T(8,128)(2,1)S(1)} %get-tuple-element.94), channel_id=1, source_target_pairs={{0,7},{1,2},{2,1},{3,4},{4,3},{5,6},{6,5},{7,0},{8,15},{9,10},{10,... | collective-permute-start | bytes 983048 | tf_op jit(solution)/shard_map/ppermute | solution.py:339
  61.4 4.0 %copy-start.5 = (bf16[256,1280]{1,0:T(8,128)(2,1)}, bf16[256,1280]{1,0:T(8,128)(2,1)S(1)}, u32[]{:S(2)}) copy-start(bf16[256,1280]{1,0:T(8,128)(2,1)S(1)} %collective-permute-done.1.late_ref) | copy-start | bytes 1966084
  66.2 5.6 %copy-start.11 = (bf16[160,128]{1,0:T(8,128)(2,1)}, bf16[160,128]{1,0:T(8,128)(2,1)S(1)}, u32[]{:S(2)}) copy-start(bf16[160,128]{1,0:T(8,128)(2,1)S(1)} %get-tuple-element.86.refs_0_) | copy-start | bytes 122884
  66.2 5.6 %collective-permute-start.15 = (bf16[160,128]{1,0:T(8,128)(2,1)S(1)}, bf16[160,128]{1,0:T(8,128)(2,1)S(1)}, u32[]{:S(2)}, u32[]{:S(2)}) collective-permute-start(bf16[160,128]{1,0:T(8,128)(2,1)S(1)} %get-tuple-element.86.refs_0_), channel_id=1, source_target_pairs={{0,32},{32,0},{1,33},{33,1},{2,34},{34,2},{3,35},{35,3},{4,36},{36... | collective-permute-start | bytes 122888 | tf_op jit(solution)/shard_map/ppermute | solution.py:24
  71.8 0.6 copy-start.16
  77.6 18.9 %collective-permute-start.17 = (f16[320,1024]{1,0:T(8,128)(2,1)}, f16[320,1024]{1,0:T(8,128)(2,1)S(1)}, u32[]{:S(2)}, u32[]{:S(2)}) collective-permute-start(f16[320,1024]{1,0:T(8,128)(2,1)} %fusion.21), channel_id=1, source_target_pairs={{0,1},{1,0},{2,3},{3,2},{4,5},{5,4},{6,7},{7,6},{8,9},{9,8},{10,11... | collective-permute-start | bytes 1966088 | tf_op jit(solution)/shard_map/ppermute | solution.py:339
  78.8 20.8 %collective-permute-start.16 = (f16[320,1024]{1,0:T(8,128)(2,1)}, f16[320,1024]{1,0:T(8,128)(2,1)}, u32[]{:S(2)}, u32[]{:S(2)}) collective-permute-start(f16[320,1024]{1,0:T(8,128)(2,1)} %fusion.20), channel_id=1, source_target_pairs={{0,7},{1,2},{2,1},{3,4},{4,3},{5,6},{6,5},{7,0},{8,15},{9,10},{10,... | collective-permute-start | bytes 1966088 | tf_op jit(solution)/shard_map/ppermute | solution.py:339
  94.5 47.3 %collective-permute-start.25 = (bf16[272,3584]{1,0:T(8,128)(2,1)}, bf16[272,3584]{1,0:T(8,128)(2,1)S(1)}, u32[]{:S(2)}, u32[]{:S(2)}) collective-permute-start(bf16[272,3584]{1,0:T(8,128)(2,1)} %shard_map.102), channel_id=1, source_target_pairs={{0,8},{8,0},{1,9},{9,1},{2,10},{10,2},{3,11},{11,3},{4,12},{12,4},... | collective-permute-start | bytes 5849096 | tf_op jit(solution)/shard_map/ppermute | solution.py:24
  99.6 7.1 %copy-start.8 = (bf16[160,256]{1,0:T(8,128)(2,1)S(1)}, bf16[160,256]{1,0:T(8,128)(2,1)}, u32[]{:S(2)}) copy-start(bf16[160,256]{1,0:T(8,128)(2,1)} %shard_map.101.refs_0_) | copy-start | bytes 245764
  102.9 23.2 %collective-permute-start.18 = (f16[320,1024]{1,0:T(8,128)(2,1)}, f16[320,1024]{1,0:T(8,128)(2,1)S(1)}, u32[]{:S(2)}, u32[]{:S(2)}) collective-permute-start(f16[320,1024]{1,0:T(8,128)(2,1)} %fusion.23), channel_id=1, source_target_pairs={{0,1},{1,0},{2,3},{3,2},{4,5},{5,4},{6,7},{7,6},{8,9},{9,8},{10,11... | collective-permute-start | bytes 1966088 | tf_op jit(solution)/shard_map/ppermute | solution.py:339
  103.4 22.8 %collective-permute-start.19 = (f16[320,1024]{1,0:T(8,128)(2,1)}, f16[320,1024]{1,0:T(8,128)(2,1)}, u32[]{:S(2)}, u32[]{:S(2)}) collective-permute-start(f16[320,1024]{1,0:T(8,128)(2,1)} %fusion.22), channel_id=1, source_target_pairs={{0,7},{1,2},{2,1},{3,4},{4,3},{5,6},{6,5},{7,0},{8,15},{9,10},{10,... | collective-permute-start | bytes 1966088 | tf_op jit(solution)/shard_map/ppermute | solution.py:339
  106.7 5.1 %collective-permute-start.20 = (bf16[160,256]{1,0:T(8,128)(2,1)S(1)}, bf16[160,256]{1,0:T(8,128)(2,1)S(1)}, u32[]{:S(2)}, u32[]{:S(2)}) collective-permute-start(bf16[160,256]{1,0:T(8,128)(2,1)S(1)} %copy-done.8), channel_id=1, source_target_pairs={{0,64},{64,0},{128,192},{192,128},{1,65},{65,1},{129,193},{193,129... | collective-permute-start | bytes 245768 | tf_op jit(solution)/shard_map/ppermute | solution.py:24
  108.2 6.1 %collective-permute-start.21 = (bf16[160,256]{1,0:T(8,128)(2,1)S(1)}, bf16[160,256]{1,0:T(8,128)(2,1)S(1)}, u32[]{:S(2)}, u32[]{:S(2)}) collective-permute-start(bf16[160,256]{1,0:T(8,128)(2,1)S(1)} %copy-done.8), channel_id=1, source_target_pairs={{0,128},{64,192},{128,0},{192,64},{1,129},{65,193},{129,1},{193,65... | collective-permute-start | bytes 245768 | tf_op jit(solution)/shard_map/ppermute | solution.py:24
  111.8 5.7 %copy-start.12 = (bf16[160,256]{1,0:T(8,128)(2,1)}, bf16[160,256]{1,0:T(8,128)(2,1)S(1)}, u32[]{:S(2)}) copy-start(bf16[160,256]{1,0:T(8,128)(2,1)S(1)} %collective-permute-done.20.refs_1_) | copy-start | bytes 245764
  111.8 5.7 %collective-permute-start.22 = (bf16[160,256]{1,0:T(8,128)(2,1)S(1)}, bf16[160,256]{1,0:T(8,128)(2,1)S(1)}, u32[]{:S(2)}, u32[]{:S(2)}) collective-permute-start(bf16[160,256]{1,0:T(8,128)(2,1)S(1)} %copy-done.8), channel_id=1, source_target_pairs={{0,192},{64,128},{128,64},{192,0},{1,193},{65,129},{129,65},{193,1... | collective-permute-start | bytes 245768 | tf_op jit(solution)/shard_map/ppermute | solution.py:24
  114.3 3.1 %copy-start.13 = (bf16[160,256]{1,0:T(8,128)(2,1)}, bf16[160,256]{1,0:T(8,128)(2,1)S(1)}, u32[]{:S(2)}) copy-start(bf16[160,256]{1,0:T(8,128)(2,1)S(1)} %collective-permute-done.21.refs_2_) | copy-start | bytes 245764
  117.4 0.6 copy-start.14
  119.8 3.7 %collective-permute-start.23 = (bf16[160,1024]{1,0:T(8,128)(2,1)}, bf16[160,1024]{1,0:T(8,128)(2,1)S(1)}, u32[]{:S(2)}, u32[]{:S(2)}) collective-permute-start(bf16[160,1024]{1,0:T(8,128)(2,1)} %shard_map.103.refs_0_), channel_id=1, source_target_pairs={{0,16},{16,0},{1,17},{17,1},{2,18},{18,2},{3,19},{19,3},{4,20},{20... | collective-permute-start | bytes 983048 | tf_op jit(solution)/shard_map/ppermute | solution.py:24
  119.8 1.4 collective-permute-start.24
  121.2 0.6 copy-start.15
  123.5 0.7 copy-start.9
  126.2 7.8 %copy-start.6 = (f32[320,64]{1,0:T(8,128)S(1)}, f32[320,64]{1,0:T(8,128)}, u32[]{:S(2)}) copy-start(f32[320,64]{1,0:T(8,128)} %shard_map.104) | copy-start | bytes 245764
  131.1 17.2 %collective-permute-start.26 = (f16[320,1024]{1,0:T(8,128)(2,1)}, f16[320,1024]{1,0:T(8,128)(2,1)S(1)}, u32[]{:S(2)}, u32[]{:S(2)}) collective-permute-start(f16[320,1024]{1,0:T(8,128)(2,1)} %get-tuple-element.89), channel_id=1, source_target_pairs={{0,1},{1,0},{2,3},{3,2},{4,5},{5,4},{6,7},{7,6},{8,9},{9,8},{10,11... | collective-permute-start | bytes 1966088 | tf_op jit(solution)/shard_map/ppermute | solution.py:398
  131.1 18.5 %collective-permute-start.27 = (f16[320,1024]{1,0:T(8,128)(2,1)}, f16[320,1024]{1,0:T(8,128)(2,1)}, u32[]{:S(2)}, u32[]{:S(2)}) collective-permute-start(f16[320,1024]{1,0:T(8,128)(2,1)} %get-tuple-element.88), channel_id=1, source_target_pairs={{0,7},{1,2},{2,1},{3,4},{4,3},{5,6},{6,5},{7,0},{8,15},{9,10},{10,... | collective-permute-start | bytes 1966088 | tf_op jit(solution)/shard_map/ppermute | solution.py:398
  141.8 1.3 copy-start.1
Sparse Core Ops, SparseCore 0:
  9.8 76.4 all-gather.2

commit v10 on v8

--- a/solution.py
+++ b/solution.py
@@ -122,6 +122,7 @@
 def products_for_partner(z, early, late, cotangent, weight):
     count = 4
     rows, features = cotangent.shape
+    total = weight.shape[0]
     wide = weight.shape[0] // count
 
     def group(i, z_ref):
@@ -137,25 +138,24 @@
 
         tokens = jnp.where(i < count // 2, early_ref[...], late_ref[...])
         keys_ref[...] += dot(tokens, weight_ref[...])
-        place = pl.multiple_of(features + group(i, z_ref) * wide, 128)
+        place = pl.multiple_of(group(i, z_ref) * wide, 128)
         grads = dot_t(cotangent_ref[...], weight_ref[...]).astype(BF16)
-        sent_ref[:rows, pl.ds(place, wide)] = grads
+        sent_ref[:, pl.ds(place, wide)] = grads
 
         @pl.when(i == count - 1)
         def _():
             keys = keys_ref[...]
             largest = jnp.maximum(jnp.max(jnp.abs(keys)) * 1.01, 1e-30)
-            sent = jnp.full((16, features), largest, F32).astype(BF16)
-            sent_ref[rows:, :features] = sent
-            sent_ref[rows:, features:] = jnp.zeros((16, weight.shape[0]), BF16)
-            scaled = keys * (TOP / sent[:1, :].astype(F32))
+            sent = jnp.full((rows, 128), largest, F32).astype(BF16)
+            sent_ref[:, total + features :] = sent
+            scaled = keys * (TOP / sent[:, :1].astype(F32))
             power = scaled * scaled
             power = power * power
             power = power * power
             power = power * power
-            sent_ref[:rows, :features] = jnp.where(scaled < 0, -power, power).astype(BF16)
-
-    sent = jax.ShapeDtypeStruct((rows + 16, features + weight.shape[0]), BF16)
+            sent_ref[:, total : total + features] = jnp.where(scaled < 0, -power, power).astype(BF16)
+
+    sent = jax.ShapeDtypeStruct((rows, total + features + 128), BF16)
     return pl.pallas_call(
         body,
         grid_spec=pltpu.PrefetchScalarGridSpec(
@@ -210,16 +210,17 @@
 
 
 def finish(x, keys, grads, back):
-    count = 5
+    count = 2
     rows, features = keys.shape
-    wide = grads.shape[1] // (2 * count)
-
-    def body(_, __, keys_ref, coded_ref, back_ref, out_ref, grads_ref):
+    total = grads.shape[1] // 2
+    wide = total // count
+
+    def body(_, __, keys_ref, low_ref, high_ref, largest_ref, back_ref, out_ref, grads_ref):
         @pl.when(pl.program_id(0) == 0)
         def _():
-            power = coded_ref[:rows, :].astype(F32)
+            power = jnp.concatenate([low_ref[...], high_ref[...]], axis=1).astype(F32)
             size = jnp.exp2(jnp.log2(jnp.abs(power)) * (1.0 / 16.0))
-            size = jnp.where(power == 0, 0.0, size) * (coded_ref[rows:, :].astype(F32)[:1] / TOP)
+            size = jnp.where(power == 0, 0.0, size) * (largest_ref[...].astype(F32)[:, :1] / TOP)
             out_ref[...] = (keys_ref[...] + jnp.where(power < 0, -size, size)).astype(BF16)
 
         grads_ref[...] = back_ref[...]
@@ -232,8 +233,10 @@
             in_specs=[
                 pl.BlockSpec(memory_space=pl.ANY),
                 whole(keys),
-                pl.BlockSpec((rows + 16, features), lambda i, x: (0, 0)),
-                pl.BlockSpec((rows, wide), lambda i, x: (0, features // wide + i)),
+                pl.BlockSpec((rows, features // 2), lambda i, x: (0, total // (features // 2))),
+                pl.BlockSpec((rows, features // 2), lambda i, x: (0, total // (features // 2) + 1)),
+                pl.BlockSpec((rows, 128), lambda i, x: (0, (total + features) // 128)),
+                pl.BlockSpec((rows, wide), lambda i, x: (0, i)),
             ],
             out_specs=[
                 whole(keys),
@@ -246,7 +249,7 @@
         ],
         input_output_aliases={1: 1},
         cost_estimate=FREE,
-    )(x.reshape(1), grads, keys, back, back)
+    )(x.reshape(1), grads, keys, back, back, back, back)
 
 
 def shards(activations, key_weights, key_cotangent, fragment, pseudo_grads, momentum):

time: 158 us -> 157 us (level)
  Pallas kernels: 27.1 us -> 25.2 us
  waiting for transfers between devices: 21.5 us -> 23.3 us
    ppermute x2, waiting for transfers between devices: 0.48 us -> 3.35 us  [shards(): even, odd = (lax.ppermute(even, 'z', EVEN), lax.ppermute(odd, 'z', ODD))]
    pallas_call x1, Pallas kernels: 5.1 us -> 3.27 us  [finish(): pl.pallas_call(body, grid_spec=pltpu.PrefetchScalarGridSpec(num_scalar_pr...]
  transfers between devices with their start and end apart: 29 -> 29, of which waited for: 8 -> 9; matrix products, arithmetic and copies ran while one was open for 23% -> 23% of each run, Pallas kernels for 17% -> 16%
where the time goes in v10:
time: 157 us; the launch traced here: 156 us
  starting transfers between devices  46.5 us (30%)
  other arithmetic  28.7 us (18%)
  Pallas kernels  25.2 us (16%)
  waiting for transfers between devices  23.3 us (15%)
  between operations  16.4 us (10%)
  local copies, waits for them, and re-layouts  9.26 us (6%)
  matrix products  6.75 us (4%)
    ppermute x20, starting transfers between devices, swap(): lax.ppermute(value, axis, [(i, i ^ mask) for i in range(SIZES[axis])])  31.7 us
    ppermute x20, waiting for transfers between devices, swap(): lax.ppermute(value, axis, [(i, i ^ mask) for i in range(SIZES[axis])])  19.2 us
    convert_element_type x6, other arithmetic, encode(): return (scaled * jnp.abs(scaled)).astype(F16)  13.6 us
    ppermute x6, starting transfers between devices, send(): return lax.ppermute(message, 'z', pairs)  12.4 us
    pallas_call x1, Pallas kernels, products_for_partner(): pl.pallas_call(body, grid_spec=pltpu.PrefetchScalarGridSpec(num_scalar_pr...  8.17 us
    pallas_call x1, Pallas kernels, products_here(): pl.pallas_call(body, grid_spec=pltpu.PrefetchScalarGridSpec(num_scalar_pr...  7.05 us
    pallas_call x4, Pallas kernels, assemble(): pl.pallas_call(body, grid_spec=pltpu.PrefetchScalarGridSpec(num_scalar_pr...  6.76 us
    dot_general x2, matrix products, product(): lax.dot_general(jnp.concatenate([first, second], axis=0), jnp.concatenate...  6.75 us
  transfers between devices with their start and end apart: 29, of which 9 were waited for; matrix products, arithmetic and copies ran while one was open for 23% of the time, Pallas kernels for 16%

profile of v10, /device:TPU:2, one launch (start us, length us, event | category | flops | bytes accessed | tf_op | source)
XLA Modules:
  0.0 156.2 jit_solution(9591398940752319753)
XLA Ops:
  7.9 2.0 %dynamic-slice_bitcast_fusion = f32[160,1024]{1,0:T(8,128)} fusion(f32[1,320,1024]{2,1,0:T(8,128)} %param.10, s32[]{:T(128)S(6)} %select_n.140), kind=kLoop, calls=%fused_computation.77 | loop fusion | bytes 1310724 | tf_op jit(solution)/shard_map/dynamic_slice | solution.py:40
  11.3 2.4 %abs_reduce_fusion = f32[5120]{0:T(1024)S(1)} fusion(bf16[256,5120]{1,0:T(8,128)(2,1)} %bitcast.24), kind=kLoop, calls=%fused_computation | loop fusion | flops 3927040 | bytes 2641920 | tf_op jit(solution)/shard_map/reduce_sum | solution.py:68
  15.0 2.3 %collective-permute-start = (f32[8,128]{1,0:T(8,128)S(1)}, f32[8,128]{1,0:T(8,128)S(1)}, u32[]{:S(2)}, u32[]{:S(2)}) collective-permute-start(f32[8,128]{1,0:T(8,128)S(1)} %iota.32), channel_id=1, source_target_pairs={{0,8},{8,0},{1,9},{9,1},{2,10},{10,2},{3,11},{11,3},{4,12},{12,4},... | collective-permute-start | bytes 12296 | tf_op jit(solution)/shard_map/ppermute | solution.py:24
  17.4 0.9 pad_maximum_fusion.3
  19.2 1.2 copy-done.4
  20.4 1.2 bitcast_add_fusion
  21.7 1.2 collective-permute-start.6
  22.9 2.9 %collective-permute-start.7 = (f32[160,256]{1,0:T(8,128)S(1)}, f32[160,256]{1,0:T(8,128)S(1)}, u32[]{:S(2)}, u32[]{:S(2)}) collective-permute-start(f32[160,256]{1,0:T(8,128)S(1)} %get-tuple-element.105), channel_id=1, source_target_pairs={{0,128},{64,192},{128,0},{192,64},{1,129},{65,193},{129,1},{193,65... | collective-permute-start | bytes 491528 | tf_op jit(solution)/shard_map/ppermute | solution.py:24
  26.0 1.9 %collective-permute-start.4 = (f32[8,128]{1,0:T(8,128)S(1)}, f32[8,128]{1,0:T(8,128)S(1)}, u32[]{:S(2)}, u32[]{:S(2)}) collective-permute-start(f32[8,128]{1,0:T(8,128)S(1)} %maximum_select_fusion.3), channel_id=1, source_target_pairs={{0,1},{1,0},{2,3},{3,2},{4,5},{5,4},{6,7},{7,6},{8,9},{9,8},{10,11... | collective-permute-start | bytes 12296 | tf_op jit(solution)/shard_map/ppermute | solution.py:24
  28.1 1.7 %collective-permute-done.4 = f32[8,128]{1,0:T(8,128)S(1)} collective-permute-done((f32[8,128]{1,0:T(8,128)S(1)}, f32[8,128]{1,0:T(8,128)S(1)}, u32[]{:S(2)}, u32[]{:S(2)}) %collective-permute-start.4) | collective-permute-done | bytes 4128 | tf_op jit(solution)/shard_map/ppermute | solution.py:24
  30.4 1.9 %collective-permute-start.3 = (bf16[256,1024]{1,0:T(8,128)(2,1)S(1)}, bf16[256,1024]{1,0:T(8,128)(2,1)S(1)}, u32[]{:S(2)}, u32[]{:S(2)}) collective-permute-start(bf16[256,1024]{1,0:T(8,128)(2,1)S(1)} %bitcast.33), channel_id=1, source_target_pairs={{0,8},{8,0},{1,9},{9,1},{2,10},{10,2},{3,11},{11,3},{4,12},{12,4},... | collective-permute-start | bytes 1572872 | tf_op jit(solution)/shard_map/ppermute | solution.py:24
  32.5 1.4 collective-permute-done.7
  33.8 3.3 %collective-permute-start.5 = (f32[8,128]{1,0:T(8,128)S(1)}, f32[8,128]{1,0:T(8,128)S(1)}, u32[]{:S(2)}, u32[]{:S(2)}) collective-permute-start(f32[8,128]{1,0:T(8,128)S(1)} %maximum_select_fusion.2), channel_id=1, source_target_pairs={{0,2},{1,3},{2,0},{3,1},{4,6},{5,7},{6,4},{7,5},{8,10},{9,11},{10,... | collective-permute-start | bytes 12296 | tf_op jit(solution)/shard_map/ppermute | solution.py:24
  37.3 2.2 %collective-permute-start.13 = (f32[160,128]{1,0:T(8,128)S(1)}, f32[160,128]{1,0:T(8,128)S(1)}, u32[]{:S(2)}, u32[]{:S(2)}) collective-permute-start(f32[160,128]{1,0:T(8,128)S(1)} %constant_dynamic-slice_fusion.1), channel_id=1, source_target_pairs={{0,32},{32,0},{1,33},{33,1},{2,34},{34,2},{3,35},{35,3},{4,36},{36... | collective-permute-start | bytes 245768 | tf_op jit(solution)/shard_map/ppermute | solution.py:24
  39.6 7.2 %collective-permute-start.10 = (f32[8,128]{1,0:T(8,128)S(1)}, f32[8,128]{1,0:T(8,128)S(1)}, u32[]{:S(2)}, u32[]{:S(2)}) collective-permute-start(f32[8,128]{1,0:T(8,128)S(1)} %maximum_select_fusion.1), channel_id=1, source_target_pairs={{0,4},{1,5},{2,6},{3,7},{4,0},{5,1},{6,2},{7,3},{8,12},{9,13},{10,... | collective-permute-start | bytes 12296 | tf_op jit(solution)/shard_map/ppermute | solution.py:24
  47.3 2.9 %fusion.26 = f32[1280,1024]{1,0:T(8,128)S(1)} fusion(bf16[256,1280]{1,0:T(8,128)(2,1)} %collective-permute-done.2.early_ref, bf16[256,640]{1,0:T(8,128)(2,1)S(1)} %get-tuple-element.99, bf16[256,640]{1,0:T(8,128)(2,1)S(1)} %get-tuple-element.98, bf16[256,1024]{1,0:T(8,128)(2,1)S(1)} %collective-permute-done.3.cotangent_ref, bf16[256,1024]{1,0:T(8,128)(2,1)S(1)} %bitcast.34), kind=kOutput, calls=%fused_computation.45 | convolution fusion | flops 1348206592 | bytes 7602176 | tf_op jit(solution)/shard_map/dot_general | solution.py:318
  53.2 4.6 %collective-permute-start.12 = (f16[160,1024]{1,0:T(8,128)(2,1)S(1)}, f16[160,1024]{1,0:T(8,128)(2,1)}, u32[]{:S(2)}, u32[]{:S(2)}) collective-permute-start(f16[160,1024]{1,0:T(8,128)(2,1)S(1)} %get-tuple-element.94), channel_id=1, source_target_pairs={{0,7},{1,2},{2,1},{3,4},{4,3},{5,6},{6,5},{7,0},{8,15},{9,10},{10,... | collective-permute-start | bytes 983048 | tf_op jit(solution)/shard_map/ppermute | solution.py:342
  57.8 3.6 %collective-permute-done.14.late_ref = bf16[256,1280]{1,0:T(8,128)(2,1)S(1)} collective-permute-done((bf16[256,1280]{1,0:T(8,128)(2,1)S(1)}, bf16[256,1280]{1,0:T(8,128)(2,1)S(1)}, u32[]{:S(2)}, u32[]{:S(2)}) %collective-permute-start.14) | collective-permute-done | bytes 655392 | tf_op jit(solution)/shard_map/ppermute | solution.py:24
  61.4 3.9 %fusion.32 = f32[1280,1024]{1,0:T(8,128)} fusion(bf16[256,1280]{1,0:T(8,128)(2,1)S(1)} %collective-permute-done.14.late_ref, bf16[256,640]{1,0:T(8,128)(2,1)S(1)} %get-tuple-element.97, bf16[256,640]{1,0:T(8,128)(2,1)S(1)} %get-tuple-element.96, bf16[256,1024]{1,0:T(8,128)(2,1)S(1)} %collective-permute-done.3.cotangent_ref, bf16[256,1024]{1,0:T(8,128)(2,1)S(1)} %bitcast.35), kind=kOutput, calls=%fused_computation.51 | convolution fusion | flops 1348206592 | bytes 7602176 | tf_op jit(solution)/shard_map/dot_general | solution.py:318
  65.3 0.9 subtract_convert_fusion
  66.2 0.8 collective-permute-start.15
  67.7 4.1 %collective-permute-done.15.refs_1_ = bf16[160,128]{1,0:T(8,128)(2,1)S(1)} collective-permute-done((bf16[160,128]{1,0:T(8,128)(2,1)S(1)}, bf16[160,128]{1,0:T(8,128)(2,1)S(1)}, u32[]{:S(2)}, u32[]{:S(2)}) %collective-permute-start.15) | collective-permute-done | bytes 40992 | tf_op jit(solution)/shard_map/ppermute | solution.py:24
  72.4 1.4 shard_map.101.refs_0_
  73.9 2.7 %dynamic-slice_multiply_fusion = (f32[160,1024]{1,0:T(8,128)S(1)}, f32[160,1024]{1,0:T(8,128)S(1)}, f32[160,1024]{1,0:T(8,128)S(1)}, f32[160,1024]{1,0:T(8,128)S(1)}) fusion(f32[1280,1024]{1,0:T(8,128)} %copy-done.2, s32[]{:T(128)S(6)} %select_n.177, f32[]{:T(128)} %bitcast.5, f16[160,1024]{1,0:T(8,128)(2,1)} %collective-permute-done.12, s32[]{:T(128)S(6)} %select_n.178, ...), kind=kLoop, calls=%fused_computation.75 | loop fusion | flops 2293760 | bytes 5898260 | tf_op jit(solution)/shard_map/mul | solution.py:336
  76.5 1.0 fusion.21
  77.7 1.0 fusion.20
  78.7 5.0 %collective-permute-start.16 = (f16[320,1024]{1,0:T(8,128)(2,1)}, f16[320,1024]{1,0:T(8,128)(2,1)}, u32[]{:S(2)}, u32[]{:S(2)}) collective-permute-start(f16[320,1024]{1,0:T(8,128)(2,1)} %fusion.20), channel_id=1, source_target_pairs={{0,7},{1,2},{2,1},{3,4},{4,3},{5,6},{6,5},{7,0},{8,15},{9,10},{10,... | collective-permute-start | bytes 1966088 | tf_op jit(solution)/shard_map/ppermute | solution.py:342
  83.7 1.6 %collective-permute-start.18 = (bf16[160,256]{1,0:T(8,128)(2,1)S(1)}, bf16[160,256]{1,0:T(8,128)(2,1)S(1)}, u32[]{:S(2)}, u32[]{:S(2)}) collective-permute-start(bf16[160,256]{1,0:T(8,128)(2,1)S(1)} %copy-done.9), channel_id=1, source_target_pairs={{0,64},{64,0},{128,192},{192,128},{1,65},{65,1},{129,193},{193,129... | collective-permute-start | bytes 245768 | tf_op jit(solution)/shard_map/ppermute | solution.py:24
  85.2 2.9 %collective-permute-start.19 = (bf16[160,256]{1,0:T(8,128)(2,1)S(1)}, bf16[160,256]{1,0:T(8,128)(2,1)S(1)}, u32[]{:S(2)}, u32[]{:S(2)}) collective-permute-start(bf16[160,256]{1,0:T(8,128)(2,1)S(1)} %copy-done.9), channel_id=1, source_target_pairs={{0,128},{64,192},{128,0},{192,64},{1,129},{65,193},{129,1},{193,65... | collective-permute-start | bytes 245768 | tf_op jit(solution)/shard_map/ppermute | solution.py:24
  88.4 8.2 %shard_map.102 = bf16[256,3712]{1,0:T(8,128)(2,1)} custom-call(s32[1]{0:T(128)} %bitcast.10.z_ref, bf16[256,1280]{1,0:T(8,128)(2,1)} %collective-permute-done.2.early_ref, bf16[256,1280]{1,0:T(8,128)(2,1)} %copy-done.6, bf16[256,1024]{1,0:T(8,128)(2,1)} %copy-done.8, bf16[2560,1024]{1,0:T(8,128)(2,1)} %bitcast.29), custom_call_target="tpu_custom_call" | custom-call | tf_op jit(solution)/shard_map/pallas_call | solution.py:159
  96.5 1.5 collective-permute-start.21
  98.7 1.8 %shard_map.103.refs_0_ = bf16[160,1024]{1,0:T(8,128)(2,1)} custom-call(s32[1]{0:T(128)} %bitcast.9.here_ref, bf16[160,256]{1,0:T(8,128)(2,1)} %shard_map.101.refs_0_, bf16[160,256]{1,0:T(8,128)(2,1)} %copy-done.13, bf16[160,256]{1,0:T(8,128)(2,1)} %copy-done.14, bf16[160,256]{1,0:T(8,128)(2,1)} %copy-done.15), custom_call_target="tpu_custom_call" | custom-call | tf_op jit(solution)/shard_map/pallas_call | solution.py:106
  100.5 3.1 %fusion.22 = f16[320,1024]{1,0:T(8,128)(2,1)} fusion(f16[320,1024]{1,0:T(8,128)(2,1)S(1)} %collective-permute-done.17, f32[1280,1024]{1,0:T(8,128)} %fusion.32, s32[]{:T(128)S(6)} %select_n.162, f32[]{:T(128)} %bitcast.5), kind=kLoop, calls=%fused_computation.41 | loop fusion | flops 2949120 | bytes 2621448 | tf_op jit(solution)/shard_map/convert_element_type | solution.py:55
  103.6 3.4 %fusion.23 = f16[320,1024]{1,0:T(8,128)(2,1)} fusion(f16[320,1024]{1,0:T(8,128)(2,1)} %collective-permute-done.16, f32[1280,1024]{1,0:T(8,128)} %copy-done.2, s32[]{:T(128)S(6)} %select_n.162, f32[]{:T(128)} %bitcast.5), kind=kLoop, calls=%fused_computation.42 | loop fusion | flops 2949120 | bytes 2621448 | tf_op jit(solution)/shard_map/convert_element_type | solution.py:55
  107.0 2.0 %collective-permute-start.23 = (f16[320,1024]{1,0:T(8,128)(2,1)}, f16[320,1024]{1,0:T(8,128)(2,1)}, u32[]{:S(2)}, u32[]{:S(2)}) collective-permute-start(f16[320,1024]{1,0:T(8,128)(2,1)} %fusion.22), channel_id=1, source_target_pairs={{0,7},{1,2},{2,1},{3,4},{4,3},{5,6},{6,5},{7,0},{8,15},{9,10},{10,... | collective-permute-start | bytes 1966088 | tf_op jit(solution)/shard_map/ppermute | solution.py:342
  109.5 7.0 %shard_map.104 = (f32[256,1024]{1,0:T(8,128)}, bf16[256,5120]{1,0:T(8,128)(2,1)}) custom-call(s32[1]{0:T(128)} %bitcast.12._, bf16[256,5120]{1,0:T(8,128)(2,1)} %bitcast.25, bf16[256,1024]{1,0:T(8,128)(2,1)} %bitcast.32, bf16[2560,1024]{1,0:T(8,128)(2,1)} %bitcast.30), custom_call_target="tpu_custom_call" | custom-call | tf_op jit(solution)/shard_map/pallas_call | solution.py:192
  117.2 1.6 %shard_map.105 = f32[320,64]{1,0:T(8,128)} custom-call(s32[1]{0:T(128)} %bitcast.13.here_ref, f32[160,64]{1,0:T(8,128)} %get-tuple-element.112.refs_0_, f32[160,64]{1,0:T(8,128)} %copy-done.16), custom_call_target="tpu_custom_call" | custom-call | tf_op jit(solution)/shard_map/pallas_call | solution.py:106
  119.6 2.0 %shard_map.106 = bf16[320,1024]{1,0:T(8,128)(2,1)} custom-call(s32[1]{0:T(128)} %bitcast.13.here_ref, bf16[160,1024]{1,0:T(8,128)(2,1)} %shard_map.103.refs_0_, bf16[160,1024]{1,0:T(8,128)(2,1)} %copy-done.10), custom_call_target="tpu_custom_call" | custom-call | tf_op jit(solution)/shard_map/pallas_call | solution.py:106
  121.6 4.9 %fusion.25 = (f16[320,1024]{1,0:T(8,128)(2,1)}, f16[320,1024]{1,0:T(8,128)(2,1)}) fusion(f16[320,1024]{1,0:T(8,128)(2,1)S(1)} %collective-permute-done.22, f32[1280,1024]{1,0:T(8,128)} %fusion.32, s32[]{:T(128)S(6)} %select_n.177, f32[]{:T(128)} %bitcast.5, f16[320,1024]{1,0:T(8,128)(2,1)} %collective-permute-done.23, s32[]{:T(128)S(6)} %select_n.164), kind=kLoop, calls=%fused_computation.44 | loop fusion | flops 5898240 | bytes 5242892 | tf_op jit(solution)/shard_map/convert_element_type | solution.py:55
  126.5 1.0 collective-permute-start.26
  127.5 1.4 collective-permute-start.27
  128.9 0.8 copy.14
  129.7 7.8 %collective-permute-done.21.low_ref.high_ref.largest_ref.back_ref = bf16[256,3712]{1,0:T(8,128)(2,1)S(1)} collective-permute-done((bf16[256,3712]{1,0:T(8,128)(2,1)}, bf16[256,3712]{1,0:T(8,128)(2,1)S(1)}, u32[]{:S(2)}, u32[]{:S(2)}) %collective-permute-start.21) | collective-permute-done | bytes 1900576 | tf_op jit(solution)/shard_map/ppermute | solution.py:24
  137.5 1.3 copy-done
  138.8 3.3 %shard_map.107 = (bf16[256,1024]{1,0:T(8,128)(2,1)}, bf16[256,5120]{1,0:T(8,128)(2,1)}) custom-call(s32[1]{0:T(128)} %bitcast._, bf16[256,5120]{1,0:T(8,128)(2,1)} %get-tuple-element.70.__, f32[256,1024]{1,0:T(8,128)} %get-tuple-element.71.keys_ref, bf16[256,3712]{1,0:T(8,128)(2,1)} %copy-done, ...), custom_call_target="tpu_custom_call", output_to_operand_aliasing={{1}: (1, {})} | custom-call | tf_op jit(solution)/shard_map/pallas_call | solution.py:228
  142.0 1.3 collective-permute-done.26
  143.4 2.0 %collective-permute-done.27 = f16[320,1024]{1,0:T(8,128)(2,1)} collective-permute-done((f16[320,1024]{1,0:T(8,128)(2,1)}, f16[320,1024]{1,0:T(8,128)(2,1)}, u32[]{:S(2)}, u32[]{:S(2)}) %collective-permute-start.27) | collective-permute-done | bytes 655392 | tf_op jit(solution)/shard_map/ppermute | solution.py:403
  145.4 4.0 %fusion.46 = bf16[1,320,1024]{2,1,0:T(8,128)(2,1)} fusion(f32[]{:T(128)} %bitcast.16, f16[320,1024]{1,0:T(8,128)(2,1)} %collective-permute-done.27, f16[320,1024]{1,0:T(8,128)(2,1)S(1)} %collective-permute-done.26, f32[]{:T(128)} %bitcast.5, f32[1280,1024]{1,0:T(8,128)} %fusion.32, s32[]{:T(128)S(6)} %select_n.165), kind=kLoop, calls=%fused_computation.78 | loop fusion | flops 4259840 | bytes 3276812 | tf_op jit(solution)/shard_map/broadcast_in_dim | solution.py:414
  (93 shorter events, 11.5 us)
Async XLA Ops:
  7.2 2.8 %copy-start.3 = (bf16[1,256,1024]{2,1,0:T(8,128)(2,1)S(1)}, bf16[1,256,1024]{2,1,0:T(8,128)(2,1)}, u32[]{:S(2)}) copy-start(bf16[1,256,1024]{2,1,0:T(8,128)(2,1)} %param.8) | copy-start | bytes 1572868
  7.2 81.2 %all-gather.3.cloned.1.call-start = ((), (), s32[]{:S(2)}) async-start(), calls=%async_computation | async-start | bytes 5898240 | tf_op jit(solution)/shard_map/all_gather | solution.py:278
  9.9 9.3 %collective-permute-start.1 = (f32[160,1024]{1,0:T(8,128)}, f32[160,1024]{1,0:T(8,128)}, u32[]{:S(2)}, u32[]{:S(2)}) collective-permute-start(f32[160,1024]{1,0:T(8,128)} %dynamic-slice_bitcast_fusion), channel_id=1, source_target_pairs={{0,16},{16,0},{1,17},{17,1},{2,18},{18,2},{3,19},{19,3},{4,20},{20... | collective-permute-start | bytes 1966088 | tf_op jit(solution)/shard_map/ppermute | solution.py:24
  11.2 6.1 %copy-start.1 = (bf16[1,256,5120]{2,1,0:T(8,128)(2,1)S(1)}, bf16[1,256,5120]{2,1,0:T(8,128)(2,1)}, u32[]{:S(2)}) copy-start(bf16[1,256,5120]{2,1,0:T(8,128)(2,1)} %param.6) | copy-start | bytes 7864324
  15.0 10.9 %collective-permute-start = (f32[8,128]{1,0:T(8,128)S(1)}, f32[8,128]{1,0:T(8,128)S(1)}, u32[]{:S(2)}, u32[]{:S(2)}) collective-permute-start(f32[8,128]{1,0:T(8,128)S(1)} %iota.32), channel_id=1, source_target_pairs={{0,8},{8,0},{1,9},{9,1},{2,10},{10,2},{3,11},{11,3},{4,12},{12,4},... | collective-permute-start | bytes 12296 | tf_op jit(solution)/shard_map/ppermute | solution.py:24
  17.3 1.1 copy-start.11
  18.3 29.0 %collective-permute-start.2 = (bf16[256,1280]{1,0:T(8,128)(2,1)}, bf16[256,1280]{1,0:T(8,128)(2,1)}, u32[]{:S(2)}, u32[]{:S(2)}) collective-permute-start(bf16[256,1280]{1,0:T(8,128)(2,1)} %pad_maximum_fusion.3), channel_id=1, source_target_pairs={{0,8},{8,0},{1,9},{9,1},{2,10},{10,2},{3,11},{11,3},{4,12},{12,4},... | collective-permute-start | bytes 1966088 | tf_op jit(solution)/shard_map/ppermute | solution.py:24
  18.6 11.8 %collective-permute-start.9 = (f32[160,64]{1,0:T(8,128)S(1)}, f32[160,64]{1,0:T(8,128)S(1)}, u32[]{:S(2)}, u32[]{:S(2)}) collective-permute-start(f32[160,64]{1,0:T(8,128)S(1)} %copy.15), channel_id=1, source_target_pairs={{0,16},{16,0},{1,17},{17,1},{2,18},{18,2},{3,19},{19,3},{4,20},{20... | collective-permute-start | bytes 122888 | tf_op jit(solution)/shard_map/ppermute | solution.py:24
  19.1 1.3 copy-start.4
  21.7 10.7 %collective-permute-start.6 = (f32[160,256]{1,0:T(8,128)S(1)}, f32[160,256]{1,0:T(8,128)S(1)}, u32[]{:S(2)}, u32[]{:S(2)}) collective-permute-start(f32[160,256]{1,0:T(8,128)S(1)} %get-tuple-element.106), channel_id=1, source_target_pairs={{0,64},{64,0},{128,192},{192,128},{1,65},{65,1},{129,193},{193,129... | collective-permute-start | bytes 491528 | tf_op jit(solution)/shard_map/ppermute | solution.py:24
  22.9 11.0 %collective-permute-start.7 = (f32[160,256]{1,0:T(8,128)S(1)}, f32[160,256]{1,0:T(8,128)S(1)}, u32[]{:S(2)}, u32[]{:S(2)}) collective-permute-start(f32[160,256]{1,0:T(8,128)S(1)} %get-tuple-element.105), channel_id=1, source_target_pairs={{0,128},{64,192},{128,0},{192,64},{1,129},{65,193},{129,1},{193,65... | collective-permute-start | bytes 491528 | tf_op jit(solution)/shard_map/ppermute | solution.py:24
  26.0 3.7 %collective-permute-start.4 = (f32[8,128]{1,0:T(8,128)S(1)}, f32[8,128]{1,0:T(8,128)S(1)}, u32[]{:S(2)}, u32[]{:S(2)}) collective-permute-start(f32[8,128]{1,0:T(8,128)S(1)} %maximum_select_fusion.3), channel_id=1, source_target_pairs={{0,1},{1,0},{2,3},{3,2},{4,5},{5,4},{6,7},{7,6},{8,9},{9,8},{10,11... | collective-permute-start | bytes 12296 | tf_op jit(solution)/shard_map/ppermute | solution.py:24
  29.7 7.5 %collective-permute-start.8 = (f32[160,256]{1,0:T(8,128)S(1)}, f32[160,256]{1,0:T(8,128)S(1)}, u32[]{:S(2)}, u32[]{:S(2)}) collective-permute-start(f32[160,256]{1,0:T(8,128)S(1)} %get-tuple-element.104), channel_id=1, source_target_pairs={{0,192},{64,128},{128,64},{192,0},{1,193},{65,129},{129,65},{193,1... | collective-permute-start | bytes 491528 | tf_op jit(solution)/shard_map/ppermute | solution.py:24
  30.4 16.9 %collective-permute-start.3 = (bf16[256,1024]{1,0:T(8,128)(2,1)S(1)}, bf16[256,1024]{1,0:T(8,128)(2,1)S(1)}, u32[]{:S(2)}, u32[]{:S(2)}) collective-permute-start(bf16[256,1024]{1,0:T(8,128)(2,1)S(1)} %bitcast.33), channel_id=1, source_target_pairs={{0,8},{8,0},{1,9},{9,1},{2,10},{10,2},{3,11},{11,3},{4,12},{12,4},... | collective-permute-start | bytes 1572872 | tf_op jit(solution)/shard_map/ppermute | solution.py:24
  32.3 29.1 %collective-permute-start.14 = (bf16[256,1280]{1,0:T(8,128)(2,1)S(1)}, bf16[256,1280]{1,0:T(8,128)(2,1)S(1)}, u32[]{:S(2)}, u32[]{:S(2)}) collective-permute-start(bf16[256,1280]{1,0:T(8,128)(2,1)S(1)} %pad_maximum_fusion.4), channel_id=1, source_target_pairs={{0,8},{8,0},{1,9},{9,1},{2,10},{10,2},{3,11},{11,3},{4,12},{12,4},... | collective-permute-start | bytes 1966088 | tf_op jit(solution)/shard_map/ppermute | solution.py:24
  33.8 5.7 %collective-permute-start.5 = (f32[8,128]{1,0:T(8,128)S(1)}, f32[8,128]{1,0:T(8,128)S(1)}, u32[]{:S(2)}, u32[]{:S(2)}) collective-permute-start(f32[8,128]{1,0:T(8,128)S(1)} %maximum_select_fusion.2), channel_id=1, source_target_pairs={{0,2},{1,3},{2,0},{3,1},{4,6},{5,7},{6,4},{7,5},{8,10},{9,11},{10,... | collective-permute-start | bytes 12296 | tf_op jit(solution)/shard_map/ppermute | solution.py:24
  37.3 27.9 %collective-permute-start.13 = (f32[160,128]{1,0:T(8,128)S(1)}, f32[160,128]{1,0:T(8,128)S(1)}, u32[]{:S(2)}, u32[]{:S(2)}) collective-permute-start(f32[160,128]{1,0:T(8,128)S(1)} %constant_dynamic-slice_fusion.1), channel_id=1, source_target_pairs={{0,32},{32,0},{1,33},{33,1},{2,34},{34,2},{3,35},{35,3},{4,36},{36... | collective-permute-start | bytes 245768 | tf_op jit(solution)/shard_map/ppermute | solution.py:24
  39.6 10.6 %collective-permute-start.10 = (f32[8,128]{1,0:T(8,128)S(1)}, f32[8,128]{1,0:T(8,128)S(1)}, u32[]{:S(2)}, u32[]{:S(2)}) collective-permute-start(f32[8,128]{1,0:T(8,128)S(1)} %maximum_select_fusion.1), channel_id=1, source_target_pairs={{0,4},{1,5},{2,6},{3,7},{4,0},{5,1},{6,2},{7,3},{8,12},{9,13},{10,... | collective-permute-start | bytes 12296 | tf_op jit(solution)/shard_map/ppermute | solution.py:24
  47.3 14.0 %copy-start.8 = (bf16[256,1024]{1,0:T(8,128)(2,1)}, bf16[256,1024]{1,0:T(8,128)(2,1)S(1)}, u32[]{:S(2)}) copy-start(bf16[256,1024]{1,0:T(8,128)(2,1)S(1)} %collective-permute-done.3.cotangent_ref) | copy-start | bytes 1572868
  50.2 15.1 %copy-start.2 = (f32[1280,1024]{1,0:T(8,128)}, f32[1280,1024]{1,0:T(8,128)S(1)}, u32[]{:S(2)}) copy-start(f32[1280,1024]{1,0:T(8,128)S(1)} %fusion.26) | copy-start | bytes 15728644
  52.6 21.3 %collective-permute-start.11 = (f16[160,1024]{1,0:T(8,128)(2,1)S(1)}, f16[160,1024]{1,0:T(8,128)(2,1)S(1)}, u32[]{:S(2)}, u32[]{:S(2)}) collective-permute-start(f16[160,1024]{1,0:T(8,128)(2,1)S(1)} %get-tuple-element.95), channel_id=1, source_target_pairs={{0,1},{1,0},{2,3},{3,2},{4,5},{5,4},{6,7},{7,6},{8,9},{9,8},{10,11... | collective-permute-start | bytes 983048 | tf_op jit(solution)/shard_map/ppermute | solution.py:342
  53.2 20.7 %collective-permute-start.12 = (f16[160,1024]{1,0:T(8,128)(2,1)S(1)}, f16[160,1024]{1,0:T(8,128)(2,1)}, u32[]{:S(2)}, u32[]{:S(2)}) collective-permute-start(f16[160,1024]{1,0:T(8,128)(2,1)S(1)} %get-tuple-element.94), channel_id=1, source_target_pairs={{0,7},{1,2},{2,1},{3,4},{4,3},{5,6},{6,5},{7,0},{8,15},{9,10},{10,... | collective-permute-start | bytes 983048 | tf_op jit(solution)/shard_map/ppermute | solution.py:342
  61.4 3.9 %copy-start.6 = (bf16[256,1280]{1,0:T(8,128)(2,1)}, bf16[256,1280]{1,0:T(8,128)(2,1)S(1)}, u32[]{:S(2)}) copy-start(bf16[256,1280]{1,0:T(8,128)(2,1)S(1)} %collective-permute-done.14.late_ref) | copy-start | bytes 1966084
  66.2 5.6 %copy-start.12 = (bf16[160,128]{1,0:T(8,128)(2,1)}, bf16[160,128]{1,0:T(8,128)(2,1)S(1)}, u32[]{:S(2)}) copy-start(bf16[160,128]{1,0:T(8,128)(2,1)S(1)} %get-tuple-element.86.refs_0_) | copy-start | bytes 122884
  66.2 5.6 %collective-permute-start.15 = (bf16[160,128]{1,0:T(8,128)(2,1)S(1)}, bf16[160,128]{1,0:T(8,128)(2,1)S(1)}, u32[]{:S(2)}, u32[]{:S(2)}) collective-permute-start(bf16[160,128]{1,0:T(8,128)(2,1)S(1)} %get-tuple-element.86.refs_0_), channel_id=1, source_target_pairs={{0,32},{32,0},{1,33},{33,1},{2,34},{34,2},{3,35},{35,3},{4,36},{36... | collective-permute-start | bytes 122888 | tf_op jit(solution)/shard_map/ppermute | solution.py:24
  71.8 0.6 copy-start.17
  77.5 6.1 %copy-start.9 = (bf16[160,256]{1,0:T(8,128)(2,1)S(1)}, bf16[160,256]{1,0:T(8,128)(2,1)}, u32[]{:S(2)}) copy-start(bf16[160,256]{1,0:T(8,128)(2,1)} %shard_map.101.refs_0_) | copy-start | bytes 245764
  77.5 23.0 %collective-permute-start.17 = (f16[320,1024]{1,0:T(8,128)(2,1)}, f16[320,1024]{1,0:T(8,128)(2,1)S(1)}, u32[]{:S(2)}, u32[]{:S(2)}) collective-permute-start(f16[320,1024]{1,0:T(8,128)(2,1)} %fusion.21), channel_id=1, source_target_pairs={{0,1},{1,0},{2,3},{3,2},{4,5},{5,4},{6,7},{7,6},{8,9},{9,8},{10,11... | collective-permute-start | bytes 1966088 | tf_op jit(solution)/shard_map/ppermute | solution.py:342
  78.7 24.9 %collective-permute-start.16 = (f16[320,1024]{1,0:T(8,128)(2,1)}, f16[320,1024]{1,0:T(8,128)(2,1)}, u32[]{:S(2)}, u32[]{:S(2)}) collective-permute-start(f16[320,1024]{1,0:T(8,128)(2,1)} %fusion.20), channel_id=1, source_target_pairs={{0,7},{1,2},{2,1},{3,4},{4,3},{5,6},{6,5},{7,0},{8,15},{9,10},{10,... | collective-permute-start | bytes 1966088 | tf_op jit(solution)/shard_map/ppermute | solution.py:342
  83.7 12.9 %collective-permute-start.18 = (bf16[160,256]{1,0:T(8,128)(2,1)S(1)}, bf16[160,256]{1,0:T(8,128)(2,1)S(1)}, u32[]{:S(2)}, u32[]{:S(2)}) collective-permute-start(bf16[160,256]{1,0:T(8,128)(2,1)S(1)} %copy-done.9), channel_id=1, source_target_pairs={{0,64},{64,0},{128,192},{192,128},{1,65},{65,1},{129,193},{193,129... | collective-permute-start | bytes 245768 | tf_op jit(solution)/shard_map/ppermute | solution.py:24
  85.2 12.8 %collective-permute-start.19 = (bf16[160,256]{1,0:T(8,128)(2,1)S(1)}, bf16[160,256]{1,0:T(8,128)(2,1)S(1)}, u32[]{:S(2)}, u32[]{:S(2)}) collective-permute-start(bf16[160,256]{1,0:T(8,128)(2,1)S(1)} %copy-done.9), channel_id=1, source_target_pairs={{0,128},{64,192},{128,0},{192,64},{1,129},{65,193},{129,1},{193,65... | collective-permute-start | bytes 245768 | tf_op jit(solution)/shard_map/ppermute | solution.py:24
  88.1 10.0 %collective-permute-start.20 = (bf16[160,256]{1,0:T(8,128)(2,1)S(1)}, bf16[160,256]{1,0:T(8,128)(2,1)S(1)}, u32[]{:S(2)}, u32[]{:S(2)}) collective-permute-start(bf16[160,256]{1,0:T(8,128)(2,1)S(1)} %copy-done.9), channel_id=1, source_target_pairs={{0,192},{64,128},{128,64},{192,0},{1,193},{65,129},{129,65},{193,1... | collective-permute-start | bytes 245768 | tf_op jit(solution)/shard_map/ppermute | solution.py:24
  96.5 1.6 copy-start.13
  96.5 41.0 %collective-permute-start.21 = (bf16[256,3712]{1,0:T(8,128)(2,1)}, bf16[256,3712]{1,0:T(8,128)(2,1)S(1)}, u32[]{:S(2)}, u32[]{:S(2)}) collective-permute-start(bf16[256,3712]{1,0:T(8,128)(2,1)} %shard_map.102), channel_id=1, source_target_pairs={{0,8},{8,0},{1,9},{9,1},{2,10},{10,2},{3,11},{11,3},{4,12},{12,4},... | collective-permute-start | bytes 5701640 | tf_op jit(solution)/shard_map/ppermute | solution.py:24
  98.1 0.6 copy-start.14
  98.1 0.6 copy-start.15
  103.6 5.4 %copy-start.5 = (bf16[160,1024]{1,0:T(8,128)(2,1)S(1)}, bf16[160,1024]{1,0:T(8,128)(2,1)}, u32[]{:S(2)}) copy-start(bf16[160,1024]{1,0:T(8,128)(2,1)} %shard_map.103.refs_0_) | copy-start | bytes 983044
  107.0 14.5 %collective-permute-start.22 = (f16[320,1024]{1,0:T(8,128)(2,1)}, f16[320,1024]{1,0:T(8,128)(2,1)S(1)}, u32[]{:S(2)}, u32[]{:S(2)}) collective-permute-start(f16[320,1024]{1,0:T(8,128)(2,1)} %fusion.23), channel_id=1, source_target_pairs={{0,1},{1,0},{2,3},{3,2},{4,5},{5,4},{6,7},{7,6},{8,9},{9,8},{10,11... | collective-permute-start | bytes 1966088 | tf_op jit(solution)/shard_map/ppermute | solution.py:342
  107.0 14.6 %collective-permute-start.23 = (f16[320,1024]{1,0:T(8,128)(2,1)}, f16[320,1024]{1,0:T(8,128)(2,1)}, u32[]{:S(2)}, u32[]{:S(2)}) collective-permute-start(f16[320,1024]{1,0:T(8,128)(2,1)} %fusion.22), channel_id=1, source_target_pairs={{0,7},{1,2},{2,1},{3,4},{4,3},{5,6},{6,5},{7,0},{8,15},{9,10},{10,... | collective-permute-start | bytes 1966088 | tf_op jit(solution)/shard_map/ppermute | solution.py:342
  109.0 9.8 %collective-permute-start.24 = (bf16[160,1024]{1,0:T(8,128)(2,1)S(1)}, bf16[160,1024]{1,0:T(8,128)(2,1)S(1)}, u32[]{:S(2)}, u32[]{:S(2)}) collective-permute-start(bf16[160,1024]{1,0:T(8,128)(2,1)S(1)} %copy-done.5), channel_id=1, source_target_pairs={{0,16},{16,0},{1,17},{17,1},{2,18},{18,2},{3,19},{19,3},{4,20},{20... | collective-permute-start | bytes 983048 | tf_op jit(solution)/shard_map/ppermute | solution.py:24
  109.0 7.6 %collective-permute-start.25 = (f32[160,64]{1,0:T(8,128)S(1)}, f32[160,64]{1,0:T(8,128)S(1)}, u32[]{:S(2)}, u32[]{:S(2)}) collective-permute-start(f32[160,64]{1,0:T(8,128)S(1)} %get-tuple-element.111), channel_id=1, source_target_pairs={{0,16},{16,0},{1,17},{17,1},{2,18},{18,2},{3,19},{19,3},{4,20},{20... | collective-permute-start | bytes 122888 | tf_op jit(solution)/shard_map/ppermute | solution.py:24
  116.6 0.6 copy-start.16
  118.8 0.8 copy-start.10
  121.5 7.4 %copy-start.7 = (f32[320,64]{1,0:T(8,128)S(1)}, f32[320,64]{1,0:T(8,128)}, u32[]{:S(2)}) copy-start(f32[320,64]{1,0:T(8,128)} %shard_map.105) | copy-start | bytes 245764
  126.5 16.9 %collective-permute-start.26 = (f16[320,1024]{1,0:T(8,128)(2,1)}, f16[320,1024]{1,0:T(8,128)(2,1)S(1)}, u32[]{:S(2)}, u32[]{:S(2)}) collective-permute-start(f16[320,1024]{1,0:T(8,128)(2,1)} %get-tuple-element.89), channel_id=1, source_target_pairs={{0,1},{1,0},{2,3},{3,2},{4,5},{5,4},{6,7},{7,6},{8,9},{9,8},{10,11... | collective-permute-start | bytes 1966088 | tf_op jit(solution)/shard_map/ppermute | solution.py:403
  127.5 17.9 %collective-permute-start.27 = (f16[320,1024]{1,0:T(8,128)(2,1)}, f16[320,1024]{1,0:T(8,128)(2,1)}, u32[]{:S(2)}, u32[]{:S(2)}) collective-permute-start(f16[320,1024]{1,0:T(8,128)(2,1)} %get-tuple-element.88), channel_id=1, source_target_pairs={{0,7},{1,2},{2,1},{3,4},{4,3},{5,6},{6,5},{7,0},{8,15},{9,10},{10,... | collective-permute-start | bytes 1966088 | tf_op jit(solution)/shard_map/ppermute | solution.py:403
  137.5 1.3 copy-start
Sparse Core Ops, SparseCore 0:
  9.8 76.4 all-gather.2
